TPU v7x, 32 devices: a whole 2x2x4 slice. The times are simulated.
32 devices in a mesh: group: 2 (over y), batch: 4 (over z), mp: 2 (over x), section: 2 (over core).
Axes of the slice: x: 2, y: 2, z: 4, core: 2. Of those that a mesh axis runs over, the one named last changes fastest.
Arguments:
- queries: bfloat16 [2, 192, 8192], P('section', ('group', 'batch'), 'mp'), parts along dimension 1, may hold values from -6 to 6
- new_keys: bfloat16 [2, 192, 1024], P('section', ('group', 'batch'), 'mp'), parts along dimension 1, may hold values from -6 to 6
- new_values: bfloat16 [2, 192, 1024], P('section', ('group', 'batch'), 'mp'), parts along dimension 1, may hold values from -6 to 6
- key_pages: bfloat16 [2, 768, 16, 1024], P('section', ('group', 'batch'), None, 'mp'), parts along dimension 1, may hold values from -6 to 6
- value_pages: bfloat16 [2, 768, 16, 1024], P('section', ('group', 'batch'), None, 'mp'), parts along dimension 1, may hold values from -6 to 6
- page_table: int32 [192, 4], P(('group', 'batch')), parts along dimension 0, may hold values from 0 to 95, as said below
- ancestry: int32 [192], P('group'), parts along dimension 0, may hold values from 0 to 95, as said below
- lengths: int32 [192], P('group'), parts along dimension 0, may hold values from 1 to 64, as said below
- step_rows: bfloat16 [8192, 4096], P(('group', 'batch', 'section'), 'mp'), parts along dimension 0, may hold values from -6 to 6
- norm_gain: float32 [4096], replicated, may hold values from 0.1 to 1.9
- head_weight: bfloat16 [4096, 4096], P(('batch', 'section'), 'mp'), may hold values from -0.09375 to 0.09375
- head_bias: float32 [4096], P('mp'), may hold values from -5 to 5
- class_weight: bfloat16 [4096, 2], P('mp'), may hold values from -0.125 to 0.125
- class_bias: float32 [2], replicated, may hold values from -4 to 4
Outputs:
- attention: bfloat16 [2, 192, 8192], P('section', ('group', 'batch'), 'mp'), parts along dimension 1
- log_odds: float32 [8192], P(('group', 'batch', 'section')), parts along dimension 0
There are 2 independent parts, one for each index of `group`. A program takes and returns all parts, laid end to end along the dimension named above; an argument that names none is the same for every part. Nothing has to cross between parts.
Inputs may be any that keep to these rules, and one draw needn't show every extreme that they name: The pages of the particles on one index of batch lie on that index; the page_table rows of those 24 particles name each of its 96 pages exactly once. Particle j belongs to problem j % 24, and ancestry[j] % 24 == j % 24. Particles j // 24 == d stand on index d of batch; the 24 slots on one index take at most 12 ancestors from any one index, and in every draw some index gives exactly 12 ancestors to the slots of every index. `lengths`: some particle has all 64 positions live in every draw.
All inputs are finite; a program needn't handle non-finite values.
Results may differ from a plain program's by a relative error of at most 0.0043.
Values may be sent and summed in bfloat16 or wider, within the bound.
No kernel may reach another device: no remote copies, remote signals or barrier semaphores. Data moves between devices by JAX's collectives and lax.ppermute only.
A program may use at most 64 MiB of HBM per device.

v0:
```python
import jax
import jax.numpy as jnp
from jax import lax
from jax.sharding import PartitionSpec as P

HD = 128


def cache_score_terms(query_head_count, cached_key_rows, cache_values, live_lengths):
    score_scale = 1.0 / HD**0.5
    attention_scores = (
        jnp.einsum(
            "bkgd,btkd->bkgt", query_head_count, cached_key_rows, preferred_element_type=jnp.float32
        )
        * score_scale
    )
    live_mask = jnp.arange(cached_key_rows.shape[1])[None, :] < live_lengths[:, None]
    attention_scores = jnp.where(live_mask[:, None, None, :], attention_scores, -1e30)
    top_score = jnp.max(attention_scores, axis=-1)
    weights = jnp.exp(attention_scores - top_score[..., None])
    denominator = jnp.sum(weights, axis=-1)
    numerator = jnp.einsum(
        "bkgt,btkd->bkgd",
        weights.astype(jnp.bfloat16),
        cache_values,
        preferred_element_type=jnp.float32,
    )
    return (numerator, top_score, denominator)


def finish(numerator, top_score, denominator, query_head_count, particle_key_rows, own_values):
    score_scale = 1.0 / HD**0.5
    own_score = (
        jnp.einsum(
            "vnrc,vnc->vnr", query_head_count, particle_key_rows, preferred_element_type=jnp.float32
        )
        * score_scale
    )
    own_weight = jnp.exp(own_score - top_score)
    result = (numerator + own_weight[..., None] * own_values.astype(jnp.float32)[:, :, None, :]) / (
        denominator + own_weight
    )[..., None]
    return result.astype(jnp.bfloat16)


def per_device(
    queries,
    new_keys,
    new_values,
    key_pages,
    value_pages,
    page_table,
    ancestry,
    lengths,
    step_rows,
    norm_gain,
    head_weight,
    head_bias,
    class_weight,
    class_bias,
):
    layer_count = queries.shape[0]
    slot_count = page_table.shape[0]
    page_count = page_table.shape[1]
    page_size = key_pages.shape[2]
    kv_width = key_pages.shape[3]
    kv_local = kv_width // HD
    group_size = queries.shape[2] // kv_width
    context = page_count * page_size
    device_count = lax.axis_size("batch")
    my_index = lax.axis_index("batch")
    capacity = max(2, (2 * slot_count + device_count - 1) // device_count)
    source = (ancestry // slot_count).reshape(device_count, slot_count)
    positions = jnp.arange(slot_count)
    earlier = positions[None, :] < positions[:, None]
    same_source = source[:, :, None] == source[:, None, :]
    source_rank = jnp.sum(same_source & earlier[None, :, :], axis=2)
    slot_ids = jnp.arange(capacity)
    served = (source == my_index)[:, None, :] & (source_rank[:, None, :] == slot_ids[None, :, None])
    served_slot = jnp.sum(jnp.where(served, positions[None, None, :], 0), axis=2)
    own_source = lax.dynamic_index_in_dim(source, my_index, 0, keepdims=False)
    own_rank = lax.dynamic_index_in_dim(source_rank, my_index, 0, keepdims=False)
    flat_index = own_source * capacity + own_rank
    local_lengths = lax.dynamic_slice_in_dim(lengths, my_index * slot_count, slot_count)
    query_head_count = queries.reshape(layer_count * slot_count, kv_local, group_size, HD)
    particle_key_rows = new_keys.reshape(layer_count * slot_count, kv_local, HD)
    own_values = new_values.reshape(layer_count * slot_count, kv_local, HD)
    served_pages = page_table[served_slot]
    wanted = (own_source[None, None, :] == jnp.arange(device_count)[:, None, None]) & (
        own_rank[None, None, :] == slot_ids[None, :, None]
    )
    request_slot = jnp.sum(jnp.where(wanted, positions[None, None, :], 0), axis=2)
    outgoing_queries = jnp.take(queries, request_slot, axis=1)
    arrived_queries = lax.all_to_all(
        outgoing_queries, "batch", split_axis=1, concat_axis=1, tiled=True
    )
    batch_rows = layer_count * device_count * capacity
    served_heads = arrived_queries.reshape(batch_rows, kv_local, group_size, HD)
    served_keys = key_pages[:, served_pages].reshape(batch_rows, context, kv_local, HD)
    served_values = value_pages[:, served_pages].reshape(batch_rows, context, kv_local, HD)
    served_lengths = jnp.tile(
        jnp.take(local_lengths, served_slot).reshape(device_count * capacity), layer_count
    )
    numerator, top_score, denominator = cache_score_terms(
        served_heads, served_keys, served_values, served_lengths
    )
    numerator = numerator.reshape(layer_count, device_count, capacity, kv_local * group_size * HD)
    top_score = top_score.reshape(layer_count, device_count, capacity, kv_local * group_size)
    denominator = denominator.reshape(layer_count, device_count, capacity, kv_local * group_size)
    returned = (
        lax.all_to_all(numerator, "batch", split_axis=1, concat_axis=1, tiled=True),
        lax.all_to_all(top_score, "batch", split_axis=1, concat_axis=1, tiled=True),
        lax.all_to_all(denominator, "batch", split_axis=1, concat_axis=1, tiled=True),
    )

    def pick_part(received, trailing):
        received = received.reshape((layer_count, device_count * capacity) + trailing)
        return jnp.take(received, flat_index, axis=1).reshape(
            (layer_count * slot_count,) + trailing
        )

    numerator = pick_part(returned[0], (kv_local, group_size, HD))
    top_score = pick_part(returned[1], (kv_local, group_size))
    denominator = pick_part(returned[2], (kv_local, group_size))
    result = finish(
        numerator, top_score, denominator, query_head_count, particle_key_rows, own_values
    )
    attention = result.reshape(layer_count, slot_count, kv_local * group_size * HD)
    full_rows = lax.all_gather(step_rows, "mp", axis=1, tiled=True)
    row_values = full_rows.astype(jnp.float32)
    power = jnp.mean(row_values * row_values, axis=1, keepdims=True)
    normed = (row_values * lax.rsqrt(power + 1e-06) * norm_gain).astype(jnp.bfloat16)
    projected = jnp.dot(
        normed,
        lax.all_gather(head_weight, ("batch", "section"), axis=0, tiled=True),
        preferred_element_type=jnp.float32,
    )
    hidden = jnp.maximum(projected + head_bias, 0.0).astype(jnp.bfloat16)
    partial_logits = jnp.dot(hidden, class_weight, preferred_element_type=jnp.float32)
    logits = lax.psum(partial_logits, "mp") + class_bias
    log_odds = logits[:, 1] - logits[:, 0]
    return (attention, log_odds)


def solution(mesh):
    placed = (
        P("section", ("group", "batch"), "mp"),
        P("section", ("group", "batch"), "mp"),
        P("section", ("group", "batch"), "mp"),
        P("section", ("group", "batch"), None, "mp"),
        P("section", ("group", "batch"), None, "mp"),
        P(("group", "batch"), None),
        P("group"),
        P("group"),
        P(("group", "batch", "section"), "mp"),
        P(),
        P(("batch", "section"), "mp"),
        P("mp"),
        P("mp", None),
        P(),
    )
    return jax.shard_map(
        per_device,
        mesh=mesh,
        in_specs=placed,
        out_specs=(P("section", ("group", "batch"), "mp"), P(("group", "batch", "section"))),
        check_vma=False,
    )
```

profile of v0, /device:TPU:0, one launch (start us, length us, event | category | flops | bytes accessed | tf_op | source)
XLA Modules:
  0.0 253.0 jit_solution(18221568556298894525)
XLA Ops:
  7.2 0.7 all-gather.3.cloned.1.call-update
  8.0 0.7 all-gather.5.cloned.1.call-update
  8.8 0.2 convert_reduce_fusion
  9.0 0.5 compare_and_fusion.1
  9.6 0.3 select_reduce_fusion
  9.9 0.1 copy.53
  10.0 0.1 copy.52
  10.1 0.1 reshape.400
  10.2 0.8 gather_fusion.1
  11.0 0.1 reshape.397
  11.1 0.9 select_bitcast_fusion
  12.0 6.3 %all-to-all-start = ((bf16[1,4,12,4096]{3,2,0,1:T(8,128)(2,1)}), bf16[1,4,12,4096]{3,2,0,1:T(8,128)(2,1)}, u32[]{:S(2)}, u32[]{:S(2)}) async-start(bf16[1,4,12,4096]{3,2,0,1:T(8,128)(2,1)} %select_bitcast_fusion), calls=%async_computation | async-start | bytes 1048576 | tf_op jit(solution)/shard_map/all_to_all | solution.py:94
  18.3 0.3 select_reduce_fusion.1
  18.6 0.1 copy.50
  18.7 0.1 reshape.390
  18.8 0.1 copy.55
  18.9 0.6 gather_fusion.2
  19.6 0.1 gather.34
  19.8 0.8 gather_fusion
  20.6 0.1 copy.57
  20.7 0.1 reshape.418
  20.9 2.7 %gather_fusion.3 = bf16[192,16,512]{2,1,0:T(8,128)(2,1)} fusion(bf16[96,16,512]{2,1,0:T(8,128)(2,1)S(1)} %bitcast.71, s32[1024]{0:T(1024)S(1)} %pad_clamp_fusion.2), kind=kCustom, calls=%fused_computation.5 | custom fusion | bytes 6292224 | tf_op jit(solution)/shard_map/gather | solution.py:99
  23.6 5.6 %reshape.355 = bf16[48,64,4,128]{3,2,1,0:T(4,128)(2,1)} reshape(bf16[192,16,512]{2,1,0:T(8,128)(2,1)} %gather_fusion.3) | data formatting | bytes 6291456 | tf_op jit(solution)/shard_map/reshape | solution.py:99
  29.3 3.6 %all-to-all-done = bf16[1,4,12,4096]{3,2,0,1:T(8,128)(2,1)} async-done(((bf16[1,4,12,4096]{3,2,0,1:T(8,128)(2,1)}), bf16[1,4,12,4096]{3,2,0,1:T(8,128)(2,1)}, u32[]{:S(2)}, u32[]{:S(2)}) %all-to-all-start) | async-done | bytes 393248 | tf_op jit(solution)/shard_map/all_to_all | solution.py:94
  32.9 2.1 reshape.354
  35.0 3.9 %fusion.35 = (f32[48,4,8]{2,1,0:T(4,128)S(1)}, f32[48,4,8,64]{3,2,1,0:T(8,128)S(1)}) fusion(bf16[48,4,8,128]{3,2,1,0:T(8,128)(2,1)} %reshape.354, bf16[48,64,4,128]{3,2,1,0:T(4,128)(2,1)} %reshape.355, pred[48,64]{1,0:T(8,128)(4,1)S(1)} %iota_compare_fusion.1), kind=kOutput, calls=%fused_computation.71 | convolution fusion | flops 25459200 | bytes 3941376 | tf_op jit(solution)/shard_map/bkgd,btkd->bkgt/dot_general | solution.py:12
  38.9 0.9 copy-done.3
  39.8 0.6 fusion.22
  40.4 0.7 reshape.479
  41.1 0.6 broadcast.324
  41.7 1.5 reduce.4
  43.2 0.7 reshape.484
  43.8 3.2 %all-to-all-start.3 = ((f32[4,1,384]{2,1,0:T(1,128)}), f32[4,1,384]{2,1,0:T(1,128)S(1)}, u32[]{:S(2)}, u32[]{:S(2)}) async-start(f32[4,1,384]{2,1,0:T(1,128)} %reshape.484), calls=%async_computation.3 | async-start | bytes 12288 | tf_op jit(solution)/shard_map/all_to_all | solution.py:113
  47.1 2.7 %gather_fusion.4 = bf16[192,16,512]{2,1,0:T(8,128)(2,1)} fusion(bf16[96,16,512]{2,1,0:T(8,128)(2,1)S(1)} %bitcast.74, s32[1024]{0:T(1024)S(1)} %pad_clamp_fusion.2), kind=kCustom, calls=%fused_computation.6 | custom fusion | bytes 6292224 | tf_op jit(solution)/shard_map/gather | solution.py:100
  49.8 5.6 %reshape.356 = bf16[48,64,4,128]{3,2,1,0:T(4,128)(2,1)} reshape(bf16[192,16,512]{2,1,0:T(8,128)(2,1)} %gather_fusion.4) | data formatting | bytes 6291456 | tf_op jit(solution)/shard_map/reshape | solution.py:100
  55.4 0.1 reshape.478
  55.6 0.7 reduce.6
  56.3 0.7 reshape.482
  57.0 5.0 %all-to-all-start.2 = ((f32[4,1,384]{2,1,0:T(1,128)}), f32[4,1,384]{2,1,0:T(1,128)S(1)}, u32[]{:S(2)}, u32[]{:S(2)}) async-start(f32[4,1,384]{2,1,0:T(1,128)} %reshape.482), calls=%async_computation.2 | async-start | bytes 12288 | tf_op jit(solution)/shard_map/all_to_all | solution.py:112
  62.1 3.8 %fusion.9 = f32[48,4,8,128]{3,2,1,0:T(8,128)} fusion(bf16[48,64,4,128]{3,2,1,0:T(4,128)(2,1)} %reshape.356, f32[48,4,8,64]{3,2,1,0:T(8,128)S(1)} %copy-done.4, f32[48,4,8]{2,1,0:T(4,128)S(1)} %get-tuple-element.9), kind=kOutput, calls=%fused_computation.17 | convolution fusion | flops 25362432 | bytes 4331520 | tf_op jit(solution)/shard_map/bkgt,btkd->bkgd/dot_general | solution.py:22
  65.8 1.8 all-to-all-done.2
  67.6 3.7 %all-to-all-start.1 = ((f32[1,4,12,4096]{3,0,2,1:T(1,128)}), f32[1,4,12,4096]{3,0,2,1:T(1,128)S(1)}, u32[]{:S(2)}, u32[]{:S(2)}) async-start(f32[1,4,12,4096]{3,0,2,1:T(1,128)} %bitcast.8), calls=%async_computation.1 | async-start | bytes 1572864 | tf_op jit(solution)/shard_map/all_to_all | solution.py:111
  71.5 0.2 fusion.36
  71.7 0.7 reduce.7
  72.4 0.1 reshape.483
  72.5 0.7 reduce.5
  73.2 0.1 reshape.485
  73.4 0.1 reshape.464
  73.6 0.1 reshape.460
  73.7 0.6 gather_fusion.7
  74.3 0.6 gather_fusion.6
  74.9 0.1 bitcast_add_fusion
  75.0 0.2 div.30
  75.3 0.9 broadcast_multiply_fusion
  76.2 1.1 mul.82
  77.3 27.6 %all-to-all-done.1 = f32[1,4,12,4096]{3,0,2,1:T(1,128)S(1)} async-done(((f32[1,4,12,4096]{3,0,2,1:T(1,128)}), f32[1,4,12,4096]{3,0,2,1:T(1,128)S(1)}, u32[]{:S(2)}, u32[]{:S(2)}) %all-to-all-start.1) | async-done | bytes 786464 | tf_op jit(solution)/shard_map/all_to_all | solution.py:111
  104.9 1.3 gather_fusion.5
  106.3 1.1 gather.38
  107.4 0.8 divide_convert_fusion
  108.2 3.2 %fusion = f32[512]{0:T(512)S(1)} fusion(bf16[512,4096]{1,0:T(8,128)(2,1)} %all-gather.3.cloned.1.call-done), kind=kLoop, calls=%fused_computation.10 | loop fusion | flops 6290944 | bytes 4196352 | tf_op jit(solution)/shard_map/reduce_sum | solution.py:131
  111.4 115.2 %all-gather.5.cloned.1.call-done = bf16[4096,2048]{1,0:T(8,128)(2,1)} async-done(((bf16[512,2048]{1,0:T(8,128)(2,1)}), bf16[4096,2048]{1,0:T(8,128)(2,1)}) %all-gather.5.cloned.1.call-update) | async-done | bytes 16777232 | tf_op jit(solution)/shard_map/all_gather | solution.py:135
  226.5 14.1 %fusion.20 = f32[512,2]{0,1:T(2,128)S(1)} fusion(bf16[2048,2]{0,1:T(2,128)(2,1)S(1)} %copy-done.11, bf16[4096,2048]{1,0:T(8,128)(2,1)} %all-gather.5.cloned.1.call-done, bf16[512,4096]{1,0:T(8,128)(2,1)} %all-gather.3.cloned.1.call-done, f32[4096]{0:T(1024)S(1)} %copy-done.10, f32[512]{0:T(512)S(1)} %add_rsqrt_fusion, f32[2048]{0:T(1024)S(1)} %copy-done.12), kind=kOutput, calls=%fused_computation.23 | convolution fusion | flops 8605663232 | bytes 21010432 | tf_op jit(solution)/shard_map/dot_general | solution.py:139
  240.6 4.9 %psum.7 = f32[512,2]{0,1:T(2,128)S(1)} all-reduce(f32[512,2]{0,1:T(2,128)S(1)} %fusion.20), channel_id=1, replica_groups=mesh['group'=2,'batch'=4,'mp'=2,'section'=2] {'mp'}, use_global_device_ids=true, to_apply=%region_6.8 | all-reduce | flops 1024 | bytes 8192 | tf_op jit(solution)/shard_map/psum | solution.py:140
  245.6 0.6 slice_subtract_fusion
  (62 shorter events, 1.0 us)
Async XLA Ops:
  7.2 13.7 %copy-start = (bf16[1,96,16,512]{3,2,1,0:T(8,128)(2,1)S(1)}, bf16[1,96,16,512]{3,2,1,0:T(8,128)(2,1)}, u32[]{:S(2)}) copy-start(bf16[1,96,16,512]{3,2,1,0:T(8,128)(2,1)} %param.19) | copy-start | bytes 4718596
  7.2 1.5 copy-start.13
  7.2 3.0 %copy-start.1 = (bf16[1,24,4096]{2,1,0:T(8,128)(2,1)S(1)}, bf16[1,24,4096]{2,1,0:T(8,128)(2,1)}, u32[]{:S(2)}) copy-start(bf16[1,24,4096]{2,1,0:T(8,128)(2,1)} %param.16) | copy-start | bytes 589828
  7.2 101.0 %all-gather.3.cloned.1.call-start = ((), (), s32[]{:S(2)}) async-start(), calls=%async_computation.4 | async-start | bytes 6291456 | tf_op jit(solution)/shard_map/all_gather | solution.py:129
  7.9 218.6 %all-gather.5.cloned.1.call-start = ((), (), s32[]{:S(2)}) async-start(), calls=%async_computation.5 | async-start | bytes 18874368 | tf_op jit(solution)/shard_map/all_gather | solution.py:135
  10.2 8.6 %copy-start.7 = (s32[24,4]{0,1:T(4,128)S(1)}, s32[24,4]{0,1:T(4,128)}, u32[]{:S(2)}) copy-start(s32[24,4]{0,1:T(4,128)} %param.21) | copy-start | bytes 1156
  10.2 9.6 %copy-start.14 = (s32[96]{0:T(128)S(1)}, s32[96]{0:T(128)}, u32[]{:S(2)}) copy-start(s32[96]{0:T(128)} %param.23) | copy-start | bytes 1156
  12.0 20.9 %all-to-all-start = ((bf16[1,4,12,4096]{3,2,0,1:T(8,128)(2,1)}), bf16[1,4,12,4096]{3,2,0,1:T(8,128)(2,1)}, u32[]{:S(2)}, u32[]{:S(2)}) async-start(bf16[1,4,12,4096]{3,2,0,1:T(8,128)(2,1)} %select_bitcast_fusion), calls=%async_computation | async-start | bytes 1048576 | tf_op jit(solution)/shard_map/all_to_all | solution.py:94
  29.3 17.8 %copy-start.2 = (bf16[1,96,16,512]{3,2,1,0:T(8,128)(2,1)S(1)}, bf16[1,96,16,512]{3,2,1,0:T(8,128)(2,1)}, u32[]{:S(2)}) copy-start(bf16[1,96,16,512]{3,2,1,0:T(8,128)(2,1)} %param.20) | copy-start | bytes 4718596
  38.9 0.9 copy-start.3
  43.8 13.1 %all-to-all-start.3 = ((f32[4,1,384]{2,1,0:T(1,128)}), f32[4,1,384]{2,1,0:T(1,128)S(1)}, u32[]{:S(2)}, u32[]{:S(2)}) async-start(f32[4,1,384]{2,1,0:T(1,128)} %reshape.484), calls=%async_computation.3 | async-start | bytes 12288 | tf_op jit(solution)/shard_map/all_to_all | solution.py:113
  49.8 12.2 %copy-start.4 = (f32[48,4,8,64]{3,2,1,0:T(8,128)S(1)}, f32[48,4,8,64]{3,2,1,0:T(8,128)}, u32[]{:S(2)}) copy-start(f32[48,4,8,64]{3,2,1,0:T(8,128)} %copy-done.3) | copy-start | bytes 1179652
  57.0 10.6 %all-to-all-start.2 = ((f32[4,1,384]{2,1,0:T(1,128)}), f32[4,1,384]{2,1,0:T(1,128)S(1)}, u32[]{:S(2)}, u32[]{:S(2)}) async-start(f32[4,1,384]{2,1,0:T(1,128)} %reshape.482), calls=%async_computation.2 | async-start | bytes 12288 | tf_op jit(solution)/shard_map/all_to_all | solution.py:112
  62.0 9.3 %copy-start.5 = (bf16[1,24,512]{2,1,0:T(8,128)(2,1)S(1)}, bf16[1,24,512]{2,1,0:T(8,128)(2,1)}, u32[]{:S(2)}) copy-start(bf16[1,24,512]{2,1,0:T(8,128)(2,1)} %param.17) | copy-start | bytes 73732
  62.0 9.3 %copy-start.6 = (bf16[1,24,512]{2,1,0:T(8,128)(2,1)S(1)}, bf16[1,24,512]{2,1,0:T(8,128)(2,1)}, u32[]{:S(2)}) copy-start(bf16[1,24,512]{2,1,0:T(8,128)(2,1)} %param.18) | copy-start | bytes 73732
  62.0 9.4 %copy-start.8 = (s32[24]{0:T(128)S(1)}, s32[24]{0:T(128)}, u32[]{:S(2)}) copy-start(s32[24]{0:T(128)} %get-tuple-element.6) | copy-start | bytes 292
  67.6 37.3 %all-to-all-start.1 = ((f32[1,4,12,4096]{3,0,2,1:T(1,128)}), f32[1,4,12,4096]{3,0,2,1:T(1,128)S(1)}, u32[]{:S(2)}, u32[]{:S(2)}) async-start(f32[1,4,12,4096]{3,0,2,1:T(1,128)} %bitcast.8), calls=%async_computation.1 | async-start | bytes 1572864 | tf_op jit(solution)/shard_map/all_to_all | solution.py:111
  106.3 120.3 %copy-start.10 = (f32[4096]{0:T(1024)S(1)}, f32[4096]{0:T(1024)}, u32[]{:S(2)}) copy-start(f32[4096]{0:T(1024)} %param.25) | copy-start | bytes 49156
  106.3 120.3 %copy-start.11 = (bf16[2048,2]{0,1:T(2,128)(2,1)S(1)}, bf16[2048,2]{0,1:T(2,128)(2,1)}, u32[]{:S(2)}) copy-start(bf16[2048,2]{0,1:T(2,128)(2,1)} %param.28) | copy-start | bytes 24580
  106.3 120.3 %copy-start.12 = (f32[2048]{0:T(1024)S(1)}, f32[2048]{0:T(1024)}, u32[]{:S(2)}) copy-start(f32[2048]{0:T(1024)} %param.27) | copy-start | bytes 24580
  111.4 134.2 %copy-start.9 = (f32[2]{0:T(128)S(1)}, f32[2]{0:T(128)}, u32[]{:S(2)}) copy-start(f32[2]{0:T(128)} %param.29) | copy-start | bytes 28
Sparse Core Ops, SparseCore 0:
  9.6 59.4 all-gather.2
  70.7 155.8 all-gather.4
where the time goes:
time: 254 us; the launch traced here: 253 us
  waiting for transfers between devices  150 us (59%)
  local copies, waits for them, and re-layouts  31.5 us (12%)
  matrix products  21.9 us (9%)
  starting transfers between devices  18.4 us (7%)
  between operations  14.4 us (6%)
  other arithmetic  12.3 us (5%)
  blocking collectives  4.95 us (2%)
    all_gather x1, waiting for transfers between devices, per_device(): lax.all_gather(head_weight, ('batch', 'section'), axis=0, tiled=True)  115 us
    all_to_all x1, waiting for transfers between devices, per_device(): lax.all_to_all(numerator, 'batch', split_axis=1, concat_axis=1, tiled=True)  27.6 us
    dot_general x1, matrix products, per_device(): jnp.dot(hidden, class_weight, preferred_element_type=jnp.float32)  14.1 us
    all_to_all x1, starting transfers between devices, per_device(): lax.all_to_all(outgoing_queries, 'batch', split_axis=1, concat_axis=1, ti...  6.32 us
    reshape x1, local copies, waits for them, and re-layouts, per_device(): key_pages[:, served_pages].reshape(batch_rows, context, kv_local, HD)  5.62 us
    reshape x1, local copies, waits for them, and re-layouts, per_device(): value_pages[:, served_pages].reshape(batch_rows, context, kv_local, HD)  5.6 us
  transfers between devices with their start and end apart: 6, of which 4 were waited for; matrix products, arithmetic and copies ran while one was open for 20% of the time, Pallas kernels for 0%

commit v1 on v0

v1 whole, which is shorter than its diff:
```python
import functools

import jax
import jax.numpy as jnp
from jax import lax
from jax.experimental import pallas as pl
from jax.experimental.pallas import tpu as pltpu
from jax.sharding import PartitionSpec as P

HD = 128
ANY = pl.BlockSpec(memory_space=pl.ANY)
VMEM = pl.BlockSpec(memory_space=pltpu.VMEM)
SMEM = pl.BlockSpec(memory_space=pltpu.SMEM)


def shift_pairs(count, step):
    return [(i, (i + step) % count) for i in range(count)]


def ring_order(count):
    return [0] + list(range(1, count, 2)) + [i for i in range(count - 1, 0, -1) if i % 2 == 0]


def attention_kernel(particle, page_table, lengths, blob, key_pages, value_pages, out, *, kv_local, unroll):
    slots = blob.shape[0]
    heads = out.shape[1]
    group_size = heads // kv_local
    pages = page_table.shape[1]
    context = pages * key_pages.shape[1]
    score_scale = 1.0 / HD**0.5
    lanes_kv = lax.broadcasted_iota(jnp.int32, (heads, kv_local * HD), 1) // HD
    rows_kv = lax.broadcasted_iota(jnp.int32, (heads, kv_local * HD), 0) // group_size
    diagonal = lanes_kv == rows_kv
    positions = lax.broadcasted_iota(jnp.int32, (heads, context), 1)

    def one(slot):
        ancestor = particle[slot]
        length = lengths[slot]
        rows = blob[slot]
        query = rows[:heads].astype(jnp.float32)
        own_key = rows[heads : heads + kv_local].astype(jnp.float32)
        own_value = rows[heads + kv_local :].astype(jnp.float32)

        def spread(x):
            return jnp.broadcast_to(x[:, None, :], (kv_local, group_size, HD)).reshape(heads, HD)

        wide = jnp.concatenate([query] * kv_local, axis=1)
        wide = jnp.where(diagonal, wide, 0.0).astype(jnp.bfloat16)
        keys = jnp.concatenate([key_pages[page_table[ancestor, i]] for i in range(pages)], axis=0)
        values = jnp.concatenate([value_pages[page_table[ancestor, i]] for i in range(pages)], axis=0)
        scores = lax.dot_general(
            wide, keys, (((1,), (1,)), ((), ())), preferred_element_type=jnp.float32
        ) * score_scale
        scores = jnp.where(positions < length, scores, -1e30)
        top = jnp.max(scores, axis=1, keepdims=True)
        weights = jnp.exp(scores - top)
        total = jnp.sum(weights, axis=1, keepdims=True)
        mixed = jnp.dot(weights.astype(jnp.bfloat16), values, preferred_element_type=jnp.float32)
        numerator = jnp.concatenate(
            [
                mixed[k * group_size : (k + 1) * group_size, k * HD : (k + 1) * HD]
                for k in range(kv_local)
            ],
            axis=0,
        )
        own_score = jnp.sum(query * spread(own_key), axis=1, keepdims=True) * score_scale
        own = jnp.exp(own_score - top)
        result = (numerator + own * spread(own_value)) / (total + own)
        out[slot] = result.astype(jnp.bfloat16)

    def body(i, carry):
        for u in range(unroll):
            one(i * unroll + u)
        return carry

    lax.fori_loop(0, slots // unroll, body, 0)


def serve(particle, page_table, lengths, blob, key_pages, value_pages):
    slots = blob.shape[0]
    kv_local = key_pages.shape[2] // HD
    heads = blob.shape[1] - 2 * kv_local
    unroll = 4 if slots % 4 == 0 else 1
    return pl.pallas_call(
        functools.partial(attention_kernel, kv_local=kv_local, unroll=unroll),
        out_shape=jax.ShapeDtypeStruct((slots, heads, HD), jnp.bfloat16),
        in_specs=[SMEM, SMEM, SMEM, VMEM, VMEM, VMEM],
        out_specs=VMEM,
        compiler_params=pltpu.CompilerParams(vmem_limit_bytes=24 << 20),
        cost_estimate=pl.CostEstimate(flops=20_000_000, bytes_accessed=6_000_000, transcendentals=100_000),
    )(particle, page_table, lengths, blob, key_pages, value_pages)


def exchange(blocks, axis):
    count = lax.axis_size(axis)
    if count <= 8:
        return [blocks[0]] + [
            lax.ppermute(blocks[k], axis, shift_pairs(count, k)) for k in range(1, count)
        ]
    me = lax.axis_index(axis)
    stacked = jnp.stack(blocks)
    order = (jnp.arange(count) - me) % count
    arrived = lax.all_to_all(stacked[order], axis, split_axis=0, concat_axis=0, tiled=True)
    back = (me - jnp.arange(count)) % count
    arrived = arrived[back]
    return [arrived[k] for k in range(count)]


def attend(queries, new_keys, new_values, key_pages, value_pages, page_table, ancestry, lengths):
    slot_count, page_count = page_table.shape
    kv_local = key_pages.shape[3] // HD
    heads = queries.shape[2] // HD
    count = lax.axis_size("batch")
    me = lax.axis_index("batch")
    capacity = max(2, (2 * slot_count + count - 1) // count)
    source = (ancestry // slot_count).reshape(count, slot_count)
    local = (ancestry % slot_count).reshape(count, slot_count)
    positions = jnp.arange(slot_count)
    earlier = positions[None, :] < positions[:, None]
    slot_ids = jnp.arange(capacity)
    shifts = jnp.arange(count)

    own_source = lax.dynamic_index_in_dim(source, me, 0, keepdims=False)
    own_rank = jnp.sum((own_source[:, None] == own_source[None, :]) & earlier, axis=1)
    wanted = (own_source[None, None, :] == ((me + shifts) % count)[:, None, None]) & (
        own_rank[None, None, :] == slot_ids[None, :, None]
    )
    wanted = wanted.reshape(count * capacity, slot_count).astype(jnp.bfloat16)
    rows = jnp.concatenate([queries[0], new_keys[0], new_values[0]], axis=1)
    outgoing = jnp.dot(wanted, rows, preferred_element_type=jnp.float32).astype(jnp.bfloat16)
    outgoing = outgoing.reshape(count, capacity, heads + 2 * kv_local, HD)
    arrived = exchange([outgoing[k] for k in range(count)], "batch")

    behind = (me - shifts) % count
    served_source = jnp.take(source, behind, axis=0)
    served_local = jnp.take(local, behind, axis=0)
    match = served_source == me
    rank = jnp.sum(match[:, None, :] & earlier[None], axis=2)
    served = match[:, None, :] & (rank[:, None, :] == slot_ids[None, :, None])
    particle = jnp.sum(jnp.where(served, served_local[:, None, :], 0), axis=2).reshape(-1)
    local_lengths = lax.dynamic_slice_in_dim(lengths, me * slot_count, slot_count)
    served_lengths = jnp.sum(
        jnp.where(particle[:, None] == positions[None, :], local_lengths[None, :], 0), axis=1
    )
    blob = jnp.concatenate(arrived, axis=0)
    result = serve(particle, page_table, served_lengths, blob, key_pages[0], value_pages[0])
    result = result.reshape(count, capacity, heads, HD)
    returned = exchange([result[(-k) % count] for k in range(count)], "batch")
    returned = jnp.concatenate([returned[(-k) % count] for k in range(count)], axis=0)
    returned = returned.reshape(count * capacity, heads * HD)
    attention = lax.dot_general(
        wanted, returned, (((0,), (0,)), ((), ())), preferred_element_type=jnp.float32
    ).astype(jnp.bfloat16)
    return attention[None]


def gemm_kernel(*refs, parts, chunks, own_rows, has_acc, final, tile):
    refs = list(refs)
    part_of, offset_of, column = refs[:3]
    del refs[:3]
    halves = [refs[:parts], refs[parts : 2 * parts]]
    del refs[: 2 * parts]
    weights = refs[: len(chunks)]
    del refs[: len(chunks)]
    acc_in = refs.pop(0) if has_acc else None
    bias = class_weight = None
    if final:
        bias, class_weight = refs[:2]
        del refs[:2]
    out = refs.pop(0)
    x_v, w_v, acc_v, sems, acc_sem = refs
    rows = halves[0][0].shape[0]
    width = acc_v.shape[1]
    starts = [sum(chunks[:i]) for i in range(len(chunks))]

    def copies(i):
        depth = chunks[i]
        offset = pl.multiple_of(offset_of[i], 128)
        found = []
        for r in range(2):
            for p in range(parts):
                found.append(
                    (
                        p,
                        pltpu.make_async_copy(
                            halves[r][p].at[:, pl.ds(offset, depth)],
                            x_v.at[pl.ds(r * rows, rows), pl.ds(starts[i], depth)],
                            sems.at[i, r],
                        ),
                    )
                )
        source = weights[i]
        if source.shape[1] != width:
            source = source.at[:, pl.ds(pl.multiple_of(column[0], 128), width)]
        return found, pltpu.make_async_copy(source, w_v.at[pl.ds(starts[i], depth)], sems.at[i, 2])

    if has_acc:
        acc_copy = pltpu.make_async_copy(acc_in, acc_v, acc_sem)
        acc_copy.start()
    for i in range(len(chunks)):
        found, weight = copies(i)
        weight.start()
        for p, copy in found:
            pl.when(part_of[i] == p)(copy.start)
    groups = []
    i = 0
    while i < len(chunks):
        j, depth = i, 0
        while j < len(chunks) and depth < 1024:
            depth += chunks[j]
            j += 1
        groups.append((i, j))
        i = j
    for g, (first, last) in enumerate(groups):
        for i in range(first, last):
            found, weight = copies(i)
            weight.wait()
            for r in range(2):
                found[r * parts][1].wait()
        if g == 0 and has_acc:
            acc_copy.wait()
        k0 = starts[first]
        k1 = starts[last - 1] + chunks[last - 1]
        fresh = g == 0 and not has_acc

        def body(m, carry):
            at = pl.ds(pl.multiple_of(m * tile, tile), tile)
            product = jnp.dot(x_v[at, k0:k1], w_v[k0:k1, :], preferred_element_type=jnp.float32)
            total = product if fresh else acc_v[at, :] + product
            if final and g == len(groups) - 1:
                hidden = jnp.maximum(total + bias[...], 0.0).astype(jnp.bfloat16)
                out[:, at] = lax.dot_general(
                    class_weight[...], hidden, (((1,), (1,)), ((), ())), preferred_element_type=jnp.float32
                )
            elif g == len(groups) - 1:
                out[at, :] = total
            else:
                acc_v[at, :] = total
            return carry

        lax.fori_loop(0, 2 * rows // tile, body, 0)


def gemm(part_of, offset_of, column, halves, weights, acc=None, tail=None):
    parts = len(halves[0])
    rows = halves[0][0].shape[0]
    chunks = [w.shape[0] for w in weights]
    width = min(w.shape[1] for w in weights)
    depth = sum(chunks)
    tile = 256 if (2 * rows) % 256 == 0 else 2 * rows
    args = [part_of, offset_of, column, *halves[0], *halves[1], *weights]
    specs = [SMEM] * 3 + [ANY] * (2 * parts + len(weights))
    if acc is not None:
        args.append(acc)
        specs.append(ANY)
    if tail is not None:
        args += list(tail)
        specs += [VMEM] * 2
        out_shape = jax.ShapeDtypeStruct((tail[1].shape[0], 2 * rows), jnp.float32)
    else:
        out_shape = jax.ShapeDtypeStruct((2 * rows, width), jnp.float32)
    return pl.pallas_call(
        functools.partial(
            gemm_kernel,
            parts=parts,
            chunks=tuple(chunks),
            own_rows=rows,
            has_acc=acc is not None,
            final=tail is not None,
            tile=tile,
        ),
        out_shape=out_shape,
        in_specs=specs,
        out_specs=VMEM,
        scratch_shapes=[
            pltpu.VMEM((2 * rows, depth), jnp.bfloat16),
            pltpu.VMEM((depth, width), jnp.bfloat16),
            pltpu.VMEM((2 * rows, width), jnp.float32),
            pltpu.SemaphoreType.DMA((len(chunks), 3)),
            pltpu.SemaphoreType.DMA,
        ],
        compiler_params=pltpu.CompilerParams(vmem_limit_bytes=40 << 20),
        cost_estimate=pl.CostEstimate(
            flops=4 * rows * width * depth,
            bytes_accessed=4 * rows * depth + 2 * depth * width + 8 * rows * width,
            transcendentals=0,
        ),
    )(*args)


def judge(step_rows, norm_gain, head_weight, head_bias, class_weight, class_bias):
    z_count, x_count = lax.axis_size("batch"), lax.axis_size("mp")
    y_count = lax.axis_size("group")
    z, x = lax.axis_index("batch"), lax.axis_index("mp")
    s, y = lax.axis_index("section"), lax.axis_index("group")
    swap = shift_pairs(2, 1)
    rows, features = step_rows.shape
    block, columns = head_weight.shape
    width = columns // 2
    share = block // y_count

    def cut(yy, ss):
        return lax.dynamic_slice(head_weight, (yy * share, ss * width), (share, width))

    travelling = [cut(y, s), lax.ppermute(cut(y, 1 - s), "section", swap)]
    siblings = [travelling[1]] + [
        lax.ppermute(cut((y + k) % y_count, 1 - s), "section", swap) for k in range(1, y_count)
    ]
    order = ring_order(z_count)
    ring = [(order[i], order[(i + 1) % z_count]) for i in range(z_count)]
    place = jnp.asarray([order.index(i) for i in range(z_count)])[z]

    values = step_rows.astype(jnp.float32)
    power = jnp.sum(values * values, axis=1)
    power = sum(
        [lax.ppermute(power, "mp", shift_pairs(x_count, k)) for k in range(1, x_count)], power
    )
    power = power / (features * x_count)
    gain = lax.dynamic_slice(norm_gain, (x * features,), (features,))
    normed = (values * lax.rsqrt(power + 1e-06)[:, None] * gain).astype(jnp.bfloat16)
    mine = [normed] + [
        lax.ppermute(normed, "mp", shift_pairs(x_count, k)) for k in range(1, x_count)
    ]
    theirs = [lax.ppermute(part, "section", swap) for part in mine]
    halves = (mine, theirs)

    def place_of(zz, ss, yy):
        feature = (2 * zz + ss) * block + yy * share
        return (x - feature // features) % x_count, feature % features

    own_place = [place_of(z, s, 0)] + [
        place_of(z, 1 - s, (y + k) % y_count) for k in range(y_count)
    ]
    hops = []
    hop_places = []
    for hop in range(1, z_count):
        travelling = [lax.ppermute(t, "batch", ring) for t in travelling]
        zz = jnp.asarray(order)[(place - hop) % z_count]
        buffers, places = [], []
        for j, t in enumerate(travelling):
            ss = s if j == 0 else 1 - s
            for k in range(y_count):
                buffers.append(t if k == 0 else lax.ppermute(t, "group", shift_pairs(y_count, k)))
                places.append(place_of(zz, ss, (y - k) % y_count))
        hops.append(buffers)
        hop_places.append(places)

    def tables(places):
        return jnp.stack([p for p, _ in places]).astype(jnp.int32), jnp.stack(
            [o for _, o in places]
        ).astype(jnp.int32)

    column = (s * width).reshape(1).astype(jnp.int32)
    early = [head_weight] + siblings + sum(hops[:-1], [])
    early_places = own_place + sum(hop_places[:-1], [])
    acc = gemm(*tables(early_places), column, halves, early)
    bias = lax.dynamic_slice(head_bias, (s * width,), (width,))[None]
    classes = lax.dynamic_slice(class_weight, (s * width, 0), (width, 2)).T
    classes = jnp.concatenate([classes, jnp.zeros((14, width), classes.dtype)], axis=0)
    logits = gemm(*tables(hop_places[-1]), column, halves, hops[-1], acc, (bias, classes))
    partial = logits[1] - logits[0]
    kept, given = partial[:rows], partial[rows:]
    total = kept + lax.ppermute(given, "section", swap)
    for k in range(1, x_count):
        total = total + lax.ppermute(kept, "mp", shift_pairs(x_count, k))
        total = total + lax.ppermute(
            given,
            ("mp", "section"),
            [
                (i * 2 + c, ((i + k) % x_count) * 2 + 1 - c)
                for i in range(x_count)
                for c in range(2)
            ],
        )
    return total + (class_bias[1] - class_bias[0])


def judge_gathered(step_rows, norm_gain, head_weight, head_bias, class_weight, class_bias):
    full_rows = lax.all_gather(step_rows, "mp", axis=1, tiled=True)
    row_values = full_rows.astype(jnp.float32)
    power = jnp.mean(row_values * row_values, axis=1, keepdims=True)
    normed = (row_values * lax.rsqrt(power + 1e-06) * norm_gain).astype(jnp.bfloat16)
    projected = jnp.dot(
        normed,
        lax.all_gather(head_weight, ("batch", "section"), axis=0, tiled=True),
        preferred_element_type=jnp.float32,
    )
    hidden = jnp.maximum(projected + head_bias, 0.0).astype(jnp.bfloat16)
    partial_logits = jnp.dot(hidden, class_weight, preferred_element_type=jnp.float32)
    logits = lax.psum(partial_logits, "mp") + class_bias
    return logits[:, 1] - logits[:, 0]


def per_device(
    queries,
    new_keys,
    new_values,
    key_pages,
    value_pages,
    page_table,
    ancestry,
    lengths,
    step_rows,
    norm_gain,
    head_weight,
    head_bias,
    class_weight,
    class_bias,
):
    attention = attend(
        queries, new_keys, new_values, key_pages, value_pages, page_table, ancestry, lengths
    )
    ring_fits = (
        lax.axis_size("batch") <= 8
        and lax.axis_size("section") == 2
        and head_weight.shape[0] % (128 * lax.axis_size("group")) == 0
        and head_weight.shape[1] % 256 == 0
        and step_rows.shape[1] % head_weight.shape[0] == 0
    )
    form = judge if ring_fits else judge_gathered
    log_odds = form(step_rows, norm_gain, head_weight, head_bias, class_weight, class_bias)
    return (attention, log_odds)


def solution(mesh):
    placed = (
        P("section", ("group", "batch"), "mp"),
        P("section", ("group", "batch"), "mp"),
        P("section", ("group", "batch"), "mp"),
        P("section", ("group", "batch"), None, "mp"),
        P("section", ("group", "batch"), None, "mp"),
        P(("group", "batch"), None),
        P("group"),
        P("group"),
        P(("group", "batch", "section"), "mp"),
        P(),
        P(("batch", "section"), "mp"),
        P("mp"),
        P("mp", None),
        P(),
    )
    return jax.shard_map(
        per_device,
        mesh=mesh,
        in_specs=placed,
        out_specs=(P("section", ("group", "batch"), "mp"), P(("group", "batch", "section"))),
        check_vma=False,
    )
```

time: 254 us -> 159 us (0.63)
  waiting for transfers between devices: 150 us -> 56.1 us
  Pallas kernels: 0 us -> 34.1 us
  matrix products: 21.9 us -> 1.21 us
  starting transfers between devices: 18.4 us -> 32.7 us
  local copies, waits for them, and re-layouts: 31.5 us -> 21.1 us
  between operations: 14.4 us -> 7.32 us
  other arithmetic: 12.3 us -> 6.02 us
  blocking collectives: 4.95 us -> 0 us
    all_gather x2 -> x0, waiting for transfers between devices: 115 us -> none  [the longest x1 115 us: per_device(): lax.all_gather(head_weight, ('batch', 'section'), axis=0, tiled=True)]
    ppermute x0 -> x27, waiting for transfers between devices: none -> 56.1 us  [the longest x6 32.7 us: judge(): travelling = [lax.ppermute(t, 'batch', ring) for t in travelling]]
    pallas_call x0 -> x3, Pallas kernels: none -> 34.1 us  [the longest x2 20 us: gemm(): pl.pallas_call(functools.partial(gemm_kernel, parts=parts, chunks=tuple(c...]
    all_to_all x4 -> x0, waiting for transfers between devices: 33.1 us -> none  [the longest x1 27.6 us: per_device(): lax.all_to_all(numerator, 'batch', split_axis=1, concat_axis=1, tiled=True)]
    ppermute x0 -> x27, starting transfers between devices: none -> 32.7 us  [the longest x6 10.2 us: exchange(): lax.ppermute(blocks[k], axis, shift_pairs(count, k))]
    dot_general x4 -> x2, matrix products: 21.9 us -> 1.21 us  [the longest x1 0.94 us: attend(): lax.dot_general(wanted, returned, (((0,), (0,)), ((), ())), preferred_ele...]
    all_to_all x4 -> x0, starting transfers between devices: 18.3 us -> none  [the longest x1 6.32 us: per_device(): lax.all_to_all(outgoing_queries, 'batch', split_axis=1, concat_axis=1, ti...]
    reshape x7 -> x3, local copies, waits for them, and re-layouts: 14.3 us -> 0.25 us  [the longest x1 0.09 us: attend(): jnp.sum(jnp.where(served, served_local[:, None, :], 0), axis=2).reshape(-1)]
  transfers between devices with their start and end apart: 6 -> 27, of which waited for: 4 -> 13; matrix products, arithmetic and copies ran while one was open for 20% -> 5% of each run, Pallas kernels for 0% -> 17%
where the time goes in v1:
time: 159 us; the launch traced here: 158 us
  waiting for transfers between devices  56.1 us (35%)
  Pallas kernels  34.1 us (21%)
  starting transfers between devices  32.7 us (21%)
  local copies, waits for them, and re-layouts  21.1 us (13%)
  between operations  7.32 us (5%)
  other arithmetic  6.02 us (4%)
    ppermute x6, waiting for transfers between devices, judge(): travelling = [lax.ppermute(t, 'batch', ring) for t in travelling]  32.7 us
    pallas_call x2, Pallas kernels, gemm(): pl.pallas_call(functools.partial(gemm_kernel, parts=parts, chunks=tuple(c...  20 us
    unnamed x71, local copies, waits for them, and re-layouts  17.1 us
    pallas_call x1, Pallas kernels, serve(): pl.pallas_call(functools.partial(attention_kernel, kv_local=kv_local, unr...  14.1 us
    ppermute x6, waiting for transfers between devices, judge(): lax.ppermute(t, 'group', shift_pairs(y_count, k))  12.2 us
    ppermute x6, starting transfers between devices, exchange(): lax.ppermute(blocks[k], axis, shift_pairs(count, k))  10.2 us
    ppermute x6, starting transfers between devices, judge(): travelling = [lax.ppermute(t, 'batch', ring) for t in travelling]  7.48 us
    ppermute x6, starting transfers between devices, judge(): lax.ppermute(t, 'group', shift_pairs(y_count, k))  7.15 us
  transfers between devices with their start and end apart: 27, of which 13 were waited for; matrix products, arithmetic and copies ran while one was open for 5% of the time, Pallas kernels for 17%

profile of v1, /device:TPU:0, one launch (start us, length us, event | category | flops | bytes accessed | tf_op | source)
XLA Modules:
  0.0 158.5 jit_solution(4028525503613084046)
XLA Ops:
  0.7 2.1 %fusion.1 = f32[512]{0:T(512)S(1)} fusion(bf16[512,2048]{1,0:T(8,128)(2,1)} %param.28), kind=kLoop, calls=%fused_computation.7 | loop fusion | flops 3145216 | bytes 2099200 | tf_op jit(solution)/shard_map/reduce_sum | solution.py:314
  2.8 3.0 %collective-permute-start.6 = (f32[512]{0:T(512)S(1)}, f32[512]{0:T(512)S(1)}, u32[]{:S(2)}, u32[]{:S(2)}) collective-permute-start(f32[512]{0:T(512)S(1)} %fusion.1), channel_id=1, source_target_pairs={{0,2},{2,0},{1,3},{3,1},{4,6},{6,4},{5,7},{7,5},{8,10},{10,8},{9,1... | collective-permute-start | bytes 6152 | tf_op jit(solution)/shard_map/ppermute | solution.py:316
  6.0 0.2 convert_reduce_fusion.1
  6.3 0.3 convolution_convert_fusion
  6.6 0.8 collective-permute-done.6
  7.4 2.1 %fusion.3.refs_3_ = bf16[512,2048]{1,0:T(8,128)(2,1)S(1)} fusion(bf16[512,2048]{1,0:T(8,128)(2,1)} %param.28, f32[2048]{0:T(1024)S(1)} %dynamic_slice.41, f32[512]{0:T(512)S(1)} %add_rsqrt_fusion), kind=kLoop, calls=%fused_computation.9 | loop fusion | flops 4194304 | bytes 4204544 | tf_op jit(solution)/shard_map/convert_element_type | solution.py:320
  9.6 2.1 %collective-permute-start.7 = (bf16[512,2048]{1,0:T(8,128)(2,1)S(1)}, bf16[512,2048]{1,0:T(8,128)(2,1)}, u32[]{:S(2)}, u32[]{:S(2)}) collective-permute-start(bf16[512,2048]{1,0:T(8,128)(2,1)S(1)} %fusion.3.refs_3_), channel_id=1, source_target_pairs={{0,2},{2,0},{1,3},{3,1},{4,6},{6,4},{5,7},{7,5},{8,10},{10,8},{9,1... | collective-permute-start | bytes 6291464 | tf_op jit(solution)/shard_map/ppermute | solution.py:322
  11.8 1.6 %collective-permute-start = (bf16[12,40,128]{2,1,0:T(8,128)(2,1)S(1)}, bf16[12,40,128]{2,1,0:T(8,128)(2,1)S(1)}, u32[]{:S(2)}, u32[]{:S(2)}) collective-permute-start(bf16[12,40,128]{2,1,0:T(8,128)(2,1)S(1)} %slice.89), channel_id=1, source_target_pairs={{0,4},{4,8},{8,12},{12,0},{1,5},{5,9},{9,13},{13,1},{2,6},{6,10},{... | collective-permute-start | bytes 368648 | tf_op jit(solution)/shard_map/ppermute | solution.py:98
  13.5 2.7 %collective-permute-start.1 = (bf16[12,40,128]{2,1,0:T(8,128)(2,1)S(1)}, bf16[12,40,128]{2,1,0:T(8,128)(2,1)S(1)}, u32[]{:S(2)}, u32[]{:S(2)}) collective-permute-start(bf16[12,40,128]{2,1,0:T(8,128)(2,1)S(1)} %slice.90), channel_id=1, source_target_pairs={{0,8},{4,12},{8,0},{12,4},{1,9},{5,13},{9,1},{13,5},{2,10},{6,14},... | collective-permute-start | bytes 368648 | tf_op jit(solution)/shard_map/ppermute | solution.py:98
  16.2 1.4 collective-permute-start.2
  17.6 0.6 gather_fusion
  18.2 0.6 gather_fusion.1
  19.1 0.3 select_reduce_fusion
  19.9 3.0 %collective-permute-done.1 = bf16[12,40,128]{2,1,0:T(8,128)(2,1)S(1)} collective-permute-done((bf16[12,40,128]{2,1,0:T(8,128)(2,1)S(1)}, bf16[12,40,128]{2,1,0:T(8,128)(2,1)S(1)}, u32[]{:S(2)}, u32[]{:S(2)}) %collective-permute-start.1) | collective-permute-done | bytes 122912 | tf_op jit(solution)/shard_map/ppermute | solution.py:98
  23.0 0.2 collective-permute-done.2
  23.2 1.4 copy-done.1
  24.6 1.4 copy-done.2
  26.0 14.1 %shard_map.185 = bf16[48,32,128]{2,1,0:T(8,128)(2,1)S(1)} custom-call(s32[48]{0:T(128)S(1)} %reshape.159.particle, s32[24,4]{1,0:T(8,128)S(1)} %copy.23.page_table, s32[48]{0:T(128)S(1)} %select_reduce_fusion.1.lengths, bf16[48,40,128]{2,1,0:T(8,128)(2,1)S(1)} %pad_maximum_fusion.blob, bf16[96,16,512]{2,1,0:T(8,128)(2,1)S(1)} %bitcast.78, ...), custom_call_target="tpu_custom_call" | custom-call | flops 20000000 | bytes 6000000 | tf_op jit(solution)/shard_map/pallas_call | solution.py:84
  40.2 3.9 %collective-permute-start.3 = (bf16[12,32,128]{2,1,0:T(8,128)(2,1)S(1)}, bf16[12,32,128]{2,1,0:T(8,128)(2,1)S(1)}, u32[]{:S(2)}, u32[]{:S(2)}) collective-permute-start(bf16[12,32,128]{2,1,0:T(8,128)(2,1)S(1)} %get-tuple-element.13), channel_id=1, source_target_pairs={{0,12},{4,0},{8,4},{12,8},{1,13},{5,1},{9,5},{13,9},{2,14},{6,2},{... | collective-permute-start | bytes 294920 | tf_op jit(solution)/shard_map/ppermute | solution.py:98
  44.0 0.4 collective-permute-start.4
  44.5 0.2 collective-permute-start.5
  44.9 2.3 %collective-permute-done.3 = bf16[12,32,128]{2,1,0:T(8,128)(2,1)S(1)} collective-permute-done((bf16[12,32,128]{2,1,0:T(8,128)(2,1)S(1)}, bf16[12,32,128]{2,1,0:T(8,128)(2,1)S(1)}, u32[]{:S(2)}, u32[]{:S(2)}) %collective-permute-start.3) | collective-permute-done | bytes 98336 | tf_op jit(solution)/shard_map/ppermute | solution.py:98
  47.2 5.6 %collective-permute-start.10 = (bf16[256,1024]{1,0:T(8,128)(2,1)S(1)}, bf16[256,1024]{1,0:T(8,128)(2,1)S(1)}, u32[]{:S(2)}, u32[]{:S(2)}) collective-permute-start(bf16[256,1024]{1,0:T(8,128)(2,1)S(1)} %get-tuple-element.5), channel_id=1, source_target_pairs={{0,4},{4,12},{12,8},{8,0},{1,5},{5,13},{13,9},{9,1},{2,6},{6,14},{... | collective-permute-start | bytes 1572872 | tf_op jit(solution)/shard_map/ppermute | solution.py:337
  52.9 1.5 collective-permute-done.4
  54.4 0.5 collective-permute-start.8
  54.9 1.3 collective-permute-done.7.refs_4_
  56.3 1.8 %collective-permute-start.15 = (bf16[256,1024]{1,0:T(8,128)(2,1)S(1)}, bf16[256,1024]{1,0:T(8,128)(2,1)S(1)}, u32[]{:S(2)}, u32[]{:S(2)}) collective-permute-start(bf16[256,1024]{1,0:T(8,128)(2,1)S(1)} %collective-permute-done.14.refs_8_), channel_id=1, source_target_pairs={{0,4},{4,12},{12,8},{8,0},{1,5},{5,13},{13,9},{9,1},{2,6},{6,14},{... | collective-permute-start | bytes 1572872 | tf_op jit(solution)/shard_map/ppermute | solution.py:337
  58.1 0.8 copy-done.3
  58.9 6.7 %collective-permute-done.10.refs_10_ = bf16[256,1024]{1,0:T(8,128)(2,1)S(1)} collective-permute-done((bf16[256,1024]{1,0:T(8,128)(2,1)S(1)}, bf16[256,1024]{1,0:T(8,128)(2,1)S(1)}, u32[]{:S(2)}, u32[]{:S(2)}) %collective-permute-start.10) | collective-permute-done | bytes 524320 | tf_op jit(solution)/shard_map/ppermute | solution.py:337
  65.6 0.8 copy-done.7
  66.5 1.5 collective-permute-start.20
  68.0 0.8 copy-done.5
  68.8 8.1 %collective-permute-done.15.refs_12_ = bf16[256,1024]{1,0:T(8,128)(2,1)S(1)} collective-permute-done((bf16[256,1024]{1,0:T(8,128)(2,1)S(1)}, bf16[256,1024]{1,0:T(8,128)(2,1)S(1)}, u32[]{:S(2)}, u32[]{:S(2)}) %collective-permute-start.15) | collective-permute-done | bytes 524320 | tf_op jit(solution)/shard_map/ppermute | solution.py:337
  76.9 11.3 %collective-permute-done.11.refs_14_ = bf16[256,1024]{1,0:T(8,128)(2,1)} collective-permute-done((bf16[256,1024]{1,0:T(8,128)(2,1)S(1)}, bf16[256,1024]{1,0:T(8,128)(2,1)}, u32[]{:S(2)}, u32[]{:S(2)}) %collective-permute-start.11) | collective-permute-done | bytes 524320 | tf_op jit(solution)/shard_map/ppermute | solution.py:337
  88.2 1.5 collective-permute-start.21
  89.7 0.8 copy-done.9
  90.5 0.8 copy-done.11
  91.3 0.5 collective-permute-start.22
  91.8 6.6 %collective-permute-done.16.refs_16_ = bf16[256,1024]{1,0:T(8,128)(2,1)} collective-permute-done((bf16[256,1024]{1,0:T(8,128)(2,1)S(1)}, bf16[256,1024]{1,0:T(8,128)(2,1)}, u32[]{:S(2)}, u32[]{:S(2)}) %collective-permute-start.16) | collective-permute-done | bytes 524320 | tf_op jit(solution)/shard_map/ppermute | solution.py:337
  98.4 4.6 %collective-permute-done.21.refs_13_ = bf16[256,1024]{1,0:T(8,128)(2,1)S(1)} collective-permute-done((bf16[256,1024]{1,0:T(8,128)(2,1)S(1)}, bf16[256,1024]{1,0:T(8,128)(2,1)S(1)}, u32[]{:S(2)}, u32[]{:S(2)}) %collective-permute-start.21) | collective-permute-done | bytes 524320 | tf_op jit(solution)/shard_map/ppermute | solution.py:343
  103.1 0.8 copy-done.13
  103.9 7.5 %collective-permute-done.22.refs_15_ = bf16[256,1024]{1,0:T(8,128)(2,1)S(1)} collective-permute-done((bf16[256,1024]{1,0:T(8,128)(2,1)}, bf16[256,1024]{1,0:T(8,128)(2,1)S(1)}, u32[]{:S(2)}, u32[]{:S(2)}) %collective-permute-start.22) | collective-permute-done | bytes 524320 | tf_op jit(solution)/shard_map/ppermute | solution.py:343
  111.4 0.8 copy-done.15
  112.2 1.5 collective-permute-start.23
  113.7 0.6 dynamic_slice.39
  116.3 0.6 fusion.26
  119.9 0.6 fusion.25
  122.2 0.9 pad.24
  123.3 0.6 collective-permute-start.13
  123.9 1.5 collective-permute-start.18
  125.4 1.0 copy-done.4
  126.4 1.0 copy-done.6
  127.5 1.0 copy-done.8
  128.5 1.0 copy-done.10
  129.6 1.0 copy-done.12
  130.6 1.0 copy-done.14
  131.6 1.0 copy-done.16
  132.7 13.1 %shard_map.186.refs_11_ = f32[1024,1024]{1,0:T(8,128)} custom-call(s32[11]{0:T(128)S(1)} %stack.123.refs_0_, s32[11]{0:T(128)S(1)} %stack.135.refs_1_, s32[1]{0:T(128)} %bitcast.17.refs_2_, bf16[512,2048]{1,0:T(8,128)(2,1)S(1)} %fusion.3.refs_3_, bf16[512,2048]{1,0:T(8,128)(2,1)} %collective-permute-done.7.refs_4_, ...), custom_call_target="tpu_custom_call" | custom-call | flops 6442450944 | bytes 16777216 | tf_op jit(solution)/shard_map/pallas_call | solution.py:262
  145.8 6.9 %shard_map.187 = f32[16,1024]{1,0:T(8,128)S(1)} custom-call(s32[4]{0:T(128)S(1)} %get-tuple-element.25.refs_0_, s32[4]{0:T(128)S(1)} %get-tuple-element.26.refs_1_, s32[1]{0:T(128)} %bitcast.17.refs_2_, bf16[512,2048]{1,0:T(8,128)(2,1)S(1)} %fusion.3.refs_3_, bf16[512,2048]{1,0:T(8,128)(2,1)} %collective-permute-done.7.refs_4_, ...), custom_call_target="tpu_custom_call" | custom-call | flops 2147483648 | bytes 8388608 | tf_op jit(solution)/shard_map/pallas_call | solution.py:262
  152.9 1.4 collective-permute-start.26
  154.3 0.7 collective-permute-start.25
  155.0 0.9 fusion
  156.0 1.9 %collective-permute-done.25 = f32[512]{0:T(512)S(1)} collective-permute-done((f32[512]{0:T(512)S(1)}, f32[512]{0:T(512)S(1)}, u32[]{:S(2)}, u32[]{:S(2)}) %collective-permute-start.25) | collective-permute-done | bytes 2080 | tf_op jit(solution)/shard_map/ppermute | solution.py:365
  157.9 0.6 add_add_fusion
  (113 shorter events, 2.4 us)
Async XLA Ops:
  0.6 119.2 %copy-start = (bf16[2048,2]{0,1:T(2,128)(2,1)S(1)}, bf16[2048,2]{0,1:T(2,128)(2,1)}, u32[]{:S(2)}) copy-start(bf16[2048,2]{0,1:T(2,128)(2,1)} %param.32) | copy-start | bytes 24580
  0.6 5.2 %copy-start.27 = (s32[96]{0:T(128)S(1)}, s32[96]{0:T(128)}, u32[]{:S(2)}) copy-start(s32[96]{0:T(128)} %param.26) | copy-start | bytes 1156
  0.7 5.6 %copy-start.18 = (bf16[1,24,4096]{2,1,0:T(8,128)(2,1)S(1)}, bf16[1,24,4096]{2,1,0:T(8,128)(2,1)}, u32[]{:S(2)}) copy-start(bf16[1,24,4096]{2,1,0:T(8,128)(2,1)} %param.20) | copy-start | bytes 589828
  0.7 5.6 %copy-start.21 = (bf16[1,24,512]{2,1,0:T(8,128)(2,1)S(1)}, bf16[1,24,512]{2,1,0:T(8,128)(2,1)}, u32[]{:S(2)}) copy-start(bf16[1,24,512]{2,1,0:T(8,128)(2,1)} %param.21) | copy-start | bytes 73732
  0.7 5.6 %copy-start.20 = (bf16[1,24,512]{2,1,0:T(8,128)(2,1)S(1)}, bf16[1,24,512]{2,1,0:T(8,128)(2,1)}, u32[]{:S(2)}) copy-start(bf16[1,24,512]{2,1,0:T(8,128)(2,1)} %param.22) | copy-start | bytes 73732
  0.7 5.9 %copy-start.23 = (f32[4096]{0:T(1024)S(1)}, f32[4096]{0:T(1024)}, u32[]{:S(2)}) copy-start(f32[4096]{0:T(1024)} %param.29) | copy-start | bytes 49156
  2.8 4.6 %collective-permute-start.6 = (f32[512]{0:T(512)S(1)}, f32[512]{0:T(512)S(1)}, u32[]{:S(2)}, u32[]{:S(2)}) collective-permute-start(f32[512]{0:T(512)S(1)} %fusion.1), channel_id=1, source_target_pairs={{0,2},{2,0},{1,3},{3,1},{4,6},{6,4},{5,7},{7,5},{8,10},{10,8},{9,1... | collective-permute-start | bytes 6152 | tf_op jit(solution)/shard_map/ppermute | solution.py:316
  9.6 10.1 %copy-start.24 = (s32[24,4]{0,1:T(4,128)S(1)}, s32[24,4]{0,1:T(4,128)}, u32[]{:S(2)}) copy-start(s32[24,4]{0,1:T(4,128)} %param.25) | copy-start | bytes 1156
  9.6 10.2 %copy-start.28 = (s32[96]{0:T(128)S(1)}, s32[96]{0:T(128)}, u32[]{:S(2)}) copy-start(s32[96]{0:T(128)} %param.27) | copy-start | bytes 1156
  9.6 46.7 %collective-permute-start.7 = (bf16[512,2048]{1,0:T(8,128)(2,1)S(1)}, bf16[512,2048]{1,0:T(8,128)(2,1)}, u32[]{:S(2)}, u32[]{:S(2)}) collective-permute-start(bf16[512,2048]{1,0:T(8,128)(2,1)S(1)} %fusion.3.refs_3_), channel_id=1, source_target_pairs={{0,2},{2,0},{1,3},{3,1},{4,6},{6,4},{5,7},{7,5},{8,10},{10,8},{9,1... | collective-permute-start | bytes 6291464 | tf_op jit(solution)/shard_map/ppermute | solution.py:322
  11.8 8.1 %collective-permute-start = (bf16[12,40,128]{2,1,0:T(8,128)(2,1)S(1)}, bf16[12,40,128]{2,1,0:T(8,128)(2,1)S(1)}, u32[]{:S(2)}, u32[]{:S(2)}) collective-permute-start(bf16[12,40,128]{2,1,0:T(8,128)(2,1)S(1)} %slice.89), channel_id=1, source_target_pairs={{0,4},{4,8},{8,12},{12,0},{1,5},{5,9},{9,13},{13,1},{2,6},{6,10},{... | collective-permute-start | bytes 368648 | tf_op jit(solution)/shard_map/ppermute | solution.py:98
  13.5 9.5 %collective-permute-start.1 = (bf16[12,40,128]{2,1,0:T(8,128)(2,1)S(1)}, bf16[12,40,128]{2,1,0:T(8,128)(2,1)S(1)}, u32[]{:S(2)}, u32[]{:S(2)}) collective-permute-start(bf16[12,40,128]{2,1,0:T(8,128)(2,1)S(1)} %slice.90), channel_id=1, source_target_pairs={{0,8},{4,12},{8,0},{12,4},{1,9},{5,13},{9,1},{13,5},{2,10},{6,14},... | collective-permute-start | bytes 368648 | tf_op jit(solution)/shard_map/ppermute | solution.py:98
  16.2 6.9 %collective-permute-start.2 = (bf16[12,40,128]{2,1,0:T(8,128)(2,1)S(1)}, bf16[12,40,128]{2,1,0:T(8,128)(2,1)S(1)}, u32[]{:S(2)}, u32[]{:S(2)}) collective-permute-start(bf16[12,40,128]{2,1,0:T(8,128)(2,1)S(1)} %slice.91), channel_id=1, source_target_pairs={{0,12},{4,0},{8,4},{12,8},{1,13},{5,1},{9,5},{13,9},{2,14},{6,2},{... | collective-permute-start | bytes 368648 | tf_op jit(solution)/shard_map/ppermute | solution.py:98
  23.2 1.4 copy-start.1
  24.6 1.4 copy-start.2
  26.0 18.6 %copy-start.17 = (bf16[512,2048]{1,0:T(8,128)(2,1)S(1)}, bf16[512,2048]{1,0:T(8,128)(2,1)}, u32[]{:S(2)}) copy-start(bf16[512,2048]{1,0:T(8,128)(2,1)} %refs_7_.1) | copy-start | bytes 6291460
  40.1 73.6 %copy-start.22 = (s32[4]{0:T(128)S(1)}, s32[4]{0:T(128)}, u32[]{:S(2)}) copy-start(s32[4]{0:T(128)} %constant.396.clone) | copy-start | bytes 52
  40.2 7.1 %collective-permute-start.3 = (bf16[12,32,128]{2,1,0:T(8,128)(2,1)S(1)}, bf16[12,32,128]{2,1,0:T(8,128)(2,1)S(1)}, u32[]{:S(2)}, u32[]{:S(2)}) collective-permute-start(bf16[12,32,128]{2,1,0:T(8,128)(2,1)S(1)} %get-tuple-element.13), channel_id=1, source_target_pairs={{0,12},{4,0},{8,4},{12,8},{1,13},{5,1},{9,5},{13,9},{2,14},{6,2},{... | collective-permute-start | bytes 294920 | tf_op jit(solution)/shard_map/ppermute | solution.py:98
  44.0 10.4 %collective-permute-start.4 = (bf16[12,32,128]{2,1,0:T(8,128)(2,1)S(1)}, bf16[12,32,128]{2,1,0:T(8,128)(2,1)S(1)}, u32[]{:S(2)}, u32[]{:S(2)}) collective-permute-start(bf16[12,32,128]{2,1,0:T(8,128)(2,1)S(1)} %get-tuple-element.12), channel_id=1, source_target_pairs={{0,8},{4,12},{8,0},{12,4},{1,9},{5,13},{9,1},{13,5},{2,10},{6,14},... | collective-permute-start | bytes 294920 | tf_op jit(solution)/shard_map/ppermute | solution.py:98
  44.5 75.1 %copy-start.25 = (f32[2048]{0:T(1024)S(1)}, f32[2048]{0:T(1024)}, u32[]{:S(2)}) copy-start(f32[2048]{0:T(1024)} %param.31) | copy-start | bytes 24580
  44.5 75.4 %copy-start.26 = (f32[2]{0:T(128)S(1)}, f32[2]{0:T(128)}, u32[]{:S(2)}) copy-start(f32[2]{0:T(128)} %param.33) | copy-start | bytes 28
  44.5 10.0 %collective-permute-start.5 = (bf16[12,32,128]{2,1,0:T(8,128)(2,1)S(1)}, bf16[12,32,128]{2,1,0:T(8,128)(2,1)S(1)}, u32[]{:S(2)}, u32[]{:S(2)}) collective-permute-start(bf16[12,32,128]{2,1,0:T(8,128)(2,1)S(1)} %get-tuple-element.11), channel_id=1, source_target_pairs={{0,4},{4,8},{8,12},{12,0},{1,5},{5,9},{9,13},{13,1},{2,6},{6,10},{... | collective-permute-start | bytes 294920 | tf_op jit(solution)/shard_map/ppermute | solution.py:98
  44.8 11.5 %collective-permute-start.14 = (bf16[256,1024]{1,0:T(8,128)(2,1)S(1)}, bf16[256,1024]{1,0:T(8,128)(2,1)S(1)}, u32[]{:S(2)}, u32[]{:S(2)}) collective-permute-start(bf16[256,1024]{1,0:T(8,128)(2,1)S(1)} %get-tuple-element.4), channel_id=1, source_target_pairs={{0,1},{1,0},{2,3},{3,2},{4,5},{5,4},{6,7},{7,6},{8,9},{9,8},{10,11... | collective-permute-start | bytes 1572872 | tf_op jit(solution)/shard_map/ppermute | solution.py:305
  47.2 18.4 %collective-permute-start.10 = (bf16[256,1024]{1,0:T(8,128)(2,1)S(1)}, bf16[256,1024]{1,0:T(8,128)(2,1)S(1)}, u32[]{:S(2)}, u32[]{:S(2)}) collective-permute-start(bf16[256,1024]{1,0:T(8,128)(2,1)S(1)} %get-tuple-element.5), channel_id=1, source_target_pairs={{0,4},{4,12},{12,8},{8,0},{1,5},{5,13},{13,9},{9,1},{2,6},{6,14},{... | collective-permute-start | bytes 1572872 | tf_op jit(solution)/shard_map/ppermute | solution.py:337
  54.4 57.0 %copy-start.19 = (bf16[12,32,128]{2,1,0:T(8,128)(2,1)}, bf16[12,32,128]{2,1,0:T(8,128)(2,1)S(1)}, u32[]{:S(2)}) copy-start(bf16[12,32,128]{2,1,0:T(8,128)(2,1)S(1)} %collective-permute-done.4) | copy-start | bytes 294916
  54.4 11.2 %collective-permute-start.19 = (bf16[256,1024]{1,0:T(8,128)(2,1)S(1)}, bf16[256,1024]{1,0:T(8,128)(2,1)S(1)}, u32[]{:S(2)}, u32[]{:S(2)}) collective-permute-start(bf16[256,1024]{1,0:T(8,128)(2,1)S(1)} %get-tuple-element.3), channel_id=1, source_target_pairs={{0,1},{1,0},{2,3},{3,2},{4,5},{5,4},{6,7},{7,6},{8,9},{9,8},{10,11... | collective-permute-start | bytes 1572872 | tf_op jit(solution)/shard_map/ppermute | solution.py:307
  54.4 71.0 %collective-permute-start.8 = (bf16[512,2048]{1,0:T(8,128)(2,1)S(1)}, bf16[512,2048]{1,0:T(8,128)(2,1)}, u32[]{:S(2)}, u32[]{:S(2)}) collective-permute-start(bf16[512,2048]{1,0:T(8,128)(2,1)S(1)} %fusion.3.refs_3_), channel_id=1, source_target_pairs={{0,1},{1,0},{2,3},{3,2},{4,5},{5,4},{6,7},{7,6},{8,9},{9,8},{10,11... | collective-permute-start | bytes 6291464 | tf_op jit(solution)/shard_map/ppermute | solution.py:324
  56.3 69.1 %collective-permute-start.9 = (bf16[512,2048]{1,0:T(8,128)(2,1)}, bf16[512,2048]{1,0:T(8,128)(2,1)}, u32[]{:S(2)}, u32[]{:S(2)}) collective-permute-start(bf16[512,2048]{1,0:T(8,128)(2,1)} %collective-permute-done.7.refs_4_), channel_id=1, source_target_pairs={{0,1},{1,0},{2,3},{3,2},{4,5},{5,4},{6,7},{7,6},{8,9},{9,8},{10,11... | collective-permute-start | bytes 6291464 | tf_op jit(solution)/shard_map/ppermute | solution.py:324
  56.3 20.6 %collective-permute-start.15 = (bf16[256,1024]{1,0:T(8,128)(2,1)S(1)}, bf16[256,1024]{1,0:T(8,128)(2,1)S(1)}, u32[]{:S(2)}, u32[]{:S(2)}) collective-permute-start(bf16[256,1024]{1,0:T(8,128)(2,1)S(1)} %collective-permute-done.14.refs_8_), channel_id=1, source_target_pairs={{0,4},{4,12},{12,8},{8,0},{1,5},{5,13},{13,9},{9,1},{2,6},{6,14},{... | collective-permute-start | bytes 1572872 | tf_op jit(solution)/shard_map/ppermute | solution.py:337
  58.1 0.8 copy-start.3
  65.6 22.6 %collective-permute-start.11 = (bf16[256,1024]{1,0:T(8,128)(2,1)S(1)}, bf16[256,1024]{1,0:T(8,128)(2,1)}, u32[]{:S(2)}, u32[]{:S(2)}) collective-permute-start(bf16[256,1024]{1,0:T(8,128)(2,1)S(1)} %collective-permute-done.10.refs_10_), channel_id=1, source_target_pairs={{0,4},{4,12},{12,8},{8,0},{1,5},{5,13},{13,9},{9,1},{2,6},{6,14},{... | collective-permute-start | bytes 1572872 | tf_op jit(solution)/shard_map/ppermute | solution.py:337
  65.6 0.8 copy-start.7
  66.5 24.1 %collective-permute-start.20 = (bf16[256,1024]{1,0:T(8,128)(2,1)S(1)}, bf16[256,1024]{1,0:T(8,128)(2,1)S(1)}, u32[]{:S(2)}, u32[]{:S(2)}) collective-permute-start(bf16[256,1024]{1,0:T(8,128)(2,1)S(1)} %collective-permute-done.10.refs_10_), channel_id=1, source_target_pairs={{0,16},{16,0},{1,17},{17,1},{2,18},{18,2},{3,19},{19,3},{4,20},{20... | collective-permute-start | bytes 1572872 | tf_op jit(solution)/shard_map/ppermute | solution.py:343
  68.0 0.8 copy-start.5
  76.9 21.6 %collective-permute-start.16 = (bf16[256,1024]{1,0:T(8,128)(2,1)S(1)}, bf16[256,1024]{1,0:T(8,128)(2,1)}, u32[]{:S(2)}, u32[]{:S(2)}) collective-permute-start(bf16[256,1024]{1,0:T(8,128)(2,1)S(1)} %collective-permute-done.15.refs_12_), channel_id=1, source_target_pairs={{0,4},{4,12},{12,8},{8,0},{1,5},{5,13},{13,9},{9,1},{2,6},{6,14},{... | collective-permute-start | bytes 1572872 | tf_op jit(solution)/shard_map/ppermute | solution.py:337
  88.2 14.9 %collective-permute-start.21 = (bf16[256,1024]{1,0:T(8,128)(2,1)S(1)}, bf16[256,1024]{1,0:T(8,128)(2,1)S(1)}, u32[]{:S(2)}, u32[]{:S(2)}) collective-permute-start(bf16[256,1024]{1,0:T(8,128)(2,1)S(1)} %collective-permute-done.15.refs_12_), channel_id=1, source_target_pairs={{0,16},{16,0},{1,17},{17,1},{2,18},{18,2},{3,19},{19,3},{4,20},{20... | collective-permute-start | bytes 1572872 | tf_op jit(solution)/shard_map/ppermute | solution.py:343
  89.7 0.8 copy-start.9
  90.5 0.8 copy-start.11
  91.3 20.0 %collective-permute-start.22 = (bf16[256,1024]{1,0:T(8,128)(2,1)}, bf16[256,1024]{1,0:T(8,128)(2,1)S(1)}, u32[]{:S(2)}, u32[]{:S(2)}) collective-permute-start(bf16[256,1024]{1,0:T(8,128)(2,1)} %collective-permute-done.11.refs_14_), channel_id=1, source_target_pairs={{0,16},{16,0},{1,17},{17,1},{2,18},{18,2},{3,19},{19,3},{4,20},{20... | collective-permute-start | bytes 1572872 | tf_op jit(solution)/shard_map/ppermute | solution.py:343
  98.4 24.8 %collective-permute-start.12 = (bf16[256,1024]{1,0:T(8,128)(2,1)}, bf16[256,1024]{1,0:T(8,128)(2,1)S(1)}, u32[]{:S(2)}, u32[]{:S(2)}) collective-permute-start(bf16[256,1024]{1,0:T(8,128)(2,1)} %collective-permute-done.11.refs_14_), channel_id=1, source_target_pairs={{0,4},{4,12},{12,8},{8,0},{1,5},{5,13},{13,9},{9,1},{2,6},{6,14},{... | collective-permute-start | bytes 1572872 | tf_op jit(solution)/shard_map/ppermute | solution.py:337
  103.1 0.8 copy-start.13
  103.9 20.0 %collective-permute-start.17 = (bf16[256,1024]{1,0:T(8,128)(2,1)}, bf16[256,1024]{1,0:T(8,128)(2,1)S(1)}, u32[]{:S(2)}, u32[]{:S(2)}) collective-permute-start(bf16[256,1024]{1,0:T(8,128)(2,1)} %collective-permute-done.16.refs_16_), channel_id=1, source_target_pairs={{0,4},{4,12},{12,8},{8,0},{1,5},{5,13},{13,9},{9,1},{2,6},{6,14},{... | collective-permute-start | bytes 1572872 | tf_op jit(solution)/shard_map/ppermute | solution.py:337
  111.4 0.8 copy-start.15
  112.2 13.2 %collective-permute-start.23 = (bf16[256,1024]{1,0:T(8,128)(2,1)}, bf16[256,1024]{1,0:T(8,128)(2,1)}, u32[]{:S(2)}, u32[]{:S(2)}) collective-permute-start(bf16[256,1024]{1,0:T(8,128)(2,1)} %collective-permute-done.16.refs_16_), channel_id=1, source_target_pairs={{0,16},{16,0},{1,17},{17,1},{2,18},{18,2},{3,19},{19,3},{4,20},{20... | collective-permute-start | bytes 1572872 | tf_op jit(solution)/shard_map/ppermute | solution.py:343
  123.3 22.5 %collective-permute-start.13 = (bf16[256,1024]{1,0:T(8,128)(2,1)S(1)}, bf16[256,1024]{1,0:T(8,128)(2,1)S(1)}, u32[]{:S(2)}, u32[]{:S(2)}) collective-permute-start(bf16[256,1024]{1,0:T(8,128)(2,1)S(1)} %collective-permute-done.12.refs_7_), channel_id=1, source_target_pairs={{0,16},{16,0},{1,17},{17,1},{2,18},{18,2},{3,19},{19,3},{4,20},{20... | collective-permute-start | bytes 1572872 | tf_op jit(solution)/shard_map/ppermute | solution.py:343
  123.9 22.0 %collective-permute-start.18 = (bf16[256,1024]{1,0:T(8,128)(2,1)S(1)}, bf16[256,1024]{1,0:T(8,128)(2,1)S(1)}, u32[]{:S(2)}, u32[]{:S(2)}) collective-permute-start(bf16[256,1024]{1,0:T(8,128)(2,1)S(1)} %collective-permute-done.17.refs_9_), channel_id=1, source_target_pairs={{0,16},{16,0},{1,17},{17,1},{2,18},{18,2},{3,19},{19,3},{4,20},{20... | collective-permute-start | bytes 1572872 | tf_op jit(solution)/shard_map/ppermute | solution.py:343
  125.4 1.0 copy-start.4
  126.4 1.0 copy-start.6
  127.5 1.0 copy-start.8
  128.5 1.0 copy-start.10
  129.6 1.0 copy-start.12
  130.6 1.0 copy-start.14
  131.6 1.0 copy-start.16
  152.8 3.2 %collective-permute-start.24 = (f32[512]{0:T(512)S(1)}, f32[512]{0:T(512)S(1)}, u32[]{:S(2)}, u32[]{:S(2)}) collective-permute-start(f32[512]{0:T(512)S(1)} %bitcast.102), channel_id=1, source_target_pairs={{0,1},{1,0},{2,3},{3,2},{4,5},{5,4},{6,7},{7,6},{8,9},{9,8},{10,11... | collective-permute-start | bytes 6152 | tf_op jit(solution)/shard_map/ppermute | solution.py:363
  152.9 5.0 %collective-permute-start.26 = (f32[512]{0:T(512)S(1)}, f32[512]{0:T(512)S(1)}, u32[]{:S(2)}, u32[]{:S(2)}) collective-permute-start(f32[512]{0:T(512)S(1)} %bitcast.103), channel_id=1, source_target_pairs={{0,3},{1,2},{2,1},{3,0},{4,7},{5,6},{6,5},{7,4},{8,11},{9,10},{10,... | collective-permute-start | bytes 6152 | tf_op jit(solution)/shard_map/ppermute | solution.py:366
  154.3 3.6 %collective-permute-start.25 = (f32[512]{0:T(512)S(1)}, f32[512]{0:T(512)S(1)}, u32[]{:S(2)}, u32[]{:S(2)}) collective-permute-start(f32[512]{0:T(512)S(1)} %bitcast.100), channel_id=1, source_target_pairs={{0,2},{2,0},{1,3},{3,1},{4,6},{6,4},{5,7},{7,5},{8,10},{10,8},{9,1... | collective-permute-start | bytes 6152 | tf_op jit(solution)/shard_map/ppermute | solution.py:365

commit v2 on v0

v2 whole, which is shorter than its diff:
```python
import functools

import jax
import jax.numpy as jnp
from jax import lax
from jax.experimental import pallas as pl
from jax.experimental.pallas import tpu as pltpu
from jax.sharding import PartitionSpec as P

HD = 128
VMEM_LIMIT = 24 << 20
BRIEF = pl.CostEstimate(flops=1, bytes_accessed=1, transcendentals=0)
ANY = pl.BlockSpec(memory_space=pltpu.HBM)
WAITED = pl.BlockSpec(memory_space=pl.ANY)
VMEM = pl.BlockSpec(memory_space=pltpu.VMEM)
SMEM = pl.BlockSpec(memory_space=pltpu.SMEM)


def pass_kernel(*refs):
    del refs


def after(passing, waited):
    many = len(passing)
    out = pl.pallas_call(
        pass_kernel,
        out_shape=[jax.ShapeDtypeStruct(a.shape, a.dtype) for a in passing],
        in_specs=[ANY] * many + [WAITED] * len(waited),
        out_specs=[ANY] * many,
        input_output_aliases={i: i for i in range(many)},
        cost_estimate=BRIEF,
        compiler_params=pltpu.CompilerParams(has_side_effects=True),
    )(*passing, *waited)
    return list(out)


def shift_pairs(count, step):
    return [(i, (i + step) % count) for i in range(count)]


def ring_order(count):
    return [0] + list(range(1, count, 2)) + [i for i in range(count - 1, 0, -1) if i % 2 == 0]


def pack_kernel(
    me, ancestry, lengths, queries, new_keys, new_values, waited,
    blobs, particle, length, pick, rows, request, seen, *, count, capacity
):
    del waited
    slots = queries.shape[0]
    at = 0
    for source in (queries, new_keys, new_values):
        for h in range(source.shape[1] // HD):
            rows[:, at, :] = source[:, h * HD : (h + 1) * HD].astype(jnp.float32)
            at += 1
    here = me[0]
    for k in range(count):
        seen[k] = 0

    def clear(i, carry):
        request[i] = 0
        particle[i] = 0
        length[i] = 1
        return carry

    lax.fori_loop(0, count * capacity, clear, 0)

    def ask(j, carry):
        owner = ancestry[here * slots + j] // slots
        rank = jnp.minimum(seen[owner], capacity - 1)
        seen[owner] = rank + 1
        pick[j] = owner * capacity + rank
        request[owner * capacity + rank] = j
        return carry

    lax.fori_loop(0, slots, ask, 0)

    def fill(i, carry):
        for k in range(count):
            blobs[k, i] = rows[request[k * capacity + i]].astype(jnp.bfloat16)
        return carry

    lax.fori_loop(0, capacity, fill, 0)
    for k in range(count):

        def answer(p, rank):
            ancestor = ancestry[k * slots + p]
            local = ancestor - here * slots
            match = (local >= 0) & (local < slots)
            at = k * capacity + jnp.minimum(rank, capacity - 1)

            @pl.when(match)
            def _():
                particle[at] = local
                length[at] = lengths[ancestor]

            return rank + match.astype(jnp.int32)

        lax.fori_loop(0, slots, answer, 0)


def pack(me, ancestry, lengths, queries, new_keys, new_values, waited, count, capacity):
    slots = queries.shape[0]
    depth = (queries.shape[1] + new_keys.shape[1] + new_values.shape[1]) // HD
    table = jax.ShapeDtypeStruct((count * capacity,), jnp.int32)
    out = pl.pallas_call(
        functools.partial(pack_kernel, count=count, capacity=capacity),
        out_shape=[jax.ShapeDtypeStruct((count, capacity, depth, HD), jnp.bfloat16)]
        + [table, table, jax.ShapeDtypeStruct((slots,), jnp.int32)],
        in_specs=[SMEM] * 3 + [VMEM] * 3 + [ANY],
        out_specs=[VMEM] + [SMEM] * 3,
        scratch_shapes=[
            pltpu.VMEM((slots, depth, HD), jnp.float32),
            pltpu.SMEM((count * capacity,), jnp.int32),
            pltpu.SMEM((count,), jnp.int32),
        ],
        cost_estimate=BRIEF,
        compiler_params=pltpu.CompilerParams(vmem_limit_bytes=VMEM_LIMIT),
    )(me, ancestry, lengths, queries, new_keys, new_values, waited)
    return out


def serve_kernel(particle, page_table, lengths, blobs, key_pages, value_pages, outs, *, kv_local, unroll):
    count, capacity, heads = outs.shape[:3]
    group_size = heads // kv_local
    pages = page_table.shape[1]
    context = pages * key_pages.shape[1]
    score_scale = 1.0 / HD**0.5
    lanes_kv = lax.broadcasted_iota(jnp.int32, (heads, kv_local * HD), 1) // HD
    rows_kv = lax.broadcasted_iota(jnp.int32, (heads, kv_local * HD), 0) // group_size
    diagonal = lanes_kv == rows_kv
    positions = lax.broadcasted_iota(jnp.int32, (heads, context), 1)

    def spread(x):
        return jnp.broadcast_to(x[:, None, :], (kv_local, group_size, HD)).reshape(heads, HD)

    def together(k, slots):
        scores, own_products, own_values = [], [], []
        for slot in slots:
            at = k * capacity + slot
            rows = blobs[k, slot]
            query = rows[:heads].astype(jnp.float32)
            own_key = rows[heads : heads + kv_local].astype(jnp.float32)
            own_value = rows[heads + kv_local :].astype(jnp.float32)
            wide = jnp.concatenate([query] * kv_local, axis=1)
            wide = jnp.where(diagonal, wide, 0.0).astype(jnp.bfloat16)
            keys = jnp.concatenate(
                [key_pages[page_table[particle[at], i]] for i in range(pages)], axis=0
            )
            score = lax.dot_general(
                wide, keys, (((1,), (1,)), ((), ())), preferred_element_type=jnp.float32
            ) * score_scale
            scores.append(jnp.where(positions < lengths[at], score, -1e30))
            own_products.append(query * spread(own_key))
            own_values.append(spread(own_value))
        score = jnp.concatenate(scores, axis=0)
        top = jnp.max(score, axis=1, keepdims=True)
        weights = jnp.exp(score - top)
        own_score = jnp.sum(jnp.concatenate(own_products, axis=0), axis=1, keepdims=True) * score_scale
        own = jnp.exp(own_score - top)
        total = jnp.sum(weights, axis=1, keepdims=True) + own
        weights = weights.astype(jnp.bfloat16)
        for u, slot in enumerate(slots):
            at = k * capacity + slot
            mine = slice(u * heads, (u + 1) * heads)
            values = jnp.concatenate(
                [value_pages[page_table[particle[at], i]] for i in range(pages)], axis=0
            )
            mixed = jnp.dot(weights[mine], values, preferred_element_type=jnp.float32)
            numerator = jnp.concatenate(
                [
                    mixed[g * group_size : (g + 1) * group_size, g * HD : (g + 1) * HD]
                    for g in range(kv_local)
                ],
                axis=0,
            )
            result = (numerator + own[mine] * own_values[u]) / total[mine]
            outs[k, slot] = result.astype(jnp.bfloat16)

    def body(k, carry):
        for i in range(0, capacity, unroll):
            together(k, range(i, min(i + unroll, capacity)))
        return carry

    lax.fori_loop(0, count, body, 0)


def serve(particle, page_table, lengths, blobs, key_pages, value_pages):
    count, capacity, depth = blobs.shape[:3]
    kv_local = key_pages.shape[2] // HD
    heads = depth - 2 * kv_local
    return pl.pallas_call(
        functools.partial(serve_kernel, kv_local=kv_local, unroll=12),
        out_shape=jax.ShapeDtypeStruct((count, capacity, heads, HD), jnp.bfloat16),
        in_specs=[SMEM] * 3 + [VMEM] * 3,
        out_specs=VMEM,
        cost_estimate=BRIEF,
        compiler_params=pltpu.CompilerParams(vmem_limit_bytes=VMEM_LIMIT),
    )(particle, page_table, lengths, blobs, key_pages, value_pages)


def pick_kernel(pick, parts, out, rows):
    slots = out.shape[0]
    capacity = parts.shape[1]

    def take(j, carry):
        rows[j] = parts[pick[j] // capacity, lax.rem(pick[j], capacity)].astype(jnp.float32)
        return carry

    lax.fori_loop(0, slots, take, 0)
    for h in range(rows.shape[1]):
        out[:, h * HD : (h + 1) * HD] = rows[:, h, :].astype(jnp.bfloat16)


def pick_up(pick, parts):
    heads = parts.shape[2]
    slots = pick.shape[0]
    return pl.pallas_call(
        pick_kernel,
        out_shape=jax.ShapeDtypeStruct((slots, heads * HD), jnp.bfloat16),
        in_specs=[SMEM, VMEM],
        out_specs=VMEM,
        scratch_shapes=[pltpu.VMEM((slots, heads, HD), jnp.float32)],
        cost_estimate=BRIEF,
        compiler_params=pltpu.CompilerParams(vmem_limit_bytes=VMEM_LIMIT),
    )(pick, parts)


class Attention:
    def __init__(self, queries, new_keys, new_values, key_pages, value_pages, page_table, ancestry, lengths):
        self.count = lax.axis_size("batch")
        slots = page_table.shape[0]
        self.capacity = max(2, (2 * slots + self.count - 1) // self.count)
        self.rows = (ancestry, lengths, queries[0], new_keys[0], new_values[0])
        self.page_table, self.keys, self.values = page_table, key_pages[0], value_pages[0]

    def pack(self, waited):
        me = lax.axis_index("batch").reshape(1).astype(jnp.int32)
        blobs, self.particle, self.lengths, self.pick = pack(
            me, *self.rows, waited, self.count, self.capacity
        )
        return blobs

    def send(self, blobs):
        return lax.all_to_all(blobs, "batch", split_axis=0, concat_axis=0, tiled=True)

    def answer(self, arrived):
        return serve(
            self.particle, self.page_table, self.lengths, arrived, self.keys, self.values
        )

    def finish(self, returned):
        return pick_up(self.pick, returned)[None]


def cut_kernel(me, weight, out, sem, *, back, other, y_count):
    share, width = out.shape
    core = 1 - me[2] if other else me[2]
    rows = pl.ds(pl.multiple_of(lax.rem(me[3] + back, y_count) * share, share), share)
    lanes = pl.ds(pl.multiple_of(core * width, width), width)
    copy = pltpu.make_async_copy(weight.at[rows, lanes], out, sem)
    copy.start()
    copy.wait()


def cut_share(me, weight, share, width, y_count, other, back):
    return pl.pallas_call(
        functools.partial(cut_kernel, back=back, other=other, y_count=y_count),
        out_shape=jax.ShapeDtypeStruct((share, width), weight.dtype),
        in_specs=[SMEM, ANY],
        out_specs=VMEM,
        scratch_shapes=[pltpu.SemaphoreType.DMA],
        cost_estimate=BRIEF,
        compiler_params=pltpu.CompilerParams(vmem_limit_bytes=VMEM_LIMIT),
    )(me, weight)


def power_kernel(x, waited, out):
    del waited
    rows, features = x.shape

    def body(i, carry):
        at = pl.ds(pl.multiple_of(i * HD, HD), HD)
        total = jnp.zeros((HD, HD), jnp.float32)
        for j in range(features // HD):
            v = x[at, j * HD : (j + 1) * HD].astype(jnp.float32)
            total = total + v * v
        out[pl.ds(i, 1), :] = jnp.sum(total.T, axis=0, keepdims=True)
        return carry

    lax.fori_loop(0, rows // HD, body, 0)


def row_power(x, waited):
    return pl.pallas_call(
        power_kernel,
        out_shape=jax.ShapeDtypeStruct((x.shape[0] // HD, HD), jnp.float32),
        in_specs=[VMEM, ANY],
        out_specs=VMEM,
        cost_estimate=BRIEF,
        compiler_params=pltpu.CompilerParams(vmem_limit_bytes=VMEM_LIMIT),
    )(x, waited)


def norm_kernel(me, x, *refs, total, count):
    powers, (gain, *outs) = refs[:count], refs[count:]
    rows, features = x.shape
    part = outs[0].shape[1]
    power = powers[0][...]
    for p in powers[1:]:
        power = power + p[...]
    scale = lax.rsqrt(power / total + 1e-06)
    start = me[0] * features

    for i in range(rows // HD):
        column = jnp.broadcast_to(scale[i : i + 1, :], (HD, HD)).T
        for j in range(features // HD):
            at = (slice(i * HD, (i + 1) * HD), slice(j * HD, (j + 1) * HD))
            lanes = pl.ds(pl.multiple_of(start + j * HD, HD), HD)
            value = (x[at].astype(jnp.float32) * column * gain[:, lanes]).astype(jnp.bfloat16)
            first = j * HD % part
            outs[j * HD // part][at[0], first : first + HD] = value


def normalise(me, x, powers, gain, pieces):
    shape = (x.shape[0], x.shape[1] // pieces)
    return pl.pallas_call(
        functools.partial(
            norm_kernel, total=gain.shape[0], count=len(powers)
        ),
        out_shape=[jax.ShapeDtypeStruct(shape, jnp.bfloat16)] * pieces,
        in_specs=[SMEM] + [VMEM] * (2 + len(powers)),
        out_specs=[VMEM] * pieces,
        cost_estimate=BRIEF,
        compiler_params=pltpu.CompilerParams(vmem_limit_bytes=VMEM_LIMIT),
    )(me, x, *powers, gain[None])


class Layout:
    def __init__(self, order, x_count, y_count, block, features, part):
        self.order, self.x_count, self.y_count = order, x_count, y_count
        self.block, self.features, self.part = block, features, part
        self.share = block // y_count

    def place(self, me, run):
        hops, other, back, row = run
        x, z, s, y = me[0], me[1], me[2], me[3]
        count = len(self.order)
        owner = 0
        for i, at in enumerate(self.order):
            owner = owner + jnp.where(z == at, self.order[(i - hops) % count], 0)
        core = 1 - s if other else s
        feature = (2 * owner + core) * self.block + row
        if back is not None:
            group = y - back
            feature = feature + jnp.where(group < 0, group + self.y_count, group) * self.share
        per_device = self.features // self.part
        index = 0
        for i in range(1, self.x_count * per_device):
            index = index + (feature >= i * self.part).astype(jnp.int32)
        offset = feature - index * self.part
        index = index - x * per_device
        return self.rotated(index, per_device, self.x_count * per_device), offset

    def rotated(self, index, per_device, blocks):
        index = jnp.where(index < 0, index + blocks, index)
        place = 0
        for ahead in range(self.x_count):
            back = (self.x_count - ahead) % self.x_count
            inside = (index >= ahead * per_device) & (index < (ahead + 1) * per_device)
            place = place + jnp.where(inside, index + (back - ahead) * per_device, 0)
        return place


def carried(hops, back, share, first, count):
    runs = []
    for other in (False, True):
        low, high = max(first, other * share), min(first + count, (other + 1) * share)
        if low < high:
            runs.append(((hops, other, back, low - other * share), low - first, high - low))
    return runs


def merge_kernel(*refs):
    *sources, out = refs
    at = 0
    for source in sources:
        out[at : at + source.shape[0]] = source[...]
        at += source.shape[0]


def merge(sources):
    rows = sum(a.shape[0] for a in sources)
    return pl.pallas_call(
        merge_kernel,
        out_shape=jax.ShapeDtypeStruct((rows,) + sources[0].shape[1:], sources[0].dtype),
        in_specs=[VMEM] * len(sources),
        out_specs=VMEM,
        cost_estimate=BRIEF,
        compiler_params=pltpu.CompilerParams(vmem_limit_bytes=VMEM_LIMIT),
    )(*sources)


def split_kernel(source, *refs, pieces):
    outs = refs[-pieces:]
    at = 0
    for out in outs:
        out[...] = source[at : at + out.shape[0]]
        at += out.shape[0]


def split(source, pieces, waited):
    shape = (source.shape[0] // pieces,) + source.shape[1:]
    return pl.pallas_call(
        functools.partial(split_kernel, pieces=pieces),
        out_shape=[jax.ShapeDtypeStruct(shape, source.dtype)] * pieces,
        in_specs=[VMEM] + [WAITED] * len(waited),
        out_specs=[VMEM] * pieces,
        cost_estimate=BRIEF,
        compiler_params=pltpu.CompilerParams(vmem_limit_bytes=VMEM_LIMIT),
    )(source, *waited)


def gemm_kernel(me, *refs, parts, sources, runs, layout, has_acc, final, tile):
    refs = list(refs)
    halves = [refs[:parts], refs[parts : 2 * parts]]
    del refs[: 2 * parts]
    weights = refs[:sources]
    del refs[:sources]
    acc_in = refs.pop(0) if has_acc else None
    bias = class_weight = None
    if final:
        bias, class_weight = refs[:2]
        del refs[:2]
        outs = [refs.pop(0), refs.pop(0)]
    else:
        out = refs.pop(0)
    x_v, w_v, sems = refs
    rows = halves[0][0].shape[0]
    width = w_v.shape[1]
    depths = [depth for _, _, _, depth in runs]
    starts = [sum(depths[:i]) for i in range(len(depths))]
    columns = pl.ds(pl.multiple_of(me[2] * width, width), width)

    def weight_copy(i):
        _, which, row, depth = runs[i]
        source = weights[which]
        lanes = slice(None) if source.shape[1] == width else columns
        source = source.at[row : row + depth, lanes]
        return pltpu.make_async_copy(source, w_v.at[pl.ds(starts[i], depths[i])], sems.at[i, 2])

    def row_copy(i, r, p, offset):
        return pltpu.make_async_copy(
            halves[r][p].at[:, pl.ds(offset, depths[i])],
            x_v.at[pl.ds(r * rows, rows), pl.ds(starts[i], depths[i])],
            sems.at[i, r],
        )

    for i, (run, _, _, _) in enumerate(runs):
        weight_copy(i).start()
        part, offset = layout.place(me, run)
        offset = pl.multiple_of(offset, HD)
        for r in range(2):
            for p in range(parts):
                pl.when(part == p)(row_copy(i, r, p, offset).start)
    groups = []
    i = 0
    while i < len(runs):
        j, depth = i, 0
        while j < len(runs) and depth < 1024:
            depth += depths[j]
            j += 1
        groups.append((i, j))
        i = j
    for g, (first, last) in enumerate(groups):
        for i in range(first, last):
            weight_copy(i).wait()
            for r in range(2):
                row_copy(i, r, 0, 0).wait()
        k0 = starts[first]
        k1 = starts[last - 1] + depths[last - 1]

        def body(m, carry, target=None, base=0):
            at = pl.ds(pl.multiple_of(base + m * tile, tile), tile)
            product = jnp.dot(x_v[at, k0:k1], w_v[k0:k1, :], preferred_element_type=jnp.float32)
            if g > 0:
                total = out[at, :] + product
            elif has_acc:
                total = acc_in[at, :] + product
            else:
                total = product
            if target is not None:
                hidden = jnp.maximum(total + bias[:, columns], 0.0).astype(jnp.bfloat16)
                logits = lax.dot_general(
                    class_weight[:, columns],
                    hidden,
                    (((1,), (1,)), ((), ())),
                    preferred_element_type=jnp.float32,
                )
                target[:, pl.ds(pl.multiple_of(m * tile, tile), tile)] = logits[1:2] - logits[0:1]
            else:
                out[at, :] = total
            return carry

        if final:
            for r in range(2):
                lax.fori_loop(
                    0, rows // tile, functools.partial(body, target=outs[r], base=r * rows), 0
                )
        else:
            lax.fori_loop(0, 2 * rows // tile, body, 0)


def gemm(me, layout, halves, chunks, acc=None, tail=None):
    weights = [w for w, _ in chunks]
    runs = [(run, i, row, d) for i, (_, found) in enumerate(chunks) for run, row, d in found]
    parts = len(halves[0])
    rows = halves[0][0].shape[0]
    depth = sum(d for _, _, _, d in runs)
    width = min(w.shape[1] for w in weights)
    args = [me, *halves[0], *halves[1], *weights]
    specs = [SMEM] + [ANY] * (2 * parts + len(weights))
    if acc is not None:
        args.append(acc)
        specs.append(VMEM)
    if tail is not None:
        args += list(tail)
        specs += [VMEM] * 2
        out_shape = [jax.ShapeDtypeStruct((1, rows), jnp.float32)] * 2
        out_specs = [VMEM] * 2
    else:
        out_shape = jax.ShapeDtypeStruct((2 * rows, width), jnp.float32)
        out_specs = VMEM
    return pl.pallas_call(
        functools.partial(
            gemm_kernel,
            parts=parts,
            sources=len(weights),
            runs=tuple(runs),
            layout=layout,
            has_acc=acc is not None,
            final=tail is not None,
            tile=256,
        ),
        out_shape=out_shape,
        in_specs=specs,
        out_specs=out_specs,
        scratch_shapes=[
            pltpu.VMEM((2 * rows, depth), jnp.bfloat16),
            pltpu.VMEM((depth, width), jnp.bfloat16),
            pltpu.SemaphoreType.DMA((len(runs), 3)),
        ],
        cost_estimate=BRIEF,
        compiler_params=pltpu.CompilerParams(vmem_limit_bytes=VMEM_LIMIT),
    )(*args)


def both(attention, step_rows, norm_gain, head_weight, head_bias, class_weight, class_bias):
    z_count, x_count = lax.axis_size("batch"), lax.axis_size("mp")
    y_count = lax.axis_size("group")
    me = jnp.stack([lax.axis_index(a) for a in ("mp", "batch", "section", "group")]).astype(jnp.int32)
    swap = shift_pairs(2, 1)
    rows, features = step_rows.shape
    block, columns = head_weight.shape
    width = columns // 2
    share = block // y_count
    order = ring_order(z_count)
    ring = [(order[i], order[(i + 1) % z_count]) for i in range(z_count)]
    pieces, final_pieces = 2, 2
    layout = Layout(order, x_count, y_count, block, features, features // pieces)

    def forward(t):
        return lax.ppermute(t, "batch", ring)

    def over_group(t):
        return [lax.ppermute(t, "group", shift_pairs(y_count, k)) for k in range(1, y_count)]

    own = cut_share(me, head_weight, share, width, y_count, False, 0)
    given = [cut_share(me, head_weight, share, width, y_count, True, k) for k in range(y_count)]
    hop = [forward(own)]
    siblings = [lax.ppermute(g, "section", swap) for g in given]
    hop.append(forward(siblings[0]))
    power = row_power(step_rows, siblings[0])
    powers = [power] + [
        lax.ppermute(power, "mp", shift_pairs(x_count, k)) for k in range(1, x_count)
    ]
    mine = list(normalise(me, step_rows, powers, norm_gain, pieces))
    raw = [
        lax.ppermute(part, "mp", shift_pairs(x_count, k))
        for k in range(1, x_count)
        for part in mine
    ]
    theirs = [lax.ppermute(part, "section", swap) for part in mine]
    arrived = attention.send(attention.pack(siblings[0]))
    tail = [head_bias[None], jnp.pad(class_weight.T, ((0, 14), (0, 0)))]
    chunks = [(head_weight, [((0, False, None, 0), 0, block)])] + [
        (t, [((0, True, (y_count - k) % y_count, 0), 0, share)]) for k, t in enumerate(siblings)
    ]
    whole = merge(hop)
    waited = siblings[1:] + mine[:1]
    for h in range(1, z_count - 2):
        swapped = over_group(whole)
        chunks += [
            (t, carried(h, k, share, 0, 2 * share)) for k, t in enumerate([whole] + swapped)
        ]
        hop = forward(whole)
        if h < z_count - 3:
            (whole,) = after([hop], waited + swapped)
            waited = []
        else:
            whole = hop
    cuts = split(whole, final_pieces, waited + swapped + raw + theirs[:1] + [arrived])
    last = [forward(t) for t in cuts]
    swapped = over_group(whole)
    second = [
        (t, carried(z_count - 2, k, share, 0, 2 * share)) for k, t in enumerate([whole] + swapped)
    ]
    mine += raw
    theirs += [lax.ppermute(part, "section", swap) for part in mine[pieces:]]
    results = attention.answer(arrived)
    returned = attention.send(results)
    acc = gemm(me, layout, (mine, theirs), chunks)
    depth = 2 * share // final_pieces
    ends = []
    marks = [[results], [acc]] + [[] for _ in last[2:]]
    for j, t in enumerate(last):
        (t,) = after([t], marks[j])
        ends.append(
            [(u, carried(z_count - 1, k, share, j * depth, depth)) for k, u in enumerate([t] + over_group(t))]
        )
    acc = gemm(me, layout, (mine, theirs), second, acc)
    attended = attention.finish(returned)
    acc = gemm(me, layout, (mine, theirs), sum(ends[:-1], []) + ends[-1][:1], acc)
    kept, given = gemm(me, layout, (mine, theirs), ends[-1][1:], acc, tail)
    total = kept + lax.ppermute(given, "section", swap)
    for k in range(1, x_count):
        total = total + lax.ppermute(kept, "mp", shift_pairs(x_count, k))
        total = total + lax.ppermute(
            given,
            ("mp", "section"),
            [
                (i * 2 + c, ((i + k) % x_count) * 2 + 1 - c)
                for i in range(x_count)
                for c in range(2)
            ],
        )
    return attended, total[0] + (class_bias[1] - class_bias[0])


def judge_gathered(step_rows, norm_gain, head_weight, head_bias, class_weight, class_bias):
    full_rows = lax.all_gather(step_rows, "mp", axis=1, tiled=True)
    row_values = full_rows.astype(jnp.float32)
    power = jnp.mean(row_values * row_values, axis=1, keepdims=True)
    normed = (row_values * lax.rsqrt(power + 1e-06) * norm_gain).astype(jnp.bfloat16)
    projected = jnp.dot(
        normed,
        lax.all_gather(head_weight, ("batch", "section"), axis=0, tiled=True),
        preferred_element_type=jnp.float32,
    )
    hidden = jnp.maximum(projected + head_bias, 0.0).astype(jnp.bfloat16)
    partial_logits = jnp.dot(hidden, class_weight, preferred_element_type=jnp.float32)
    logits = lax.psum(partial_logits, "mp") + class_bias
    return logits[:, 1] - logits[:, 0]


def per_device(
    queries,
    new_keys,
    new_values,
    key_pages,
    value_pages,
    page_table,
    ancestry,
    lengths,
    step_rows,
    norm_gain,
    head_weight,
    head_bias,
    class_weight,
    class_bias,
):
    attention = Attention(
        queries, new_keys, new_values, key_pages, value_pages, page_table, ancestry, lengths
    )
    verifier = (step_rows, norm_gain, head_weight, head_bias, class_weight, class_bias)
    ring_fits = (
        4 <= lax.axis_size("batch") <= 8
        and lax.axis_size("mp") > 1
        and lax.axis_size("section") == 2
        and head_weight.shape[0] % (128 * lax.axis_size("group")) == 0
        and step_rows.shape[1] % (2 * head_weight.shape[0]) == 0
        and head_weight.shape[1] % 256 == 0
        and step_rows.shape[1] % head_weight.shape[0] == 0
    )
    if ring_fits:
        return both(attention, *verifier)
    arrived = attention.send(attention.pack(step_rows))
    returned = attention.send(attention.answer(arrived))
    return attention.finish(returned), judge_gathered(*verifier)


def solution(mesh):
    placed = (
        P("section", ("group", "batch"), "mp"),
        P("section", ("group", "batch"), "mp"),
        P("section", ("group", "batch"), "mp"),
        P("section", ("group", "batch"), None, "mp"),
        P("section", ("group", "batch"), None, "mp"),
        P(("group", "batch"), None),
        P("group"),
        P("group"),
        P(("group", "batch", "section"), "mp"),
        P(),
        P(("batch", "section"), "mp"),
        P("mp"),
        P("mp", None),
        P(),
    )
    return jax.shard_map(
        per_device,
        mesh=mesh,
        in_specs=placed,
        out_specs=(P("section", ("group", "batch"), "mp"), P(("group", "batch", "section"))),
        check_vma=False,
    )
```

time: 254 us -> 139 us (0.55)
  waiting for transfers between devices: 150 us -> 51.2 us
  Pallas kernels: 0 us -> 39.3 us
  matrix products: 21.9 us -> 0 us
  local copies, waits for them, and re-layouts: 31.5 us -> 14.4 us
  between operations: 14.4 us -> 2.26 us
  starting transfers between devices: 18.4 us -> 30.2 us
  other arithmetic: 12.3 us -> 0.67 us
  blocking collectives: 4.95 us -> 0 us
    all_gather x2 -> x0, waiting for transfers between devices: 115 us -> none  [the longest x1 115 us: per_device(): lax.all_gather(head_weight, ('batch', 'section'), axis=0, tiled=True)]
    ppermute x0 -> x21, waiting for transfers between devices: none -> 44.9 us  [the longest x5 23.4 us: forward(): return lax.ppermute(t, 'batch', ring)]
    pallas_call x0 -> x16, Pallas kernels: none -> 39.3 us  [the longest x4 21.6 us: gemm(): pl.pallas_call(functools.partial(gemm_kernel, parts=parts, sources=len(we...]
    all_to_all x4 -> x2, waiting for transfers between devices: 33.1 us -> 6.3 us  [send(): lax.all_to_all(blobs, 'batch', split_axis=0, concat_axis=0, tiled=True)]
    dot_general x4 -> x0, matrix products: 21.9 us -> none  [the longest x1 14.1 us: per_device(): jnp.dot(hidden, class_weight, preferred_element_type=jnp.float32)]
    ppermute x0 -> x21, starting transfers between devices: none -> 19.9 us  [the longest x5 7.63 us: forward(): return lax.ppermute(t, 'batch', ring)]
    reshape x7 -> x0, local copies, waits for them, and re-layouts: 14.3 us -> none  [the longest x1 5.62 us: per_device(): key_pages[:, served_pages].reshape(batch_rows, context, kv_local, HD)]
    gather x12 -> x0, local copies, waits for them, and re-layouts: 11.5 us -> none  [the longest x4 3.63 us: pick_part(): jnp.take(received, flat_index, axis=1)]
  transfers between devices with their start and end apart: 6 -> 23, of which waited for: 4 -> 6; matrix products, arithmetic and copies ran while one was open for 20% -> 0% of each run, Pallas kernels for 0% -> 28%
where the time goes in v2:
time: 139 us; the launch traced here: 138 us
  waiting for transfers between devices  51.2 us (37%)
  Pallas kernels  39.3 us (28%)
  starting transfers between devices  30.2 us (22%)
  local copies, waits for them, and re-layouts  14.4 us (10%)
  between operations  2.26 us (2%)
    ppermute x5, waiting for transfers between devices, forward(): return lax.ppermute(t, 'batch', ring)  23.4 us
    pallas_call x4, Pallas kernels, gemm(): pl.pallas_call(functools.partial(gemm_kernel, parts=parts, sources=len(we...  21.6 us
    ppermute x2, waiting for transfers between devices, both(): lax.ppermute(part, 'mp', shift_pairs(x_count, k))  19.4 us
    unnamed x55, local copies, waits for them, and re-layouts  13.8 us
    all_to_all x2, starting transfers between devices, send(): lax.all_to_all(blobs, 'batch', split_axis=0, concat_axis=0, tiled=True)  10.3 us
    ppermute x5, starting transfers between devices, forward(): return lax.ppermute(t, 'batch', ring)  7.63 us
    all_to_all x2, waiting for transfers between devices, send(): lax.all_to_all(blobs, 'batch', split_axis=0, concat_axis=0, tiled=True)  6.3 us
    ppermute x4, starting transfers between devices, over_group(): lax.ppermute(t, 'group', shift_pairs(y_count, k))  4.14 us
  transfers between devices with their start and end apart: 23, of which 6 were waited for; matrix products, arithmetic and copies ran while one was open for 0% of the time, Pallas kernels for 28%

profile of v2, /device:TPU:0, one launch (start us, length us, event | category | flops | bytes accessed | tf_op | source)
XLA Modules:
  0.0 138.2 jit_solution(8563924866852331980)
XLA Ops:
  0.6 0.1 pad_add_fusion.me
  0.7 1.6 %copy-done.2 = bf16[512,2048]{1,0:T(8,128)(2,1)S(1)} copy-done((bf16[512,2048]{1,0:T(8,128)(2,1)S(1)}, bf16[512,2048]{1,0:T(8,128)(2,1)}, u32[]{:S(2)}) %copy-start.2) | copy-done | bytes 2097176
  2.3 0.6 shard_map.149
  2.9 0.0 copy-start.7
  2.9 0.5 collective-permute-start
  3.5 0.6 shard_map.155
  4.1 0.0 copy-start.20
  4.1 2.6 %collective-permute-start.8 = (bf16[256,1024]{1,0:T(8,128)(2,1)S(1)}, bf16[256,1024]{1,0:T(8,128)(2,1)S(1)}, u32[]{:S(2)}, u32[]{:S(2)}) collective-permute-start(bf16[256,1024]{1,0:T(8,128)(2,1)S(1)} %shard_map.155), channel_id=1, source_target_pairs={{0,4},{4,12},{12,8},{8,0},{1,5},{5,13},{13,9},{9,1},{2,6},{6,14},{... | collective-permute-start | bytes 1572872 | tf_op jit(solution)/shard_map/ppermute | solution.py:573
  6.7 0.0 collective-permute-done.waited.refs_9_
  6.7 2.6 %collective-permute-start.9 = (bf16[256,1024]{1,0:T(8,128)(2,1)S(1)}, bf16[256,1024]{1,0:T(8,128)(2,1)S(1)}, u32[]{:S(2)}, u32[]{:S(2)}) collective-permute-start(bf16[256,1024]{1,0:T(8,128)(2,1)S(1)} %collective-permute-done.waited.refs_9_), channel_id=1, source_target_pairs={{0,4},{4,12},{12,8},{8,0},{1,5},{5,13},{13,9},{9,1},{2,6},{6,14},{... | collective-permute-start | bytes 1572872 | tf_op jit(solution)/shard_map/ppermute | solution.py:573
  9.3 0.6 shard_map.157
  9.9 0.1 collective-permute-start.11
  10.0 0.7 shard_map.153.refs_0_
  10.7 1.6 %collective-permute-start.1 = (f32[4,128]{1,0:T(4,128)S(1)}, f32[4,128]{1,0:T(4,128)S(1)}, u32[]{:S(2)}, u32[]{:S(2)}) collective-permute-start(f32[4,128]{1,0:T(4,128)S(1)} %shard_map.153.refs_0_), channel_id=1, source_target_pairs={{0,2},{2,0},{1,3},{3,1},{4,6},{6,4},{5,7},{7,5},{8,10},{10,8},{9,1... | collective-permute-start | bytes 6152 | tf_op jit(solution)/shard_map/ppermute | solution.py:585
  12.3 2.1 %collective-permute-done.1.refs_1_ = f32[4,128]{1,0:T(4,128)S(1)} collective-permute-done((f32[4,128]{1,0:T(4,128)S(1)}, f32[4,128]{1,0:T(4,128)S(1)}, u32[]{:S(2)}, u32[]{:S(2)}) %collective-permute-start.1) | collective-permute-done | bytes 2080 | tf_op jit(solution)/shard_map/ppermute | solution.py:585
  14.4 0.0 copy-start.22
  14.4 0.0 copy-start.23
  14.4 2.2 %shard_map.154 = (bf16[512,1024]{1,0:T(8,128)(2,1)S(1)}, bf16[512,1024]{1,0:T(8,128)(2,1)}) custom-call(s32[4]{0:T(128)S(1)} %pad_add_fusion.me, bf16[512,2048]{1,0:T(8,128)(2,1)S(1)} %copy-done.7, f32[4,128]{1,0:T(4,128)S(1)} %shard_map.153.refs_0_, f32[4,128]{1,0:T(4,128)S(1)} %collective-permute-done.1.refs_1_, f32[1,4096]{1,0:T(1,128)S(1)} %bitcast.20), custom_call_target="tpu_custom_call" | custom-call | flops 1 | bytes 1 | tf_op jit(solution)/shard_map/pallas_call | solution.py:327
  16.6 1.5 %collective-permute-start.3 = (bf16[512,1024]{1,0:T(8,128)(2,1)}, bf16[512,1024]{1,0:T(8,128)(2,1)}, u32[]{:S(2)}, u32[]{:S(2)}) collective-permute-start(bf16[512,1024]{1,0:T(8,128)(2,1)} %get-tuple-element.17.refs_1_), channel_id=1, source_target_pairs={{0,2},{2,0},{1,3},{3,1},{4,6},{6,4},{5,7},{7,5},{8,10},{10,8},{9,1... | collective-permute-start | bytes 3145736 | tf_op jit(solution)/shard_map/ppermute | solution.py:589
  18.1 0.0 collective-permute-start.4
  18.1 2.4 %collective-permute-done.8.refs_0_ = bf16[256,1024]{1,0:T(8,128)(2,1)S(1)} collective-permute-done((bf16[256,1024]{1,0:T(8,128)(2,1)S(1)}, bf16[256,1024]{1,0:T(8,128)(2,1)S(1)}, u32[]{:S(2)}, u32[]{:S(2)}) %collective-permute-start.8) | collective-permute-done | bytes 524320 | tf_op jit(solution)/shard_map/ppermute | solution.py:573
  20.5 1.7 %collective-permute-start.2 = (bf16[512,1024]{1,0:T(8,128)(2,1)S(1)}, bf16[512,1024]{1,0:T(8,128)(2,1)}, u32[]{:S(2)}, u32[]{:S(2)}) collective-permute-start(bf16[512,1024]{1,0:T(8,128)(2,1)S(1)} %get-tuple-element.16.refs_1_.refs_0_), channel_id=1, source_target_pairs={{0,2},{2,0},{1,3},{3,1},{4,6},{6,4},{5,7},{7,5},{8,10},{10,8},{9,1... | collective-permute-start | bytes 3145736 | tf_op jit(solution)/shard_map/ppermute | solution.py:589
  22.3 9.3 %collective-permute-done.9.refs_1_ = bf16[256,1024]{1,0:T(8,128)(2,1)S(1)} collective-permute-done((bf16[256,1024]{1,0:T(8,128)(2,1)S(1)}, bf16[256,1024]{1,0:T(8,128)(2,1)S(1)}, u32[]{:S(2)}, u32[]{:S(2)}) %collective-permute-start.9) | collective-permute-done | bytes 524320 | tf_op jit(solution)/shard_map/ppermute | solution.py:573
  31.5 1.1 shard_map.156.refs_11_
  32.6 1.6 %collective-permute-start.12 = (bf16[512,1024]{1,0:T(8,128)(2,1)}, bf16[512,1024]{1,0:T(8,128)(2,1)}, u32[]{:S(2)}, u32[]{:S(2)}) collective-permute-start(bf16[512,1024]{1,0:T(8,128)(2,1)} %shard_map.156.refs_11_), channel_id=1, source_target_pairs={{0,16},{16,0},{1,17},{17,1},{2,18},{18,2},{3,19},{19,3},{4,20},{20... | collective-permute-start | bytes 3145736 | tf_op jit(solution)/shard_map/ppermute | solution.py:576
  34.2 0.8 collective-permute-start.10
  35.0 3.6 %shard_map.150 = (bf16[4,12,40,128]{3,2,1,0:T(8,128)(2,1)S(1)}, s32[48]{0:T(128)S(1)}, s32[48]{0:T(128)S(1)}, s32[24]{0:T(128)S(1)}) custom-call(s32[1]{0:T(128)} %bitcast.me, s32[96]{0:T(128)S(1)} %copy-done.22, s32[96]{0:T(128)S(1)} %copy-done.23, bf16[24,4096]{1,0:T(8,128)(2,1)S(1)} %bitcast.17, bf16[24,512]{1,0:T(8,128)(2,1)S(1)} %bitcast.18, ...), custom_call_target="tpu_custom_call" | custom-call | flops 1 | bytes 1 | tf_op jit(solution)/shard_map/pallas_call | solution.py:106
  38.6 0.8 copy-done.16
  39.4 4.6 %all-to-all-start = ((bf16[4,12,40,128]{3,2,1,0:T(8,128)(2,1)}), bf16[4,12,40,128]{3,2,1,0:T(8,128)(2,1)S(1)}, u32[]{:S(2)}, u32[]{:S(2)}) async-start(bf16[4,12,40,128]{3,2,1,0:T(8,128)(2,1)} %copy-done.16), calls=%async_computation | async-start | bytes 983040 | tf_op jit(solution)/shard_map/all_to_all | solution.py:245
  44.1 0.0 collective-permute-done.3.refs_4_.refs_3_
  44.1 0.1 collective-permute-start.5
  44.2 0.5 collective-permute-start.7
  44.7 19.4 %collective-permute-done.2.refs_3_.refs_2_ = bf16[512,1024]{1,0:T(8,128)(2,1)} collective-permute-done((bf16[512,1024]{1,0:T(8,128)(2,1)S(1)}, bf16[512,1024]{1,0:T(8,128)(2,1)}, u32[]{:S(2)}, u32[]{:S(2)}) %collective-permute-start.2) | collective-permute-done | bytes 1048608 | tf_op jit(solution)/shard_map/ppermute | solution.py:589
  64.1 6.3 %all-to-all-done.blobs.refs_6_ = bf16[4,12,40,128]{3,2,1,0:T(8,128)(2,1)S(1)} async-done(((bf16[4,12,40,128]{3,2,1,0:T(8,128)(2,1)}), bf16[4,12,40,128]{3,2,1,0:T(8,128)(2,1)S(1)}, u32[]{:S(2)}, u32[]{:S(2)}) %all-to-all-start) | async-done | bytes 491552 | tf_op jit(solution)/shard_map/all_to_all | solution.py:245
  70.4 2.3 %shard_map.158 = (bf16[256,1024]{1,0:T(8,128)(2,1)S(1)}, bf16[256,1024]{1,0:T(8,128)(2,1)}) custom-call(bf16[512,1024]{1,0:T(8,128)(2,1)} %collective-permute-done.10.source.refs_8_, bf16[256,1024]{1,0:T(8,128)(2,1)S(1)} %collective-permute-done.11.refs_0_.refs_10_, bf16[512,1024]{1,0:T(8,128)(2,1)S(1)} %get-tuple-element.16.refs_1_.refs_0_, ...), custom_call_target="tpu_custom_call" | custom-call | flops 1 | bytes 1 | tf_op jit(solution)/shard_map/pallas_call | solution.py:414
  72.7 0.9 collective-permute-start.15
  73.6 0.5 collective-permute-start.17
  74.1 11.7 %collective-permute-done.15.refs_0_ = bf16[256,1024]{1,0:T(8,128)(2,1)} collective-permute-done((bf16[256,1024]{1,0:T(8,128)(2,1)S(1)}, bf16[256,1024]{1,0:T(8,128)(2,1)}, u32[]{:S(2)}, u32[]{:S(2)}) %collective-permute-start.15) | collective-permute-done | bytes 524320 | tf_op jit(solution)/shard_map/ppermute | solution.py:573
  85.8 0.7 collective-permute-start.13
  86.5 0.1 copy.18.page_table
  86.5 1.0 copy-done.11
  87.6 1.4 %copy-done.14 = bf16[1,96,16,512]{3,2,1,0:T(8,128)(2,1)S(1)} copy-done((bf16[1,96,16,512]{3,2,1,0:T(8,128)(2,1)S(1)}, bf16[1,96,16,512]{3,2,1,0:T(8,128)(2,1)}, u32[]{:S(2)}) %copy-start.14) | copy-done | bytes 1572888
  89.0 1.4 %copy-done.15 = bf16[1,96,16,512]{3,2,1,0:T(8,128)(2,1)S(1)} copy-done((bf16[1,96,16,512]{3,2,1,0:T(8,128)(2,1)S(1)}, bf16[1,96,16,512]{3,2,1,0:T(8,128)(2,1)}, u32[]{:S(2)}) %copy-start.15) | copy-done | bytes 1572888
  90.4 4.0 %shard_map.151.refs_1_ = bf16[4,12,32,128]{3,2,1,0:T(8,128)(2,1)} custom-call(s32[48]{0:T(128)S(1)} %get-tuple-element.13.particle, s32[24,4]{1,0:T(8,128)S(1)} %copy.18.page_table, s32[48]{0:T(128)S(1)} %get-tuple-element.14.lengths, bf16[4,12,40,128]{3,2,1,0:T(8,128)(2,1)S(1)} %copy-done.11, bf16[96,16,512]{2,1,0:T(8,128)(2,1)S(1)} %bitcast.15, ...), custom_call_target="tpu_custom_call" | custom-call | flops 1 | bytes 1 | tf_op jit(solution)/shard_map/pallas_call | solution.py:192
  94.4 0.5 collective-permute-start.16
  94.9 1.2 copy-done.5
  96.1 1.0 copy-done.9
  97.2 1.0 copy-done.13
  98.2 7.3 %shard_map.159.refs_1_.refs_10_ = f32[1024,1024]{1,0:T(8,128)S(1)} custom-call(s32[4]{0:T(128)S(1)} %pad_add_fusion.me, bf16[512,1024]{1,0:T(8,128)(2,1)S(1)} %get-tuple-element.16.refs_1_.refs_0_, bf16[512,1024]{1,0:T(8,128)(2,1)} %get-tuple-element.17.refs_1_, bf16[512,1024]{1,0:T(8,128)(2,1)} %collective-permute-done.2.refs_3_.refs_2_, ...), custom_call_target="tpu_custom_call" | custom-call | flops 1 | bytes 1 | tf_op jit(solution)/shard_map/pallas_call | solution.py:534
  105.5 2.0 %copy-done = f32[1024,1024]{1,0:T(8,128)} copy-done((f32[1024,1024]{1,0:T(8,128)}, f32[1024,1024]{1,0:T(8,128)S(1)}, u32[]{:S(2)}) %copy-start) | copy-done | bytes 4194328
  107.5 1.6 %collective-permute-start.14 = (bf16[256,1024]{1,0:T(8,128)(2,1)}, bf16[256,1024]{1,0:T(8,128)(2,1)S(1)}, u32[]{:S(2)}, u32[]{:S(2)}) collective-permute-start(bf16[256,1024]{1,0:T(8,128)(2,1)} %shard_map.160.refs_10_), channel_id=1, source_target_pairs={{0,16},{16,0},{1,17},{17,1},{2,18},{18,2},{3,19},{19,3},{4,20},{20... | collective-permute-start | bytes 1572872 | tf_op jit(solution)/shard_map/ppermute | solution.py:576
  109.1 5.7 %all-to-all-start.1 = ((bf16[4,12,32,128]{3,2,1,0:T(8,128)(2,1)}), bf16[4,12,32,128]{3,2,1,0:T(8,128)(2,1)S(1)}, u32[]{:S(2)}, u32[]{:S(2)}) async-start(bf16[4,12,32,128]{3,2,1,0:T(8,128)(2,1)} %shard_map.151.refs_1_), calls=%async_computation.1 | async-start | bytes 786432 | tf_op jit(solution)/shard_map/all_to_all | solution.py:245
  114.8 2.2 %copy-done.1 = f32[1024,1024]{1,0:T(8,128)S(1)} copy-done((f32[1024,1024]{1,0:T(8,128)S(1)}, f32[1024,1024]{1,0:T(8,128)}, u32[]{:S(2)}) %copy-start.1) | copy-done | bytes 4194328
  117.0 5.7 %shard_map.162.refs_11_ = f32[1024,1024]{1,0:T(8,128)S(1)} custom-call(s32[4]{0:T(128)S(1)} %pad_add_fusion.me, bf16[512,1024]{1,0:T(8,128)(2,1)S(1)} %get-tuple-element.16.refs_1_.refs_0_, bf16[512,1024]{1,0:T(8,128)(2,1)} %get-tuple-element.17.refs_1_, bf16[512,1024]{1,0:T(8,128)(2,1)} %collective-permute-done.2.refs_3_.refs_2_, ...), custom_call_target="tpu_custom_call" | custom-call | flops 1 | bytes 1 | tf_op jit(solution)/shard_map/pallas_call | solution.py:534
  122.7 0.0 copy-start.21
  122.7 4.8 %shard_map.163.refs_9_ = f32[1024,1024]{1,0:T(8,128)S(1)} custom-call(s32[4]{0:T(128)S(1)} %pad_add_fusion.me, bf16[512,1024]{1,0:T(8,128)(2,1)S(1)} %get-tuple-element.16.refs_1_.refs_0_, bf16[512,1024]{1,0:T(8,128)(2,1)} %get-tuple-element.17.refs_1_, bf16[512,1024]{1,0:T(8,128)(2,1)} %collective-permute-done.2.refs_3_.refs_2_, ...), custom_call_target="tpu_custom_call" | custom-call | flops 1 | bytes 1 | tf_op jit(solution)/shard_map/pallas_call | solution.py:534
  127.5 0.0 copy-start.26
  127.5 3.9 %shard_map.164 = (f32[1,512]{1,0:T(1,128)S(1)}, f32[1,512]{1,0:T(1,128)S(1)}) custom-call(s32[4]{0:T(128)S(1)} %pad_add_fusion.me, bf16[512,1024]{1,0:T(8,128)(2,1)S(1)} %get-tuple-element.16.refs_1_.refs_0_, bf16[512,1024]{1,0:T(8,128)(2,1)} %get-tuple-element.17.refs_1_, bf16[512,1024]{1,0:T(8,128)(2,1)} %collective-permute-done.2.refs_3_.refs_2_, ...), custom_call_target="tpu_custom_call" | custom-call | flops 1 | bytes 1 | tf_op jit(solution)/shard_map/pallas_call | solution.py:534
  131.4 0.1 collective-permute-start.20
  131.5 1.6 %collective-permute-start.18 = (f32[1,512]{1,0:T(1,128)S(1)}, f32[1,512]{1,0:T(1,128)S(1)}, u32[]{:S(2)}, u32[]{:S(2)}) collective-permute-start(f32[1,512]{1,0:T(1,128)S(1)} %get-tuple-element.21), channel_id=1, source_target_pairs={{0,1},{1,0},{2,3},{3,2},{4,5},{5,4},{6,7},{7,6},{8,9},{9,8},{10,11... | collective-permute-start | bytes 6152 | tf_op jit(solution)/shard_map/ppermute | solution.py:635
  133.1 0.5 collective-permute-start.19
  133.6 0.6 fusion
  135.5 2.1 %shard_map.152 = bf16[24,4096]{1,0:T(8,128)(2,1)} custom-call(s32[24]{0:T(128)S(1)} %get-tuple-element.12.pick, bf16[4,12,32,128]{3,2,1,0:T(8,128)(2,1)S(1)} %all-to-all-done.1.parts), custom_call_target="tpu_custom_call" | custom-call | flops 1 | bytes 1 | tf_op jit(solution)/shard_map/pallas_call | solution.py:218
  137.6 0.6 add_add_fusion
  (57 shorter events, 0.1 us)
Async XLA Ops:
  0.7 1.6 %copy-start.2 = (bf16[512,2048]{1,0:T(8,128)(2,1)S(1)}, bf16[512,2048]{1,0:T(8,128)(2,1)}, u32[]{:S(2)}) copy-start(bf16[512,2048]{1,0:T(8,128)(2,1)} %refs_8_.1) | copy-start | bytes 6291460
  2.9 7.1 %copy-start.7 = (bf16[512,2048]{1,0:T(8,128)(2,1)S(1)}, bf16[512,2048]{1,0:T(8,128)(2,1)}, u32[]{:S(2)}) copy-start(bf16[512,2048]{1,0:T(8,128)(2,1)} %x.5) | copy-start | bytes 6291460
  2.9 3.8 %collective-permute-start = (bf16[256,1024]{1,0:T(8,128)(2,1)S(1)}, bf16[256,1024]{1,0:T(8,128)(2,1)S(1)}, u32[]{:S(2)}, u32[]{:S(2)}) collective-permute-start(bf16[256,1024]{1,0:T(8,128)(2,1)S(1)} %shard_map.149), channel_id=1, source_target_pairs={{0,1},{1,0},{2,3},{3,2},{4,5},{5,4},{6,7},{7,6},{8,9},{9,8},{10,11... | collective-permute-start | bytes 1572872 | tf_op jit(solution)/shard_map/ppermute | solution.py:581
  4.1 10.3 %copy-start.20 = (f32[4096]{0:T(1024)S(1)}, f32[4096]{0:T(1024)}, u32[]{:S(2)}) copy-start(f32[4096]{0:T(1024)} %param.23) | copy-start | bytes 49156
  4.1 16.4 %collective-permute-start.8 = (bf16[256,1024]{1,0:T(8,128)(2,1)S(1)}, bf16[256,1024]{1,0:T(8,128)(2,1)S(1)}, u32[]{:S(2)}, u32[]{:S(2)}) collective-permute-start(bf16[256,1024]{1,0:T(8,128)(2,1)S(1)} %shard_map.155), channel_id=1, source_target_pairs={{0,4},{4,12},{12,8},{8,0},{1,5},{5,13},{13,9},{9,1},{2,6},{6,14},{... | collective-permute-start | bytes 1572872 | tf_op jit(solution)/shard_map/ppermute | solution.py:573
  6.7 28.3 %copy-start.8 = (bf16[256,1024]{1,0:T(8,128)(2,1)}, bf16[256,1024]{1,0:T(8,128)(2,1)S(1)}, u32[]{:S(2)}) copy-start(bf16[256,1024]{1,0:T(8,128)(2,1)S(1)} %collective-permute-done.waited.refs_9_) | copy-start | bytes 1572868
  6.7 24.8 %collective-permute-start.9 = (bf16[256,1024]{1,0:T(8,128)(2,1)S(1)}, bf16[256,1024]{1,0:T(8,128)(2,1)S(1)}, u32[]{:S(2)}, u32[]{:S(2)}) collective-permute-start(bf16[256,1024]{1,0:T(8,128)(2,1)S(1)} %collective-permute-done.waited.refs_9_), channel_id=1, source_target_pairs={{0,4},{4,12},{12,8},{8,0},{1,5},{5,13},{13,9},{9,1},{2,6},{6,14},{... | collective-permute-start | bytes 1572872 | tf_op jit(solution)/shard_map/ppermute | solution.py:573
  9.9 24.3 %collective-permute-start.11 = (bf16[256,1024]{1,0:T(8,128)(2,1)S(1)}, bf16[256,1024]{1,0:T(8,128)(2,1)S(1)}, u32[]{:S(2)}, u32[]{:S(2)}) collective-permute-start(bf16[256,1024]{1,0:T(8,128)(2,1)S(1)} %shard_map.157), channel_id=1, source_target_pairs={{0,1},{1,0},{2,3},{3,2},{4,5},{5,4},{6,7},{7,6},{8,9},{9,8},{10,11... | collective-permute-start | bytes 1572872 | tf_op jit(solution)/shard_map/ppermute | solution.py:581
  10.7 3.7 %collective-permute-start.1 = (f32[4,128]{1,0:T(4,128)S(1)}, f32[4,128]{1,0:T(4,128)S(1)}, u32[]{:S(2)}, u32[]{:S(2)}) collective-permute-start(f32[4,128]{1,0:T(4,128)S(1)} %shard_map.153.refs_0_), channel_id=1, source_target_pairs={{0,2},{2,0},{1,3},{3,1},{4,6},{6,4},{5,7},{7,5},{8,10},{10,8},{9,1... | collective-permute-start | bytes 6152 | tf_op jit(solution)/shard_map/ppermute | solution.py:585
  14.4 20.6 %copy-start.17 = (bf16[1,24,4096]{2,1,0:T(8,128)(2,1)S(1)}, bf16[1,24,4096]{2,1,0:T(8,128)(2,1)}, u32[]{:S(2)}) copy-start(bf16[1,24,4096]{2,1,0:T(8,128)(2,1)} %param.14) | copy-start | bytes 589828
  14.4 20.6 %copy-start.18 = (bf16[1,24,512]{2,1,0:T(8,128)(2,1)S(1)}, bf16[1,24,512]{2,1,0:T(8,128)(2,1)}, u32[]{:S(2)}) copy-start(bf16[1,24,512]{2,1,0:T(8,128)(2,1)} %param.15) | copy-start | bytes 73732
  14.4 20.6 %copy-start.19 = (bf16[1,24,512]{2,1,0:T(8,128)(2,1)S(1)}, bf16[1,24,512]{2,1,0:T(8,128)(2,1)}, u32[]{:S(2)}) copy-start(bf16[1,24,512]{2,1,0:T(8,128)(2,1)} %param.16) | copy-start | bytes 73732
  14.4 20.6 %copy-start.22 = (s32[96]{0:T(128)S(1)}, s32[96]{0:T(128)}, u32[]{:S(2)}) copy-start(s32[96]{0:T(128)} %ancestry.1) | copy-start | bytes 1156
  14.4 20.6 %copy-start.23 = (s32[96]{0:T(128)S(1)}, s32[96]{0:T(128)}, u32[]{:S(2)}) copy-start(s32[96]{0:T(128)} %lengths.1) | copy-start | bytes 1156
  16.6 27.5 %collective-permute-start.3 = (bf16[512,1024]{1,0:T(8,128)(2,1)}, bf16[512,1024]{1,0:T(8,128)(2,1)}, u32[]{:S(2)}, u32[]{:S(2)}) collective-permute-start(bf16[512,1024]{1,0:T(8,128)(2,1)} %get-tuple-element.17.refs_1_), channel_id=1, source_target_pairs={{0,2},{2,0},{1,3},{3,1},{4,6},{6,4},{5,7},{7,5},{8,10},{10,8},{9,1... | collective-permute-start | bytes 3145736 | tf_op jit(solution)/shard_map/ppermute | solution.py:589
  18.1 26.1 %collective-permute-start.4 = (bf16[512,1024]{1,0:T(8,128)(2,1)S(1)}, bf16[512,1024]{1,0:T(8,128)(2,1)S(1)}, u32[]{:S(2)}, u32[]{:S(2)}) collective-permute-start(bf16[512,1024]{1,0:T(8,128)(2,1)S(1)} %get-tuple-element.16.refs_1_.refs_0_), channel_id=1, source_target_pairs={{0,1},{1,0},{2,3},{3,2},{4,5},{5,4},{6,7},{7,6},{8,9},{9,8},{10,11... | collective-permute-start | bytes 3145736 | tf_op jit(solution)/shard_map/ppermute | solution.py:593
  20.5 43.6 %collective-permute-start.2 = (bf16[512,1024]{1,0:T(8,128)(2,1)S(1)}, bf16[512,1024]{1,0:T(8,128)(2,1)}, u32[]{:S(2)}, u32[]{:S(2)}) collective-permute-start(bf16[512,1024]{1,0:T(8,128)(2,1)S(1)} %get-tuple-element.16.refs_1_.refs_0_), channel_id=1, source_target_pairs={{0,2},{2,0},{1,3},{3,1},{4,6},{6,4},{5,7},{7,5},{8,10},{10,8},{9,1... | collective-permute-start | bytes 3145736 | tf_op jit(solution)/shard_map/ppermute | solution.py:589
  32.6 37.8 %collective-permute-start.12 = (bf16[512,1024]{1,0:T(8,128)(2,1)}, bf16[512,1024]{1,0:T(8,128)(2,1)}, u32[]{:S(2)}, u32[]{:S(2)}) collective-permute-start(bf16[512,1024]{1,0:T(8,128)(2,1)} %shard_map.156.refs_11_), channel_id=1, source_target_pairs={{0,16},{16,0},{1,17},{17,1},{2,18},{18,2},{3,19},{19,3},{4,20},{20... | collective-permute-start | bytes 3145736 | tf_op jit(solution)/shard_map/ppermute | solution.py:576
  34.2 38.5 %copy-start.12 = (bf16[256,1024]{1,0:T(8,128)(2,1)}, bf16[256,1024]{1,0:T(8,128)(2,1)S(1)}, u32[]{:S(2)}) copy-start(bf16[256,1024]{1,0:T(8,128)(2,1)S(1)} %collective-permute-done.11.refs_0_.refs_10_) | copy-start | bytes 1572868
  34.2 36.2 %collective-permute-start.10 = (bf16[512,1024]{1,0:T(8,128)(2,1)}, bf16[512,1024]{1,0:T(8,128)(2,1)}, u32[]{:S(2)}, u32[]{:S(2)}) collective-permute-start(bf16[512,1024]{1,0:T(8,128)(2,1)} %shard_map.156.refs_11_), channel_id=1, source_target_pairs={{0,4},{4,12},{12,8},{8,0},{1,5},{5,13},{13,9},{9,1},{2,6},{6,14},{... | collective-permute-start | bytes 3145736 | tf_op jit(solution)/shard_map/ppermute | solution.py:573
  38.6 0.8 copy-start.16
  39.4 31.0 %all-to-all-start = ((bf16[4,12,40,128]{3,2,1,0:T(8,128)(2,1)}), bf16[4,12,40,128]{3,2,1,0:T(8,128)(2,1)S(1)}, u32[]{:S(2)}, u32[]{:S(2)}) async-start(bf16[4,12,40,128]{3,2,1,0:T(8,128)(2,1)} %copy-done.16), calls=%async_computation | async-start | bytes 983040 | tf_op jit(solution)/shard_map/all_to_all | solution.py:245
  44.1 42.4 %copy-start.25 = (s32[24,4]{0,1:T(4,128)S(1)}, s32[24,4]{0,1:T(4,128)}, u32[]{:S(2)}) copy-start(s32[24,4]{0,1:T(4,128)} %param.19) | copy-start | bytes 1156
  44.1 50.3 %collective-permute-start.5 = (bf16[512,1024]{1,0:T(8,128)(2,1)}, bf16[512,1024]{1,0:T(8,128)(2,1)}, u32[]{:S(2)}, u32[]{:S(2)}) collective-permute-start(bf16[512,1024]{1,0:T(8,128)(2,1)} %get-tuple-element.17.refs_1_), channel_id=1, source_target_pairs={{0,1},{1,0},{2,3},{3,2},{4,5},{5,4},{6,7},{7,6},{8,9},{9,8},{10,11... | collective-permute-start | bytes 3145736 | tf_op jit(solution)/shard_map/ppermute | solution.py:593
  44.2 28.5 %copy-start.4 = (bf16[512,1024]{1,0:T(8,128)(2,1)}, bf16[512,1024]{1,0:T(8,128)(2,1)S(1)}, u32[]{:S(2)}) copy-start(bf16[512,1024]{1,0:T(8,128)(2,1)S(1)} %collective-permute-done.4.refs_5_.refs_4_) | copy-start | bytes 3145732
  44.2 50.7 %collective-permute-start.7 = (bf16[512,1024]{1,0:T(8,128)(2,1)}, bf16[512,1024]{1,0:T(8,128)(2,1)}, u32[]{:S(2)}, u32[]{:S(2)}) collective-permute-start(bf16[512,1024]{1,0:T(8,128)(2,1)} %collective-permute-done.3.refs_4_.refs_3_), channel_id=1, source_target_pairs={{0,1},{1,0},{2,3},{3,2},{4,5},{5,4},{6,7},{7,6},{8,9},{9,8},{10,11... | collective-permute-start | bytes 3145736 | tf_op jit(solution)/shard_map/ppermute | solution.py:619
  64.1 30.8 %collective-permute-start.6 = (bf16[512,1024]{1,0:T(8,128)(2,1)}, bf16[512,1024]{1,0:T(8,128)(2,1)}, u32[]{:S(2)}, u32[]{:S(2)}) collective-permute-start(bf16[512,1024]{1,0:T(8,128)(2,1)} %collective-permute-done.2.refs_3_.refs_2_), channel_id=1, source_target_pairs={{0,1},{1,0},{2,3},{3,2},{4,5},{5,4},{6,7},{7,6},{8,9},{9,8},{10,11... | collective-permute-start | bytes 3145736 | tf_op jit(solution)/shard_map/ppermute | solution.py:619
  70.4 2.3 %copy-start.10 = (bf16[4,12,40,128]{3,2,1,0:T(8,128)(2,1)}, bf16[4,12,40,128]{3,2,1,0:T(8,128)(2,1)S(1)}, u32[]{:S(2)}) copy-start(bf16[4,12,40,128]{3,2,1,0:T(8,128)(2,1)S(1)} %all-to-all-done.blobs.refs_6_) | copy-start | bytes 1474564
  72.7 13.1 %collective-permute-start.15 = (bf16[256,1024]{1,0:T(8,128)(2,1)S(1)}, bf16[256,1024]{1,0:T(8,128)(2,1)}, u32[]{:S(2)}, u32[]{:S(2)}) collective-permute-start(bf16[256,1024]{1,0:T(8,128)(2,1)S(1)} %get-tuple-element.19), channel_id=1, source_target_pairs={{0,4},{4,12},{12,8},{8,0},{1,5},{5,13},{13,9},{9,1},{2,6},{6,14},{... | collective-permute-start | bytes 1572872 | tf_op jit(solution)/shard_map/ppermute | solution.py:573
  73.6 41.2 %collective-permute-start.17 = (bf16[512,1024]{1,0:T(8,128)(2,1)}, bf16[512,1024]{1,0:T(8,128)(2,1)}, u32[]{:S(2)}, u32[]{:S(2)}) collective-permute-start(bf16[512,1024]{1,0:T(8,128)(2,1)} %collective-permute-done.10.source.refs_8_), channel_id=1, source_target_pairs={{0,16},{16,0},{1,17},{17,1},{2,18},{18,2},{3,19},{19,3},{4,20},{20... | collective-permute-start | bytes 3145736 | tf_op jit(solution)/shard_map/ppermute | solution.py:576
  85.8 21.7 %collective-permute-start.13 = (bf16[256,1024]{1,0:T(8,128)(2,1)}, bf16[256,1024]{1,0:T(8,128)(2,1)}, u32[]{:S(2)}, u32[]{:S(2)}) collective-permute-start(bf16[256,1024]{1,0:T(8,128)(2,1)} %get-tuple-element.18), channel_id=1, source_target_pairs={{0,4},{4,12},{12,8},{8,0},{1,5},{5,13},{13,9},{9,1},{2,6},{6,14},{... | collective-permute-start | bytes 1572872 | tf_op jit(solution)/shard_map/ppermute | solution.py:573
  86.5 1.0 copy-start.11
  87.6 1.4 %copy-start.14 = (bf16[1,96,16,512]{3,2,1,0:T(8,128)(2,1)S(1)}, bf16[1,96,16,512]{3,2,1,0:T(8,128)(2,1)}, u32[]{:S(2)}) copy-start(bf16[1,96,16,512]{3,2,1,0:T(8,128)(2,1)} %param.17) | copy-start | bytes 4718596
  89.0 1.4 %copy-start.15 = (bf16[1,96,16,512]{3,2,1,0:T(8,128)(2,1)S(1)}, bf16[1,96,16,512]{3,2,1,0:T(8,128)(2,1)}, u32[]{:S(2)}) copy-start(bf16[1,96,16,512]{3,2,1,0:T(8,128)(2,1)} %param.18) | copy-start | bytes 4718596
  90.4 4.5 %copy-start.3 = (bf16[512,2048]{1,0:T(8,128)(2,1)S(1)}, bf16[512,2048]{1,0:T(8,128)(2,1)}, u32[]{:S(2)}) copy-start(bf16[512,2048]{1,0:T(8,128)(2,1)} %refs_8_.1) | copy-start | bytes 6291460
  94.4 28.3 %collective-permute-start.16 = (bf16[256,1024]{1,0:T(8,128)(2,1)}, bf16[256,1024]{1,0:T(8,128)(2,1)}, u32[]{:S(2)}, u32[]{:S(2)}) collective-permute-start(bf16[256,1024]{1,0:T(8,128)(2,1)} %shard_map.161.refs_8_), channel_id=1, source_target_pairs={{0,16},{16,0},{1,17},{17,1},{2,18},{18,2},{3,19},{19,3},{4,20},{20... | collective-permute-start | bytes 1572872 | tf_op jit(solution)/shard_map/ppermute | solution.py:576
  94.9 1.2 copy-start.5
  96.1 1.0 copy-start.9
  97.2 1.0 copy-start.13
  105.5 2.0 %copy-start = (f32[1024,1024]{1,0:T(8,128)}, f32[1024,1024]{1,0:T(8,128)S(1)}, u32[]{:S(2)}) copy-start(f32[1024,1024]{1,0:T(8,128)S(1)} %shard_map.159.refs_1_.refs_10_) | copy-start | bytes 12582916
  107.5 7.3 %copy-start.24 = (bf16[2048,2]{0,1:T(2,128)(2,1)S(1)}, bf16[2048,2]{0,1:T(2,128)(2,1)}, u32[]{:S(2)}) copy-start(bf16[2048,2]{0,1:T(2,128)(2,1)} %param.26) | copy-start | bytes 24580
  107.5 7.3 %copy-start.6 = (bf16[512,1024]{1,0:T(8,128)(2,1)S(1)}, bf16[512,1024]{1,0:T(8,128)(2,1)}, u32[]{:S(2)}) copy-start(bf16[512,1024]{1,0:T(8,128)(2,1)} %copy-done.4) | copy-start | bytes 3145732
  107.5 20.0 %collective-permute-start.14 = (bf16[256,1024]{1,0:T(8,128)(2,1)}, bf16[256,1024]{1,0:T(8,128)(2,1)S(1)}, u32[]{:S(2)}, u32[]{:S(2)}) collective-permute-start(bf16[256,1024]{1,0:T(8,128)(2,1)} %shard_map.160.refs_10_), channel_id=1, source_target_pairs={{0,16},{16,0},{1,17},{17,1},{2,18},{18,2},{3,19},{19,3},{4,20},{20... | collective-permute-start | bytes 1572872 | tf_op jit(solution)/shard_map/ppermute | solution.py:576
  109.1 26.4 %all-to-all-start.1 = ((bf16[4,12,32,128]{3,2,1,0:T(8,128)(2,1)}), bf16[4,12,32,128]{3,2,1,0:T(8,128)(2,1)S(1)}, u32[]{:S(2)}, u32[]{:S(2)}) async-start(bf16[4,12,32,128]{3,2,1,0:T(8,128)(2,1)} %shard_map.151.refs_1_), calls=%async_computation.1 | async-start | bytes 786432 | tf_op jit(solution)/shard_map/all_to_all | solution.py:245
  114.8 2.2 %copy-start.1 = (f32[1024,1024]{1,0:T(8,128)S(1)}, f32[1024,1024]{1,0:T(8,128)}, u32[]{:S(2)}) copy-start(f32[1024,1024]{1,0:T(8,128)} %copy-done) | copy-start | bytes 12582916
  122.7 4.8 %copy-start.21 = (f32[2048]{0:T(1024)S(1)}, f32[2048]{0:T(1024)}, u32[]{:S(2)}) copy-start(f32[2048]{0:T(1024)} %param.25) | copy-start | bytes 24580
  127.5 6.1 %copy-start.26 = (f32[2]{0:T(128)S(1)}, f32[2]{0:T(128)}, u32[]{:S(2)}) copy-start(f32[2]{0:T(128)} %param.27) | copy-start | bytes 28
  131.4 6.2 %collective-permute-start.20 = (f32[1,512]{1,0:T(1,128)S(1)}, f32[1,512]{1,0:T(1,128)S(1)}, u32[]{:S(2)}, u32[]{:S(2)}) collective-permute-start(f32[1,512]{1,0:T(1,128)S(1)} %get-tuple-element.21), channel_id=1, source_target_pairs={{0,3},{1,2},{2,1},{3,0},{4,7},{5,6},{6,5},{7,4},{8,11},{9,10},{10,... | collective-permute-start | bytes 6152 | tf_op jit(solution)/shard_map/ppermute | solution.py:638
  131.5 6.1 %collective-permute-start.18 = (f32[1,512]{1,0:T(1,128)S(1)}, f32[1,512]{1,0:T(1,128)S(1)}, u32[]{:S(2)}, u32[]{:S(2)}) collective-permute-start(f32[1,512]{1,0:T(1,128)S(1)} %get-tuple-element.21), channel_id=1, source_target_pairs={{0,1},{1,0},{2,3},{3,2},{4,5},{5,4},{6,7},{7,6},{8,9},{9,8},{10,11... | collective-permute-start | bytes 6152 | tf_op jit(solution)/shard_map/ppermute | solution.py:635
  133.1 4.5 %collective-permute-start.19 = (f32[1,512]{1,0:T(1,128)S(1)}, f32[1,512]{1,0:T(1,128)S(1)}, u32[]{:S(2)}, u32[]{:S(2)}) collective-permute-start(f32[1,512]{1,0:T(1,128)S(1)} %get-tuple-element.20), channel_id=1, source_target_pairs={{0,2},{2,0},{1,3},{3,1},{4,6},{6,4},{5,7},{7,5},{8,10},{10,8},{9,1... | collective-permute-start | bytes 6152 | tf_op jit(solution)/shard_map/ppermute | solution.py:637

commit v3 on v2

--- a/solution.py
+++ b/solution.py
@@ -14,6 +14,10 @@
 WAITED = pl.BlockSpec(memory_space=pl.ANY)
 VMEM = pl.BlockSpec(memory_space=pltpu.VMEM)
 SMEM = pl.BlockSpec(memory_space=pltpu.SMEM)
+
+
+def in_hbm(arrays):
+    return [pltpu.with_memory_space_constraint(a, pltpu.HBM) for a in arrays]
 
 
 def pass_kernel(*refs):
@@ -120,7 +124,18 @@
     return out
 
 
-def serve_kernel(particle, page_table, lengths, blobs, key_pages, value_pages, outs, *, kv_local, unroll):
+def serve_kernel(
+    particle, page_table, lengths, blobs, key_source, value_source, outs,
+    key_pages, value_pages, sems, *, kv_local, unroll
+):
+    copies = [
+        pltpu.make_async_copy(key_source, key_pages, sems.at[0]),
+        pltpu.make_async_copy(value_source, value_pages, sems.at[1]),
+    ]
+    for c in copies:
+        c.start()
+    for c in copies:
+        c.wait()
     count, capacity, heads = outs.shape[:3]
     group_size = heads // kv_local
     pages = page_table.shape[1]
@@ -192,14 +207,20 @@
     return pl.pallas_call(
         functools.partial(serve_kernel, kv_local=kv_local, unroll=12),
         out_shape=jax.ShapeDtypeStruct((count, capacity, heads, HD), jnp.bfloat16),
-        in_specs=[SMEM] * 3 + [VMEM] * 3,
+        in_specs=[SMEM] * 3 + [VMEM] + [ANY] * 2,
         out_specs=VMEM,
-        cost_estimate=BRIEF,
-        compiler_params=pltpu.CompilerParams(vmem_limit_bytes=VMEM_LIMIT),
-    )(particle, page_table, lengths, blobs, key_pages, value_pages)
-
-
-def pick_kernel(pick, parts, out, rows):
+        scratch_shapes=[
+            pltpu.VMEM(key_pages.shape, key_pages.dtype),
+            pltpu.VMEM(value_pages.shape, value_pages.dtype),
+            pltpu.SemaphoreType.DMA((2,)),
+        ],
+        cost_estimate=BRIEF,
+        compiler_params=pltpu.CompilerParams(vmem_limit_bytes=VMEM_LIMIT),
+    )(particle, page_table, lengths, blobs, *in_hbm([key_pages, value_pages]))
+
+
+def pick_kernel(pick, parts, *refs):
+    out, rows = refs[-2:]
     slots = out.shape[0]
     capacity = parts.shape[1]
 
@@ -212,18 +233,18 @@
         out[:, h * HD : (h + 1) * HD] = rows[:, h, :].astype(jnp.bfloat16)
 
 
-def pick_up(pick, parts):
+def pick_up(pick, parts, waited):
     heads = parts.shape[2]
     slots = pick.shape[0]
     return pl.pallas_call(
         pick_kernel,
         out_shape=jax.ShapeDtypeStruct((slots, heads * HD), jnp.bfloat16),
-        in_specs=[SMEM, VMEM],
+        in_specs=[SMEM, VMEM] + [WAITED] * len(waited),
         out_specs=VMEM,
         scratch_shapes=[pltpu.VMEM((slots, heads, HD), jnp.float32)],
         cost_estimate=BRIEF,
         compiler_params=pltpu.CompilerParams(vmem_limit_bytes=VMEM_LIMIT),
-    )(pick, parts)
+    )(pick, parts, *waited)
 
 
 class Attention:
@@ -249,8 +270,8 @@
             self.particle, self.page_table, self.lengths, arrived, self.keys, self.values
         )
 
-    def finish(self, returned):
-        return pick_up(self.pick, returned)[None]
+    def finish(self, returned, *waited):
+        return pick_up(self.pick, returned, waited)[None]
 
 
 def cut_kernel(me, weight, out, sem, *, back, other, y_count):
@@ -303,7 +324,7 @@
 
 
 def norm_kernel(me, x, *refs, total, count):
-    powers, (gain, *outs) = refs[:count], refs[count:]
+    powers, (gain, _, *outs) = refs[:count], refs[count:]
     rows, features = x.shape
     part = outs[0].shape[1]
     power = powers[0][...]
@@ -322,18 +343,18 @@
             outs[j * HD // part][at[0], first : first + HD] = value
 
 
-def normalise(me, x, powers, gain, pieces):
+def normalise(me, x, powers, gain, pieces, waited):
     shape = (x.shape[0], x.shape[1] // pieces)
     return pl.pallas_call(
         functools.partial(
             norm_kernel, total=gain.shape[0], count=len(powers)
         ),
         out_shape=[jax.ShapeDtypeStruct(shape, jnp.bfloat16)] * pieces,
-        in_specs=[SMEM] + [VMEM] * (2 + len(powers)),
+        in_specs=[SMEM] + [VMEM] * (2 + len(powers)) + [WAITED],
         out_specs=[VMEM] * pieces,
         cost_estimate=BRIEF,
         compiler_params=pltpu.CompilerParams(vmem_limit_bytes=VMEM_LIMIT),
-    )(me, x, *powers, gain[None])
+    )(me, x, *powers, gain[None], waited)
 
 
 class Layout:
@@ -402,11 +423,16 @@
 
 
 def split_kernel(source, *refs, pieces):
-    outs = refs[-pieces:]
-    at = 0
-    for out in outs:
-        out[...] = source[at : at + out.shape[0]]
-        at += out.shape[0]
+    outs, sems = refs[-pieces - 1 : -1], refs[-1]
+    rows = outs[0].shape[0]
+    copies = [
+        pltpu.make_async_copy(source.at[pl.ds(i * rows, rows)], out, sems.at[i])
+        for i, out in enumerate(outs)
+    ]
+    for c in copies:
+        c.start()
+    for c in copies:
+        c.wait()
 
 
 def split(source, pieces, waited):
@@ -414,8 +440,9 @@
     return pl.pallas_call(
         functools.partial(split_kernel, pieces=pieces),
         out_shape=[jax.ShapeDtypeStruct(shape, source.dtype)] * pieces,
-        in_specs=[VMEM] + [WAITED] * len(waited),
+        in_specs=[ANY] + [WAITED] * len(waited),
         out_specs=[VMEM] * pieces,
+        scratch_shapes=[pltpu.SemaphoreType.DMA((pieces,))],
         cost_estimate=BRIEF,
         compiler_params=pltpu.CompilerParams(vmem_limit_bytes=VMEM_LIMIT),
     )(source, *waited)
@@ -434,13 +461,17 @@
         del refs[:2]
         outs = [refs.pop(0), refs.pop(0)]
     else:
-        out = refs.pop(0)
+        out, token = refs.pop(0), refs.pop(0)
+        token[...] = jnp.zeros_like(token)
     x_v, w_v, sems = refs
     rows = halves[0][0].shape[0]
     width = w_v.shape[1]
     depths = [depth for _, _, _, depth in runs]
     starts = [sum(depths[:i]) for i in range(len(depths))]
     columns = pl.ds(pl.multiple_of(me[2] * width, width), width)
+
+    if final:
+        classes = class_weight[1:2, columns] - class_weight[0:1, columns]
 
     def weight_copy(i):
         _, which, row, depth = runs[i]
@@ -491,13 +522,14 @@
                 total = product
             if target is not None:
                 hidden = jnp.maximum(total + bias[:, columns], 0.0).astype(jnp.bfloat16)
-                logits = lax.dot_general(
-                    class_weight[:, columns],
-                    hidden,
-                    (((1,), (1,)), ((), ())),
-                    preferred_element_type=jnp.float32,
-                )
-                target[:, pl.ds(pl.multiple_of(m * tile, tile), tile)] = logits[1:2] - logits[0:1]
+                weighed = hidden.astype(jnp.float32) * classes
+                folded = weighed[:, :HD]
+                for j in range(1, width // HD):
+                    folded = folded + weighed[:, j * HD : (j + 1) * HD]
+                for j in range(tile // HD):
+                    turned = folded[j * HD : (j + 1) * HD, :].T
+                    lanes = pl.ds(pl.multiple_of(m * tile + j * HD, HD), HD)
+                    target[:, lanes] = jnp.sum(turned, axis=0, keepdims=True)
             else:
                 out[at, :] = total
             return carry
@@ -518,10 +550,10 @@
     rows = halves[0][0].shape[0]
     depth = sum(d for _, _, _, d in runs)
     width = min(w.shape[1] for w in weights)
-    args = [me, *halves[0], *halves[1], *weights]
+    args = [me, *in_hbm([*halves[0], *halves[1]]), *weights]
     specs = [SMEM] + [ANY] * (2 * parts + len(weights))
     if acc is not None:
-        args.append(acc)
+        args.append(pltpu.with_memory_space_constraint(acc, pltpu.VMEM))
         specs.append(VMEM)
     if tail is not None:
         args += list(tail)
@@ -529,8 +561,11 @@
         out_shape = [jax.ShapeDtypeStruct((1, rows), jnp.float32)] * 2
         out_specs = [VMEM] * 2
     else:
-        out_shape = jax.ShapeDtypeStruct((2 * rows, width), jnp.float32)
-        out_specs = VMEM
+        out_shape = [
+            pltpu.VMEM((2 * rows, width), jnp.float32),
+            jax.ShapeDtypeStruct((8, HD), jnp.float32),
+        ]
+        out_specs = [VMEM] * 2
     return pl.pallas_call(
         functools.partial(
             gemm_kernel,
@@ -577,60 +612,71 @@
 
     own = cut_share(me, head_weight, share, width, y_count, False, 0)
     given = [cut_share(me, head_weight, share, width, y_count, True, k) for k in range(y_count)]
-    hop = [forward(own)]
     siblings = [lax.ppermute(g, "section", swap) for g in given]
-    hop.append(forward(siblings[0]))
-    power = row_power(step_rows, siblings[0])
+    merged = merge([own, siblings[0]])
+    whole = forward(merged)
+    power = row_power(step_rows, own)
     powers = [power] + [
         lax.ppermute(power, "mp", shift_pairs(x_count, k)) for k in range(1, x_count)
     ]
-    mine = list(normalise(me, step_rows, powers, norm_gain, pieces))
+    mine = list(normalise(me, step_rows, powers, norm_gain, pieces, merged))
     raw = [
         lax.ppermute(part, "mp", shift_pairs(x_count, k))
         for k in range(1, x_count)
         for part in mine
     ]
     theirs = [lax.ppermute(part, "section", swap) for part in mine]
-    arrived = attention.send(attention.pack(siblings[0]))
-    tail = [head_bias[None], jnp.pad(class_weight.T, ((0, 14), (0, 0)))]
+    blobs = attention.pack(siblings[0])
+    arrived = attention.send(blobs)
+    tail = [head_bias[None], class_weight.T.astype(jnp.float32)]
     chunks = [(head_weight, [((0, False, None, 0), 0, block)])] + [
         (t, [((0, True, (y_count - k) % y_count, 0), 0, share)]) for k, t in enumerate(siblings)
     ]
-    whole = merge(hop)
-    waited = siblings[1:] + mine[:1]
+    waited = siblings[1:] + theirs
     for h in range(1, z_count - 2):
+        if h > 1:
+            whole = forward(whole)
         swapped = over_group(whole)
         chunks += [
             (t, carried(h, k, share, 0, 2 * share)) for k, t in enumerate([whole] + swapped)
         ]
-        hop = forward(whole)
         if h < z_count - 3:
-            (whole,) = after([hop], waited + swapped)
-            waited = []
-        else:
-            whole = hop
-    cuts = split(whole, final_pieces, waited + swapped + raw + theirs[:1] + [arrived])
-    last = [forward(t) for t in cuts]
-    swapped = over_group(whole)
-    second = [
-        (t, carried(z_count - 2, k, share, 0, 2 * share)) for k, t in enumerate([whole] + swapped)
-    ]
-    mine += raw
-    theirs += [lax.ppermute(part, "section", swap) for part in mine[pieces:]]
+            (whole,) = after([whole], waited)
+            waited = swapped
+    cuts = [forward(t) for t in split(whole, final_pieces, waited)]
+    depth = 2 * share // final_pieces
     results = attention.answer(arrived)
+    marks = [[blobs] + swapped + raw, [results]]
+    second, last, travelled = [], [], []
+    for j, t in enumerate(cuts):
+        (t,) = after([t], marks[j])
+        last.append(forward(t))
+        swapped = over_group(t)
+        if j + 1 < final_pieces:
+            marks[j + 1] += swapped
+        second += [
+            (u, carried(z_count - 2, k, share, j * depth, depth))
+            for k, u in enumerate([t] + swapped)
+        ]
+        travelled.append(t)
+    for i, part in enumerate(raw):
+        (part,) = after([part], [travelled[0]])
+        mine.append(part)
+        theirs.append(lax.ppermute(part, "section", swap))
     returned = attention.send(results)
-    acc = gemm(me, layout, (mine, theirs), chunks)
-    depth = 2 * share // final_pieces
+    acc, early = gemm(me, layout, (mine, theirs), chunks)
     ends = []
-    marks = [[results], [acc]] + [[] for _ in last[2:]]
+    marks = [[], [early]]
     for j, t in enumerate(last):
         (t,) = after([t], marks[j])
         ends.append(
-            [(u, carried(z_count - 1, k, share, j * depth, depth)) for k, u in enumerate([t] + over_group(t))]
+            [
+                (u, carried(z_count - 1, k, share, j * depth, depth))
+                for k, u in enumerate([t] + over_group(t))
+            ]
         )
-    acc = gemm(me, layout, (mine, theirs), second, acc)
-    attended = attention.finish(returned)
-    acc = gemm(me, layout, (mine, theirs), sum(ends[:-1], []) + ends[-1][:1], acc)
+    attended = attention.finish(returned, early)
+    acc, _ = gemm(me, layout, (mine, theirs), second + sum(ends[:-1], []) + ends[-1][:1], acc)
     kept, given = gemm(me, layout, (mine, theirs), ends[-1][1:], acc, tail)
     total = kept + lax.ppermute(given, "section", swap)
     for k in range(1, x_count):

time: 139 us -> 128 us (0.921)
  waiting for transfers between devices: 51.2 us -> 40.1 us
  starting transfers between devices: 30.2 us -> 36 us
  local copies, waits for them, and re-layouts: 14.4 us -> 8.98 us
    ppermute x5, waiting for transfers between devices: 23.4 us -> 15.8 us  [forward(): return lax.ppermute(t, 'batch', ring)]
    all_to_all x2, waiting for transfers between devices: 6.3 us -> 0.01 us  [send(): lax.all_to_all(blobs, 'batch', split_axis=0, concat_axis=0, tiled=True)]
    unnamed x55 -> x51, local copies, waits for them, and re-layouts: 13.8 us -> 8.37 us
    ppermute x4 -> x5, waiting for transfers between devices: 0.01 us -> 4.46 us  [over_group(): lax.ppermute(t, 'group', shift_pairs(y_count, k))]
    ppermute x2, waiting for transfers between devices: 19.4 us -> 15.3 us  [both(): lax.ppermute(part, 'mp', shift_pairs(x_count, k))]
    ppermute x5, starting transfers between devices: 7.63 us -> 11.2 us  [forward(): return lax.ppermute(t, 'batch', ring)]
    ppermute x2, waiting for transfers between devices: 0.01 us -> 2.98 us  [both(): siblings = [lax.ppermute(g, 'section', swap) for g in given]]
    ppermute x4 -> x5, starting transfers between devices: 4.14 us -> 6.7 us  [over_group(): lax.ppermute(t, 'group', shift_pairs(y_count, k))]
  transfers between devices with their start and end apart: 23 -> 24, of which waited for: 6 -> 8; matrix products, arithmetic and copies ran while one was open for 0% -> 1% of each run, Pallas kernels for 28% -> 30%
where the time goes in v3:
time: 128 us; the launch traced here: 127 us
  waiting for transfers between devices  40.1 us (31%)
  Pallas kernels  39.5 us (31%)
  starting transfers between devices  36 us (28%)
  local copies, waits for them, and re-layouts  8.98 us (7%)
  between operations  2.24 us (2%)
    pallas_call x3, Pallas kernels, gemm(): pl.pallas_call(functools.partial(gemm_kernel, parts=parts, sources=len(we...  19.8 us
    ppermute x5, waiting for transfers between devices, forward(): return lax.ppermute(t, 'batch', ring)  15.8 us
    ppermute x2, waiting for transfers between devices, both(): lax.ppermute(part, 'mp', shift_pairs(x_count, k))  15.3 us
    ppermute x5, starting transfers between devices, forward(): return lax.ppermute(t, 'batch', ring)  11.2 us
    all_to_all x2, starting transfers between devices, send(): lax.all_to_all(blobs, 'batch', split_axis=0, concat_axis=0, tiled=True)  9.68 us
    unnamed x51, local copies, waits for them, and re-layouts  8.37 us
    ppermute x5, starting transfers between devices, over_group(): lax.ppermute(t, 'group', shift_pairs(y_count, k))  6.7 us
    pallas_call x1, Pallas kernels, serve(): pl.pallas_call(functools.partial(serve_kernel, kv_local=kv_local, unroll=...  5.89 us
  transfers between devices with their start and end apart: 24, of which 8 were waited for; matrix products, arithmetic and copies ran while one was open for 1% of the time, Pallas kernels for 30%

profile of v3, /device:TPU:0, one launch (start us, length us, event | category | flops | bytes accessed | tf_op | source)
XLA Modules:
  0.0 127.4 jit_solution(14105179070276701031)
XLA Ops:
  0.6 0.1 pad_add_fusion.me
  0.7 1.6 %copy-done = bf16[512,2048]{1,0:T(8,128)(2,1)S(1)} copy-done((bf16[512,2048]{1,0:T(8,128)(2,1)S(1)}, bf16[512,2048]{1,0:T(8,128)(2,1)}, u32[]{:S(2)}) %copy-start) | copy-done | bytes 2097176
  2.3 0.6 shard_map.149
  2.9 0.0 copy-start.4
  2.9 0.5 collective-permute-start
  3.5 0.6 shard_map.152.waited.refs_0_
  4.1 0.0 copy-start.1
  4.1 0.9 collective-permute-done.waited.refs_1_.refs_9_
  5.0 0.1 shard_map.154.refs_3_
  5.1 0.0 copy-start.16
  5.1 3.0 %collective-permute-start.3 = (bf16[512,1024]{1,0:T(8,128)(2,1)S(1)}, bf16[512,1024]{1,0:T(8,128)(2,1)}, u32[]{:S(2)}, u32[]{:S(2)}) collective-permute-start(bf16[512,1024]{1,0:T(8,128)(2,1)S(1)} %shard_map.154.refs_3_), channel_id=1, source_target_pairs={{0,4},{4,12},{12,8},{8,0},{1,5},{5,13},{13,9},{9,1},{2,6},{6,14},{... | collective-permute-start | bytes 3145736 | tf_op jit(solution)/shard_map/ppermute | solution.py:608
  8.1 0.7 shard_map.153.refs_0_
  8.8 1.6 %collective-permute-start.1 = (f32[4,128]{1,0:T(4,128)S(1)}, f32[4,128]{1,0:T(4,128)S(1)}, u32[]{:S(2)}, u32[]{:S(2)}) collective-permute-start(f32[4,128]{1,0:T(4,128)S(1)} %shard_map.153.refs_0_), channel_id=1, source_target_pairs={{0,2},{2,0},{1,3},{3,1},{4,6},{6,4},{5,7},{7,5},{8,10},{10,8},{9,1... | collective-permute-start | bytes 6152 | tf_op jit(solution)/shard_map/ppermute | solution.py:620
  10.4 0.6 shard_map.156
  11.0 1.5 %collective-permute-done.1.refs_1_ = f32[4,128]{1,0:T(4,128)S(1)} collective-permute-done((f32[4,128]{1,0:T(4,128)S(1)}, f32[4,128]{1,0:T(4,128)S(1)}, u32[]{:S(2)}, u32[]{:S(2)}) %collective-permute-start.1) | collective-permute-done | bytes 2080 | tf_op jit(solution)/shard_map/ppermute | solution.py:620
  12.5 2.5 %shard_map.155 = (bf16[512,1024]{1,0:T(8,128)(2,1)}, bf16[512,1024]{1,0:T(8,128)(2,1)}) custom-call(s32[4]{0:T(128)S(1)} %pad_add_fusion.me, bf16[512,2048]{1,0:T(8,128)(2,1)S(1)} %copy-done.4, f32[4,128]{1,0:T(4,128)S(1)} %shard_map.153.refs_0_, f32[4,128]{1,0:T(4,128)S(1)} %collective-permute-done.1.refs_1_, f32[1,4096]{1,0:T(1,128)S(1)} %bitcast.19, ...), custom_call_target="tpu_custom_call" | custom-call | flops 1 | bytes 1 | tf_op jit(solution)/shard_map/pallas_call | solution.py:348
  15.0 0.0 copy-start.21
  15.0 0.1 collective-permute-start.5
  15.1 0.5 collective-permute-start.6
  15.6 0.1 collective-permute-start.4
  15.7 1.5 %collective-permute-start.2 = (bf16[512,1024]{1,0:T(8,128)(2,1)}, bf16[512,1024]{1,0:T(8,128)(2,1)}, u32[]{:S(2)}, u32[]{:S(2)}) collective-permute-start(bf16[512,1024]{1,0:T(8,128)(2,1)} %get-tuple-element.19.refs_0_), channel_id=1, source_target_pairs={{0,2},{2,0},{1,3},{3,1},{4,6},{6,4},{5,7},{7,5},{8,10},{10,8},{9,1... | collective-permute-start | bytes 3145736 | tf_op jit(solution)/shard_map/ppermute | solution.py:624
  17.1 2.1 %collective-permute-done.4.refs_0_.refs_10_ = bf16[256,1024]{1,0:T(8,128)(2,1)S(1)} collective-permute-done((bf16[256,1024]{1,0:T(8,128)(2,1)S(1)}, bf16[256,1024]{1,0:T(8,128)(2,1)S(1)}, u32[]{:S(2)}, u32[]{:S(2)}) %collective-permute-start.4) | collective-permute-done | bytes 524320 | tf_op jit(solution)/shard_map/ppermute | solution.py:615
  19.2 1.5 %collective-permute-start.9 = (bf16[512,1024]{1,0:T(8,128)(2,1)}, bf16[512,1024]{1,0:T(8,128)(2,1)}, u32[]{:S(2)}, u32[]{:S(2)}) collective-permute-start(bf16[512,1024]{1,0:T(8,128)(2,1)} %get-tuple-element.20.refs_1_), channel_id=1, source_target_pairs={{0,2},{2,0},{1,3},{3,1},{4,6},{6,4},{5,7},{7,5},{8,10},{10,8},{9,1... | collective-permute-start | bytes 3145736 | tf_op jit(solution)/shard_map/ppermute | solution.py:624
  20.7 11.9 %collective-permute-done.3.source.refs_11_ = bf16[512,1024]{1,0:T(8,128)(2,1)} collective-permute-done((bf16[512,1024]{1,0:T(8,128)(2,1)S(1)}, bf16[512,1024]{1,0:T(8,128)(2,1)}, u32[]{:S(2)}, u32[]{:S(2)}) %collective-permute-start.3) | collective-permute-done | bytes 1048608 | tf_op jit(solution)/shard_map/ppermute | solution.py:608
  32.7 1.6 %collective-permute-start.8 = (bf16[512,1024]{1,0:T(8,128)(2,1)}, bf16[512,1024]{1,0:T(8,128)(2,1)}, u32[]{:S(2)}, u32[]{:S(2)}) collective-permute-start(bf16[512,1024]{1,0:T(8,128)(2,1)} %collective-permute-done.3.source.refs_11_), channel_id=1, source_target_pairs={{0,16},{16,0},{1,17},{17,1},{2,18},{18,2},{3,19},{19,3},{4,20},{20... | collective-permute-start | bytes 3145736 | tf_op jit(solution)/shard_map/ppermute | solution.py:611
  34.2 0.0 collective-permute-done.5.refs_1_.refs_4_
  34.2 0.0 collective-permute-done.6.refs_2_.refs_5_
  34.2 2.8 %shard_map.157 = (bf16[256,1024]{1,0:T(8,128)(2,1)S(1)}, bf16[256,1024]{1,0:T(8,128)(2,1)}) custom-call(bf16[512,1024]{1,0:T(8,128)(2,1)} %collective-permute-done.3.source.refs_11_, bf16[256,1024]{1,0:T(8,128)(2,1)S(1)} %collective-permute-done.4.refs_0_.refs_10_, bf16[512,1024]{1,0:T(8,128)(2,1)S(1)} %collective-permute-done.5.refs_1_.refs_4_, ...), custom_call_target="tpu_custom_call" | custom-call | flops 1 | bytes 1 | tf_op jit(solution)/shard_map/pallas_call | solution.py:440
  37.0 0.7 collective-permute-start.7
  37.8 3.8 %shard_map.150 = (bf16[4,12,40,128]{3,2,1,0:T(8,128)(2,1)}, s32[48]{0:T(128)S(1)}, s32[48]{0:T(128)S(1)}, s32[24]{0:T(128)S(1)}) custom-call(s32[1]{0:T(128)} %bitcast.me, s32[96]{0:T(128)S(1)} %copy-done.20, s32[96]{0:T(128)S(1)} %copy-done.21, bf16[24,4096]{1,0:T(8,128)(2,1)S(1)} %bitcast.16, bf16[24,512]{1,0:T(8,128)(2,1)S(1)} %bitcast.17, ...), custom_call_target="tpu_custom_call" | custom-call | flops 1 | bytes 1 | tf_op jit(solution)/shard_map/pallas_call | solution.py:110
  41.6 4.8 %all-to-all-start = ((bf16[4,12,40,128]{3,2,1,0:T(8,128)(2,1)}), bf16[4,12,40,128]{3,2,1,0:T(8,128)(2,1)S(1)}, u32[]{:S(2)}, u32[]{:S(2)}) async-start(bf16[4,12,40,128]{3,2,1,0:T(8,128)(2,1)} %get-tuple-element.18.refs_1_), calls=%async_computation | async-start | bytes 983040 | tf_op jit(solution)/shard_map/all_to_all | solution.py:266
  46.4 2.2 %collective-permute-start.12 = (bf16[256,1024]{1,0:T(8,128)(2,1)}, bf16[256,1024]{1,0:T(8,128)(2,1)}, u32[]{:S(2)}, u32[]{:S(2)}) collective-permute-start(bf16[256,1024]{1,0:T(8,128)(2,1)} %get-tuple-element.23), channel_id=1, source_target_pairs={{0,4},{4,12},{12,8},{8,0},{1,5},{5,13},{13,9},{9,1},{2,6},{6,14},{... | collective-permute-start | bytes 1572872 | tf_op jit(solution)/shard_map/ppermute | solution.py:608
  48.6 0.0 collective-permute-done.2.refs_3_.refs_0_
  48.6 15.3 %collective-permute-done.9.refs_4_.refs_0_ = bf16[512,1024]{1,0:T(8,128)(2,1)} collective-permute-done((bf16[512,1024]{1,0:T(8,128)(2,1)}, bf16[512,1024]{1,0:T(8,128)(2,1)}, u32[]{:S(2)}, u32[]{:S(2)}) %collective-permute-start.9) | collective-permute-done | bytes 1048608 | tf_op jit(solution)/shard_map/ppermute | solution.py:624
  64.0 1.6 %collective-permute-start.13 = (bf16[256,1024]{1,0:T(8,128)(2,1)}, bf16[256,1024]{1,0:T(8,128)(2,1)}, u32[]{:S(2)}, u32[]{:S(2)}) collective-permute-start(bf16[256,1024]{1,0:T(8,128)(2,1)} %shard_map.158.refs_1_.refs_8_), channel_id=1, source_target_pairs={{0,16},{16,0},{1,17},{17,1},{2,18},{18,2},{3,19},{19,3},{4,20},{20... | collective-permute-start | bytes 1572872 | tf_op jit(solution)/shard_map/ppermute | solution.py:611
  65.6 0.5 collective-permute-start.11
  66.1 0.1 copy.22.page_table
  66.2 2.6 %collective-permute-start.17 = (bf16[256,1024]{1,0:T(8,128)(2,1)}, bf16[256,1024]{1,0:T(8,128)(2,1)S(1)}, u32[]{:S(2)}, u32[]{:S(2)}) collective-permute-start(bf16[256,1024]{1,0:T(8,128)(2,1)} %shard_map.158.refs_1_.refs_8_), channel_id=1, source_target_pairs={{0,4},{4,12},{12,8},{8,0},{1,5},{5,13},{13,9},{9,1},{2,6},{6,14},{... | collective-permute-start | bytes 1572872 | tf_op jit(solution)/shard_map/ppermute | solution.py:608
  68.7 5.9 %shard_map.151.refs_1_ = bf16[4,12,32,128]{3,2,1,0:T(8,128)(2,1)} custom-call(s32[48]{0:T(128)S(1)} %get-tuple-element.16.particle, s32[24,4]{1,0:T(8,128)S(1)} %copy.22.page_table, s32[48]{0:T(128)S(1)} %get-tuple-element.17.lengths, bf16[4,12,40,128]{3,2,1,0:T(8,128)(2,1)S(1)} %all-to-all-done.blobs, bf16[96,16,512]{2,1,0:T(8,128)(2,1)} %bitcast.21, ...), custom_call_target="tpu_custom_call" | custom-call | flops 1 | bytes 1 | tf_op jit(solution)/shard_map/pallas_call | solution.py:207
  74.7 0.0 collective-permute-done.12.refs_0_
  74.7 3.1 %collective-permute-done.13.refs_2_.refs_9_ = bf16[256,1024]{1,0:T(8,128)(2,1)} collective-permute-done((bf16[256,1024]{1,0:T(8,128)(2,1)}, bf16[256,1024]{1,0:T(8,128)(2,1)}, u32[]{:S(2)}, u32[]{:S(2)}) %collective-permute-start.13) | collective-permute-done | bytes 524320 | tf_op jit(solution)/shard_map/ppermute | solution.py:611
  77.8 2.6 %collective-permute-start.14 = (bf16[256,1024]{1,0:T(8,128)(2,1)}, bf16[256,1024]{1,0:T(8,128)(2,1)}, u32[]{:S(2)}, u32[]{:S(2)}) collective-permute-start(bf16[256,1024]{1,0:T(8,128)(2,1)} %shard_map.163.refs_10_), channel_id=1, source_target_pairs={{0,4},{4,12},{12,8},{8,0},{1,5},{5,13},{13,9},{9,1},{2,6},{6,14},{... | collective-permute-start | bytes 1572872 | tf_op jit(solution)/shard_map/ppermute | solution.py:608
  80.4 1.5 %collective-permute-start.16 = (bf16[256,1024]{1,0:T(8,128)(2,1)}, bf16[256,1024]{1,0:T(8,128)(2,1)}, u32[]{:S(2)}, u32[]{:S(2)}) collective-permute-start(bf16[256,1024]{1,0:T(8,128)(2,1)} %shard_map.163.refs_10_), channel_id=1, source_target_pairs={{0,16},{16,0},{1,17},{17,1},{2,18},{18,2},{3,19},{19,3},{4,20},{20... | collective-permute-start | bytes 1572872 | tf_op jit(solution)/shard_map/ppermute | solution.py:611
  81.9 3.9 %collective-permute-done.17.refs_0_ = bf16[256,1024]{1,0:T(8,128)(2,1)S(1)} collective-permute-done((bf16[256,1024]{1,0:T(8,128)(2,1)}, bf16[256,1024]{1,0:T(8,128)(2,1)S(1)}, u32[]{:S(2)}, u32[]{:S(2)}) %collective-permute-start.17) | collective-permute-done | bytes 524320 | tf_op jit(solution)/shard_map/ppermute | solution.py:608
  85.8 0.8 copy-done.9
  86.6 0.5 collective-permute-start.18
  87.1 1.0 copy-done.12
  88.1 8.2 %shard_map.161 = (f32[1024,1024]{1,0:T(8,128)S(1)}, f32[8,128]{1,0:T(8,128)S(1)}) custom-call(s32[4]{0:T(128)S(1)} %pad_add_fusion.me, bf16[512,1024]{1,0:T(8,128)(2,1)} %get-tuple-element.19.refs_0_, bf16[512,1024]{1,0:T(8,128)(2,1)} %get-tuple-element.20.refs_1_, bf16[512,1024]{1,0:T(8,128)(2,1)} %shard_map.159.refs_2_, ...), custom_call_target="tpu_custom_call" | custom-call | flops 1 | bytes 1 | tf_op jit(solution)/shard_map/pallas_call | solution.py:569
  96.3 2.0 %copy-done.7 = f32[1024,1024]{1,0:T(8,128)} copy-done((f32[1024,1024]{1,0:T(8,128)}, f32[1024,1024]{1,0:T(8,128)S(1)}, u32[]{:S(2)}) %copy-start.7) | copy-done | bytes 4194328
  98.3 0.6 copy-done.17
  98.9 1.6 %collective-permute-start.15 = (bf16[256,1024]{1,0:T(8,128)(2,1)}, bf16[256,1024]{1,0:T(8,128)(2,1)S(1)}, u32[]{:S(2)}, u32[]{:S(2)}) collective-permute-start(bf16[256,1024]{1,0:T(8,128)(2,1)} %shard_map.164.refs_14_), channel_id=1, source_target_pairs={{0,16},{16,0},{1,17},{17,1},{2,18},{18,2},{3,19},{19,3},{4,20},{20... | collective-permute-start | bytes 1572872 | tf_op jit(solution)/shard_map/ppermute | solution.py:611
  100.5 4.9 %all-to-all-start.1 = ((bf16[4,12,32,128]{3,2,1,0:T(8,128)(2,1)}), bf16[4,12,32,128]{3,2,1,0:T(8,128)(2,1)S(1)}, u32[]{:S(2)}, u32[]{:S(2)}) async-start(bf16[4,12,32,128]{3,2,1,0:T(8,128)(2,1)} %shard_map.151.refs_1_), calls=%async_computation.1 | async-start | bytes 786432 | tf_op jit(solution)/shard_map/all_to_all | solution.py:266
  105.4 1.3 %collective-permute-done.18.refs_13_ = bf16[256,1024]{1,0:T(8,128)(2,1)S(1)} collective-permute-done((bf16[256,1024]{1,0:T(8,128)(2,1)}, bf16[256,1024]{1,0:T(8,128)(2,1)S(1)}, u32[]{:S(2)}, u32[]{:S(2)}) %collective-permute-start.18) | collective-permute-done | bytes 524320 | tf_op jit(solution)/shard_map/ppermute | solution.py:611
  106.7 2.2 %copy-done.8 = f32[1024,1024]{1,0:T(8,128)S(1)} copy-done((f32[1024,1024]{1,0:T(8,128)S(1)}, f32[1024,1024]{1,0:T(8,128)}, u32[]{:S(2)}) %copy-start.8) | copy-done | bytes 4194328
  108.9 8.1 %shard_map.166 = (f32[1024,1024]{1,0:T(8,128)S(1)}, f32[8,128]{1,0:T(8,128)}) custom-call(s32[4]{0:T(128)S(1)} %pad_add_fusion.me, bf16[512,1024]{1,0:T(8,128)(2,1)} %get-tuple-element.19.refs_0_, bf16[512,1024]{1,0:T(8,128)(2,1)} %get-tuple-element.20.refs_1_, bf16[512,1024]{1,0:T(8,128)(2,1)} %shard_map.159.refs_2_, bf16[512,1024]{1,0:T(8,128)(2,1)} %shard_map.160.refs_3_, ...), custom_call_target="tpu_custom_call" | custom-call | flops 1 | bytes 1 | tf_op jit(solution)/shard_map/pallas_call | solution.py:569
  117.0 0.0 copy-start.24
  117.1 0.0 copy-start.18
  117.1 3.5 %shard_map.167 = (f32[1,512]{1,0:T(1,128)S(1)}, f32[1,512]{1,0:T(1,128)S(1)}) custom-call(s32[4]{0:T(128)S(1)} %pad_add_fusion.me, bf16[512,1024]{1,0:T(8,128)(2,1)} %get-tuple-element.19.refs_0_, bf16[512,1024]{1,0:T(8,128)(2,1)} %get-tuple-element.20.refs_1_, bf16[512,1024]{1,0:T(8,128)(2,1)} %shard_map.159.refs_2_, bf16[512,1024]{1,0:T(8,128)(2,1)} %shard_map.160.refs_3_, ...), custom_call_target="tpu_custom_call" | custom-call | flops 1 | bytes 1 | tf_op jit(solution)/shard_map/pallas_call | solution.py:569
  120.6 0.1 collective-permute-start.21
  120.7 1.6 %collective-permute-start.19 = (f32[1,512]{1,0:T(1,128)S(1)}, f32[1,512]{1,0:T(1,128)S(1)}, u32[]{:S(2)}, u32[]{:S(2)}) collective-permute-start(f32[1,512]{1,0:T(1,128)S(1)} %get-tuple-element.27), channel_id=1, source_target_pairs={{0,1},{1,0},{2,3},{3,2},{4,5},{5,4},{6,7},{7,6},{8,9},{9,8},{10,11... | collective-permute-start | bytes 6152 | tf_op jit(solution)/shard_map/ppermute | solution.py:681
  122.3 0.5 collective-permute-start.20
  122.8 0.6 fusion
  124.8 2.1 %shard_map.162 = bf16[24,4096]{1,0:T(8,128)(2,1)} custom-call(s32[24]{0:T(128)S(1)} %get-tuple-element.15.pick, bf16[4,12,32,128]{3,2,1,0:T(8,128)(2,1)S(1)} %all-to-all-done.1.parts, f32[8,128]{1,0:T(8,128)S(1)} %copy-done.18), custom_call_target="tpu_custom_call" | custom-call | flops 1 | bytes 1 | tf_op jit(solution)/shard_map/pallas_call | solution.py:239
  126.8 0.6 add_add_fusion
  (58 shorter events, 0.1 us)
Async XLA Ops:
  0.7 1.6 %copy-start = (bf16[512,2048]{1,0:T(8,128)(2,1)S(1)}, bf16[512,2048]{1,0:T(8,128)(2,1)}, u32[]{:S(2)}) copy-start(bf16[512,2048]{1,0:T(8,128)(2,1)} %refs_8_.1) | copy-start | bytes 6291460
  2.9 5.2 %copy-start.4 = (bf16[512,2048]{1,0:T(8,128)(2,1)S(1)}, bf16[512,2048]{1,0:T(8,128)(2,1)}, u32[]{:S(2)}) copy-start(bf16[512,2048]{1,0:T(8,128)(2,1)} %x.3) | copy-start | bytes 6291460
  2.9 2.1 %collective-permute-start = (bf16[256,1024]{1,0:T(8,128)(2,1)S(1)}, bf16[256,1024]{1,0:T(8,128)(2,1)S(1)}, u32[]{:S(2)}, u32[]{:S(2)}) collective-permute-start(bf16[256,1024]{1,0:T(8,128)(2,1)S(1)} %shard_map.149), channel_id=1, source_target_pairs={{0,1},{1,0},{2,3},{3,2},{4,5},{5,4},{6,7},{7,6},{8,9},{9,8},{10,11... | collective-permute-start | bytes 1572872 | tf_op jit(solution)/shard_map/ppermute | solution.py:615
  4.1 6.3 %copy-start.1 = (bf16[512,2048]{1,0:T(8,128)(2,1)S(1)}, bf16[512,2048]{1,0:T(8,128)(2,1)}, u32[]{:S(2)}) copy-start(bf16[512,2048]{1,0:T(8,128)(2,1)} %refs_8_.1) | copy-start | bytes 6291460
  5.0 32.8 %copy-start.5 = (bf16[256,1024]{1,0:T(8,128)(2,1)}, bf16[256,1024]{1,0:T(8,128)(2,1)S(1)}, u32[]{:S(2)}) copy-start(bf16[256,1024]{1,0:T(8,128)(2,1)S(1)} %collective-permute-done.waited.refs_1_.refs_9_) | copy-start | bytes 1572868
  5.1 7.4 %copy-start.16 = (f32[4096]{0:T(1024)S(1)}, f32[4096]{0:T(1024)}, u32[]{:S(2)}) copy-start(f32[4096]{0:T(1024)} %param.23) | copy-start | bytes 49156
  5.1 27.6 %collective-permute-start.3 = (bf16[512,1024]{1,0:T(8,128)(2,1)S(1)}, bf16[512,1024]{1,0:T(8,128)(2,1)}, u32[]{:S(2)}, u32[]{:S(2)}) collective-permute-start(bf16[512,1024]{1,0:T(8,128)(2,1)S(1)} %shard_map.154.refs_3_), channel_id=1, source_target_pairs={{0,4},{4,12},{12,8},{8,0},{1,5},{5,13},{13,9},{9,1},{2,6},{6,14},{... | collective-permute-start | bytes 3145736 | tf_op jit(solution)/shard_map/ppermute | solution.py:608
  8.8 3.7 %collective-permute-start.1 = (f32[4,128]{1,0:T(4,128)S(1)}, f32[4,128]{1,0:T(4,128)S(1)}, u32[]{:S(2)}, u32[]{:S(2)}) collective-permute-start(f32[4,128]{1,0:T(4,128)S(1)} %shard_map.153.refs_0_), channel_id=1, source_target_pairs={{0,2},{2,0},{1,3},{3,1},{4,6},{6,4},{5,7},{7,5},{8,10},{10,8},{9,1... | collective-permute-start | bytes 6152 | tf_op jit(solution)/shard_map/ppermute | solution.py:620
  15.0 22.8 %copy-start.13 = (bf16[1,24,4096]{2,1,0:T(8,128)(2,1)S(1)}, bf16[1,24,4096]{2,1,0:T(8,128)(2,1)}, u32[]{:S(2)}) copy-start(bf16[1,24,4096]{2,1,0:T(8,128)(2,1)} %param.14) | copy-start | bytes 589828
  15.0 22.8 %copy-start.14 = (bf16[1,24,512]{2,1,0:T(8,128)(2,1)S(1)}, bf16[1,24,512]{2,1,0:T(8,128)(2,1)}, u32[]{:S(2)}) copy-start(bf16[1,24,512]{2,1,0:T(8,128)(2,1)} %param.15) | copy-start | bytes 73732
  15.0 22.8 %copy-start.15 = (bf16[1,24,512]{2,1,0:T(8,128)(2,1)S(1)}, bf16[1,24,512]{2,1,0:T(8,128)(2,1)}, u32[]{:S(2)}) copy-start(bf16[1,24,512]{2,1,0:T(8,128)(2,1)} %param.16) | copy-start | bytes 73732
  15.0 22.8 %copy-start.20 = (s32[96]{0:T(128)S(1)}, s32[96]{0:T(128)}, u32[]{:S(2)}) copy-start(s32[96]{0:T(128)} %ancestry.1) | copy-start | bytes 1156
  15.0 22.8 %copy-start.21 = (s32[96]{0:T(128)S(1)}, s32[96]{0:T(128)}, u32[]{:S(2)}) copy-start(s32[96]{0:T(128)} %lengths.1) | copy-start | bytes 1156
  15.0 19.2 %collective-permute-start.5 = (bf16[512,1024]{1,0:T(8,128)(2,1)}, bf16[512,1024]{1,0:T(8,128)(2,1)S(1)}, u32[]{:S(2)}, u32[]{:S(2)}) collective-permute-start(bf16[512,1024]{1,0:T(8,128)(2,1)} %get-tuple-element.19.refs_0_), channel_id=1, source_target_pairs={{0,1},{1,0},{2,3},{3,2},{4,5},{5,4},{6,7},{7,6},{8,9},{9,8},{10,11... | collective-permute-start | bytes 3145736 | tf_op jit(solution)/shard_map/ppermute | solution.py:628
  15.1 19.2 %collective-permute-start.6 = (bf16[512,1024]{1,0:T(8,128)(2,1)}, bf16[512,1024]{1,0:T(8,128)(2,1)S(1)}, u32[]{:S(2)}, u32[]{:S(2)}) collective-permute-start(bf16[512,1024]{1,0:T(8,128)(2,1)} %get-tuple-element.20.refs_1_), channel_id=1, source_target_pairs={{0,1},{1,0},{2,3},{3,2},{4,5},{5,4},{6,7},{7,6},{8,9},{9,8},{10,11... | collective-permute-start | bytes 3145736 | tf_op jit(solution)/shard_map/ppermute | solution.py:628
  15.6 3.6 %collective-permute-start.4 = (bf16[256,1024]{1,0:T(8,128)(2,1)S(1)}, bf16[256,1024]{1,0:T(8,128)(2,1)S(1)}, u32[]{:S(2)}, u32[]{:S(2)}) collective-permute-start(bf16[256,1024]{1,0:T(8,128)(2,1)S(1)} %shard_map.156), channel_id=1, source_target_pairs={{0,1},{1,0},{2,3},{3,2},{4,5},{5,4},{6,7},{7,6},{8,9},{9,8},{10,11... | collective-permute-start | bytes 1572872 | tf_op jit(solution)/shard_map/ppermute | solution.py:615
  15.7 33.0 %collective-permute-start.2 = (bf16[512,1024]{1,0:T(8,128)(2,1)}, bf16[512,1024]{1,0:T(8,128)(2,1)}, u32[]{:S(2)}, u32[]{:S(2)}) collective-permute-start(bf16[512,1024]{1,0:T(8,128)(2,1)} %get-tuple-element.19.refs_0_), channel_id=1, source_target_pairs={{0,2},{2,0},{1,3},{3,1},{4,6},{6,4},{5,7},{7,5},{8,10},{10,8},{9,1... | collective-permute-start | bytes 3145736 | tf_op jit(solution)/shard_map/ppermute | solution.py:624
  19.2 22.4 %copy-start.11 = (bf16[256,1024]{1,0:T(8,128)(2,1)}, bf16[256,1024]{1,0:T(8,128)(2,1)S(1)}, u32[]{:S(2)}) copy-start(bf16[256,1024]{1,0:T(8,128)(2,1)S(1)} %collective-permute-done.4.refs_0_.refs_10_) | copy-start | bytes 1572868
  19.2 44.7 %collective-permute-start.9 = (bf16[512,1024]{1,0:T(8,128)(2,1)}, bf16[512,1024]{1,0:T(8,128)(2,1)}, u32[]{:S(2)}, u32[]{:S(2)}) collective-permute-start(bf16[512,1024]{1,0:T(8,128)(2,1)} %get-tuple-element.20.refs_1_), channel_id=1, source_target_pairs={{0,2},{2,0},{1,3},{3,1},{4,6},{6,4},{5,7},{7,5},{8,10},{10,8},{9,1... | collective-permute-start | bytes 3145736 | tf_op jit(solution)/shard_map/ppermute | solution.py:624
  32.7 31.3 %collective-permute-start.8 = (bf16[512,1024]{1,0:T(8,128)(2,1)}, bf16[512,1024]{1,0:T(8,128)(2,1)}, u32[]{:S(2)}, u32[]{:S(2)}) collective-permute-start(bf16[512,1024]{1,0:T(8,128)(2,1)} %collective-permute-done.3.source.refs_11_), channel_id=1, source_target_pairs={{0,16},{16,0},{1,17},{17,1},{2,18},{18,2},{3,19},{19,3},{4,20},{20... | collective-permute-start | bytes 3145736 | tf_op jit(solution)/shard_map/ppermute | solution.py:611
  34.2 7.4 %copy-start.2 = (bf16[512,1024]{1,0:T(8,128)(2,1)}, bf16[512,1024]{1,0:T(8,128)(2,1)S(1)}, u32[]{:S(2)}) copy-start(bf16[512,1024]{1,0:T(8,128)(2,1)S(1)} %collective-permute-done.5.refs_1_.refs_4_) | copy-start | bytes 3145732
  34.2 7.4 %copy-start.3 = (bf16[512,1024]{1,0:T(8,128)(2,1)}, bf16[512,1024]{1,0:T(8,128)(2,1)S(1)}, u32[]{:S(2)}) copy-start(bf16[512,1024]{1,0:T(8,128)(2,1)S(1)} %collective-permute-done.6.refs_2_.refs_5_) | copy-start | bytes 3145732
  37.0 26.9 %collective-permute-start.7 = (bf16[256,1024]{1,0:T(8,128)(2,1)S(1)}, bf16[256,1024]{1,0:T(8,128)(2,1)}, u32[]{:S(2)}, u32[]{:S(2)}) collective-permute-start(bf16[256,1024]{1,0:T(8,128)(2,1)S(1)} %get-tuple-element.21), channel_id=1, source_target_pairs={{0,4},{4,12},{12,8},{8,0},{1,5},{5,13},{13,9},{9,1},{2,6},{6,14},{... | collective-permute-start | bytes 1572872 | tf_op jit(solution)/shard_map/ppermute | solution.py:608
  41.6 27.1 %all-to-all-start = ((bf16[4,12,40,128]{3,2,1,0:T(8,128)(2,1)}), bf16[4,12,40,128]{3,2,1,0:T(8,128)(2,1)S(1)}, u32[]{:S(2)}, u32[]{:S(2)}) async-start(bf16[4,12,40,128]{3,2,1,0:T(8,128)(2,1)} %get-tuple-element.18.refs_1_), calls=%async_computation | async-start | bytes 983040 | tf_op jit(solution)/shard_map/all_to_all | solution.py:266
  46.4 28.3 %collective-permute-start.12 = (bf16[256,1024]{1,0:T(8,128)(2,1)}, bf16[256,1024]{1,0:T(8,128)(2,1)}, u32[]{:S(2)}, u32[]{:S(2)}) collective-permute-start(bf16[256,1024]{1,0:T(8,128)(2,1)} %get-tuple-element.23), channel_id=1, source_target_pairs={{0,4},{4,12},{12,8},{8,0},{1,5},{5,13},{13,9},{9,1},{2,6},{6,14},{... | collective-permute-start | bytes 1572872 | tf_op jit(solution)/shard_map/ppermute | solution.py:608
  64.0 2.1 %copy-start.23 = (s32[24,4]{0,1:T(4,128)S(1)}, s32[24,4]{0,1:T(4,128)}, u32[]{:S(2)}) copy-start(s32[24,4]{0,1:T(4,128)} %param.19) | copy-start | bytes 1156
  64.0 13.9 %collective-permute-start.13 = (bf16[256,1024]{1,0:T(8,128)(2,1)}, bf16[256,1024]{1,0:T(8,128)(2,1)}, u32[]{:S(2)}, u32[]{:S(2)}) collective-permute-start(bf16[256,1024]{1,0:T(8,128)(2,1)} %shard_map.158.refs_1_.refs_8_), channel_id=1, source_target_pairs={{0,16},{16,0},{1,17},{17,1},{2,18},{18,2},{3,19},{19,3},{4,20},{20... | collective-permute-start | bytes 1572872 | tf_op jit(solution)/shard_map/ppermute | solution.py:611
  65.6 21.5 %collective-permute-start.10 = (bf16[512,1024]{1,0:T(8,128)(2,1)}, bf16[512,1024]{1,0:T(8,128)(2,1)}, u32[]{:S(2)}, u32[]{:S(2)}) collective-permute-start(bf16[512,1024]{1,0:T(8,128)(2,1)} %shard_map.159.refs_2_), channel_id=1, source_target_pairs={{0,1},{1,0},{2,3},{3,2},{4,5},{5,4},{6,7},{7,6},{8,9},{9,8},{10,11... | collective-permute-start | bytes 3145736 | tf_op jit(solution)/shard_map/ppermute | solution.py:665
  65.6 21.5 %collective-permute-start.11 = (bf16[512,1024]{1,0:T(8,128)(2,1)}, bf16[512,1024]{1,0:T(8,128)(2,1)}, u32[]{:S(2)}, u32[]{:S(2)}) collective-permute-start(bf16[512,1024]{1,0:T(8,128)(2,1)} %shard_map.160.refs_3_), channel_id=1, source_target_pairs={{0,1},{1,0},{2,3},{3,2},{4,5},{5,4},{6,7},{7,6},{8,9},{9,8},{10,11... | collective-permute-start | bytes 3145736 | tf_op jit(solution)/shard_map/ppermute | solution.py:665
  66.2 19.7 %collective-permute-start.17 = (bf16[256,1024]{1,0:T(8,128)(2,1)}, bf16[256,1024]{1,0:T(8,128)(2,1)S(1)}, u32[]{:S(2)}, u32[]{:S(2)}) collective-permute-start(bf16[256,1024]{1,0:T(8,128)(2,1)} %shard_map.158.refs_1_.refs_8_), channel_id=1, source_target_pairs={{0,4},{4,12},{12,8},{8,0},{1,5},{5,13},{13,9},{9,1},{2,6},{6,14},{... | collective-permute-start | bytes 1572872 | tf_op jit(solution)/shard_map/ppermute | solution.py:608
  74.6 12.5 %copy-start.6 = (bf16[256,1024]{1,0:T(8,128)(2,1)S(1)}, bf16[256,1024]{1,0:T(8,128)(2,1)}, u32[]{:S(2)}) copy-start(bf16[256,1024]{1,0:T(8,128)(2,1)} %copy-done.5) | copy-start | bytes 1572868
  77.8 21.1 %collective-permute-start.14 = (bf16[256,1024]{1,0:T(8,128)(2,1)}, bf16[256,1024]{1,0:T(8,128)(2,1)}, u32[]{:S(2)}, u32[]{:S(2)}) collective-permute-start(bf16[256,1024]{1,0:T(8,128)(2,1)} %shard_map.163.refs_10_), channel_id=1, source_target_pairs={{0,4},{4,12},{12,8},{8,0},{1,5},{5,13},{13,9},{9,1},{2,6},{6,14},{... | collective-permute-start | bytes 1572872 | tf_op jit(solution)/shard_map/ppermute | solution.py:608
  80.4 26.3 %collective-permute-start.16 = (bf16[256,1024]{1,0:T(8,128)(2,1)}, bf16[256,1024]{1,0:T(8,128)(2,1)}, u32[]{:S(2)}, u32[]{:S(2)}) collective-permute-start(bf16[256,1024]{1,0:T(8,128)(2,1)} %shard_map.163.refs_10_), channel_id=1, source_target_pairs={{0,16},{16,0},{1,17},{17,1},{2,18},{18,2},{3,19},{19,3},{4,20},{20... | collective-permute-start | bytes 1572872 | tf_op jit(solution)/shard_map/ppermute | solution.py:611
  85.8 0.8 copy-start.9
  86.6 18.8 %copy-start.22 = (bf16[2048,2]{0,1:T(2,128)(2,1)S(1)}, bf16[2048,2]{0,1:T(2,128)(2,1)}, u32[]{:S(2)}) copy-start(bf16[2048,2]{0,1:T(2,128)(2,1)} %param.26) | copy-start | bytes 24580
  86.6 20.1 %collective-permute-start.18 = (bf16[256,1024]{1,0:T(8,128)(2,1)}, bf16[256,1024]{1,0:T(8,128)(2,1)S(1)}, u32[]{:S(2)}, u32[]{:S(2)}) collective-permute-start(bf16[256,1024]{1,0:T(8,128)(2,1)} %shard_map.165.refs_12_), channel_id=1, source_target_pairs={{0,16},{16,0},{1,17},{17,1},{2,18},{18,2},{3,19},{19,3},{4,20},{20... | collective-permute-start | bytes 1572872 | tf_op jit(solution)/shard_map/ppermute | solution.py:611
  87.1 1.0 copy-start.12
  96.3 2.0 %copy-start.7 = (f32[1024,1024]{1,0:T(8,128)}, f32[1024,1024]{1,0:T(8,128)S(1)}, u32[]{:S(2)}) copy-start(f32[1024,1024]{1,0:T(8,128)S(1)} %get-tuple-element.24.refs_15_) | copy-start | bytes 12582916
  98.3 0.6 copy-start.17
  98.9 7.8 %copy-start.10 = (bf16[256,1024]{1,0:T(8,128)(2,1)S(1)}, bf16[256,1024]{1,0:T(8,128)(2,1)}, u32[]{:S(2)}) copy-start(bf16[256,1024]{1,0:T(8,128)(2,1)} %shard_map.165.refs_12_) | copy-start | bytes 1572868
  98.9 18.1 %collective-permute-start.15 = (bf16[256,1024]{1,0:T(8,128)(2,1)}, bf16[256,1024]{1,0:T(8,128)(2,1)S(1)}, u32[]{:S(2)}, u32[]{:S(2)}) collective-permute-start(bf16[256,1024]{1,0:T(8,128)(2,1)} %shard_map.164.refs_14_), channel_id=1, source_target_pairs={{0,16},{16,0},{1,17},{17,1},{2,18},{18,2},{3,19},{19,3},{4,20},{20... | collective-permute-start | bytes 1572872 | tf_op jit(solution)/shard_map/ppermute | solution.py:611
  100.5 24.2 %all-to-all-start.1 = ((bf16[4,12,32,128]{3,2,1,0:T(8,128)(2,1)}), bf16[4,12,32,128]{3,2,1,0:T(8,128)(2,1)S(1)}, u32[]{:S(2)}, u32[]{:S(2)}) async-start(bf16[4,12,32,128]{3,2,1,0:T(8,128)(2,1)} %shard_map.151.refs_1_), calls=%async_computation.1 | async-start | bytes 786432 | tf_op jit(solution)/shard_map/all_to_all | solution.py:266
  106.7 2.2 %copy-start.8 = (f32[1024,1024]{1,0:T(8,128)S(1)}, f32[1024,1024]{1,0:T(8,128)}, u32[]{:S(2)}) copy-start(f32[1024,1024]{1,0:T(8,128)} %copy-done.7) | copy-start | bytes 12582916
  108.9 8.1 %copy-start.19 = (f32[2048]{0:T(1024)S(1)}, f32[2048]{0:T(1024)}, u32[]{:S(2)}) copy-start(f32[2048]{0:T(1024)} %param.25) | copy-start | bytes 24580
  117.0 5.8 %copy-start.24 = (f32[2]{0:T(128)S(1)}, f32[2]{0:T(128)}, u32[]{:S(2)}) copy-start(f32[2]{0:T(128)} %param.27) | copy-start | bytes 28
  117.1 7.7 %copy-start.18 = (f32[8,128]{1,0:T(8,128)S(1)}, f32[8,128]{1,0:T(8,128)}, u32[]{:S(2)}) copy-start(f32[8,128]{1,0:T(8,128)} %copy-done.17) | copy-start | bytes 12292
  120.6 6.2 %collective-permute-start.21 = (f32[1,512]{1,0:T(1,128)S(1)}, f32[1,512]{1,0:T(1,128)S(1)}, u32[]{:S(2)}, u32[]{:S(2)}) collective-permute-start(f32[1,512]{1,0:T(1,128)S(1)} %get-tuple-element.27), channel_id=1, source_target_pairs={{0,3},{1,2},{2,1},{3,0},{4,7},{5,6},{6,5},{7,4},{8,11},{9,10},{10,... | collective-permute-start | bytes 6152 | tf_op jit(solution)/shard_map/ppermute | solution.py:684
  120.7 6.1 %collective-permute-start.19 = (f32[1,512]{1,0:T(1,128)S(1)}, f32[1,512]{1,0:T(1,128)S(1)}, u32[]{:S(2)}, u32[]{:S(2)}) collective-permute-start(f32[1,512]{1,0:T(1,128)S(1)} %get-tuple-element.27), channel_id=1, source_target_pairs={{0,1},{1,0},{2,3},{3,2},{4,5},{5,4},{6,7},{7,6},{8,9},{9,8},{10,11... | collective-permute-start | bytes 6152 | tf_op jit(solution)/shard_map/ppermute | solution.py:681
  122.3 4.5 %collective-permute-start.20 = (f32[1,512]{1,0:T(1,128)S(1)}, f32[1,512]{1,0:T(1,128)S(1)}, u32[]{:S(2)}, u32[]{:S(2)}) collective-permute-start(f32[1,512]{1,0:T(1,128)S(1)} %get-tuple-element.26), channel_id=1, source_target_pairs={{0,2},{2,0},{1,3},{3,1},{4,6},{6,4},{5,7},{7,5},{8,10},{10,8},{9,1... | collective-permute-start | bytes 6152 | tf_op jit(solution)/shard_map/ppermute | solution.py:683

commit v4 on v3

--- a/solution.py
+++ b/solution.py
@@ -402,24 +402,24 @@
     return runs
 
 
-def merge_kernel(*refs):
-    *sources, out = refs
+def merge_kernel(*refs, count):
+    sources, out = refs[:count], refs[-1]
     at = 0
     for source in sources:
         out[at : at + source.shape[0]] = source[...]
         at += source.shape[0]
 
 
-def merge(sources):
+def merge(sources, waited):
     rows = sum(a.shape[0] for a in sources)
     return pl.pallas_call(
-        merge_kernel,
+        functools.partial(merge_kernel, count=len(sources)),
         out_shape=jax.ShapeDtypeStruct((rows,) + sources[0].shape[1:], sources[0].dtype),
-        in_specs=[VMEM] * len(sources),
+        in_specs=[VMEM] * len(sources) + [WAITED] * len(waited),
         out_specs=VMEM,
         cost_estimate=BRIEF,
         compiler_params=pltpu.CompilerParams(vmem_limit_bytes=VMEM_LIMIT),
-    )(*sources)
+    )(*sources, *waited)
 
 
 def split_kernel(source, *refs, pieces):
@@ -448,7 +448,7 @@
     )(source, *waited)
 
 
-def gemm_kernel(me, *refs, parts, sources, runs, layout, has_acc, final, tile):
+def gemm_kernel(me, *refs, parts, sources, runs, layout, has_acc, final, tile, via_hbm):
     refs = list(refs)
     halves = [refs[:parts], refs[parts : 2 * parts]]
     del refs[: 2 * parts]
@@ -457,13 +457,14 @@
     acc_in = refs.pop(0) if has_acc else None
     bias = class_weight = None
     if final:
-        bias, class_weight = refs[:2]
-        del refs[:2]
+        bias, class_weight, class_bias = refs[:3]
+        del refs[:3]
         outs = [refs.pop(0), refs.pop(0)]
+        biased = refs.pop(0)
     else:
         out, token = refs.pop(0), refs.pop(0)
         token[...] = jnp.zeros_like(token)
-    x_v, w_v, sems = refs
+    x_v, w_v, sems, acc_v, acc_sem = refs if via_hbm else refs + [None, None]
     rows = halves[0][0].shape[0]
     width = w_v.shape[1]
     depths = [depth for _, _, _, depth in runs]
@@ -494,6 +495,11 @@
         for r in range(2):
             for p in range(parts):
                 pl.when(part == p)(row_copy(i, r, p, offset).start)
+    held = out if not final else None
+    if via_hbm:
+        held = acc_v
+        if has_acc:
+            pltpu.make_async_copy(acc_in, acc_v, acc_sem).start()
     groups = []
     i = 0
     while i < len(runs):
@@ -508,14 +514,20 @@
             weight_copy(i).wait()
             for r in range(2):
                 row_copy(i, r, 0, 0).wait()
+        if g == len(groups) - 1 and via_hbm and has_acc:
+            pltpu.make_async_copy(acc_in, acc_v, acc_sem).wait()
         k0 = starts[first]
         k1 = starts[last - 1] + depths[last - 1]
 
         def body(m, carry, target=None, base=0):
             at = pl.ds(pl.multiple_of(base + m * tile, tile), tile)
             product = jnp.dot(x_v[at, k0:k1], w_v[k0:k1, :], preferred_element_type=jnp.float32)
-            if g > 0:
-                total = out[at, :] + product
+            if via_hbm and has_acc:
+                total = out[at, :] + product if g > 0 else product
+                if g == len(groups) - 1:
+                    total = total + acc_v[at, :]
+            elif g > 0:
+                total = held[at, :] + product
             elif has_acc:
                 total = acc_in[at, :] + product
             else:
@@ -530,8 +542,12 @@
                     turned = folded[j * HD : (j + 1) * HD, :].T
                     lanes = pl.ds(pl.multiple_of(m * tile + j * HD, HD), HD)
                     target[:, lanes] = jnp.sum(turned, axis=0, keepdims=True)
+            elif via_hbm and has_acc:
+                out[at, :] = total
             else:
-                out[at, :] = total
+                held[at, :] = total
+                if via_hbm and g == len(groups) - 1:
+                    pltpu.make_async_copy(held.at[at, :], out.at[at, :], acc_sem).start()
             return carry
 
         if final:
@@ -539,11 +555,14 @@
                 lax.fori_loop(
                     0, rows // tile, functools.partial(body, target=outs[r], base=r * rows), 0
                 )
+            biased[...] = outs[0][...] + (class_bias[1] - class_bias[0])
         else:
             lax.fori_loop(0, 2 * rows // tile, body, 0)
-
-
-def gemm(me, layout, halves, chunks, acc=None, tail=None):
+    if via_hbm and not has_acc:
+        pltpu.make_async_copy(held, out, acc_sem).wait()
+
+
+def gemm(me, layout, halves, chunks, acc=None, tail=None, via_hbm=False):
     weights = [w for w, _ in chunks]
     runs = [(run, i, row, d) for i, (_, found) in enumerate(chunks) for run, row, d in found]
     parts = len(halves[0])
@@ -553,19 +572,20 @@
     args = [me, *in_hbm([*halves[0], *halves[1]]), *weights]
     specs = [SMEM] + [ANY] * (2 * parts + len(weights))
     if acc is not None:
-        args.append(pltpu.with_memory_space_constraint(acc, pltpu.VMEM))
-        specs.append(VMEM)
+        space = pltpu.HBM if via_hbm else pltpu.VMEM
+        args.append(pltpu.with_memory_space_constraint(acc, space))
+        specs.append(ANY if via_hbm else VMEM)
     if tail is not None:
         args += list(tail)
-        specs += [VMEM] * 2
-        out_shape = [jax.ShapeDtypeStruct((1, rows), jnp.float32)] * 2
-        out_specs = [VMEM] * 2
+        specs += [VMEM] * 2 + [SMEM]
+        out_shape = [jax.ShapeDtypeStruct((1, rows), jnp.float32)] * 3
+        out_specs = [VMEM] * 3
     else:
         out_shape = [
-            pltpu.VMEM((2 * rows, width), jnp.float32),
+            (pltpu.HBM if via_hbm and acc is None else pltpu.VMEM)((2 * rows, width), jnp.float32),
             jax.ShapeDtypeStruct((8, HD), jnp.float32),
         ]
-        out_specs = [VMEM] * 2
+        out_specs = [ANY if via_hbm and acc is None else VMEM, VMEM]
     return pl.pallas_call(
         functools.partial(
             gemm_kernel,
@@ -576,6 +596,7 @@
             has_acc=acc is not None,
             final=tail is not None,
             tile=256,
+            via_hbm=via_hbm,
         ),
         out_shape=out_shape,
         in_specs=specs,
@@ -584,7 +605,8 @@
             pltpu.VMEM((2 * rows, depth), jnp.bfloat16),
             pltpu.VMEM((depth, width), jnp.bfloat16),
             pltpu.SemaphoreType.DMA((len(runs), 3)),
-        ],
+        ]
+        + ([pltpu.VMEM((2 * rows, width), jnp.float32), pltpu.SemaphoreType.DMA] if via_hbm else []),
         cost_estimate=BRIEF,
         compiler_params=pltpu.CompilerParams(vmem_limit_bytes=VMEM_LIMIT),
     )(*args)
@@ -613,9 +635,9 @@
     own = cut_share(me, head_weight, share, width, y_count, False, 0)
     given = [cut_share(me, head_weight, share, width, y_count, True, k) for k in range(y_count)]
     siblings = [lax.ppermute(g, "section", swap) for g in given]
-    merged = merge([own, siblings[0]])
+    power = row_power(step_rows, own)
+    merged = merge([own, siblings[0]], [power])
     whole = forward(merged)
-    power = row_power(step_rows, own)
     powers = [power] + [
         lax.ppermute(power, "mp", shift_pairs(x_count, k)) for k in range(1, x_count)
     ]
@@ -628,7 +650,7 @@
     theirs = [lax.ppermute(part, "section", swap) for part in mine]
     blobs = attention.pack(siblings[0])
     arrived = attention.send(blobs)
-    tail = [head_bias[None], class_weight.T.astype(jnp.float32)]
+    tail = [head_bias[None], class_weight.T.astype(jnp.float32), class_bias]
     chunks = [(head_weight, [((0, False, None, 0), 0, block)])] + [
         (t, [((0, True, (y_count - k) % y_count, 0), 0, share)]) for k, t in enumerate(siblings)
     ]
@@ -663,8 +685,9 @@
         (part,) = after([part], [travelled[0]])
         mine.append(part)
         theirs.append(lax.ppermute(part, "section", swap))
+    acc, early = gemm(me, layout, (mine, theirs), chunks, via_hbm=True)
+    (results,) = after([results], [early])
     returned = attention.send(results)
-    acc, early = gemm(me, layout, (mine, theirs), chunks)
     ends = []
     marks = [[], [early]]
     for j, t in enumerate(last):
@@ -676,9 +699,10 @@
             ]
         )
     attended = attention.finish(returned, early)
-    acc, _ = gemm(me, layout, (mine, theirs), second + sum(ends[:-1], []) + ends[-1][:1], acc)
-    kept, given = gemm(me, layout, (mine, theirs), ends[-1][1:], acc, tail)
-    total = kept + lax.ppermute(given, "section", swap)
+    middle = second + sum(ends[:-1], []) + ends[-1][:1]
+    acc, _ = gemm(me, layout, (mine, theirs), middle, acc, via_hbm=True)
+    kept, given, total = gemm(me, layout, (mine, theirs), ends[-1][1:], acc, tail)
+    total = total + lax.ppermute(given, "section", swap)
     for k in range(1, x_count):
         total = total + lax.ppermute(kept, "mp", shift_pairs(x_count, k))
         total = total + lax.ppermute(
@@ -690,7 +714,7 @@
                 for c in range(2)
             ],
         )
-    return attended, total[0] + (class_bias[1] - class_bias[0])
+    return attended, total[0]
 
 
 def judge_gathered(step_rows, norm_gain, head_weight, head_bias, class_weight, class_bias):

time: 128 us -> 126 us (0.984)
  local copies, waits for them, and re-layouts: 8.98 us -> 4.92 us
  waiting for transfers between devices: 40.1 us -> 42.6 us
  between operations: 2.24 us -> 0.89 us
    unnamed x51 -> x45, local copies, waits for them, and re-layouts: 8.37 us -> 4.92 us
    ppermute x5, waiting for transfers between devices: 15.8 us -> 18 us  [forward(): return lax.ppermute(t, 'batch', ring)]
    ppermute x1, waiting for transfers between devices: 0.01 us -> 1.78 us  [both(): total = total + lax.ppermute(kept, 'mp', shift_pairs(x_count, k))]
    ppermute x1, starting transfers between devices: 1.6 us -> 0.07 us  [both(): total = total + lax.ppermute(given, 'section', swap)]
    ppermute x2, waiting for transfers between devices: 15.3 us -> 13.9 us  [both(): lax.ppermute(part, 'mp', shift_pairs(x_count, k))]
  transfers between devices with their start and end apart: 24 -> 24, of which waited for: 8 -> 12; matrix products, arithmetic and copies ran while one was open for 1% -> 1% of each run, Pallas kernels for 30% -> 30%
where the time goes in v4:
time: 126 us; the launch traced here: 125 us
  waiting for transfers between devices  42.6 us (34%)
  Pallas kernels  40 us (32%)
  starting transfers between devices  36.4 us (29%)
  local copies, waits for them, and re-layouts  4.92 us (4%)
    pallas_call x3, Pallas kernels, gemm(): pl.pallas_call(functools.partial(gemm_kernel, parts=parts, sources=len(we...  20.8 us
    ppermute x5, waiting for transfers between devices, forward(): return lax.ppermute(t, 'batch', ring)  18 us
    ppermute x2, waiting for transfers between devices, both(): lax.ppermute(part, 'mp', shift_pairs(x_count, k))  13.9 us
    ppermute x5, starting transfers between devices, forward(): return lax.ppermute(t, 'batch', ring)  11.8 us
    all_to_all x2, starting transfers between devices, send(): lax.all_to_all(blobs, 'batch', split_axis=0, concat_axis=0, tiled=True)  9.68 us
    ppermute x5, starting transfers between devices, over_group(): lax.ppermute(t, 'group', shift_pairs(y_count, k))  6.76 us
    pallas_call x1, Pallas kernels, serve(): pl.pallas_call(functools.partial(serve_kernel, kv_local=kv_local, unroll=...  5.43 us
    unnamed x45, local copies, waits for them, and re-layouts  4.92 us
  transfers between devices with their start and end apart: 24, of which 12 were waited for; matrix products, arithmetic and copies ran while one was open for 1% of the time, Pallas kernels for 30%

profile of v4, /device:TPU:0, one launch (start us, length us, event | category | flops | bytes accessed | tf_op | source)
XLA Modules:
  0.0 125.5 jit_solution(15801495945923390183)
XLA Ops:
  0.6 0.1 pad_add_fusion.me
  0.7 1.6 %copy-done = bf16[512,2048]{1,0:T(8,128)(2,1)S(1)} copy-done((bf16[512,2048]{1,0:T(8,128)(2,1)S(1)}, bf16[512,2048]{1,0:T(8,128)(2,1)}, u32[]{:S(2)}) %copy-start) | copy-done | bytes 2097176
  2.3 0.6 shard_map.149
  2.9 0.5 collective-permute-start
  3.4 0.6 shard_map.152.waited.refs_0_
  4.1 0.0 copy-start.1
  4.1 0.7 shard_map.153.refs_2_.refs_0_
  4.8 0.0 copy-start.15
  4.8 0.2 collective-permute-done.waited.refs_1_.refs_9_
  5.0 0.1 shard_map.154.refs_3_
  5.1 3.0 %collective-permute-start.3 = (bf16[512,1024]{1,0:T(8,128)(2,1)S(1)}, bf16[512,1024]{1,0:T(8,128)(2,1)}, u32[]{:S(2)}, u32[]{:S(2)}) collective-permute-start(bf16[512,1024]{1,0:T(8,128)(2,1)S(1)} %shard_map.154.refs_3_), channel_id=1, source_target_pairs={{0,4},{4,12},{12,8},{8,0},{1,5},{5,13},{13,9},{9,1},{2,6},{6,14},{... | collective-permute-start | bytes 3145736 | tf_op jit(solution)/shard_map/ppermute | solution.py:630
  8.0 1.5 %collective-permute-start.1 = (f32[4,128]{1,0:T(4,128)S(1)}, f32[4,128]{1,0:T(4,128)S(1)}, u32[]{:S(2)}, u32[]{:S(2)}) collective-permute-start(f32[4,128]{1,0:T(4,128)S(1)} %shard_map.153.refs_2_.refs_0_), channel_id=1, source_target_pairs={{0,2},{2,0},{1,3},{3,1},{4,6},{6,4},{5,7},{7,5},{8,10},{10,8},{9,1... | collective-permute-start | bytes 6152 | tf_op jit(solution)/shard_map/ppermute | solution.py:642
  9.5 0.6 shard_map.156
  10.2 1.5 %collective-permute-done.1.refs_1_ = f32[4,128]{1,0:T(4,128)S(1)} collective-permute-done((f32[4,128]{1,0:T(4,128)S(1)}, f32[4,128]{1,0:T(4,128)S(1)}, u32[]{:S(2)}, u32[]{:S(2)}) %collective-permute-start.1) | collective-permute-done | bytes 2080 | tf_op jit(solution)/shard_map/ppermute | solution.py:642
  11.6 2.5 %shard_map.155 = (bf16[512,1024]{1,0:T(8,128)(2,1)}, bf16[512,1024]{1,0:T(8,128)(2,1)}) custom-call(s32[4]{0:T(128)S(1)} %pad_add_fusion.me, bf16[512,2048]{1,0:T(8,128)(2,1)S(1)} %copy-done.4, f32[4,128]{1,0:T(4,128)S(1)} %shard_map.153.refs_2_.refs_0_, f32[4,128]{1,0:T(4,128)S(1)} %collective-permute-done.1.refs_1_, f32[1,4096]{1,0:T(1,128)S(1)} %bitcast.18, ...), custom_call_target="tpu_custom_call" | custom-call | flops 1 | bytes 1 | tf_op jit(solution)/shard_map/pallas_call | solution.py:348
  14.2 0.0 copy-start.19
  14.2 0.1 collective-permute-start.5
  14.3 0.5 collective-permute-start.6
  14.8 0.1 collective-permute-start.4
  14.8 1.5 %collective-permute-start.2 = (bf16[512,1024]{1,0:T(8,128)(2,1)}, bf16[512,1024]{1,0:T(8,128)(2,1)}, u32[]{:S(2)}, u32[]{:S(2)}) collective-permute-start(bf16[512,1024]{1,0:T(8,128)(2,1)} %get-tuple-element.20.refs_0_), channel_id=1, source_target_pairs={{0,2},{2,0},{1,3},{3,1},{4,6},{6,4},{5,7},{7,5},{8,10},{10,8},{9,1... | collective-permute-start | bytes 3145736 | tf_op jit(solution)/shard_map/ppermute | solution.py:646
  16.3 2.1 %collective-permute-done.4.refs_0_.refs_10_ = bf16[256,1024]{1,0:T(8,128)(2,1)S(1)} collective-permute-done((bf16[256,1024]{1,0:T(8,128)(2,1)S(1)}, bf16[256,1024]{1,0:T(8,128)(2,1)S(1)}, u32[]{:S(2)}, u32[]{:S(2)}) %collective-permute-start.4) | collective-permute-done | bytes 524320 | tf_op jit(solution)/shard_map/ppermute | solution.py:637
  18.4 1.5 %collective-permute-start.9 = (bf16[512,1024]{1,0:T(8,128)(2,1)}, bf16[512,1024]{1,0:T(8,128)(2,1)}, u32[]{:S(2)}, u32[]{:S(2)}) collective-permute-start(bf16[512,1024]{1,0:T(8,128)(2,1)} %get-tuple-element.21.refs_1_), channel_id=1, source_target_pairs={{0,2},{2,0},{1,3},{3,1},{4,6},{6,4},{5,7},{7,5},{8,10},{10,8},{9,1... | collective-permute-start | bytes 3145736 | tf_op jit(solution)/shard_map/ppermute | solution.py:646
  19.9 12.7 %collective-permute-done.3.source.refs_11_ = bf16[512,1024]{1,0:T(8,128)(2,1)} collective-permute-done((bf16[512,1024]{1,0:T(8,128)(2,1)S(1)}, bf16[512,1024]{1,0:T(8,128)(2,1)}, u32[]{:S(2)}, u32[]{:S(2)}) %collective-permute-start.3) | collective-permute-done | bytes 1048608 | tf_op jit(solution)/shard_map/ppermute | solution.py:630
  32.6 1.6 %collective-permute-start.8 = (bf16[512,1024]{1,0:T(8,128)(2,1)}, bf16[512,1024]{1,0:T(8,128)(2,1)}, u32[]{:S(2)}, u32[]{:S(2)}) collective-permute-start(bf16[512,1024]{1,0:T(8,128)(2,1)} %collective-permute-done.3.source.refs_11_), channel_id=1, source_target_pairs={{0,16},{16,0},{1,17},{17,1},{2,18},{18,2},{3,19},{19,3},{4,20},{20... | collective-permute-start | bytes 3145736 | tf_op jit(solution)/shard_map/ppermute | solution.py:633
  34.2 0.0 collective-permute-done.6.refs_2_.refs_5_
  34.2 2.8 %shard_map.157 = (bf16[256,1024]{1,0:T(8,128)(2,1)S(1)}, bf16[256,1024]{1,0:T(8,128)(2,1)}) custom-call(bf16[512,1024]{1,0:T(8,128)(2,1)} %collective-permute-done.3.source.refs_11_, bf16[256,1024]{1,0:T(8,128)(2,1)S(1)} %collective-permute-done.4.refs_0_.refs_10_, bf16[512,1024]{1,0:T(8,128)(2,1)S(1)} %collective-permute-done.5.refs_1_.refs_4_, ...), custom_call_target="tpu_custom_call" | custom-call | flops 1 | bytes 1 | tf_op jit(solution)/shard_map/pallas_call | solution.py:440
  37.0 0.7 collective-permute-start.7
  37.8 3.8 %shard_map.150 = (bf16[4,12,40,128]{3,2,1,0:T(8,128)(2,1)}, s32[48]{0:T(128)S(1)}, s32[48]{0:T(128)S(1)}, s32[24]{0:T(128)S(1)}) custom-call(s32[1]{0:T(128)} %bitcast.me, s32[96]{0:T(128)S(1)} %copy-done.18, s32[96]{0:T(128)S(1)} %copy-done.19, bf16[24,4096]{1,0:T(8,128)(2,1)S(1)} %bitcast.15, bf16[24,512]{1,0:T(8,128)(2,1)S(1)} %bitcast.16, ...), custom_call_target="tpu_custom_call" | custom-call | flops 1 | bytes 1 | tf_op jit(solution)/shard_map/pallas_call | solution.py:110
  41.6 4.8 %all-to-all-start = ((bf16[4,12,40,128]{3,2,1,0:T(8,128)(2,1)}), bf16[4,12,40,128]{3,2,1,0:T(8,128)(2,1)}, u32[]{:S(2)}, u32[]{:S(2)}) async-start(bf16[4,12,40,128]{3,2,1,0:T(8,128)(2,1)} %get-tuple-element.19.refs_1_), calls=%async_computation | async-start | bytes 983040 | tf_op jit(solution)/shard_map/all_to_all | solution.py:266
  46.4 2.9 %collective-permute-start.12 = (bf16[256,1024]{1,0:T(8,128)(2,1)}, bf16[256,1024]{1,0:T(8,128)(2,1)}, u32[]{:S(2)}, u32[]{:S(2)}) collective-permute-start(bf16[256,1024]{1,0:T(8,128)(2,1)} %get-tuple-element.24), channel_id=1, source_target_pairs={{0,4},{4,12},{12,8},{8,0},{1,5},{5,13},{13,9},{9,1},{2,6},{6,14},{... | collective-permute-start | bytes 1572872 | tf_op jit(solution)/shard_map/ppermute | solution.py:630
  49.3 13.9 %collective-permute-done.9.refs_4_.refs_0_ = bf16[512,1024]{1,0:T(8,128)(2,1)} collective-permute-done((bf16[512,1024]{1,0:T(8,128)(2,1)}, bf16[512,1024]{1,0:T(8,128)(2,1)}, u32[]{:S(2)}, u32[]{:S(2)}) %collective-permute-start.9) | collective-permute-done | bytes 1048608 | tf_op jit(solution)/shard_map/ppermute | solution.py:646
  63.1 0.0 collective-permute-done.8.refs_2_.refs_12_
  63.1 1.6 %collective-permute-start.13 = (bf16[256,1024]{1,0:T(8,128)(2,1)}, bf16[256,1024]{1,0:T(8,128)(2,1)}, u32[]{:S(2)}, u32[]{:S(2)}) collective-permute-start(bf16[256,1024]{1,0:T(8,128)(2,1)} %shard_map.158.refs_1_.refs_8_), channel_id=1, source_target_pairs={{0,16},{16,0},{1,17},{17,1},{2,18},{18,2},{3,19},{19,3},{4,20},{20... | collective-permute-start | bytes 1572872 | tf_op jit(solution)/shard_map/ppermute | solution.py:633
  64.7 0.0 collective-permute-start.11
  64.7 0.5 collective-permute-start.10
  65.3 0.1 copy.23.page_table
  65.3 2.6 %collective-permute-start.17 = (bf16[256,1024]{1,0:T(8,128)(2,1)}, bf16[256,1024]{1,0:T(8,128)(2,1)S(1)}, u32[]{:S(2)}, u32[]{:S(2)}) collective-permute-start(bf16[256,1024]{1,0:T(8,128)(2,1)} %shard_map.158.refs_1_.refs_8_), channel_id=1, source_target_pairs={{0,4},{4,12},{12,8},{8,0},{1,5},{5,13},{13,9},{9,1},{2,6},{6,14},{... | collective-permute-start | bytes 1572872 | tf_op jit(solution)/shard_map/ppermute | solution.py:630
  67.9 5.4 %shard_map.151.refs_0_.refs_1_ = bf16[4,12,32,128]{3,2,1,0:T(8,128)(2,1)S(1)} custom-call(s32[48]{0:T(128)S(1)} %get-tuple-element.17.particle, s32[24,4]{1,0:T(8,128)S(1)} %copy.23.page_table, s32[48]{0:T(128)S(1)} %get-tuple-element.18.lengths, bf16[4,12,40,128]{3,2,1,0:T(8,128)(2,1)} %all-to-all-done.blobs, bf16[96,16,512]{2,1,0:T(8,128)(2,1)} %bitcast.20, ...), custom_call_target="tpu_custom_call" | custom-call | flops 1 | bytes 1 | tf_op jit(solution)/shard_map/pallas_call | solution.py:207
  73.4 0.7 copy-done.5
  74.1 0.6 collective-permute-done.12.refs_0_
  74.7 2.3 %collective-permute-done.13.refs_2_.refs_9_ = bf16[256,1024]{1,0:T(8,128)(2,1)} collective-permute-done((bf16[256,1024]{1,0:T(8,128)(2,1)}, bf16[256,1024]{1,0:T(8,128)(2,1)}, u32[]{:S(2)}, u32[]{:S(2)}) %collective-permute-start.13) | collective-permute-done | bytes 524320 | tf_op jit(solution)/shard_map/ppermute | solution.py:633
  77.0 2.6 %collective-permute-start.14 = (bf16[256,1024]{1,0:T(8,128)(2,1)}, bf16[256,1024]{1,0:T(8,128)(2,1)}, u32[]{:S(2)}, u32[]{:S(2)}) collective-permute-start(bf16[256,1024]{1,0:T(8,128)(2,1)} %shard_map.164.refs_10_), channel_id=1, source_target_pairs={{0,4},{4,12},{12,8},{8,0},{1,5},{5,13},{13,9},{9,1},{2,6},{6,14},{... | collective-permute-start | bytes 1572872 | tf_op jit(solution)/shard_map/ppermute | solution.py:630
  79.6 1.5 %collective-permute-start.16 = (bf16[256,1024]{1,0:T(8,128)(2,1)}, bf16[256,1024]{1,0:T(8,128)(2,1)}, u32[]{:S(2)}, u32[]{:S(2)}) collective-permute-start(bf16[256,1024]{1,0:T(8,128)(2,1)} %shard_map.164.refs_10_), channel_id=1, source_target_pairs={{0,16},{16,0},{1,17},{17,1},{2,18},{18,2},{3,19},{19,3},{4,20},{20... | collective-permute-start | bytes 1572872 | tf_op jit(solution)/shard_map/ppermute | solution.py:633
  81.1 4.7 %collective-permute-done.17.refs_0_ = bf16[256,1024]{1,0:T(8,128)(2,1)S(1)} collective-permute-done((bf16[256,1024]{1,0:T(8,128)(2,1)}, bf16[256,1024]{1,0:T(8,128)(2,1)S(1)}, u32[]{:S(2)}, u32[]{:S(2)}) %collective-permute-start.17) | collective-permute-done | bytes 524320 | tf_op jit(solution)/shard_map/ppermute | solution.py:630
  85.8 0.8 copy-done.6
  86.6 0.5 collective-permute-start.18
  87.1 1.0 copy-done.9
  88.1 9.2 %shard_map.161 = (f32[1024,1024]{1,0:T(8,128)}, f32[8,128]{1,0:T(8,128)S(1)}) custom-call(s32[4]{0:T(128)S(1)} %pad_add_fusion.me, bf16[512,1024]{1,0:T(8,128)(2,1)} %get-tuple-element.20.refs_0_, bf16[512,1024]{1,0:T(8,128)(2,1)} %get-tuple-element.21.refs_1_, bf16[512,1024]{1,0:T(8,128)(2,1)} %shard_map.159.refs_2_, bf16[512,1024]{1,0:T(8,128)(2,1)} %shard_map.160.refs_3_, ...), custom_call_target="tpu_custom_call" | custom-call | flops 1 | bytes 1 | tf_op jit(solution)/shard_map/pallas_call | solution.py:589
  97.3 0.0 copy-start.11
  97.3 0.6 copy-done.11
  97.9 1.6 %collective-permute-start.15 = (bf16[256,1024]{1,0:T(8,128)(2,1)}, bf16[256,1024]{1,0:T(8,128)(2,1)S(1)}, u32[]{:S(2)}, u32[]{:S(2)}) collective-permute-start(bf16[256,1024]{1,0:T(8,128)(2,1)} %shard_map.165.refs_14_), channel_id=1, source_target_pairs={{0,16},{16,0},{1,17},{17,1},{2,18},{18,2},{3,19},{19,3},{4,20},{20... | collective-permute-start | bytes 1572872 | tf_op jit(solution)/shard_map/ppermute | solution.py:633
  99.5 4.9 %all-to-all-start.1 = ((bf16[4,12,32,128]{3,2,1,0:T(8,128)(2,1)}), bf16[4,12,32,128]{3,2,1,0:T(8,128)(2,1)S(1)}, u32[]{:S(2)}, u32[]{:S(2)}) async-start(bf16[4,12,32,128]{3,2,1,0:T(8,128)(2,1)} %shard_map.162), calls=%async_computation.1 | async-start | bytes 786432 | tf_op jit(solution)/shard_map/all_to_all | solution.py:266
  104.5 1.4 %collective-permute-done.18.refs_13_ = bf16[256,1024]{1,0:T(8,128)(2,1)S(1)} collective-permute-done((bf16[256,1024]{1,0:T(8,128)(2,1)}, bf16[256,1024]{1,0:T(8,128)(2,1)S(1)}, u32[]{:S(2)}, u32[]{:S(2)}) %collective-permute-start.18) | collective-permute-done | bytes 524320 | tf_op jit(solution)/shard_map/ppermute | solution.py:633
  105.9 8.1 %shard_map.167 = (f32[1024,1024]{1,0:T(8,128)S(1)}, f32[8,128]{1,0:T(8,128)}) custom-call(s32[4]{0:T(128)S(1)} %pad_add_fusion.me, bf16[512,1024]{1,0:T(8,128)(2,1)} %get-tuple-element.20.refs_0_, bf16[512,1024]{1,0:T(8,128)(2,1)} %get-tuple-element.21.refs_1_, bf16[512,1024]{1,0:T(8,128)(2,1)} %shard_map.159.refs_2_, bf16[512,1024]{1,0:T(8,128)(2,1)} %shard_map.160.refs_3_, ...), custom_call_target="tpu_custom_call" | custom-call | flops 1 | bytes 1 | tf_op jit(solution)/shard_map/pallas_call | solution.py:589
  114.0 0.6 collective-permute-done.15.refs_8_
  114.6 3.6 %shard_map.168 = (f32[1,512]{1,0:T(1,128)S(1)}, f32[1,512]{1,0:T(1,128)S(1)}, f32[1,512]{1,0:T(1,128)S(1)}) custom-call(s32[4]{0:T(128)S(1)} %pad_add_fusion.me, bf16[512,1024]{1,0:T(8,128)(2,1)} %get-tuple-element.20.refs_0_, bf16[512,1024]{1,0:T(8,128)(2,1)} %get-tuple-element.21.refs_1_, bf16[512,1024]{1,0:T(8,128)(2,1)} %shard_map.159.refs_2_, ...), custom_call_target="tpu_custom_call" | custom-call | flops 1 | bytes 1 | tf_op jit(solution)/shard_map/pallas_call | solution.py:589
  118.2 0.1 collective-permute-start.19
  118.3 1.6 %collective-permute-start.20 = (f32[1,512]{1,0:T(1,128)S(1)}, f32[1,512]{1,0:T(1,128)S(1)}, u32[]{:S(2)}, u32[]{:S(2)}) collective-permute-start(f32[1,512]{1,0:T(1,128)S(1)} %get-tuple-element.29), channel_id=1, source_target_pairs={{0,2},{2,0},{1,3},{3,1},{4,6},{6,4},{5,7},{7,5},{8,10},{10,8},{9,1... | collective-permute-start | bytes 6152 | tf_op jit(solution)/shard_map/ppermute | solution.py:707
  119.8 0.3 collective-permute-start.21
  120.1 0.0 collective-permute-done.19
  120.1 1.8 %collective-permute-done.20 = f32[1,512]{1,0:T(1,128)S(1)} collective-permute-done((f32[1,512]{1,0:T(1,128)S(1)}, f32[1,512]{1,0:T(1,128)S(1)}, u32[]{:S(2)}, u32[]{:S(2)}) %collective-permute-start.20) | collective-permute-done | bytes 2080 | tf_op jit(solution)/shard_map/ppermute | solution.py:707
  121.9 0.9 collective-permute-done.21
  122.8 0.6 add_add_fusion
  123.4 2.1 %shard_map.163 = bf16[24,4096]{1,0:T(8,128)(2,1)} custom-call(s32[24]{0:T(128)S(1)} %get-tuple-element.16.pick, bf16[4,12,32,128]{3,2,1,0:T(8,128)(2,1)S(1)} %all-to-all-done.1.parts, f32[8,128]{1,0:T(8,128)S(1)} %copy-done.12), custom_call_target="tpu_custom_call" | custom-call | flops 1 | bytes 1 | tf_op jit(solution)/shard_map/pallas_call | solution.py:239
  (52 shorter events, 0.1 us)
Async XLA Ops:
  0.7 1.6 %copy-start = (bf16[512,2048]{1,0:T(8,128)(2,1)S(1)}, bf16[512,2048]{1,0:T(8,128)(2,1)}, u32[]{:S(2)}) copy-start(bf16[512,2048]{1,0:T(8,128)(2,1)} %refs_8_.1) | copy-start | bytes 6291460
  2.3 1.8 %copy-start.4 = (bf16[512,2048]{1,0:T(8,128)(2,1)S(1)}, bf16[512,2048]{1,0:T(8,128)(2,1)}, u32[]{:S(2)}) copy-start(bf16[512,2048]{1,0:T(8,128)(2,1)} %x.3) | copy-start | bytes 6291460
  2.9 2.1 %collective-permute-start = (bf16[256,1024]{1,0:T(8,128)(2,1)S(1)}, bf16[256,1024]{1,0:T(8,128)(2,1)S(1)}, u32[]{:S(2)}, u32[]{:S(2)}) collective-permute-start(bf16[256,1024]{1,0:T(8,128)(2,1)S(1)} %shard_map.149), channel_id=1, source_target_pairs={{0,1},{1,0},{2,3},{3,2},{4,5},{5,4},{6,7},{7,6},{8,9},{9,8},{10,11... | collective-permute-start | bytes 1572872 | tf_op jit(solution)/shard_map/ppermute | solution.py:637
  4.1 5.5 %copy-start.1 = (bf16[512,2048]{1,0:T(8,128)(2,1)S(1)}, bf16[512,2048]{1,0:T(8,128)(2,1)}, u32[]{:S(2)}) copy-start(bf16[512,2048]{1,0:T(8,128)(2,1)} %refs_8_.1) | copy-start | bytes 6291460
  4.8 6.8 %copy-start.15 = (f32[4096]{0:T(1024)S(1)}, f32[4096]{0:T(1024)}, u32[]{:S(2)}) copy-start(f32[4096]{0:T(1024)} %param.23) | copy-start | bytes 49156
  5.1 27.6 %collective-permute-start.3 = (bf16[512,1024]{1,0:T(8,128)(2,1)S(1)}, bf16[512,1024]{1,0:T(8,128)(2,1)}, u32[]{:S(2)}, u32[]{:S(2)}) collective-permute-start(bf16[512,1024]{1,0:T(8,128)(2,1)S(1)} %shard_map.154.refs_3_), channel_id=1, source_target_pairs={{0,4},{4,12},{12,8},{8,0},{1,5},{5,13},{13,9},{9,1},{2,6},{6,14},{... | collective-permute-start | bytes 3145736 | tf_op jit(solution)/shard_map/ppermute | solution.py:630
  8.0 3.6 %collective-permute-start.1 = (f32[4,128]{1,0:T(4,128)S(1)}, f32[4,128]{1,0:T(4,128)S(1)}, u32[]{:S(2)}, u32[]{:S(2)}) collective-permute-start(f32[4,128]{1,0:T(4,128)S(1)} %shard_map.153.refs_2_.refs_0_), channel_id=1, source_target_pairs={{0,2},{2,0},{1,3},{3,1},{4,6},{6,4},{5,7},{7,5},{8,10},{10,8},{9,1... | collective-permute-start | bytes 6152 | tf_op jit(solution)/shard_map/ppermute | solution.py:642
  14.2 23.6 %copy-start.10 = (bf16[1,24,4096]{2,1,0:T(8,128)(2,1)S(1)}, bf16[1,24,4096]{2,1,0:T(8,128)(2,1)}, u32[]{:S(2)}) copy-start(bf16[1,24,4096]{2,1,0:T(8,128)(2,1)} %param.14) | copy-start | bytes 589828
  14.2 23.6 %copy-start.13 = (bf16[1,24,512]{2,1,0:T(8,128)(2,1)S(1)}, bf16[1,24,512]{2,1,0:T(8,128)(2,1)}, u32[]{:S(2)}) copy-start(bf16[1,24,512]{2,1,0:T(8,128)(2,1)} %param.15) | copy-start | bytes 73732
  14.2 23.6 %copy-start.14 = (bf16[1,24,512]{2,1,0:T(8,128)(2,1)S(1)}, bf16[1,24,512]{2,1,0:T(8,128)(2,1)}, u32[]{:S(2)}) copy-start(bf16[1,24,512]{2,1,0:T(8,128)(2,1)} %param.16) | copy-start | bytes 73732
  14.2 23.6 %copy-start.18 = (s32[96]{0:T(128)S(1)}, s32[96]{0:T(128)}, u32[]{:S(2)}) copy-start(s32[96]{0:T(128)} %ancestry.1) | copy-start | bytes 1156
  14.2 23.6 %copy-start.19 = (s32[96]{0:T(128)S(1)}, s32[96]{0:T(128)}, u32[]{:S(2)}) copy-start(s32[96]{0:T(128)} %lengths.1) | copy-start | bytes 1156
  14.2 20.0 %collective-permute-start.5 = (bf16[512,1024]{1,0:T(8,128)(2,1)}, bf16[512,1024]{1,0:T(8,128)(2,1)S(1)}, u32[]{:S(2)}, u32[]{:S(2)}) collective-permute-start(bf16[512,1024]{1,0:T(8,128)(2,1)} %get-tuple-element.20.refs_0_), channel_id=1, source_target_pairs={{0,1},{1,0},{2,3},{3,2},{4,5},{5,4},{6,7},{7,6},{8,9},{9,8},{10,11... | collective-permute-start | bytes 3145736 | tf_op jit(solution)/shard_map/ppermute | solution.py:650
  14.3 19.9 %collective-permute-start.6 = (bf16[512,1024]{1,0:T(8,128)(2,1)}, bf16[512,1024]{1,0:T(8,128)(2,1)S(1)}, u32[]{:S(2)}, u32[]{:S(2)}) collective-permute-start(bf16[512,1024]{1,0:T(8,128)(2,1)} %get-tuple-element.21.refs_1_), channel_id=1, source_target_pairs={{0,1},{1,0},{2,3},{3,2},{4,5},{5,4},{6,7},{7,6},{8,9},{9,8},{10,11... | collective-permute-start | bytes 3145736 | tf_op jit(solution)/shard_map/ppermute | solution.py:650
  14.8 3.6 %collective-permute-start.4 = (bf16[256,1024]{1,0:T(8,128)(2,1)S(1)}, bf16[256,1024]{1,0:T(8,128)(2,1)S(1)}, u32[]{:S(2)}, u32[]{:S(2)}) collective-permute-start(bf16[256,1024]{1,0:T(8,128)(2,1)S(1)} %shard_map.156), channel_id=1, source_target_pairs={{0,1},{1,0},{2,3},{3,2},{4,5},{5,4},{6,7},{7,6},{8,9},{9,8},{10,11... | collective-permute-start | bytes 1572872 | tf_op jit(solution)/shard_map/ppermute | solution.py:637
  14.8 34.4 %collective-permute-start.2 = (bf16[512,1024]{1,0:T(8,128)(2,1)}, bf16[512,1024]{1,0:T(8,128)(2,1)}, u32[]{:S(2)}, u32[]{:S(2)}) collective-permute-start(bf16[512,1024]{1,0:T(8,128)(2,1)} %get-tuple-element.20.refs_0_), channel_id=1, source_target_pairs={{0,2},{2,0},{1,3},{3,1},{4,6},{6,4},{5,7},{7,5},{8,10},{10,8},{9,1... | collective-permute-start | bytes 3145736 | tf_op jit(solution)/shard_map/ppermute | solution.py:646
  18.4 23.2 %copy-start.8 = (bf16[256,1024]{1,0:T(8,128)(2,1)}, bf16[256,1024]{1,0:T(8,128)(2,1)S(1)}, u32[]{:S(2)}) copy-start(bf16[256,1024]{1,0:T(8,128)(2,1)S(1)} %collective-permute-done.4.refs_0_.refs_10_) | copy-start | bytes 1572868
  18.4 44.7 %collective-permute-start.9 = (bf16[512,1024]{1,0:T(8,128)(2,1)}, bf16[512,1024]{1,0:T(8,128)(2,1)}, u32[]{:S(2)}, u32[]{:S(2)}) collective-permute-start(bf16[512,1024]{1,0:T(8,128)(2,1)} %get-tuple-element.21.refs_1_), channel_id=1, source_target_pairs={{0,2},{2,0},{1,3},{3,1},{4,6},{6,4},{5,7},{7,5},{8,10},{10,8},{9,1... | collective-permute-start | bytes 3145736 | tf_op jit(solution)/shard_map/ppermute | solution.py:646
  32.6 30.5 %collective-permute-start.8 = (bf16[512,1024]{1,0:T(8,128)(2,1)}, bf16[512,1024]{1,0:T(8,128)(2,1)}, u32[]{:S(2)}, u32[]{:S(2)}) collective-permute-start(bf16[512,1024]{1,0:T(8,128)(2,1)} %collective-permute-done.3.source.refs_11_), channel_id=1, source_target_pairs={{0,16},{16,0},{1,17},{17,1},{2,18},{18,2},{3,19},{19,3},{4,20},{20... | collective-permute-start | bytes 3145736 | tf_op jit(solution)/shard_map/ppermute | solution.py:633
  34.2 7.4 %copy-start.2 = (bf16[512,1024]{1,0:T(8,128)(2,1)}, bf16[512,1024]{1,0:T(8,128)(2,1)S(1)}, u32[]{:S(2)}) copy-start(bf16[512,1024]{1,0:T(8,128)(2,1)S(1)} %collective-permute-done.5.refs_1_.refs_4_) | copy-start | bytes 3145732
  34.2 7.4 %copy-start.3 = (bf16[512,1024]{1,0:T(8,128)(2,1)}, bf16[512,1024]{1,0:T(8,128)(2,1)S(1)}, u32[]{:S(2)}) copy-start(bf16[512,1024]{1,0:T(8,128)(2,1)S(1)} %collective-permute-done.6.refs_2_.refs_5_) | copy-start | bytes 3145732
  37.0 26.1 %collective-permute-start.7 = (bf16[256,1024]{1,0:T(8,128)(2,1)S(1)}, bf16[256,1024]{1,0:T(8,128)(2,1)}, u32[]{:S(2)}, u32[]{:S(2)}) collective-permute-start(bf16[256,1024]{1,0:T(8,128)(2,1)S(1)} %get-tuple-element.22), channel_id=1, source_target_pairs={{0,4},{4,12},{12,8},{8,0},{1,5},{5,13},{13,9},{9,1},{2,6},{6,14},{... | collective-permute-start | bytes 1572872 | tf_op jit(solution)/shard_map/ppermute | solution.py:630
  41.6 26.3 %all-to-all-start = ((bf16[4,12,40,128]{3,2,1,0:T(8,128)(2,1)}), bf16[4,12,40,128]{3,2,1,0:T(8,128)(2,1)}, u32[]{:S(2)}, u32[]{:S(2)}) async-start(bf16[4,12,40,128]{3,2,1,0:T(8,128)(2,1)} %get-tuple-element.19.refs_1_), calls=%async_computation | async-start | bytes 983040 | tf_op jit(solution)/shard_map/all_to_all | solution.py:266
  46.4 28.3 %collective-permute-start.12 = (bf16[256,1024]{1,0:T(8,128)(2,1)}, bf16[256,1024]{1,0:T(8,128)(2,1)}, u32[]{:S(2)}, u32[]{:S(2)}) collective-permute-start(bf16[256,1024]{1,0:T(8,128)(2,1)} %get-tuple-element.24), channel_id=1, source_target_pairs={{0,4},{4,12},{12,8},{8,0},{1,5},{5,13},{13,9},{9,1},{2,6},{6,14},{... | collective-permute-start | bytes 1572872 | tf_op jit(solution)/shard_map/ppermute | solution.py:630
  63.1 2.1 %copy-start.21 = (s32[24,4]{0,1:T(4,128)S(1)}, s32[24,4]{0,1:T(4,128)}, u32[]{:S(2)}) copy-start(s32[24,4]{0,1:T(4,128)} %param.19) | copy-start | bytes 1156
  63.1 13.9 %collective-permute-start.13 = (bf16[256,1024]{1,0:T(8,128)(2,1)}, bf16[256,1024]{1,0:T(8,128)(2,1)}, u32[]{:S(2)}, u32[]{:S(2)}) collective-permute-start(bf16[256,1024]{1,0:T(8,128)(2,1)} %shard_map.158.refs_1_.refs_8_), channel_id=1, source_target_pairs={{0,16},{16,0},{1,17},{17,1},{2,18},{18,2},{3,19},{19,3},{4,20},{20... | collective-permute-start | bytes 1572872 | tf_op jit(solution)/shard_map/ppermute | solution.py:633
  64.7 22.3 %collective-permute-start.11 = (bf16[512,1024]{1,0:T(8,128)(2,1)}, bf16[512,1024]{1,0:T(8,128)(2,1)}, u32[]{:S(2)}, u32[]{:S(2)}) collective-permute-start(bf16[512,1024]{1,0:T(8,128)(2,1)} %shard_map.160.refs_3_), channel_id=1, source_target_pairs={{0,1},{1,0},{2,3},{3,2},{4,5},{5,4},{6,7},{7,6},{8,9},{9,8},{10,11... | collective-permute-start | bytes 3145736 | tf_op jit(solution)/shard_map/ppermute | solution.py:687
  64.7 22.3 %collective-permute-start.10 = (bf16[512,1024]{1,0:T(8,128)(2,1)}, bf16[512,1024]{1,0:T(8,128)(2,1)}, u32[]{:S(2)}, u32[]{:S(2)}) collective-permute-start(bf16[512,1024]{1,0:T(8,128)(2,1)} %shard_map.159.refs_2_), channel_id=1, source_target_pairs={{0,1},{1,0},{2,3},{3,2},{4,5},{5,4},{6,7},{7,6},{8,9},{9,8},{10,11... | collective-permute-start | bytes 3145736 | tf_op jit(solution)/shard_map/ppermute | solution.py:687
  65.3 20.5 %collective-permute-start.17 = (bf16[256,1024]{1,0:T(8,128)(2,1)}, bf16[256,1024]{1,0:T(8,128)(2,1)S(1)}, u32[]{:S(2)}, u32[]{:S(2)}) collective-permute-start(bf16[256,1024]{1,0:T(8,128)(2,1)} %shard_map.158.refs_1_.refs_8_), channel_id=1, source_target_pairs={{0,4},{4,12},{12,8},{8,0},{1,5},{5,13},{13,9},{9,1},{2,6},{6,14},{... | collective-permute-start | bytes 1572872 | tf_op jit(solution)/shard_map/ppermute | solution.py:630
  73.4 0.8 copy-start.5
  77.0 20.9 %collective-permute-start.14 = (bf16[256,1024]{1,0:T(8,128)(2,1)}, bf16[256,1024]{1,0:T(8,128)(2,1)}, u32[]{:S(2)}, u32[]{:S(2)}) collective-permute-start(bf16[256,1024]{1,0:T(8,128)(2,1)} %shard_map.164.refs_10_), channel_id=1, source_target_pairs={{0,4},{4,12},{12,8},{8,0},{1,5},{5,13},{13,9},{9,1},{2,6},{6,14},{... | collective-permute-start | bytes 1572872 | tf_op jit(solution)/shard_map/ppermute | solution.py:630
  79.6 24.9 %collective-permute-start.16 = (bf16[256,1024]{1,0:T(8,128)(2,1)}, bf16[256,1024]{1,0:T(8,128)(2,1)}, u32[]{:S(2)}, u32[]{:S(2)}) collective-permute-start(bf16[256,1024]{1,0:T(8,128)(2,1)} %shard_map.164.refs_10_), channel_id=1, source_target_pairs={{0,16},{16,0},{1,17},{17,1},{2,18},{18,2},{3,19},{19,3},{4,20},{20... | collective-permute-start | bytes 1572872 | tf_op jit(solution)/shard_map/ppermute | solution.py:633
  85.8 0.8 copy-start.6
  86.6 19.3 %collective-permute-start.18 = (bf16[256,1024]{1,0:T(8,128)(2,1)}, bf16[256,1024]{1,0:T(8,128)(2,1)S(1)}, u32[]{:S(2)}, u32[]{:S(2)}) collective-permute-start(bf16[256,1024]{1,0:T(8,128)(2,1)} %shard_map.166.refs_12_), channel_id=1, source_target_pairs={{0,16},{16,0},{1,17},{17,1},{2,18},{18,2},{3,19},{19,3},{4,20},{20... | collective-permute-start | bytes 1572872 | tf_op jit(solution)/shard_map/ppermute | solution.py:633
  87.1 1.0 copy-start.9
  97.3 0.6 copy-start.11
  97.9 6.6 %copy-start.20 = (bf16[2048,2]{0,1:T(2,128)(2,1)S(1)}, bf16[2048,2]{0,1:T(2,128)(2,1)}, u32[]{:S(2)}) copy-start(bf16[2048,2]{0,1:T(2,128)(2,1)} %param.26) | copy-start | bytes 24580
  97.9 8.0 %copy-start.7 = (bf16[256,1024]{1,0:T(8,128)(2,1)S(1)}, bf16[256,1024]{1,0:T(8,128)(2,1)}, u32[]{:S(2)}) copy-start(bf16[256,1024]{1,0:T(8,128)(2,1)} %shard_map.166.refs_12_) | copy-start | bytes 1572868
  97.9 16.7 %collective-permute-start.15 = (bf16[256,1024]{1,0:T(8,128)(2,1)}, bf16[256,1024]{1,0:T(8,128)(2,1)S(1)}, u32[]{:S(2)}, u32[]{:S(2)}) collective-permute-start(bf16[256,1024]{1,0:T(8,128)(2,1)} %shard_map.165.refs_14_), channel_id=1, source_target_pairs={{0,16},{16,0},{1,17},{17,1},{2,18},{18,2},{3,19},{19,3},{4,20},{20... | collective-permute-start | bytes 1572872 | tf_op jit(solution)/shard_map/ppermute | solution.py:633
  99.5 23.9 %all-to-all-start.1 = ((bf16[4,12,32,128]{3,2,1,0:T(8,128)(2,1)}), bf16[4,12,32,128]{3,2,1,0:T(8,128)(2,1)S(1)}, u32[]{:S(2)}, u32[]{:S(2)}) async-start(bf16[4,12,32,128]{3,2,1,0:T(8,128)(2,1)} %shard_map.162), calls=%async_computation.1 | async-start | bytes 786432 | tf_op jit(solution)/shard_map/all_to_all | solution.py:266
  105.9 8.7 %copy-start.16 = (f32[2048]{0:T(1024)S(1)}, f32[2048]{0:T(1024)}, u32[]{:S(2)}) copy-start(f32[2048]{0:T(1024)} %param.25) | copy-start | bytes 24580
  105.9 8.7 %copy-start.17 = (f32[2]{0:T(128)S(1)}, f32[2]{0:T(128)}, u32[]{:S(2)}) copy-start(f32[2]{0:T(128)} %refs_12_.1) | copy-start | bytes 28
  114.6 8.8 %copy-start.12 = (f32[8,128]{1,0:T(8,128)S(1)}, f32[8,128]{1,0:T(8,128)}, u32[]{:S(2)}) copy-start(f32[8,128]{1,0:T(8,128)} %copy-done.11) | copy-start | bytes 12292
  118.2 1.9 %collective-permute-start.19 = (f32[1,512]{1,0:T(1,128)S(1)}, f32[1,512]{1,0:T(1,128)S(1)}, u32[]{:S(2)}, u32[]{:S(2)}) collective-permute-start(f32[1,512]{1,0:T(1,128)S(1)} %get-tuple-element.28), channel_id=1, source_target_pairs={{0,1},{1,0},{2,3},{3,2},{4,5},{5,4},{6,7},{7,6},{8,9},{9,8},{10,11... | collective-permute-start | bytes 6152 | tf_op jit(solution)/shard_map/ppermute | solution.py:705
  118.3 3.7 %collective-permute-start.20 = (f32[1,512]{1,0:T(1,128)S(1)}, f32[1,512]{1,0:T(1,128)S(1)}, u32[]{:S(2)}, u32[]{:S(2)}) collective-permute-start(f32[1,512]{1,0:T(1,128)S(1)} %get-tuple-element.29), channel_id=1, source_target_pairs={{0,2},{2,0},{1,3},{3,1},{4,6},{6,4},{5,7},{7,5},{8,10},{10,8},{9,1... | collective-permute-start | bytes 6152 | tf_op jit(solution)/shard_map/ppermute | solution.py:707
  119.8 3.0 %collective-permute-start.21 = (f32[1,512]{1,0:T(1,128)S(1)}, f32[1,512]{1,0:T(1,128)S(1)}, u32[]{:S(2)}, u32[]{:S(2)}) collective-permute-start(f32[1,512]{1,0:T(1,128)S(1)} %get-tuple-element.28), channel_id=1, source_target_pairs={{0,3},{1,2},{2,1},{3,0},{4,7},{5,6},{6,5},{7,4},{8,11},{9,10},{10,... | collective-permute-start | bytes 6152 | tf_op jit(solution)/shard_map/ppermute | solution.py:708

commit v5 on v4

--- a/solution.py
+++ b/solution.py
@@ -224,11 +224,9 @@
     slots = out.shape[0]
     capacity = parts.shape[1]
 
-    def take(j, carry):
-        rows[j] = parts[pick[j] // capacity, lax.rem(pick[j], capacity)].astype(jnp.float32)
-        return carry
-
-    lax.fori_loop(0, slots, take, 0)
+    flat = parts.reshape(parts.shape[0] * capacity, *parts.shape[2:])
+    for j in range(slots):
+        rows[j] = flat[pick[j]].astype(jnp.float32)
     for h in range(rows.shape[1]):
         out[:, h * HD : (h + 1) * HD] = rows[:, h, :].astype(jnp.bfloat16)
 
@@ -448,31 +446,22 @@
     )(source, *waited)
 
 
-def gemm_kernel(me, *refs, parts, sources, runs, layout, has_acc, final, tile, via_hbm):
+def gemm_kernel(me, *refs, parts, sources, runs, layout, has_acc, tile, via_hbm, later):
     refs = list(refs)
     halves = [refs[:parts], refs[parts : 2 * parts]]
     del refs[: 2 * parts]
     weights = refs[:sources]
     del refs[:sources]
     acc_in = refs.pop(0) if has_acc else None
-    bias = class_weight = None
-    if final:
-        bias, class_weight, class_bias = refs[:3]
-        del refs[:3]
-        outs = [refs.pop(0), refs.pop(0)]
-        biased = refs.pop(0)
-    else:
-        out, token = refs.pop(0), refs.pop(0)
-        token[...] = jnp.zeros_like(token)
-    x_v, w_v, sems, acc_v, acc_sem = refs if via_hbm else refs + [None, None]
+    out, token = refs.pop(0), refs.pop(0)
+    token[...] = jnp.zeros_like(token)
+    ahead = refs.pop(0) if later else None
+    x_v, w_v, sems, acc_v, acc_sem, later_sem = refs
     rows = halves[0][0].shape[0]
     width = w_v.shape[1]
     depths = [depth for _, _, _, depth in runs]
     starts = [sum(depths[:i]) for i in range(len(depths))]
     columns = pl.ds(pl.multiple_of(me[2] * width, width), width)
-
-    if final:
-        classes = class_weight[1:2, columns] - class_weight[0:1, columns]
 
     def weight_copy(i):
         _, which, row, depth = runs[i]
@@ -495,11 +484,22 @@
         for r in range(2):
             for p in range(parts):
                 pl.when(part == p)(row_copy(i, r, p, offset).start)
-    held = out if not final else None
-    if via_hbm:
-        held = acc_v
-        if has_acc:
-            pltpu.make_async_copy(acc_in, acc_v, acc_sem).start()
+    held = acc_v if via_hbm else out
+    if has_acc:
+        pltpu.make_async_copy(acc_in, acc_v, acc_sem).start()
+    first_lane = 0
+    for run, depth in later:
+        part, offset = layout.place(me, run)
+        offset = pl.multiple_of(offset, HD)
+        for r in range(2):
+            for p in range(parts):
+                copy = pltpu.make_async_copy(
+                    halves[r][p].at[:, pl.ds(offset, depth)],
+                    ahead.at[pl.ds(r * rows, rows), pl.ds(first_lane, depth)],
+                    later_sem,
+                )
+                pl.when(part == p)(copy.start)
+        first_lane += depth
     groups = []
     i = 0
     while i < len(runs):
@@ -514,55 +514,75 @@
             weight_copy(i).wait()
             for r in range(2):
                 row_copy(i, r, 0, 0).wait()
-        if g == len(groups) - 1 and via_hbm and has_acc:
+        if g == len(groups) - 1 and has_acc:
             pltpu.make_async_copy(acc_in, acc_v, acc_sem).wait()
         k0 = starts[first]
         k1 = starts[last - 1] + depths[last - 1]
 
-        def body(m, carry, target=None, base=0):
-            at = pl.ds(pl.multiple_of(base + m * tile, tile), tile)
+        def body(m, carry):
+            at = pl.ds(pl.multiple_of(m * tile, tile), tile)
             product = jnp.dot(x_v[at, k0:k1], w_v[k0:k1, :], preferred_element_type=jnp.float32)
-            if via_hbm and has_acc:
-                total = out[at, :] + product if g > 0 else product
-                if g == len(groups) - 1:
-                    total = total + acc_v[at, :]
-            elif g > 0:
-                total = held[at, :] + product
-            elif has_acc:
-                total = acc_in[at, :] + product
-            else:
-                total = product
-            if target is not None:
-                hidden = jnp.maximum(total + bias[:, columns], 0.0).astype(jnp.bfloat16)
-                weighed = hidden.astype(jnp.float32) * classes
-                folded = weighed[:, :HD]
-                for j in range(1, width // HD):
-                    folded = folded + weighed[:, j * HD : (j + 1) * HD]
-                for j in range(tile // HD):
-                    turned = folded[j * HD : (j + 1) * HD, :].T
-                    lanes = pl.ds(pl.multiple_of(m * tile + j * HD, HD), HD)
-                    target[:, lanes] = jnp.sum(turned, axis=0, keepdims=True)
-            elif via_hbm and has_acc:
-                out[at, :] = total
-            else:
-                held[at, :] = total
-                if via_hbm and g == len(groups) - 1:
-                    pltpu.make_async_copy(held.at[at, :], out.at[at, :], acc_sem).start()
+            total = held[at, :] + product if g > 0 else product
+            if has_acc and g == len(groups) - 1:
+                total = total + acc_v[at, :]
+            held[at, :] = total
+            if via_hbm and g == len(groups) - 1:
+                pltpu.make_async_copy(held.at[at, :], out.at[at, :], acc_sem).start()
             return carry
 
-        if final:
-            for r in range(2):
-                lax.fori_loop(
-                    0, rows // tile, functools.partial(body, target=outs[r], base=r * rows), 0
+        lax.fori_loop(0, 2 * rows // tile, body, 0)
+    if via_hbm:
+        pltpu.make_async_copy(held, out, acc_sem).wait()
+    if later:
+        pltpu.make_async_copy(ahead, ahead, later_sem).wait()
+
+
+def last_kernel(me, x, acc, *refs, tile):
+    *weights, bias, class_weight, class_bias, kept, given, biased = refs
+    rows, width = kept.shape[1], acc.shape[1]
+    columns = pl.ds(pl.multiple_of(me[2] * width, width), width)
+    classes = class_weight[1:2, columns] - class_weight[0:1, columns]
+    for r, target in enumerate((kept, given)):
+
+        def body(m, carry):
+            at = pl.ds(pl.multiple_of(r * rows + m * tile, tile), tile)
+            total = acc[at, :]
+            first = 0
+            for weight in weights:
+                depth = weight.shape[0]
+                total = total + jnp.dot(
+                    x[at, first : first + depth], weight[...], preferred_element_type=jnp.float32
                 )
-            biased[...] = outs[0][...] + (class_bias[1] - class_bias[0])
-        else:
-            lax.fori_loop(0, 2 * rows // tile, body, 0)
-    if via_hbm and not has_acc:
-        pltpu.make_async_copy(held, out, acc_sem).wait()
-
-
-def gemm(me, layout, halves, chunks, acc=None, tail=None, via_hbm=False):
+                first += depth
+            hidden = jnp.maximum(total + bias[:, columns], 0.0).astype(jnp.bfloat16)
+            weighed = hidden.astype(jnp.float32) * classes
+            folded = weighed[:, :HD]
+            for j in range(1, width // HD):
+                folded = folded + weighed[:, j * HD : (j + 1) * HD]
+            for j in range(tile // HD):
+                turned = folded[j * HD : (j + 1) * HD, :].T
+                lanes = pl.ds(pl.multiple_of(m * tile + j * HD, HD), HD)
+                target[:, lanes] = jnp.sum(turned, axis=0, keepdims=True)
+            return carry
+
+        lax.fori_loop(0, rows // tile, body, 0)
+    biased[...] = kept[...] + (class_bias[1] - class_bias[0])
+
+
+def last_phase(me, x, acc, weights, bias, class_weight, class_bias):
+    rows = x.shape[0] // 2
+    near = [pltpu.with_memory_space_constraint(a, pltpu.VMEM) for a in (x, acc)]
+    return pl.pallas_call(
+        functools.partial(last_kernel, tile=256),
+        out_shape=[jax.ShapeDtypeStruct((1, rows), jnp.float32)] * 3,
+        in_specs=[SMEM] + [VMEM] * (4 + len(weights)) + [SMEM],
+        out_specs=[VMEM] * 3,
+        cost_estimate=BRIEF,
+        compiler_params=pltpu.CompilerParams(vmem_limit_bytes=VMEM_LIMIT),
+    )(me, *near, *weights, bias, class_weight, class_bias)
+
+
+def gemm(me, layout, halves, chunks, acc=None, later=()):
     weights = [w for w, _ in chunks]
     runs = [(run, i, row, d) for i, (_, found) in enumerate(chunks) for run, row, d in found]
     parts = len(halves[0])
@@ -570,22 +590,17 @@
     depth = sum(d for _, _, _, d in runs)
     width = min(w.shape[1] for w in weights)
     args = [me, *in_hbm([*halves[0], *halves[1]]), *weights]
-    specs = [SMEM] + [ANY] * (2 * parts + len(weights))
     if acc is not None:
-        space = pltpu.HBM if via_hbm else pltpu.VMEM
-        args.append(pltpu.with_memory_space_constraint(acc, space))
-        specs.append(ANY if via_hbm else VMEM)
-    if tail is not None:
-        args += list(tail)
-        specs += [VMEM] * 2 + [SMEM]
-        out_shape = [jax.ShapeDtypeStruct((1, rows), jnp.float32)] * 3
-        out_specs = [VMEM] * 3
-    else:
-        out_shape = [
-            (pltpu.HBM if via_hbm and acc is None else pltpu.VMEM)((2 * rows, width), jnp.float32),
-            jax.ShapeDtypeStruct((8, HD), jnp.float32),
-        ]
-        out_specs = [ANY if via_hbm and acc is None else VMEM, VMEM]
+        args += in_hbm([acc])
+    space = pltpu.HBM if acc is None else pltpu.VMEM
+    out_shape = [
+        space((2 * rows, width), jnp.float32),
+        jax.ShapeDtypeStruct((8, HD), jnp.float32),
+    ]
+    out_specs = [ANY if acc is None else VMEM, VMEM]
+    if later:
+        out_shape.append(pltpu.VMEM((2 * rows, sum(d for _, d in later)), jnp.bfloat16))
+        out_specs.append(VMEM)
     return pl.pallas_call(
         functools.partial(
             gemm_kernel,
@@ -594,19 +609,21 @@
             runs=tuple(runs),
             layout=layout,
             has_acc=acc is not None,
-            final=tail is not None,
             tile=256,
-            via_hbm=via_hbm,
+            via_hbm=acc is None,
+            later=tuple(later),
         ),
         out_shape=out_shape,
-        in_specs=specs,
+        in_specs=[SMEM] + [ANY] * (len(args) - 1),
         out_specs=out_specs,
         scratch_shapes=[
             pltpu.VMEM((2 * rows, depth), jnp.bfloat16),
             pltpu.VMEM((depth, width), jnp.bfloat16),
             pltpu.SemaphoreType.DMA((len(runs), 3)),
-        ]
-        + ([pltpu.VMEM((2 * rows, width), jnp.float32), pltpu.SemaphoreType.DMA] if via_hbm else []),
+            pltpu.VMEM((2 * rows, width), jnp.float32),
+            pltpu.SemaphoreType.DMA,
+            pltpu.SemaphoreType.DMA,
+        ],
         cost_estimate=BRIEF,
         compiler_params=pltpu.CompilerParams(vmem_limit_bytes=VMEM_LIMIT),
     )(*args)
@@ -685,7 +702,7 @@
         (part,) = after([part], [travelled[0]])
         mine.append(part)
         theirs.append(lax.ppermute(part, "section", swap))
-    acc, early = gemm(me, layout, (mine, theirs), chunks, via_hbm=True)
+    acc, early = gemm(me, layout, (mine, theirs), chunks)
     (results,) = after([results], [early])
     returned = attention.send(results)
     ends = []
@@ -700,8 +717,10 @@
         )
     attended = attention.finish(returned, early)
     middle = second + sum(ends[:-1], []) + ends[-1][:1]
-    acc, _ = gemm(me, layout, (mine, theirs), middle, acc, via_hbm=True)
-    kept, given, total = gemm(me, layout, (mine, theirs), ends[-1][1:], acc, tail)
+    final = ends[-1][1:]
+    later = [(run, d) for _, found in final for run, _, d in found]
+    acc, _, ahead = gemm(me, layout, (mine, theirs), middle, acc, later)
+    kept, given, total = last_phase(me, ahead, acc, [t for t, _ in final], *tail)
     total = total + lax.ppermute(given, "section", swap)
     for k in range(1, x_count):
         total = total + lax.ppermute(kept, "mp", shift_pairs(x_count, k))

time: 126 us -> 123 us (0.976)
  waiting for transfers between devices: 42.6 us -> 41.1 us
    pallas_call x3 -> x2, Pallas kernels: 20.8 us -> 17.9 us  [gemm(): pl.pallas_call(functools.partial(gemm_kernel, parts=parts, sources=len(we...]
    pallas_call x0 -> x1, Pallas kernels: none -> 2.43 us  [last_phase(): pl.pallas_call(functools.partial(last_kernel, tile=256), out_shape=[jax.S...]
  transfers between devices with their start and end apart: 24 -> 24, of which waited for: 12 -> 11; matrix products, arithmetic and copies ran while one was open for 1% -> 1% of each run, Pallas kernels for 30% -> 30%
where the time goes in v5:
time: 123 us
  waiting for transfers between devices  41.1 us (33%)
  Pallas kernels  39.1 us (32%)
  starting transfers between devices  36.3 us (30%)
  local copies, waits for them, and re-layouts  4.92 us (4%)
    ppermute x5, waiting for transfers between devices, forward(): return lax.ppermute(t, 'batch', ring)  18 us
    pallas_call x2, Pallas kernels, gemm(): pl.pallas_call(functools.partial(gemm_kernel, parts=parts, sources=len(we...  17.9 us
    ppermute x2, waiting for transfers between devices, both(): lax.ppermute(part, 'mp', shift_pairs(x_count, k))  13.9 us
    ppermute x5, starting transfers between devices, forward(): return lax.ppermute(t, 'batch', ring)  11.8 us
    all_to_all x2, starting transfers between devices, send(): lax.all_to_all(blobs, 'batch', split_axis=0, concat_axis=0, tiled=True)  9.68 us
    ppermute x5, starting transfers between devices, over_group(): lax.ppermute(t, 'group', shift_pairs(y_count, k))  6.76 us
    pallas_call x1, Pallas kernels, serve(): pl.pallas_call(functools.partial(serve_kernel, kv_local=kv_local, unroll=...  5.43 us
    unnamed x45, local copies, waits for them, and re-layouts  4.92 us
  transfers between devices with their start and end apart: 24, of which 11 were waited for; matrix products, arithmetic and copies ran while one was open for 1% of the time, Pallas kernels for 30%

profile of v5, /device:TPU:0, one launch (start us, length us, event | category | flops | bytes accessed | tf_op | source)
XLA Modules:
  0.0 123.1 jit_solution(7115729771479614691)
XLA Ops:
  0.6 0.1 pad_add_fusion.me
  0.7 1.6 %copy-done = bf16[512,2048]{1,0:T(8,128)(2,1)S(1)} copy-done((bf16[512,2048]{1,0:T(8,128)(2,1)S(1)}, bf16[512,2048]{1,0:T(8,128)(2,1)}, u32[]{:S(2)}) %copy-start) | copy-done | bytes 2097176
  2.3 0.6 shard_map.149
  2.9 0.5 collective-permute-start
  3.4 0.6 shard_map.152.waited.refs_0_
  4.1 0.0 copy-start.1
  4.1 0.7 shard_map.153.refs_2_.refs_0_
  4.8 0.0 copy-start.15
  4.8 0.2 collective-permute-done.waited.refs_1_.refs_9_
  5.0 0.1 shard_map.154.refs_3_
  5.1 3.0 %collective-permute-start.3 = (bf16[512,1024]{1,0:T(8,128)(2,1)S(1)}, bf16[512,1024]{1,0:T(8,128)(2,1)}, u32[]{:S(2)}, u32[]{:S(2)}) collective-permute-start(bf16[512,1024]{1,0:T(8,128)(2,1)S(1)} %shard_map.154.refs_3_), channel_id=1, source_target_pairs={{0,4},{4,12},{12,8},{8,0},{1,5},{5,13},{13,9},{9,1},{2,6},{6,14},{... | collective-permute-start | bytes 3145736 | tf_op jit(solution)/shard_map/ppermute | solution.py:647
  8.0 1.5 %collective-permute-start.1 = (f32[4,128]{1,0:T(4,128)S(1)}, f32[4,128]{1,0:T(4,128)S(1)}, u32[]{:S(2)}, u32[]{:S(2)}) collective-permute-start(f32[4,128]{1,0:T(4,128)S(1)} %shard_map.153.refs_2_.refs_0_), channel_id=1, source_target_pairs={{0,2},{2,0},{1,3},{3,1},{4,6},{6,4},{5,7},{7,5},{8,10},{10,8},{9,1... | collective-permute-start | bytes 6152 | tf_op jit(solution)/shard_map/ppermute | solution.py:659
  9.5 0.6 shard_map.156
  10.2 1.5 %collective-permute-done.1.refs_1_ = f32[4,128]{1,0:T(4,128)S(1)} collective-permute-done((f32[4,128]{1,0:T(4,128)S(1)}, f32[4,128]{1,0:T(4,128)S(1)}, u32[]{:S(2)}, u32[]{:S(2)}) %collective-permute-start.1) | collective-permute-done | bytes 2080 | tf_op jit(solution)/shard_map/ppermute | solution.py:659
  11.6 2.5 %shard_map.155 = (bf16[512,1024]{1,0:T(8,128)(2,1)}, bf16[512,1024]{1,0:T(8,128)(2,1)}) custom-call(s32[4]{0:T(128)S(1)} %pad_add_fusion.me, bf16[512,2048]{1,0:T(8,128)(2,1)S(1)} %copy-done.4, f32[4,128]{1,0:T(4,128)S(1)} %shard_map.153.refs_2_.refs_0_, f32[4,128]{1,0:T(4,128)S(1)} %collective-permute-done.1.refs_1_, f32[1,4096]{1,0:T(1,128)S(1)} %bitcast.18, ...), custom_call_target="tpu_custom_call" | custom-call | flops 1 | bytes 1 | tf_op jit(solution)/shard_map/pallas_call | solution.py:346
  14.2 0.0 copy-start.19
  14.2 0.1 collective-permute-start.5
  14.3 0.5 collective-permute-start.6
  14.8 0.1 collective-permute-start.4
  14.8 1.5 %collective-permute-start.2 = (bf16[512,1024]{1,0:T(8,128)(2,1)}, bf16[512,1024]{1,0:T(8,128)(2,1)}, u32[]{:S(2)}, u32[]{:S(2)}) collective-permute-start(bf16[512,1024]{1,0:T(8,128)(2,1)} %get-tuple-element.21.refs_0_), channel_id=1, source_target_pairs={{0,2},{2,0},{1,3},{3,1},{4,6},{6,4},{5,7},{7,5},{8,10},{10,8},{9,1... | collective-permute-start | bytes 3145736 | tf_op jit(solution)/shard_map/ppermute | solution.py:663
  16.3 2.1 %collective-permute-done.4.refs_0_.refs_10_ = bf16[256,1024]{1,0:T(8,128)(2,1)S(1)} collective-permute-done((bf16[256,1024]{1,0:T(8,128)(2,1)S(1)}, bf16[256,1024]{1,0:T(8,128)(2,1)S(1)}, u32[]{:S(2)}, u32[]{:S(2)}) %collective-permute-start.4) | collective-permute-done | bytes 524320 | tf_op jit(solution)/shard_map/ppermute | solution.py:654
  18.4 1.5 %collective-permute-start.9 = (bf16[512,1024]{1,0:T(8,128)(2,1)}, bf16[512,1024]{1,0:T(8,128)(2,1)}, u32[]{:S(2)}, u32[]{:S(2)}) collective-permute-start(bf16[512,1024]{1,0:T(8,128)(2,1)} %get-tuple-element.22.refs_1_), channel_id=1, source_target_pairs={{0,2},{2,0},{1,3},{3,1},{4,6},{6,4},{5,7},{7,5},{8,10},{10,8},{9,1... | collective-permute-start | bytes 3145736 | tf_op jit(solution)/shard_map/ppermute | solution.py:663
  19.9 12.7 %collective-permute-done.3.source.refs_11_ = bf16[512,1024]{1,0:T(8,128)(2,1)} collective-permute-done((bf16[512,1024]{1,0:T(8,128)(2,1)S(1)}, bf16[512,1024]{1,0:T(8,128)(2,1)}, u32[]{:S(2)}, u32[]{:S(2)}) %collective-permute-start.3) | collective-permute-done | bytes 1048608 | tf_op jit(solution)/shard_map/ppermute | solution.py:647
  32.6 1.6 %collective-permute-start.8 = (bf16[512,1024]{1,0:T(8,128)(2,1)}, bf16[512,1024]{1,0:T(8,128)(2,1)}, u32[]{:S(2)}, u32[]{:S(2)}) collective-permute-start(bf16[512,1024]{1,0:T(8,128)(2,1)} %collective-permute-done.3.source.refs_11_), channel_id=1, source_target_pairs={{0,16},{16,0},{1,17},{17,1},{2,18},{18,2},{3,19},{19,3},{4,20},{20... | collective-permute-start | bytes 3145736 | tf_op jit(solution)/shard_map/ppermute | solution.py:650
  34.2 0.0 collective-permute-done.5.refs_1_.refs_4_
  34.2 2.8 %shard_map.157 = (bf16[256,1024]{1,0:T(8,128)(2,1)S(1)}, bf16[256,1024]{1,0:T(8,128)(2,1)}) custom-call(bf16[512,1024]{1,0:T(8,128)(2,1)} %collective-permute-done.3.source.refs_11_, bf16[256,1024]{1,0:T(8,128)(2,1)S(1)} %collective-permute-done.4.refs_0_.refs_10_, bf16[512,1024]{1,0:T(8,128)(2,1)S(1)} %collective-permute-done.5.refs_1_.refs_4_, ...), custom_call_target="tpu_custom_call" | custom-call | flops 1 | bytes 1 | tf_op jit(solution)/shard_map/pallas_call | solution.py:438
  37.0 0.7 collective-permute-start.7
  37.8 3.8 %shard_map.150 = (bf16[4,12,40,128]{3,2,1,0:T(8,128)(2,1)}, s32[48]{0:T(128)S(1)}, s32[48]{0:T(128)S(1)}, s32[24]{0:T(128)S(1)}) custom-call(s32[1]{0:T(128)} %bitcast.me, s32[96]{0:T(128)S(1)} %copy-done.18, s32[96]{0:T(128)S(1)} %copy-done.19, bf16[24,4096]{1,0:T(8,128)(2,1)S(1)} %bitcast.15, bf16[24,512]{1,0:T(8,128)(2,1)S(1)} %bitcast.16, ...), custom_call_target="tpu_custom_call" | custom-call | flops 1 | bytes 1 | tf_op jit(solution)/shard_map/pallas_call | solution.py:110
  41.6 4.8 %all-to-all-start = ((bf16[4,12,40,128]{3,2,1,0:T(8,128)(2,1)}), bf16[4,12,40,128]{3,2,1,0:T(8,128)(2,1)}, u32[]{:S(2)}, u32[]{:S(2)}) async-start(bf16[4,12,40,128]{3,2,1,0:T(8,128)(2,1)} %get-tuple-element.20.refs_1_), calls=%async_computation | async-start | bytes 983040 | tf_op jit(solution)/shard_map/all_to_all | solution.py:264
  46.4 2.9 %collective-permute-start.13 = (bf16[256,1024]{1,0:T(8,128)(2,1)}, bf16[256,1024]{1,0:T(8,128)(2,1)}, u32[]{:S(2)}, u32[]{:S(2)}) collective-permute-start(bf16[256,1024]{1,0:T(8,128)(2,1)} %get-tuple-element.25), channel_id=1, source_target_pairs={{0,4},{4,12},{12,8},{8,0},{1,5},{5,13},{13,9},{9,1},{2,6},{6,14},{... | collective-permute-start | bytes 1572872 | tf_op jit(solution)/shard_map/ppermute | solution.py:647
  49.3 0.0 collective-permute-done.2.refs_3_.refs_0_
  49.3 13.9 %collective-permute-done.9.refs_4_.refs_0_ = bf16[512,1024]{1,0:T(8,128)(2,1)} collective-permute-done((bf16[512,1024]{1,0:T(8,128)(2,1)}, bf16[512,1024]{1,0:T(8,128)(2,1)}, u32[]{:S(2)}, u32[]{:S(2)}) %collective-permute-start.9) | collective-permute-done | bytes 1048608 | tf_op jit(solution)/shard_map/ppermute | solution.py:663
  63.1 0.0 collective-permute-done.7.refs_0_
  63.1 0.0 collective-permute-done.8.refs_2_.refs_12_
  63.1 1.6 %collective-permute-start.12 = (bf16[256,1024]{1,0:T(8,128)(2,1)}, bf16[256,1024]{1,0:T(8,128)(2,1)}, u32[]{:S(2)}, u32[]{:S(2)}) collective-permute-start(bf16[256,1024]{1,0:T(8,128)(2,1)} %shard_map.158.refs_1_.refs_8_), channel_id=1, source_target_pairs={{0,16},{16,0},{1,17},{17,1},{2,18},{18,2},{3,19},{19,3},{4,20},{20... | collective-permute-start | bytes 1572872 | tf_op jit(solution)/shard_map/ppermute | solution.py:650
  64.7 0.5 collective-permute-start.11
  65.3 0.1 copy.23.page_table
  65.3 2.6 %collective-permute-start.15 = (bf16[256,1024]{1,0:T(8,128)(2,1)}, bf16[256,1024]{1,0:T(8,128)(2,1)S(1)}, u32[]{:S(2)}, u32[]{:S(2)}) collective-permute-start(bf16[256,1024]{1,0:T(8,128)(2,1)} %shard_map.158.refs_1_.refs_8_), channel_id=1, source_target_pairs={{0,4},{4,12},{12,8},{8,0},{1,5},{5,13},{13,9},{9,1},{2,6},{6,14},{... | collective-permute-start | bytes 1572872 | tf_op jit(solution)/shard_map/ppermute | solution.py:647
  67.9 5.4 %shard_map.151.refs_0_.refs_1_ = bf16[4,12,32,128]{3,2,1,0:T(8,128)(2,1)S(1)} custom-call(s32[48]{0:T(128)S(1)} %get-tuple-element.18.particle, s32[24,4]{1,0:T(8,128)S(1)} %copy.23.page_table, s32[48]{0:T(128)S(1)} %get-tuple-element.19.lengths, bf16[4,12,40,128]{3,2,1,0:T(8,128)(2,1)} %all-to-all-done.blobs, bf16[96,16,512]{2,1,0:T(8,128)(2,1)} %bitcast.20, ...), custom_call_target="tpu_custom_call" | custom-call | flops 1 | bytes 1 | tf_op jit(solution)/shard_map/pallas_call | solution.py:207
  73.4 0.7 copy-done.5
  74.1 0.6 collective-permute-done.13.refs_0_
  74.7 2.3 %collective-permute-done.12.refs_2_.refs_9_ = bf16[256,1024]{1,0:T(8,128)(2,1)} collective-permute-done((bf16[256,1024]{1,0:T(8,128)(2,1)}, bf16[256,1024]{1,0:T(8,128)(2,1)}, u32[]{:S(2)}, u32[]{:S(2)}) %collective-permute-start.12) | collective-permute-done | bytes 524320 | tf_op jit(solution)/shard_map/ppermute | solution.py:650
  77.0 2.6 %collective-permute-start.17 = (bf16[256,1024]{1,0:T(8,128)(2,1)}, bf16[256,1024]{1,0:T(8,128)(2,1)}, u32[]{:S(2)}, u32[]{:S(2)}) collective-permute-start(bf16[256,1024]{1,0:T(8,128)(2,1)} %shard_map.164.refs_10_), channel_id=1, source_target_pairs={{0,4},{4,12},{12,8},{8,0},{1,5},{5,13},{13,9},{9,1},{2,6},{6,14},{... | collective-permute-start | bytes 1572872 | tf_op jit(solution)/shard_map/ppermute | solution.py:647
  79.6 1.5 %collective-permute-start.14 = (bf16[256,1024]{1,0:T(8,128)(2,1)}, bf16[256,1024]{1,0:T(8,128)(2,1)}, u32[]{:S(2)}, u32[]{:S(2)}) collective-permute-start(bf16[256,1024]{1,0:T(8,128)(2,1)} %shard_map.164.refs_10_), channel_id=1, source_target_pairs={{0,16},{16,0},{1,17},{17,1},{2,18},{18,2},{3,19},{19,3},{4,20},{20... | collective-permute-start | bytes 1572872 | tf_op jit(solution)/shard_map/ppermute | solution.py:650
  81.1 4.7 %collective-permute-done.15.refs_0_ = bf16[256,1024]{1,0:T(8,128)(2,1)S(1)} collective-permute-done((bf16[256,1024]{1,0:T(8,128)(2,1)}, bf16[256,1024]{1,0:T(8,128)(2,1)S(1)}, u32[]{:S(2)}, u32[]{:S(2)}) %collective-permute-start.15) | collective-permute-done | bytes 524320 | tf_op jit(solution)/shard_map/ppermute | solution.py:647
  85.8 0.8 copy-done.6
  86.6 0.5 collective-permute-start.16
  87.1 1.0 copy-done.9
  88.1 9.2 %shard_map.161 = (f32[1024,1024]{1,0:T(8,128)}, f32[8,128]{1,0:T(8,128)S(1)}) custom-call(s32[4]{0:T(128)S(1)} %pad_add_fusion.me, bf16[512,1024]{1,0:T(8,128)(2,1)} %get-tuple-element.21.refs_0_, bf16[512,1024]{1,0:T(8,128)(2,1)} %get-tuple-element.22.refs_1_, bf16[512,1024]{1,0:T(8,128)(2,1)} %shard_map.159.refs_2_, bf16[512,1024]{1,0:T(8,128)(2,1)} %shard_map.160.refs_3_, ...), custom_call_target="tpu_custom_call" | custom-call | flops 1 | bytes 1 | tf_op jit(solution)/shard_map/pallas_call | solution.py:604
  97.3 0.0 copy-start.11
  97.3 0.6 copy-done.11
  97.9 1.6 %collective-permute-start.18 = (bf16[256,1024]{1,0:T(8,128)(2,1)}, bf16[256,1024]{1,0:T(8,128)(2,1)S(1)}, u32[]{:S(2)}, u32[]{:S(2)}) collective-permute-start(bf16[256,1024]{1,0:T(8,128)(2,1)} %shard_map.166.refs_14_), channel_id=1, source_target_pairs={{0,16},{16,0},{1,17},{17,1},{2,18},{18,2},{3,19},{19,3},{4,20},{20... | collective-permute-start | bytes 1572872 | tf_op jit(solution)/shard_map/ppermute | solution.py:650
  99.6 4.9 %all-to-all-start.1 = ((bf16[4,12,32,128]{3,2,1,0:T(8,128)(2,1)}), bf16[4,12,32,128]{3,2,1,0:T(8,128)(2,1)S(1)}, u32[]{:S(2)}, u32[]{:S(2)}) async-start(bf16[4,12,32,128]{3,2,1,0:T(8,128)(2,1)} %shard_map.162), calls=%async_computation.1 | async-start | bytes 786432 | tf_op jit(solution)/shard_map/all_to_all | solution.py:264
  104.5 1.4 %collective-permute-done.16.refs_13_ = bf16[256,1024]{1,0:T(8,128)(2,1)S(1)} collective-permute-done((bf16[256,1024]{1,0:T(8,128)(2,1)}, bf16[256,1024]{1,0:T(8,128)(2,1)S(1)}, u32[]{:S(2)}, u32[]{:S(2)}) %collective-permute-start.16) | collective-permute-done | bytes 524320 | tf_op jit(solution)/shard_map/ppermute | solution.py:650
  105.9 8.7 %shard_map.167 = (f32[1024,1024]{1,0:T(8,128)S(1)}, f32[8,128]{1,0:T(8,128)}, bf16[1024,256]{1,0:T(8,128)(2,1)S(1)}) custom-call(s32[4]{0:T(128)S(1)} %pad_add_fusion.me, bf16[512,1024]{1,0:T(8,128)(2,1)} %get-tuple-element.21.refs_0_, bf16[512,1024]{1,0:T(8,128)(2,1)} %get-tuple-element.22.refs_1_, bf16[512,1024]{1,0:T(8,128)(2,1)} %shard_map.159.refs_2_, ...), custom_call_target="tpu_custom_call" | custom-call | flops 1 | bytes 1 | tf_op jit(solution)/shard_map/pallas_call | solution.py:604
  114.6 0.0 copy-start.12
  114.7 2.4 %shard_map.168 = (f32[1,512]{1,0:T(1,128)S(1)}, f32[1,512]{1,0:T(1,128)S(1)}, f32[1,512]{1,0:T(1,128)S(1)}) custom-call(s32[4]{0:T(128)S(1)} %pad_add_fusion.me, bf16[1024,256]{1,0:T(8,128)(2,1)S(1)} %get-tuple-element.27.x, f32[1024,1024]{1,0:T(8,128)S(1)} %get-tuple-element.28.acc, bf16[256,1024]{1,0:T(8,128)(2,1)S(1)} %collective-permute-done.18.refs_0_, ...), custom_call_target="tpu_custom_call" | custom-call | flops 1 | bytes 1 | tf_op jit(solution)/shard_map/pallas_call | solution.py:575
  117.1 0.1 collective-permute-start.21
  117.2 1.6 %collective-permute-start.20 = (f32[1,512]{1,0:T(1,128)S(1)}, f32[1,512]{1,0:T(1,128)S(1)}, u32[]{:S(2)}, u32[]{:S(2)}) collective-permute-start(f32[1,512]{1,0:T(1,128)S(1)} %get-tuple-element.31), channel_id=1, source_target_pairs={{0,2},{2,0},{1,3},{3,1},{4,6},{6,4},{5,7},{7,5},{8,10},{10,8},{9,1... | collective-permute-start | bytes 6152 | tf_op jit(solution)/shard_map/ppermute | solution.py:726
  118.7 0.3 collective-permute-start.19
  119.0 1.1 collective-permute-done.21
  120.2 0.7 collective-permute-done.20
  120.8 0.6 add_add_fusion
  121.4 1.6 %shard_map.163 = bf16[24,4096]{1,0:T(8,128)(2,1)} custom-call(s32[24]{0:T(128)S(1)} %get-tuple-element.17.pick, bf16[4,12,32,128]{3,2,1,0:T(8,128)(2,1)S(1)} %all-to-all-done.1.parts, f32[8,128]{1,0:T(8,128)S(1)} %copy-done.12), custom_call_target="tpu_custom_call" | custom-call | flops 1 | bytes 1 | tf_op jit(solution)/shard_map/pallas_call | solution.py:237
  (52 shorter events, 0.1 us)
Async XLA Ops:
  0.7 1.6 %copy-start = (bf16[512,2048]{1,0:T(8,128)(2,1)S(1)}, bf16[512,2048]{1,0:T(8,128)(2,1)}, u32[]{:S(2)}) copy-start(bf16[512,2048]{1,0:T(8,128)(2,1)} %refs_8_.1) | copy-start | bytes 6291460
  2.3 1.8 %copy-start.4 = (bf16[512,2048]{1,0:T(8,128)(2,1)S(1)}, bf16[512,2048]{1,0:T(8,128)(2,1)}, u32[]{:S(2)}) copy-start(bf16[512,2048]{1,0:T(8,128)(2,1)} %x.3) | copy-start | bytes 6291460
  2.9 2.1 %collective-permute-start = (bf16[256,1024]{1,0:T(8,128)(2,1)S(1)}, bf16[256,1024]{1,0:T(8,128)(2,1)S(1)}, u32[]{:S(2)}, u32[]{:S(2)}) collective-permute-start(bf16[256,1024]{1,0:T(8,128)(2,1)S(1)} %shard_map.149), channel_id=1, source_target_pairs={{0,1},{1,0},{2,3},{3,2},{4,5},{5,4},{6,7},{7,6},{8,9},{9,8},{10,11... | collective-permute-start | bytes 1572872 | tf_op jit(solution)/shard_map/ppermute | solution.py:654
  4.1 5.5 %copy-start.1 = (bf16[512,2048]{1,0:T(8,128)(2,1)S(1)}, bf16[512,2048]{1,0:T(8,128)(2,1)}, u32[]{:S(2)}) copy-start(bf16[512,2048]{1,0:T(8,128)(2,1)} %refs_8_.1) | copy-start | bytes 6291460
  4.8 6.8 %copy-start.15 = (f32[4096]{0:T(1024)S(1)}, f32[4096]{0:T(1024)}, u32[]{:S(2)}) copy-start(f32[4096]{0:T(1024)} %param.23) | copy-start | bytes 49156
  5.1 27.6 %collective-permute-start.3 = (bf16[512,1024]{1,0:T(8,128)(2,1)S(1)}, bf16[512,1024]{1,0:T(8,128)(2,1)}, u32[]{:S(2)}, u32[]{:S(2)}) collective-permute-start(bf16[512,1024]{1,0:T(8,128)(2,1)S(1)} %shard_map.154.refs_3_), channel_id=1, source_target_pairs={{0,4},{4,12},{12,8},{8,0},{1,5},{5,13},{13,9},{9,1},{2,6},{6,14},{... | collective-permute-start | bytes 3145736 | tf_op jit(solution)/shard_map/ppermute | solution.py:647
  8.0 3.6 %collective-permute-start.1 = (f32[4,128]{1,0:T(4,128)S(1)}, f32[4,128]{1,0:T(4,128)S(1)}, u32[]{:S(2)}, u32[]{:S(2)}) collective-permute-start(f32[4,128]{1,0:T(4,128)S(1)} %shard_map.153.refs_2_.refs_0_), channel_id=1, source_target_pairs={{0,2},{2,0},{1,3},{3,1},{4,6},{6,4},{5,7},{7,5},{8,10},{10,8},{9,1... | collective-permute-start | bytes 6152 | tf_op jit(solution)/shard_map/ppermute | solution.py:659
  14.2 23.6 %copy-start.10 = (bf16[1,24,4096]{2,1,0:T(8,128)(2,1)S(1)}, bf16[1,24,4096]{2,1,0:T(8,128)(2,1)}, u32[]{:S(2)}) copy-start(bf16[1,24,4096]{2,1,0:T(8,128)(2,1)} %param.14) | copy-start | bytes 589828
  14.2 23.6 %copy-start.13 = (bf16[1,24,512]{2,1,0:T(8,128)(2,1)S(1)}, bf16[1,24,512]{2,1,0:T(8,128)(2,1)}, u32[]{:S(2)}) copy-start(bf16[1,24,512]{2,1,0:T(8,128)(2,1)} %param.15) | copy-start | bytes 73732
  14.2 23.6 %copy-start.14 = (bf16[1,24,512]{2,1,0:T(8,128)(2,1)S(1)}, bf16[1,24,512]{2,1,0:T(8,128)(2,1)}, u32[]{:S(2)}) copy-start(bf16[1,24,512]{2,1,0:T(8,128)(2,1)} %param.16) | copy-start | bytes 73732
  14.2 23.6 %copy-start.18 = (s32[96]{0:T(128)S(1)}, s32[96]{0:T(128)}, u32[]{:S(2)}) copy-start(s32[96]{0:T(128)} %ancestry.1) | copy-start | bytes 1156
  14.2 23.6 %copy-start.19 = (s32[96]{0:T(128)S(1)}, s32[96]{0:T(128)}, u32[]{:S(2)}) copy-start(s32[96]{0:T(128)} %lengths.1) | copy-start | bytes 1156
  14.2 20.0 %collective-permute-start.5 = (bf16[512,1024]{1,0:T(8,128)(2,1)}, bf16[512,1024]{1,0:T(8,128)(2,1)S(1)}, u32[]{:S(2)}, u32[]{:S(2)}) collective-permute-start(bf16[512,1024]{1,0:T(8,128)(2,1)} %get-tuple-element.21.refs_0_), channel_id=1, source_target_pairs={{0,1},{1,0},{2,3},{3,2},{4,5},{5,4},{6,7},{7,6},{8,9},{9,8},{10,11... | collective-permute-start | bytes 3145736 | tf_op jit(solution)/shard_map/ppermute | solution.py:667
  14.3 19.9 %collective-permute-start.6 = (bf16[512,1024]{1,0:T(8,128)(2,1)}, bf16[512,1024]{1,0:T(8,128)(2,1)S(1)}, u32[]{:S(2)}, u32[]{:S(2)}) collective-permute-start(bf16[512,1024]{1,0:T(8,128)(2,1)} %get-tuple-element.22.refs_1_), channel_id=1, source_target_pairs={{0,1},{1,0},{2,3},{3,2},{4,5},{5,4},{6,7},{7,6},{8,9},{9,8},{10,11... | collective-permute-start | bytes 3145736 | tf_op jit(solution)/shard_map/ppermute | solution.py:667
  14.8 3.6 %collective-permute-start.4 = (bf16[256,1024]{1,0:T(8,128)(2,1)S(1)}, bf16[256,1024]{1,0:T(8,128)(2,1)S(1)}, u32[]{:S(2)}, u32[]{:S(2)}) collective-permute-start(bf16[256,1024]{1,0:T(8,128)(2,1)S(1)} %shard_map.156), channel_id=1, source_target_pairs={{0,1},{1,0},{2,3},{3,2},{4,5},{5,4},{6,7},{7,6},{8,9},{9,8},{10,11... | collective-permute-start | bytes 1572872 | tf_op jit(solution)/shard_map/ppermute | solution.py:654
  14.8 34.4 %collective-permute-start.2 = (bf16[512,1024]{1,0:T(8,128)(2,1)}, bf16[512,1024]{1,0:T(8,128)(2,1)}, u32[]{:S(2)}, u32[]{:S(2)}) collective-permute-start(bf16[512,1024]{1,0:T(8,128)(2,1)} %get-tuple-element.21.refs_0_), channel_id=1, source_target_pairs={{0,2},{2,0},{1,3},{3,1},{4,6},{6,4},{5,7},{7,5},{8,10},{10,8},{9,1... | collective-permute-start | bytes 3145736 | tf_op jit(solution)/shard_map/ppermute | solution.py:663
  18.4 23.2 %copy-start.8 = (bf16[256,1024]{1,0:T(8,128)(2,1)}, bf16[256,1024]{1,0:T(8,128)(2,1)S(1)}, u32[]{:S(2)}) copy-start(bf16[256,1024]{1,0:T(8,128)(2,1)S(1)} %collective-permute-done.4.refs_0_.refs_10_) | copy-start | bytes 1572868
  18.4 44.7 %collective-permute-start.9 = (bf16[512,1024]{1,0:T(8,128)(2,1)}, bf16[512,1024]{1,0:T(8,128)(2,1)}, u32[]{:S(2)}, u32[]{:S(2)}) collective-permute-start(bf16[512,1024]{1,0:T(8,128)(2,1)} %get-tuple-element.22.refs_1_), channel_id=1, source_target_pairs={{0,2},{2,0},{1,3},{3,1},{4,6},{6,4},{5,7},{7,5},{8,10},{10,8},{9,1... | collective-permute-start | bytes 3145736 | tf_op jit(solution)/shard_map/ppermute | solution.py:663
  32.6 30.5 %collective-permute-start.8 = (bf16[512,1024]{1,0:T(8,128)(2,1)}, bf16[512,1024]{1,0:T(8,128)(2,1)}, u32[]{:S(2)}, u32[]{:S(2)}) collective-permute-start(bf16[512,1024]{1,0:T(8,128)(2,1)} %collective-permute-done.3.source.refs_11_), channel_id=1, source_target_pairs={{0,16},{16,0},{1,17},{17,1},{2,18},{18,2},{3,19},{19,3},{4,20},{20... | collective-permute-start | bytes 3145736 | tf_op jit(solution)/shard_map/ppermute | solution.py:650
  34.2 7.4 %copy-start.2 = (bf16[512,1024]{1,0:T(8,128)(2,1)}, bf16[512,1024]{1,0:T(8,128)(2,1)S(1)}, u32[]{:S(2)}) copy-start(bf16[512,1024]{1,0:T(8,128)(2,1)S(1)} %collective-permute-done.5.refs_1_.refs_4_) | copy-start | bytes 3145732
  34.2 7.4 %copy-start.3 = (bf16[512,1024]{1,0:T(8,128)(2,1)}, bf16[512,1024]{1,0:T(8,128)(2,1)S(1)}, u32[]{:S(2)}) copy-start(bf16[512,1024]{1,0:T(8,128)(2,1)S(1)} %collective-permute-done.6.refs_2_.refs_5_) | copy-start | bytes 3145732
  37.0 26.1 %collective-permute-start.7 = (bf16[256,1024]{1,0:T(8,128)(2,1)S(1)}, bf16[256,1024]{1,0:T(8,128)(2,1)}, u32[]{:S(2)}, u32[]{:S(2)}) collective-permute-start(bf16[256,1024]{1,0:T(8,128)(2,1)S(1)} %get-tuple-element.23), channel_id=1, source_target_pairs={{0,4},{4,12},{12,8},{8,0},{1,5},{5,13},{13,9},{9,1},{2,6},{6,14},{... | collective-permute-start | bytes 1572872 | tf_op jit(solution)/shard_map/ppermute | solution.py:647
  41.6 26.3 %all-to-all-start = ((bf16[4,12,40,128]{3,2,1,0:T(8,128)(2,1)}), bf16[4,12,40,128]{3,2,1,0:T(8,128)(2,1)}, u32[]{:S(2)}, u32[]{:S(2)}) async-start(bf16[4,12,40,128]{3,2,1,0:T(8,128)(2,1)} %get-tuple-element.20.refs_1_), calls=%async_computation | async-start | bytes 983040 | tf_op jit(solution)/shard_map/all_to_all | solution.py:264
  46.4 28.3 %collective-permute-start.13 = (bf16[256,1024]{1,0:T(8,128)(2,1)}, bf16[256,1024]{1,0:T(8,128)(2,1)}, u32[]{:S(2)}, u32[]{:S(2)}) collective-permute-start(bf16[256,1024]{1,0:T(8,128)(2,1)} %get-tuple-element.25), channel_id=1, source_target_pairs={{0,4},{4,12},{12,8},{8,0},{1,5},{5,13},{13,9},{9,1},{2,6},{6,14},{... | collective-permute-start | bytes 1572872 | tf_op jit(solution)/shard_map/ppermute | solution.py:647
  63.1 2.1 %copy-start.21 = (s32[24,4]{0,1:T(4,128)S(1)}, s32[24,4]{0,1:T(4,128)}, u32[]{:S(2)}) copy-start(s32[24,4]{0,1:T(4,128)} %param.19) | copy-start | bytes 1156
  63.1 13.9 %collective-permute-start.12 = (bf16[256,1024]{1,0:T(8,128)(2,1)}, bf16[256,1024]{1,0:T(8,128)(2,1)}, u32[]{:S(2)}, u32[]{:S(2)}) collective-permute-start(bf16[256,1024]{1,0:T(8,128)(2,1)} %shard_map.158.refs_1_.refs_8_), channel_id=1, source_target_pairs={{0,16},{16,0},{1,17},{17,1},{2,18},{18,2},{3,19},{19,3},{4,20},{20... | collective-permute-start | bytes 1572872 | tf_op jit(solution)/shard_map/ppermute | solution.py:650
  64.7 22.3 %collective-permute-start.10 = (bf16[512,1024]{1,0:T(8,128)(2,1)}, bf16[512,1024]{1,0:T(8,128)(2,1)}, u32[]{:S(2)}, u32[]{:S(2)}) collective-permute-start(bf16[512,1024]{1,0:T(8,128)(2,1)} %shard_map.159.refs_2_), channel_id=1, source_target_pairs={{0,1},{1,0},{2,3},{3,2},{4,5},{5,4},{6,7},{7,6},{8,9},{9,8},{10,11... | collective-permute-start | bytes 3145736 | tf_op jit(solution)/shard_map/ppermute | solution.py:704
  64.7 22.3 %collective-permute-start.11 = (bf16[512,1024]{1,0:T(8,128)(2,1)}, bf16[512,1024]{1,0:T(8,128)(2,1)}, u32[]{:S(2)}, u32[]{:S(2)}) collective-permute-start(bf16[512,1024]{1,0:T(8,128)(2,1)} %shard_map.160.refs_3_), channel_id=1, source_target_pairs={{0,1},{1,0},{2,3},{3,2},{4,5},{5,4},{6,7},{7,6},{8,9},{9,8},{10,11... | collective-permute-start | bytes 3145736 | tf_op jit(solution)/shard_map/ppermute | solution.py:704
  65.3 20.5 %collective-permute-start.15 = (bf16[256,1024]{1,0:T(8,128)(2,1)}, bf16[256,1024]{1,0:T(8,128)(2,1)S(1)}, u32[]{:S(2)}, u32[]{:S(2)}) collective-permute-start(bf16[256,1024]{1,0:T(8,128)(2,1)} %shard_map.158.refs_1_.refs_8_), channel_id=1, source_target_pairs={{0,4},{4,12},{12,8},{8,0},{1,5},{5,13},{13,9},{9,1},{2,6},{6,14},{... | collective-permute-start | bytes 1572872 | tf_op jit(solution)/shard_map/ppermute | solution.py:647
  73.4 0.8 copy-start.5
  77.0 20.9 %collective-permute-start.17 = (bf16[256,1024]{1,0:T(8,128)(2,1)}, bf16[256,1024]{1,0:T(8,128)(2,1)}, u32[]{:S(2)}, u32[]{:S(2)}) collective-permute-start(bf16[256,1024]{1,0:T(8,128)(2,1)} %shard_map.164.refs_10_), channel_id=1, source_target_pairs={{0,4},{4,12},{12,8},{8,0},{1,5},{5,13},{13,9},{9,1},{2,6},{6,14},{... | collective-permute-start | bytes 1572872 | tf_op jit(solution)/shard_map/ppermute | solution.py:647
  79.6 24.9 %collective-permute-start.14 = (bf16[256,1024]{1,0:T(8,128)(2,1)}, bf16[256,1024]{1,0:T(8,128)(2,1)}, u32[]{:S(2)}, u32[]{:S(2)}) collective-permute-start(bf16[256,1024]{1,0:T(8,128)(2,1)} %shard_map.164.refs_10_), channel_id=1, source_target_pairs={{0,16},{16,0},{1,17},{17,1},{2,18},{18,2},{3,19},{19,3},{4,20},{20... | collective-permute-start | bytes 1572872 | tf_op jit(solution)/shard_map/ppermute | solution.py:650
  85.8 0.8 copy-start.6
  86.6 19.3 %collective-permute-start.16 = (bf16[256,1024]{1,0:T(8,128)(2,1)}, bf16[256,1024]{1,0:T(8,128)(2,1)S(1)}, u32[]{:S(2)}, u32[]{:S(2)}) collective-permute-start(bf16[256,1024]{1,0:T(8,128)(2,1)} %shard_map.165.refs_12_), channel_id=1, source_target_pairs={{0,16},{16,0},{1,17},{17,1},{2,18},{18,2},{3,19},{19,3},{4,20},{20... | collective-permute-start | bytes 1572872 | tf_op jit(solution)/shard_map/ppermute | solution.py:650
  87.1 1.0 copy-start.9
  97.3 0.6 copy-start.11
  97.9 6.6 %copy-start.20 = (bf16[2048,2]{0,1:T(2,128)(2,1)S(1)}, bf16[2048,2]{0,1:T(2,128)(2,1)}, u32[]{:S(2)}) copy-start(bf16[2048,2]{0,1:T(2,128)(2,1)} %param.26) | copy-start | bytes 24580
  97.9 8.0 %copy-start.7 = (bf16[256,1024]{1,0:T(8,128)(2,1)S(1)}, bf16[256,1024]{1,0:T(8,128)(2,1)}, u32[]{:S(2)}) copy-start(bf16[256,1024]{1,0:T(8,128)(2,1)} %shard_map.165.refs_12_) | copy-start | bytes 1572868
  97.9 16.7 %collective-permute-start.18 = (bf16[256,1024]{1,0:T(8,128)(2,1)}, bf16[256,1024]{1,0:T(8,128)(2,1)S(1)}, u32[]{:S(2)}, u32[]{:S(2)}) collective-permute-start(bf16[256,1024]{1,0:T(8,128)(2,1)} %shard_map.166.refs_14_), channel_id=1, source_target_pairs={{0,16},{16,0},{1,17},{17,1},{2,18},{18,2},{3,19},{19,3},{4,20},{20... | collective-permute-start | bytes 1572872 | tf_op jit(solution)/shard_map/ppermute | solution.py:650
  99.6 21.9 %all-to-all-start.1 = ((bf16[4,12,32,128]{3,2,1,0:T(8,128)(2,1)}), bf16[4,12,32,128]{3,2,1,0:T(8,128)(2,1)S(1)}, u32[]{:S(2)}, u32[]{:S(2)}) async-start(bf16[4,12,32,128]{3,2,1,0:T(8,128)(2,1)} %shard_map.162), calls=%async_computation.1 | async-start | bytes 786432 | tf_op jit(solution)/shard_map/all_to_all | solution.py:264
  105.9 8.7 %copy-start.16 = (f32[2048]{0:T(1024)S(1)}, f32[2048]{0:T(1024)}, u32[]{:S(2)}) copy-start(f32[2048]{0:T(1024)} %param.25) | copy-start | bytes 24580
  105.9 8.7 %copy-start.17 = (f32[2]{0:T(128)S(1)}, f32[2]{0:T(128)}, u32[]{:S(2)}) copy-start(f32[2]{0:T(128)} %refs_3_.1) | copy-start | bytes 28
  114.6 6.8 %copy-start.12 = (f32[8,128]{1,0:T(8,128)S(1)}, f32[8,128]{1,0:T(8,128)}, u32[]{:S(2)}) copy-start(f32[8,128]{1,0:T(8,128)} %copy-done.11) | copy-start | bytes 12292
  117.1 3.1 %collective-permute-start.21 = (f32[1,512]{1,0:T(1,128)S(1)}, f32[1,512]{1,0:T(1,128)S(1)}, u32[]{:S(2)}, u32[]{:S(2)}) collective-permute-start(f32[1,512]{1,0:T(1,128)S(1)} %get-tuple-element.30), channel_id=1, source_target_pairs={{0,3},{1,2},{2,1},{3,0},{4,7},{5,6},{6,5},{7,4},{8,11},{9,10},{10,... | collective-permute-start | bytes 6152 | tf_op jit(solution)/shard_map/ppermute | solution.py:727
  117.2 3.7 %collective-permute-start.20 = (f32[1,512]{1,0:T(1,128)S(1)}, f32[1,512]{1,0:T(1,128)S(1)}, u32[]{:S(2)}, u32[]{:S(2)}) collective-permute-start(f32[1,512]{1,0:T(1,128)S(1)} %get-tuple-element.31), channel_id=1, source_target_pairs={{0,2},{2,0},{1,3},{3,1},{4,6},{6,4},{5,7},{7,5},{8,10},{10,8},{9,1... | collective-permute-start | bytes 6152 | tf_op jit(solution)/shard_map/ppermute | solution.py:726
  118.7 2.1 %collective-permute-start.19 = (f32[1,512]{1,0:T(1,128)S(1)}, f32[1,512]{1,0:T(1,128)S(1)}, u32[]{:S(2)}, u32[]{:S(2)}) collective-permute-start(f32[1,512]{1,0:T(1,128)S(1)} %get-tuple-element.30), channel_id=1, source_target_pairs={{0,1},{1,0},{2,3},{3,2},{4,5},{5,4},{6,7},{7,6},{8,9},{9,8},{10,11... | collective-permute-start | bytes 6152 | tf_op jit(solution)/shard_map/ppermute | solution.py:724

commit v6 on v5

--- a/solution.py
+++ b/solution.py
@@ -573,7 +573,7 @@
     rows = x.shape[0] // 2
     near = [pltpu.with_memory_space_constraint(a, pltpu.VMEM) for a in (x, acc)]
     return pl.pallas_call(
-        functools.partial(last_kernel, tile=256),
+        functools.partial(last_kernel, tile=512),
         out_shape=[jax.ShapeDtypeStruct((1, rows), jnp.float32)] * 3,
         in_specs=[SMEM] + [VMEM] * (4 + len(weights)) + [SMEM],
         out_specs=[VMEM] * 3,
@@ -609,7 +609,7 @@
             runs=tuple(runs),
             layout=layout,
             has_acc=acc is not None,
-            tile=256,
+            tile=512,
             via_hbm=acc is None,
             later=tuple(later),
         ),
@@ -778,6 +778,7 @@
         and lax.axis_size("section") == 2
         and head_weight.shape[0] % (128 * lax.axis_size("group")) == 0
         and step_rows.shape[1] % (2 * head_weight.shape[0]) == 0
+        and step_rows.shape[0] % 512 == 0
         and head_weight.shape[1] % 256 == 0
         and step_rows.shape[1] % head_weight.shape[0] == 0
     )

time: 123 us -> 123 us (level)
  Pallas kernels: 39.1 us -> 37.4 us
  transfers between devices with their start and end apart: 24 -> 24, of which waited for: 11 -> 12; matrix products, arithmetic and copies ran while one was open for 1% -> 1% of each run, Pallas kernels for 30% -> 29%
where the time goes in v6:
time: 123 us; the launch traced here: 122 us
  waiting for transfers between devices  42.1 us (34%)
  Pallas kernels  37.4 us (30%)
  starting transfers between devices  36.3 us (30%)
  local copies, waits for them, and re-layouts  4.92 us (4%)
    ppermute x5, waiting for transfers between devices, forward(): return lax.ppermute(t, 'batch', ring)  18 us
    pallas_call x2, Pallas kernels, gemm(): pl.pallas_call(functools.partial(gemm_kernel, parts=parts, sources=len(we...  16.9 us
    ppermute x2, waiting for transfers between devices, both(): lax.ppermute(part, 'mp', shift_pairs(x_count, k))  13.9 us
    ppermute x5, starting transfers between devices, forward(): return lax.ppermute(t, 'batch', ring)  11.8 us
    all_to_all x2, starting transfers between devices, send(): lax.all_to_all(blobs, 'batch', split_axis=0, concat_axis=0, tiled=True)  9.68 us
    ppermute x5, starting transfers between devices, over_group(): lax.ppermute(t, 'group', shift_pairs(y_count, k))  6.76 us
    pallas_call x1, Pallas kernels, serve(): pl.pallas_call(functools.partial(serve_kernel, kv_local=kv_local, unroll=...  5.43 us
    unnamed x45, local copies, waits for them, and re-layouts  4.92 us
  transfers between devices with their start and end apart: 24, of which 12 were waited for; matrix products, arithmetic and copies ran while one was open for 1% of the time, Pallas kernels for 29%

profile of v6, /device:TPU:0, one launch (start us, length us, event | category | flops | bytes accessed | tf_op | source)
XLA Modules:
  0.0 122.3 jit_solution(4695130434936393396)
XLA Ops:
  0.6 0.1 pad_add_fusion.me
  0.7 1.6 %copy-done = bf16[512,2048]{1,0:T(8,128)(2,1)S(1)} copy-done((bf16[512,2048]{1,0:T(8,128)(2,1)S(1)}, bf16[512,2048]{1,0:T(8,128)(2,1)}, u32[]{:S(2)}) %copy-start) | copy-done | bytes 2097176
  2.3 0.6 shard_map.149
  2.9 0.5 collective-permute-start
  3.4 0.6 shard_map.152.waited.refs_0_
  4.1 0.0 copy-start.1
  4.1 0.7 shard_map.153.refs_2_.refs_0_
  4.8 0.0 copy-start.15
  4.8 0.2 collective-permute-done.waited.refs_1_.refs_9_
  5.0 0.1 shard_map.154.refs_3_
  5.1 3.0 %collective-permute-start.3 = (bf16[512,1024]{1,0:T(8,128)(2,1)S(1)}, bf16[512,1024]{1,0:T(8,128)(2,1)}, u32[]{:S(2)}, u32[]{:S(2)}) collective-permute-start(bf16[512,1024]{1,0:T(8,128)(2,1)S(1)} %shard_map.154.refs_3_), channel_id=1, source_target_pairs={{0,4},{4,12},{12,8},{8,0},{1,5},{5,13},{13,9},{9,1},{2,6},{6,14},{... | collective-permute-start | bytes 3145736 | tf_op jit(solution)/shard_map/ppermute | solution.py:647
  8.0 1.5 %collective-permute-start.1 = (f32[4,128]{1,0:T(4,128)S(1)}, f32[4,128]{1,0:T(4,128)S(1)}, u32[]{:S(2)}, u32[]{:S(2)}) collective-permute-start(f32[4,128]{1,0:T(4,128)S(1)} %shard_map.153.refs_2_.refs_0_), channel_id=1, source_target_pairs={{0,2},{2,0},{1,3},{3,1},{4,6},{6,4},{5,7},{7,5},{8,10},{10,8},{9,1... | collective-permute-start | bytes 6152 | tf_op jit(solution)/shard_map/ppermute | solution.py:659
  9.5 0.6 shard_map.156
  10.2 1.5 %collective-permute-done.1.refs_1_ = f32[4,128]{1,0:T(4,128)S(1)} collective-permute-done((f32[4,128]{1,0:T(4,128)S(1)}, f32[4,128]{1,0:T(4,128)S(1)}, u32[]{:S(2)}, u32[]{:S(2)}) %collective-permute-start.1) | collective-permute-done | bytes 2080 | tf_op jit(solution)/shard_map/ppermute | solution.py:659
  11.6 2.5 %shard_map.155 = (bf16[512,1024]{1,0:T(8,128)(2,1)}, bf16[512,1024]{1,0:T(8,128)(2,1)}) custom-call(s32[4]{0:T(128)S(1)} %pad_add_fusion.me, bf16[512,2048]{1,0:T(8,128)(2,1)S(1)} %copy-done.4, f32[4,128]{1,0:T(4,128)S(1)} %shard_map.153.refs_2_.refs_0_, f32[4,128]{1,0:T(4,128)S(1)} %collective-permute-done.1.refs_1_, f32[1,4096]{1,0:T(1,128)S(1)} %bitcast.18, ...), custom_call_target="tpu_custom_call" | custom-call | flops 1 | bytes 1 | tf_op jit(solution)/shard_map/pallas_call | solution.py:346
  14.2 0.0 copy-start.19
  14.2 0.1 collective-permute-start.5
  14.3 0.5 collective-permute-start.6
  14.8 0.1 collective-permute-start.4
  14.8 1.5 %collective-permute-start.2 = (bf16[512,1024]{1,0:T(8,128)(2,1)}, bf16[512,1024]{1,0:T(8,128)(2,1)}, u32[]{:S(2)}, u32[]{:S(2)}) collective-permute-start(bf16[512,1024]{1,0:T(8,128)(2,1)} %get-tuple-element.21.refs_0_), channel_id=1, source_target_pairs={{0,2},{2,0},{1,3},{3,1},{4,6},{6,4},{5,7},{7,5},{8,10},{10,8},{9,1... | collective-permute-start | bytes 3145736 | tf_op jit(solution)/shard_map/ppermute | solution.py:663
  16.3 2.1 %collective-permute-done.4.refs_0_.refs_10_ = bf16[256,1024]{1,0:T(8,128)(2,1)S(1)} collective-permute-done((bf16[256,1024]{1,0:T(8,128)(2,1)S(1)}, bf16[256,1024]{1,0:T(8,128)(2,1)S(1)}, u32[]{:S(2)}, u32[]{:S(2)}) %collective-permute-start.4) | collective-permute-done | bytes 524320 | tf_op jit(solution)/shard_map/ppermute | solution.py:654
  18.4 1.5 %collective-permute-start.9 = (bf16[512,1024]{1,0:T(8,128)(2,1)}, bf16[512,1024]{1,0:T(8,128)(2,1)}, u32[]{:S(2)}, u32[]{:S(2)}) collective-permute-start(bf16[512,1024]{1,0:T(8,128)(2,1)} %get-tuple-element.22.refs_1_), channel_id=1, source_target_pairs={{0,2},{2,0},{1,3},{3,1},{4,6},{6,4},{5,7},{7,5},{8,10},{10,8},{9,1... | collective-permute-start | bytes 3145736 | tf_op jit(solution)/shard_map/ppermute | solution.py:663
  19.9 12.7 %collective-permute-done.3.source.refs_11_ = bf16[512,1024]{1,0:T(8,128)(2,1)} collective-permute-done((bf16[512,1024]{1,0:T(8,128)(2,1)S(1)}, bf16[512,1024]{1,0:T(8,128)(2,1)}, u32[]{:S(2)}, u32[]{:S(2)}) %collective-permute-start.3) | collective-permute-done | bytes 1048608 | tf_op jit(solution)/shard_map/ppermute | solution.py:647
  32.6 1.6 %collective-permute-start.8 = (bf16[512,1024]{1,0:T(8,128)(2,1)}, bf16[512,1024]{1,0:T(8,128)(2,1)}, u32[]{:S(2)}, u32[]{:S(2)}) collective-permute-start(bf16[512,1024]{1,0:T(8,128)(2,1)} %collective-permute-done.3.source.refs_11_), channel_id=1, source_target_pairs={{0,16},{16,0},{1,17},{17,1},{2,18},{18,2},{3,19},{19,3},{4,20},{20... | collective-permute-start | bytes 3145736 | tf_op jit(solution)/shard_map/ppermute | solution.py:650
  34.2 0.0 collective-permute-done.6.refs_2_.refs_5_
  34.2 2.8 %shard_map.157 = (bf16[256,1024]{1,0:T(8,128)(2,1)S(1)}, bf16[256,1024]{1,0:T(8,128)(2,1)}) custom-call(bf16[512,1024]{1,0:T(8,128)(2,1)} %collective-permute-done.3.source.refs_11_, bf16[256,1024]{1,0:T(8,128)(2,1)S(1)} %collective-permute-done.4.refs_0_.refs_10_, bf16[512,1024]{1,0:T(8,128)(2,1)S(1)} %collective-permute-done.5.refs_1_.refs_4_, ...), custom_call_target="tpu_custom_call" | custom-call | flops 1 | bytes 1 | tf_op jit(solution)/shard_map/pallas_call | solution.py:438
  37.0 0.7 collective-permute-start.7
  37.8 3.8 %shard_map.150 = (bf16[4,12,40,128]{3,2,1,0:T(8,128)(2,1)}, s32[48]{0:T(128)S(1)}, s32[48]{0:T(128)S(1)}, s32[24]{0:T(128)S(1)}) custom-call(s32[1]{0:T(128)} %bitcast.me, s32[96]{0:T(128)S(1)} %copy-done.18, s32[96]{0:T(128)S(1)} %copy-done.19, bf16[24,4096]{1,0:T(8,128)(2,1)S(1)} %bitcast.15, bf16[24,512]{1,0:T(8,128)(2,1)S(1)} %bitcast.16, ...), custom_call_target="tpu_custom_call" | custom-call | flops 1 | bytes 1 | tf_op jit(solution)/shard_map/pallas_call | solution.py:110
  41.6 4.8 %all-to-all-start = ((bf16[4,12,40,128]{3,2,1,0:T(8,128)(2,1)}), bf16[4,12,40,128]{3,2,1,0:T(8,128)(2,1)}, u32[]{:S(2)}, u32[]{:S(2)}) async-start(bf16[4,12,40,128]{3,2,1,0:T(8,128)(2,1)} %get-tuple-element.20.refs_1_), calls=%async_computation | async-start | bytes 983040 | tf_op jit(solution)/shard_map/all_to_all | solution.py:264
  46.4 2.9 %collective-permute-start.13 = (bf16[256,1024]{1,0:T(8,128)(2,1)}, bf16[256,1024]{1,0:T(8,128)(2,1)}, u32[]{:S(2)}, u32[]{:S(2)}) collective-permute-start(bf16[256,1024]{1,0:T(8,128)(2,1)} %get-tuple-element.25), channel_id=1, source_target_pairs={{0,4},{4,12},{12,8},{8,0},{1,5},{5,13},{13,9},{9,1},{2,6},{6,14},{... | collective-permute-start | bytes 1572872 | tf_op jit(solution)/shard_map/ppermute | solution.py:647
  49.3 13.9 %collective-permute-done.9.refs_4_.refs_0_ = bf16[512,1024]{1,0:T(8,128)(2,1)} collective-permute-done((bf16[512,1024]{1,0:T(8,128)(2,1)}, bf16[512,1024]{1,0:T(8,128)(2,1)}, u32[]{:S(2)}, u32[]{:S(2)}) %collective-permute-start.9) | collective-permute-done | bytes 1048608 | tf_op jit(solution)/shard_map/ppermute | solution.py:663
  63.1 1.6 %collective-permute-start.12 = (bf16[256,1024]{1,0:T(8,128)(2,1)}, bf16[256,1024]{1,0:T(8,128)(2,1)}, u32[]{:S(2)}, u32[]{:S(2)}) collective-permute-start(bf16[256,1024]{1,0:T(8,128)(2,1)} %shard_map.158.refs_1_.refs_8_), channel_id=1, source_target_pairs={{0,16},{16,0},{1,17},{17,1},{2,18},{18,2},{3,19},{19,3},{4,20},{20... | collective-permute-start | bytes 1572872 | tf_op jit(solution)/shard_map/ppermute | solution.py:650
  64.7 0.0 collective-permute-start.10
  64.7 0.5 collective-permute-start.11
  65.3 0.1 copy.23.page_table
  65.3 2.6 %collective-permute-start.15 = (bf16[256,1024]{1,0:T(8,128)(2,1)}, bf16[256,1024]{1,0:T(8,128)(2,1)S(1)}, u32[]{:S(2)}, u32[]{:S(2)}) collective-permute-start(bf16[256,1024]{1,0:T(8,128)(2,1)} %shard_map.158.refs_1_.refs_8_), channel_id=1, source_target_pairs={{0,4},{4,12},{12,8},{8,0},{1,5},{5,13},{13,9},{9,1},{2,6},{6,14},{... | collective-permute-start | bytes 1572872 | tf_op jit(solution)/shard_map/ppermute | solution.py:647
  67.9 0.0 all-to-all-done.blobs
  67.9 5.4 %shard_map.151.refs_0_.refs_1_ = bf16[4,12,32,128]{3,2,1,0:T(8,128)(2,1)S(1)} custom-call(s32[48]{0:T(128)S(1)} %get-tuple-element.18.particle, s32[24,4]{1,0:T(8,128)S(1)} %copy.23.page_table, s32[48]{0:T(128)S(1)} %get-tuple-element.19.lengths, bf16[4,12,40,128]{3,2,1,0:T(8,128)(2,1)} %all-to-all-done.blobs, bf16[96,16,512]{2,1,0:T(8,128)(2,1)} %bitcast.20, ...), custom_call_target="tpu_custom_call" | custom-call | flops 1 | bytes 1 | tf_op jit(solution)/shard_map/pallas_call | solution.py:207
  73.4 0.7 copy-done.5
  74.1 0.6 collective-permute-done.13.refs_0_
  74.7 2.3 %collective-permute-done.12.refs_2_.refs_9_ = bf16[256,1024]{1,0:T(8,128)(2,1)} collective-permute-done((bf16[256,1024]{1,0:T(8,128)(2,1)}, bf16[256,1024]{1,0:T(8,128)(2,1)}, u32[]{:S(2)}, u32[]{:S(2)}) %collective-permute-start.12) | collective-permute-done | bytes 524320 | tf_op jit(solution)/shard_map/ppermute | solution.py:650
  77.0 2.6 %collective-permute-start.17 = (bf16[256,1024]{1,0:T(8,128)(2,1)}, bf16[256,1024]{1,0:T(8,128)(2,1)}, u32[]{:S(2)}, u32[]{:S(2)}) collective-permute-start(bf16[256,1024]{1,0:T(8,128)(2,1)} %shard_map.164.refs_10_), channel_id=1, source_target_pairs={{0,4},{4,12},{12,8},{8,0},{1,5},{5,13},{13,9},{9,1},{2,6},{6,14},{... | collective-permute-start | bytes 1572872 | tf_op jit(solution)/shard_map/ppermute | solution.py:647
  79.6 1.5 %collective-permute-start.14 = (bf16[256,1024]{1,0:T(8,128)(2,1)}, bf16[256,1024]{1,0:T(8,128)(2,1)}, u32[]{:S(2)}, u32[]{:S(2)}) collective-permute-start(bf16[256,1024]{1,0:T(8,128)(2,1)} %shard_map.164.refs_10_), channel_id=1, source_target_pairs={{0,16},{16,0},{1,17},{17,1},{2,18},{18,2},{3,19},{19,3},{4,20},{20... | collective-permute-start | bytes 1572872 | tf_op jit(solution)/shard_map/ppermute | solution.py:650
  81.1 4.7 %collective-permute-done.15.refs_0_ = bf16[256,1024]{1,0:T(8,128)(2,1)S(1)} collective-permute-done((bf16[256,1024]{1,0:T(8,128)(2,1)}, bf16[256,1024]{1,0:T(8,128)(2,1)S(1)}, u32[]{:S(2)}, u32[]{:S(2)}) %collective-permute-start.15) | collective-permute-done | bytes 524320 | tf_op jit(solution)/shard_map/ppermute | solution.py:647
  85.8 0.8 copy-done.6
  86.6 0.5 collective-permute-start.16
  87.1 1.0 copy-done.9
  88.1 8.9 %shard_map.161 = (f32[1024,1024]{1,0:T(8,128)}, f32[8,128]{1,0:T(8,128)S(1)}) custom-call(s32[4]{0:T(128)S(1)} %pad_add_fusion.me, bf16[512,1024]{1,0:T(8,128)(2,1)} %get-tuple-element.21.refs_0_, bf16[512,1024]{1,0:T(8,128)(2,1)} %get-tuple-element.22.refs_1_, bf16[512,1024]{1,0:T(8,128)(2,1)} %shard_map.159.refs_2_, bf16[512,1024]{1,0:T(8,128)(2,1)} %shard_map.160.refs_3_, ...), custom_call_target="tpu_custom_call" | custom-call | flops 1 | bytes 1 | tf_op jit(solution)/shard_map/pallas_call | solution.py:604
  97.0 0.0 copy-start.11
  97.0 0.6 copy-done.11
  97.6 1.6 %collective-permute-start.18 = (bf16[256,1024]{1,0:T(8,128)(2,1)}, bf16[256,1024]{1,0:T(8,128)(2,1)S(1)}, u32[]{:S(2)}, u32[]{:S(2)}) collective-permute-start(bf16[256,1024]{1,0:T(8,128)(2,1)} %shard_map.166.refs_14_), channel_id=1, source_target_pairs={{0,16},{16,0},{1,17},{17,1},{2,18},{18,2},{3,19},{19,3},{4,20},{20... | collective-permute-start | bytes 1572872 | tf_op jit(solution)/shard_map/ppermute | solution.py:650
  99.2 4.9 %all-to-all-start.1 = ((bf16[4,12,32,128]{3,2,1,0:T(8,128)(2,1)}), bf16[4,12,32,128]{3,2,1,0:T(8,128)(2,1)S(1)}, u32[]{:S(2)}, u32[]{:S(2)}) async-start(bf16[4,12,32,128]{3,2,1,0:T(8,128)(2,1)} %shard_map.162), calls=%async_computation.1 | async-start | bytes 786432 | tf_op jit(solution)/shard_map/all_to_all | solution.py:264
  104.2 1.7 %collective-permute-done.16.refs_13_ = bf16[256,1024]{1,0:T(8,128)(2,1)S(1)} collective-permute-done((bf16[256,1024]{1,0:T(8,128)(2,1)}, bf16[256,1024]{1,0:T(8,128)(2,1)S(1)}, u32[]{:S(2)}, u32[]{:S(2)}) %collective-permute-start.16) | collective-permute-done | bytes 524320 | tf_op jit(solution)/shard_map/ppermute | solution.py:650
  105.9 8.0 %shard_map.167 = (f32[1024,1024]{1,0:T(8,128)S(1)}, f32[8,128]{1,0:T(8,128)}, bf16[1024,256]{1,0:T(8,128)(2,1)S(1)}) custom-call(s32[4]{0:T(128)S(1)} %pad_add_fusion.me, bf16[512,1024]{1,0:T(8,128)(2,1)} %get-tuple-element.21.refs_0_, bf16[512,1024]{1,0:T(8,128)(2,1)} %get-tuple-element.22.refs_1_, bf16[512,1024]{1,0:T(8,128)(2,1)} %shard_map.159.refs_2_, ...), custom_call_target="tpu_custom_call" | custom-call | flops 1 | bytes 1 | tf_op jit(solution)/shard_map/pallas_call | solution.py:604
  113.9 0.7 collective-permute-done.18.refs_0_
  114.6 1.7 %shard_map.168 = (f32[1,512]{1,0:T(1,128)S(1)}, f32[1,512]{1,0:T(1,128)S(1)}, f32[1,512]{1,0:T(1,128)S(1)}) custom-call(s32[4]{0:T(128)S(1)} %pad_add_fusion.me, bf16[1024,256]{1,0:T(8,128)(2,1)S(1)} %get-tuple-element.27.x, f32[1024,1024]{1,0:T(8,128)S(1)} %get-tuple-element.28.acc, bf16[256,1024]{1,0:T(8,128)(2,1)S(1)} %collective-permute-done.18.refs_0_, ...), custom_call_target="tpu_custom_call" | custom-call | flops 1 | bytes 1 | tf_op jit(solution)/shard_map/pallas_call | solution.py:575
  116.4 0.1 collective-permute-start.21
  116.4 1.6 %collective-permute-start.20 = (f32[1,512]{1,0:T(1,128)S(1)}, f32[1,512]{1,0:T(1,128)S(1)}, u32[]{:S(2)}, u32[]{:S(2)}) collective-permute-start(f32[1,512]{1,0:T(1,128)S(1)} %get-tuple-element.31), channel_id=1, source_target_pairs={{0,2},{2,0},{1,3},{3,1},{4,6},{6,4},{5,7},{7,5},{8,10},{10,8},{9,1... | collective-permute-start | bytes 6152 | tf_op jit(solution)/shard_map/ppermute | solution.py:726
  118.0 0.3 collective-permute-start.19
  118.3 1.1 collective-permute-done.21
  119.4 0.7 collective-permute-done.20
  120.1 0.0 collective-permute-done.19
  120.1 0.6 add_add_fusion
  120.7 1.6 %shard_map.163 = bf16[24,4096]{1,0:T(8,128)(2,1)} custom-call(s32[24]{0:T(128)S(1)} %get-tuple-element.17.pick, bf16[4,12,32,128]{3,2,1,0:T(8,128)(2,1)S(1)} %all-to-all-done.1.parts, f32[8,128]{1,0:T(8,128)S(1)} %copy-done.12), custom_call_target="tpu_custom_call" | custom-call | flops 1 | bytes 1 | tf_op jit(solution)/shard_map/pallas_call | solution.py:237
  (52 shorter events, 0.1 us)
Async XLA Ops:
  0.7 1.6 %copy-start = (bf16[512,2048]{1,0:T(8,128)(2,1)S(1)}, bf16[512,2048]{1,0:T(8,128)(2,1)}, u32[]{:S(2)}) copy-start(bf16[512,2048]{1,0:T(8,128)(2,1)} %refs_8_.1) | copy-start | bytes 6291460
  2.3 1.8 %copy-start.4 = (bf16[512,2048]{1,0:T(8,128)(2,1)S(1)}, bf16[512,2048]{1,0:T(8,128)(2,1)}, u32[]{:S(2)}) copy-start(bf16[512,2048]{1,0:T(8,128)(2,1)} %x.3) | copy-start | bytes 6291460
  2.9 2.1 %collective-permute-start = (bf16[256,1024]{1,0:T(8,128)(2,1)S(1)}, bf16[256,1024]{1,0:T(8,128)(2,1)S(1)}, u32[]{:S(2)}, u32[]{:S(2)}) collective-permute-start(bf16[256,1024]{1,0:T(8,128)(2,1)S(1)} %shard_map.149), channel_id=1, source_target_pairs={{0,1},{1,0},{2,3},{3,2},{4,5},{5,4},{6,7},{7,6},{8,9},{9,8},{10,11... | collective-permute-start | bytes 1572872 | tf_op jit(solution)/shard_map/ppermute | solution.py:654
  4.1 5.5 %copy-start.1 = (bf16[512,2048]{1,0:T(8,128)(2,1)S(1)}, bf16[512,2048]{1,0:T(8,128)(2,1)}, u32[]{:S(2)}) copy-start(bf16[512,2048]{1,0:T(8,128)(2,1)} %refs_8_.1) | copy-start | bytes 6291460
  4.8 6.8 %copy-start.15 = (f32[4096]{0:T(1024)S(1)}, f32[4096]{0:T(1024)}, u32[]{:S(2)}) copy-start(f32[4096]{0:T(1024)} %param.23) | copy-start | bytes 49156
  5.1 27.6 %collective-permute-start.3 = (bf16[512,1024]{1,0:T(8,128)(2,1)S(1)}, bf16[512,1024]{1,0:T(8,128)(2,1)}, u32[]{:S(2)}, u32[]{:S(2)}) collective-permute-start(bf16[512,1024]{1,0:T(8,128)(2,1)S(1)} %shard_map.154.refs_3_), channel_id=1, source_target_pairs={{0,4},{4,12},{12,8},{8,0},{1,5},{5,13},{13,9},{9,1},{2,6},{6,14},{... | collective-permute-start | bytes 3145736 | tf_op jit(solution)/shard_map/ppermute | solution.py:647
  8.0 3.6 %collective-permute-start.1 = (f32[4,128]{1,0:T(4,128)S(1)}, f32[4,128]{1,0:T(4,128)S(1)}, u32[]{:S(2)}, u32[]{:S(2)}) collective-permute-start(f32[4,128]{1,0:T(4,128)S(1)} %shard_map.153.refs_2_.refs_0_), channel_id=1, source_target_pairs={{0,2},{2,0},{1,3},{3,1},{4,6},{6,4},{5,7},{7,5},{8,10},{10,8},{9,1... | collective-permute-start | bytes 6152 | tf_op jit(solution)/shard_map/ppermute | solution.py:659
  14.2 23.6 %copy-start.10 = (bf16[1,24,4096]{2,1,0:T(8,128)(2,1)S(1)}, bf16[1,24,4096]{2,1,0:T(8,128)(2,1)}, u32[]{:S(2)}) copy-start(bf16[1,24,4096]{2,1,0:T(8,128)(2,1)} %param.14) | copy-start | bytes 589828
  14.2 23.6 %copy-start.13 = (bf16[1,24,512]{2,1,0:T(8,128)(2,1)S(1)}, bf16[1,24,512]{2,1,0:T(8,128)(2,1)}, u32[]{:S(2)}) copy-start(bf16[1,24,512]{2,1,0:T(8,128)(2,1)} %param.15) | copy-start | bytes 73732
  14.2 23.6 %copy-start.14 = (bf16[1,24,512]{2,1,0:T(8,128)(2,1)S(1)}, bf16[1,24,512]{2,1,0:T(8,128)(2,1)}, u32[]{:S(2)}) copy-start(bf16[1,24,512]{2,1,0:T(8,128)(2,1)} %param.16) | copy-start | bytes 73732
  14.2 23.6 %copy-start.18 = (s32[96]{0:T(128)S(1)}, s32[96]{0:T(128)}, u32[]{:S(2)}) copy-start(s32[96]{0:T(128)} %ancestry.1) | copy-start | bytes 1156
  14.2 23.6 %copy-start.19 = (s32[96]{0:T(128)S(1)}, s32[96]{0:T(128)}, u32[]{:S(2)}) copy-start(s32[96]{0:T(128)} %lengths.1) | copy-start | bytes 1156
  14.2 20.0 %collective-permute-start.5 = (bf16[512,1024]{1,0:T(8,128)(2,1)}, bf16[512,1024]{1,0:T(8,128)(2,1)S(1)}, u32[]{:S(2)}, u32[]{:S(2)}) collective-permute-start(bf16[512,1024]{1,0:T(8,128)(2,1)} %get-tuple-element.21.refs_0_), channel_id=1, source_target_pairs={{0,1},{1,0},{2,3},{3,2},{4,5},{5,4},{6,7},{7,6},{8,9},{9,8},{10,11... | collective-permute-start | bytes 3145736 | tf_op jit(solution)/shard_map/ppermute | solution.py:667
  14.3 19.9 %collective-permute-start.6 = (bf16[512,1024]{1,0:T(8,128)(2,1)}, bf16[512,1024]{1,0:T(8,128)(2,1)S(1)}, u32[]{:S(2)}, u32[]{:S(2)}) collective-permute-start(bf16[512,1024]{1,0:T(8,128)(2,1)} %get-tuple-element.22.refs_1_), channel_id=1, source_target_pairs={{0,1},{1,0},{2,3},{3,2},{4,5},{5,4},{6,7},{7,6},{8,9},{9,8},{10,11... | collective-permute-start | bytes 3145736 | tf_op jit(solution)/shard_map/ppermute | solution.py:667
  14.8 3.6 %collective-permute-start.4 = (bf16[256,1024]{1,0:T(8,128)(2,1)S(1)}, bf16[256,1024]{1,0:T(8,128)(2,1)S(1)}, u32[]{:S(2)}, u32[]{:S(2)}) collective-permute-start(bf16[256,1024]{1,0:T(8,128)(2,1)S(1)} %shard_map.156), channel_id=1, source_target_pairs={{0,1},{1,0},{2,3},{3,2},{4,5},{5,4},{6,7},{7,6},{8,9},{9,8},{10,11... | collective-permute-start | bytes 1572872 | tf_op jit(solution)/shard_map/ppermute | solution.py:654
  14.8 34.4 %collective-permute-start.2 = (bf16[512,1024]{1,0:T(8,128)(2,1)}, bf16[512,1024]{1,0:T(8,128)(2,1)}, u32[]{:S(2)}, u32[]{:S(2)}) collective-permute-start(bf16[512,1024]{1,0:T(8,128)(2,1)} %get-tuple-element.21.refs_0_), channel_id=1, source_target_pairs={{0,2},{2,0},{1,3},{3,1},{4,6},{6,4},{5,7},{7,5},{8,10},{10,8},{9,1... | collective-permute-start | bytes 3145736 | tf_op jit(solution)/shard_map/ppermute | solution.py:663
  18.4 23.2 %copy-start.8 = (bf16[256,1024]{1,0:T(8,128)(2,1)}, bf16[256,1024]{1,0:T(8,128)(2,1)S(1)}, u32[]{:S(2)}) copy-start(bf16[256,1024]{1,0:T(8,128)(2,1)S(1)} %collective-permute-done.4.refs_0_.refs_10_) | copy-start | bytes 1572868
  18.4 44.7 %collective-permute-start.9 = (bf16[512,1024]{1,0:T(8,128)(2,1)}, bf16[512,1024]{1,0:T(8,128)(2,1)}, u32[]{:S(2)}, u32[]{:S(2)}) collective-permute-start(bf16[512,1024]{1,0:T(8,128)(2,1)} %get-tuple-element.22.refs_1_), channel_id=1, source_target_pairs={{0,2},{2,0},{1,3},{3,1},{4,6},{6,4},{5,7},{7,5},{8,10},{10,8},{9,1... | collective-permute-start | bytes 3145736 | tf_op jit(solution)/shard_map/ppermute | solution.py:663
  32.6 30.5 %collective-permute-start.8 = (bf16[512,1024]{1,0:T(8,128)(2,1)}, bf16[512,1024]{1,0:T(8,128)(2,1)}, u32[]{:S(2)}, u32[]{:S(2)}) collective-permute-start(bf16[512,1024]{1,0:T(8,128)(2,1)} %collective-permute-done.3.source.refs_11_), channel_id=1, source_target_pairs={{0,16},{16,0},{1,17},{17,1},{2,18},{18,2},{3,19},{19,3},{4,20},{20... | collective-permute-start | bytes 3145736 | tf_op jit(solution)/shard_map/ppermute | solution.py:650
  34.2 7.4 %copy-start.2 = (bf16[512,1024]{1,0:T(8,128)(2,1)}, bf16[512,1024]{1,0:T(8,128)(2,1)S(1)}, u32[]{:S(2)}) copy-start(bf16[512,1024]{1,0:T(8,128)(2,1)S(1)} %collective-permute-done.5.refs_1_.refs_4_) | copy-start | bytes 3145732
  34.2 7.4 %copy-start.3 = (bf16[512,1024]{1,0:T(8,128)(2,1)}, bf16[512,1024]{1,0:T(8,128)(2,1)S(1)}, u32[]{:S(2)}) copy-start(bf16[512,1024]{1,0:T(8,128)(2,1)S(1)} %collective-permute-done.6.refs_2_.refs_5_) | copy-start | bytes 3145732
  37.0 26.1 %collective-permute-start.7 = (bf16[256,1024]{1,0:T(8,128)(2,1)S(1)}, bf16[256,1024]{1,0:T(8,128)(2,1)}, u32[]{:S(2)}, u32[]{:S(2)}) collective-permute-start(bf16[256,1024]{1,0:T(8,128)(2,1)S(1)} %get-tuple-element.23), channel_id=1, source_target_pairs={{0,4},{4,12},{12,8},{8,0},{1,5},{5,13},{13,9},{9,1},{2,6},{6,14},{... | collective-permute-start | bytes 1572872 | tf_op jit(solution)/shard_map/ppermute | solution.py:647
  41.6 26.3 %all-to-all-start = ((bf16[4,12,40,128]{3,2,1,0:T(8,128)(2,1)}), bf16[4,12,40,128]{3,2,1,0:T(8,128)(2,1)}, u32[]{:S(2)}, u32[]{:S(2)}) async-start(bf16[4,12,40,128]{3,2,1,0:T(8,128)(2,1)} %get-tuple-element.20.refs_1_), calls=%async_computation | async-start | bytes 983040 | tf_op jit(solution)/shard_map/all_to_all | solution.py:264
  46.4 28.3 %collective-permute-start.13 = (bf16[256,1024]{1,0:T(8,128)(2,1)}, bf16[256,1024]{1,0:T(8,128)(2,1)}, u32[]{:S(2)}, u32[]{:S(2)}) collective-permute-start(bf16[256,1024]{1,0:T(8,128)(2,1)} %get-tuple-element.25), channel_id=1, source_target_pairs={{0,4},{4,12},{12,8},{8,0},{1,5},{5,13},{13,9},{9,1},{2,6},{6,14},{... | collective-permute-start | bytes 1572872 | tf_op jit(solution)/shard_map/ppermute | solution.py:647
  63.1 2.1 %copy-start.21 = (s32[24,4]{0,1:T(4,128)S(1)}, s32[24,4]{0,1:T(4,128)}, u32[]{:S(2)}) copy-start(s32[24,4]{0,1:T(4,128)} %param.19) | copy-start | bytes 1156
  63.1 13.9 %collective-permute-start.12 = (bf16[256,1024]{1,0:T(8,128)(2,1)}, bf16[256,1024]{1,0:T(8,128)(2,1)}, u32[]{:S(2)}, u32[]{:S(2)}) collective-permute-start(bf16[256,1024]{1,0:T(8,128)(2,1)} %shard_map.158.refs_1_.refs_8_), channel_id=1, source_target_pairs={{0,16},{16,0},{1,17},{17,1},{2,18},{18,2},{3,19},{19,3},{4,20},{20... | collective-permute-start | bytes 1572872 | tf_op jit(solution)/shard_map/ppermute | solution.py:650
  64.7 22.3 %collective-permute-start.10 = (bf16[512,1024]{1,0:T(8,128)(2,1)}, bf16[512,1024]{1,0:T(8,128)(2,1)}, u32[]{:S(2)}, u32[]{:S(2)}) collective-permute-start(bf16[512,1024]{1,0:T(8,128)(2,1)} %shard_map.159.refs_2_), channel_id=1, source_target_pairs={{0,1},{1,0},{2,3},{3,2},{4,5},{5,4},{6,7},{7,6},{8,9},{9,8},{10,11... | collective-permute-start | bytes 3145736 | tf_op jit(solution)/shard_map/ppermute | solution.py:704
  64.7 22.3 %collective-permute-start.11 = (bf16[512,1024]{1,0:T(8,128)(2,1)}, bf16[512,1024]{1,0:T(8,128)(2,1)}, u32[]{:S(2)}, u32[]{:S(2)}) collective-permute-start(bf16[512,1024]{1,0:T(8,128)(2,1)} %shard_map.160.refs_3_), channel_id=1, source_target_pairs={{0,1},{1,0},{2,3},{3,2},{4,5},{5,4},{6,7},{7,6},{8,9},{9,8},{10,11... | collective-permute-start | bytes 3145736 | tf_op jit(solution)/shard_map/ppermute | solution.py:704
  65.3 20.5 %collective-permute-start.15 = (bf16[256,1024]{1,0:T(8,128)(2,1)}, bf16[256,1024]{1,0:T(8,128)(2,1)S(1)}, u32[]{:S(2)}, u32[]{:S(2)}) collective-permute-start(bf16[256,1024]{1,0:T(8,128)(2,1)} %shard_map.158.refs_1_.refs_8_), channel_id=1, source_target_pairs={{0,4},{4,12},{12,8},{8,0},{1,5},{5,13},{13,9},{9,1},{2,6},{6,14},{... | collective-permute-start | bytes 1572872 | tf_op jit(solution)/shard_map/ppermute | solution.py:647
  73.4 0.8 copy-start.5
  77.0 20.6 %collective-permute-start.17 = (bf16[256,1024]{1,0:T(8,128)(2,1)}, bf16[256,1024]{1,0:T(8,128)(2,1)}, u32[]{:S(2)}, u32[]{:S(2)}) collective-permute-start(bf16[256,1024]{1,0:T(8,128)(2,1)} %shard_map.164.refs_10_), channel_id=1, source_target_pairs={{0,4},{4,12},{12,8},{8,0},{1,5},{5,13},{13,9},{9,1},{2,6},{6,14},{... | collective-permute-start | bytes 1572872 | tf_op jit(solution)/shard_map/ppermute | solution.py:647
  79.6 24.6 %collective-permute-start.14 = (bf16[256,1024]{1,0:T(8,128)(2,1)}, bf16[256,1024]{1,0:T(8,128)(2,1)}, u32[]{:S(2)}, u32[]{:S(2)}) collective-permute-start(bf16[256,1024]{1,0:T(8,128)(2,1)} %shard_map.164.refs_10_), channel_id=1, source_target_pairs={{0,16},{16,0},{1,17},{17,1},{2,18},{18,2},{3,19},{19,3},{4,20},{20... | collective-permute-start | bytes 1572872 | tf_op jit(solution)/shard_map/ppermute | solution.py:650
  85.8 0.8 copy-start.6
  86.6 19.3 %collective-permute-start.16 = (bf16[256,1024]{1,0:T(8,128)(2,1)}, bf16[256,1024]{1,0:T(8,128)(2,1)S(1)}, u32[]{:S(2)}, u32[]{:S(2)}) collective-permute-start(bf16[256,1024]{1,0:T(8,128)(2,1)} %shard_map.165.refs_12_), channel_id=1, source_target_pairs={{0,16},{16,0},{1,17},{17,1},{2,18},{18,2},{3,19},{19,3},{4,20},{20... | collective-permute-start | bytes 1572872 | tf_op jit(solution)/shard_map/ppermute | solution.py:650
  87.1 1.0 copy-start.9
  97.0 0.6 copy-start.11
  97.6 6.6 %copy-start.20 = (bf16[2048,2]{0,1:T(2,128)(2,1)S(1)}, bf16[2048,2]{0,1:T(2,128)(2,1)}, u32[]{:S(2)}) copy-start(bf16[2048,2]{0,1:T(2,128)(2,1)} %param.26) | copy-start | bytes 24580
  97.6 8.3 %copy-start.7 = (bf16[256,1024]{1,0:T(8,128)(2,1)S(1)}, bf16[256,1024]{1,0:T(8,128)(2,1)}, u32[]{:S(2)}) copy-start(bf16[256,1024]{1,0:T(8,128)(2,1)} %shard_map.165.refs_12_) | copy-start | bytes 1572868
  97.6 17.0 %collective-permute-start.18 = (bf16[256,1024]{1,0:T(8,128)(2,1)}, bf16[256,1024]{1,0:T(8,128)(2,1)S(1)}, u32[]{:S(2)}, u32[]{:S(2)}) collective-permute-start(bf16[256,1024]{1,0:T(8,128)(2,1)} %shard_map.166.refs_14_), channel_id=1, source_target_pairs={{0,16},{16,0},{1,17},{17,1},{2,18},{18,2},{3,19},{19,3},{4,20},{20... | collective-permute-start | bytes 1572872 | tf_op jit(solution)/shard_map/ppermute | solution.py:650
  99.2 21.4 %all-to-all-start.1 = ((bf16[4,12,32,128]{3,2,1,0:T(8,128)(2,1)}), bf16[4,12,32,128]{3,2,1,0:T(8,128)(2,1)S(1)}, u32[]{:S(2)}, u32[]{:S(2)}) async-start(bf16[4,12,32,128]{3,2,1,0:T(8,128)(2,1)} %shard_map.162), calls=%async_computation.1 | async-start | bytes 786432 | tf_op jit(solution)/shard_map/all_to_all | solution.py:264
  105.9 8.7 %copy-start.16 = (f32[2048]{0:T(1024)S(1)}, f32[2048]{0:T(1024)}, u32[]{:S(2)}) copy-start(f32[2048]{0:T(1024)} %param.25) | copy-start | bytes 24580
  105.9 8.7 %copy-start.17 = (f32[2]{0:T(128)S(1)}, f32[2]{0:T(128)}, u32[]{:S(2)}) copy-start(f32[2]{0:T(128)} %refs_3_.1) | copy-start | bytes 28
  114.6 6.1 %copy-start.12 = (f32[8,128]{1,0:T(8,128)S(1)}, f32[8,128]{1,0:T(8,128)}, u32[]{:S(2)}) copy-start(f32[8,128]{1,0:T(8,128)} %copy-done.11) | copy-start | bytes 12292
  116.4 3.1 %collective-permute-start.21 = (f32[1,512]{1,0:T(1,128)S(1)}, f32[1,512]{1,0:T(1,128)S(1)}, u32[]{:S(2)}, u32[]{:S(2)}) collective-permute-start(f32[1,512]{1,0:T(1,128)S(1)} %get-tuple-element.30), channel_id=1, source_target_pairs={{0,3},{1,2},{2,1},{3,0},{4,7},{5,6},{6,5},{7,4},{8,11},{9,10},{10,... | collective-permute-start | bytes 6152 | tf_op jit(solution)/shard_map/ppermute | solution.py:727
  116.4 3.7 %collective-permute-start.20 = (f32[1,512]{1,0:T(1,128)S(1)}, f32[1,512]{1,0:T(1,128)S(1)}, u32[]{:S(2)}, u32[]{:S(2)}) collective-permute-start(f32[1,512]{1,0:T(1,128)S(1)} %get-tuple-element.31), channel_id=1, source_target_pairs={{0,2},{2,0},{1,3},{3,1},{4,6},{6,4},{5,7},{7,5},{8,10},{10,8},{9,1... | collective-permute-start | bytes 6152 | tf_op jit(solution)/shard_map/ppermute | solution.py:726
  118.0 2.1 %collective-permute-start.19 = (f32[1,512]{1,0:T(1,128)S(1)}, f32[1,512]{1,0:T(1,128)S(1)}, u32[]{:S(2)}, u32[]{:S(2)}) collective-permute-start(f32[1,512]{1,0:T(1,128)S(1)} %get-tuple-element.30), channel_id=1, source_target_pairs={{0,1},{1,0},{2,3},{3,2},{4,5},{5,4},{6,7},{7,6},{8,9},{9,8},{10,11... | collective-permute-start | bytes 6152 | tf_op jit(solution)/shard_map/ppermute | solution.py:724

commit v7 on v6

--- a/solution.py
+++ b/solution.py
@@ -8,7 +8,7 @@
 from jax.sharding import PartitionSpec as P
 
 HD = 128
-VMEM_LIMIT = 24 << 20
+VMEM_LIMIT = 32 << 20
 BRIEF = pl.CostEstimate(flops=1, bytes_accessed=1, transcendentals=0)
 ANY = pl.BlockSpec(memory_space=pltpu.HBM)
 WAITED = pl.BlockSpec(memory_space=pl.ANY)

time: 123 us -> 123 us (level)
  no operation moved by 1% of the time
where the time goes in v7:
time: 123 us; the launch traced here: 122 us
  waiting for transfers between devices  42.1 us (34%)
  Pallas kernels  37.4 us (30%)
  starting transfers between devices  36.3 us (30%)
  local copies, waits for them, and re-layouts  4.92 us (4%)
    ppermute x5, waiting for transfers between devices, forward(): return lax.ppermute(t, 'batch', ring)  18 us
    pallas_call x2, Pallas kernels, gemm(): pl.pallas_call(functools.partial(gemm_kernel, parts=parts, sources=len(we...  16.9 us
    ppermute x2, waiting for transfers between devices, both(): lax.ppermute(part, 'mp', shift_pairs(x_count, k))  13.9 us
    ppermute x5, starting transfers between devices, forward(): return lax.ppermute(t, 'batch', ring)  11.8 us
    all_to_all x2, starting transfers between devices, send(): lax.all_to_all(blobs, 'batch', split_axis=0, concat_axis=0, tiled=True)  9.68 us
    ppermute x5, starting transfers between devices, over_group(): lax.ppermute(t, 'group', shift_pairs(y_count, k))  6.76 us
    pallas_call x1, Pallas kernels, serve(): pl.pallas_call(functools.partial(serve_kernel, kv_local=kv_local, unroll=...  5.43 us
    unnamed x45, local copies, waits for them, and re-layouts  4.92 us
  transfers between devices with their start and end apart: 24, of which 12 were waited for; matrix products, arithmetic and copies ran while one was open for 1% of the time, Pallas kernels for 29%

profile of v7, /device:TPU:0, one launch (start us, length us, event | category | flops | bytes accessed | tf_op | source)
XLA Modules:
  0.0 122.3 jit_solution(2587698387504945706)
XLA Ops:
  0.6 0.1 pad_add_fusion.me
  0.7 1.6 %copy-done = bf16[512,2048]{1,0:T(8,128)(2,1)S(1)} copy-done((bf16[512,2048]{1,0:T(8,128)(2,1)S(1)}, bf16[512,2048]{1,0:T(8,128)(2,1)}, u32[]{:S(2)}) %copy-start) | copy-done | bytes 2097176
  2.3 0.6 shard_map.149
  2.9 0.5 collective-permute-start
  3.4 0.6 shard_map.152.waited.refs_0_
  4.1 0.0 copy-start.1
  4.1 0.7 shard_map.153.refs_2_.refs_0_
  4.8 0.0 copy-start.15
  4.8 0.2 collective-permute-done.waited.refs_1_.refs_9_
  5.0 0.1 shard_map.154.refs_3_
  5.1 3.0 %collective-permute-start.3 = (bf16[512,1024]{1,0:T(8,128)(2,1)S(1)}, bf16[512,1024]{1,0:T(8,128)(2,1)}, u32[]{:S(2)}, u32[]{:S(2)}) collective-permute-start(bf16[512,1024]{1,0:T(8,128)(2,1)S(1)} %shard_map.154.refs_3_), channel_id=1, source_target_pairs={{0,4},{4,12},{12,8},{8,0},{1,5},{5,13},{13,9},{9,1},{2,6},{6,14},{... | collective-permute-start | bytes 3145736 | tf_op jit(solution)/shard_map/ppermute | solution.py:647
  8.0 1.5 %collective-permute-start.1 = (f32[4,128]{1,0:T(4,128)S(1)}, f32[4,128]{1,0:T(4,128)S(1)}, u32[]{:S(2)}, u32[]{:S(2)}) collective-permute-start(f32[4,128]{1,0:T(4,128)S(1)} %shard_map.153.refs_2_.refs_0_), channel_id=1, source_target_pairs={{0,2},{2,0},{1,3},{3,1},{4,6},{6,4},{5,7},{7,5},{8,10},{10,8},{9,1... | collective-permute-start | bytes 6152 | tf_op jit(solution)/shard_map/ppermute | solution.py:659
  9.5 0.6 shard_map.156
  10.2 1.5 %collective-permute-done.1.refs_1_ = f32[4,128]{1,0:T(4,128)S(1)} collective-permute-done((f32[4,128]{1,0:T(4,128)S(1)}, f32[4,128]{1,0:T(4,128)S(1)}, u32[]{:S(2)}, u32[]{:S(2)}) %collective-permute-start.1) | collective-permute-done | bytes 2080 | tf_op jit(solution)/shard_map/ppermute | solution.py:659
  11.6 2.5 %shard_map.155 = (bf16[512,1024]{1,0:T(8,128)(2,1)}, bf16[512,1024]{1,0:T(8,128)(2,1)}) custom-call(s32[4]{0:T(128)S(1)} %pad_add_fusion.me, bf16[512,2048]{1,0:T(8,128)(2,1)S(1)} %copy-done.4, f32[4,128]{1,0:T(4,128)S(1)} %shard_map.153.refs_2_.refs_0_, f32[4,128]{1,0:T(4,128)S(1)} %collective-permute-done.1.refs_1_, f32[1,4096]{1,0:T(1,128)S(1)} %bitcast.18, ...), custom_call_target="tpu_custom_call" | custom-call | flops 1 | bytes 1 | tf_op jit(solution)/shard_map/pallas_call | solution.py:346
  14.2 0.0 copy-start.19
  14.2 0.1 collective-permute-start.5
  14.3 0.5 collective-permute-start.6
  14.8 0.1 collective-permute-start.4
  14.8 1.5 %collective-permute-start.2 = (bf16[512,1024]{1,0:T(8,128)(2,1)}, bf16[512,1024]{1,0:T(8,128)(2,1)}, u32[]{:S(2)}, u32[]{:S(2)}) collective-permute-start(bf16[512,1024]{1,0:T(8,128)(2,1)} %get-tuple-element.21.refs_0_), channel_id=1, source_target_pairs={{0,2},{2,0},{1,3},{3,1},{4,6},{6,4},{5,7},{7,5},{8,10},{10,8},{9,1... | collective-permute-start | bytes 3145736 | tf_op jit(solution)/shard_map/ppermute | solution.py:663
  16.3 2.1 %collective-permute-done.4.refs_0_.refs_10_ = bf16[256,1024]{1,0:T(8,128)(2,1)S(1)} collective-permute-done((bf16[256,1024]{1,0:T(8,128)(2,1)S(1)}, bf16[256,1024]{1,0:T(8,128)(2,1)S(1)}, u32[]{:S(2)}, u32[]{:S(2)}) %collective-permute-start.4) | collective-permute-done | bytes 524320 | tf_op jit(solution)/shard_map/ppermute | solution.py:654
  18.4 1.5 %collective-permute-start.9 = (bf16[512,1024]{1,0:T(8,128)(2,1)}, bf16[512,1024]{1,0:T(8,128)(2,1)}, u32[]{:S(2)}, u32[]{:S(2)}) collective-permute-start(bf16[512,1024]{1,0:T(8,128)(2,1)} %get-tuple-element.22.refs_1_), channel_id=1, source_target_pairs={{0,2},{2,0},{1,3},{3,1},{4,6},{6,4},{5,7},{7,5},{8,10},{10,8},{9,1... | collective-permute-start | bytes 3145736 | tf_op jit(solution)/shard_map/ppermute | solution.py:663
  19.9 12.7 %collective-permute-done.3.source.refs_11_ = bf16[512,1024]{1,0:T(8,128)(2,1)} collective-permute-done((bf16[512,1024]{1,0:T(8,128)(2,1)S(1)}, bf16[512,1024]{1,0:T(8,128)(2,1)}, u32[]{:S(2)}, u32[]{:S(2)}) %collective-permute-start.3) | collective-permute-done | bytes 1048608 | tf_op jit(solution)/shard_map/ppermute | solution.py:647
  32.6 1.6 %collective-permute-start.8 = (bf16[512,1024]{1,0:T(8,128)(2,1)}, bf16[512,1024]{1,0:T(8,128)(2,1)}, u32[]{:S(2)}, u32[]{:S(2)}) collective-permute-start(bf16[512,1024]{1,0:T(8,128)(2,1)} %collective-permute-done.3.source.refs_11_), channel_id=1, source_target_pairs={{0,16},{16,0},{1,17},{17,1},{2,18},{18,2},{3,19},{19,3},{4,20},{20... | collective-permute-start | bytes 3145736 | tf_op jit(solution)/shard_map/ppermute | solution.py:650
  34.2 2.8 %shard_map.157 = (bf16[256,1024]{1,0:T(8,128)(2,1)S(1)}, bf16[256,1024]{1,0:T(8,128)(2,1)}) custom-call(bf16[512,1024]{1,0:T(8,128)(2,1)} %collective-permute-done.3.source.refs_11_, bf16[256,1024]{1,0:T(8,128)(2,1)S(1)} %collective-permute-done.4.refs_0_.refs_10_, bf16[512,1024]{1,0:T(8,128)(2,1)S(1)} %collective-permute-done.5.refs_1_.refs_4_, ...), custom_call_target="tpu_custom_call" | custom-call | flops 1 | bytes 1 | tf_op jit(solution)/shard_map/pallas_call | solution.py:438
  37.0 0.7 collective-permute-start.7
  37.8 3.8 %shard_map.150 = (bf16[4,12,40,128]{3,2,1,0:T(8,128)(2,1)}, s32[48]{0:T(128)S(1)}, s32[48]{0:T(128)S(1)}, s32[24]{0:T(128)S(1)}) custom-call(s32[1]{0:T(128)} %bitcast.me, s32[96]{0:T(128)S(1)} %copy-done.18, s32[96]{0:T(128)S(1)} %copy-done.19, bf16[24,4096]{1,0:T(8,128)(2,1)S(1)} %bitcast.15, bf16[24,512]{1,0:T(8,128)(2,1)S(1)} %bitcast.16, ...), custom_call_target="tpu_custom_call" | custom-call | flops 1 | bytes 1 | tf_op jit(solution)/shard_map/pallas_call | solution.py:110
  41.6 4.8 %all-to-all-start = ((bf16[4,12,40,128]{3,2,1,0:T(8,128)(2,1)}), bf16[4,12,40,128]{3,2,1,0:T(8,128)(2,1)}, u32[]{:S(2)}, u32[]{:S(2)}) async-start(bf16[4,12,40,128]{3,2,1,0:T(8,128)(2,1)} %get-tuple-element.20.refs_1_), calls=%async_computation | async-start | bytes 983040 | tf_op jit(solution)/shard_map/all_to_all | solution.py:264
  46.4 2.9 %collective-permute-start.13 = (bf16[256,1024]{1,0:T(8,128)(2,1)}, bf16[256,1024]{1,0:T(8,128)(2,1)}, u32[]{:S(2)}, u32[]{:S(2)}) collective-permute-start(bf16[256,1024]{1,0:T(8,128)(2,1)} %get-tuple-element.25), channel_id=1, source_target_pairs={{0,4},{4,12},{12,8},{8,0},{1,5},{5,13},{13,9},{9,1},{2,6},{6,14},{... | collective-permute-start | bytes 1572872 | tf_op jit(solution)/shard_map/ppermute | solution.py:647
  49.3 13.9 %collective-permute-done.9.refs_4_.refs_0_ = bf16[512,1024]{1,0:T(8,128)(2,1)} collective-permute-done((bf16[512,1024]{1,0:T(8,128)(2,1)}, bf16[512,1024]{1,0:T(8,128)(2,1)}, u32[]{:S(2)}, u32[]{:S(2)}) %collective-permute-start.9) | collective-permute-done | bytes 1048608 | tf_op jit(solution)/shard_map/ppermute | solution.py:663
  63.1 0.0 collective-permute-done.7.refs_0_
  63.1 0.0 collective-permute-done.8.refs_2_.refs_12_
  63.1 1.6 %collective-permute-start.12 = (bf16[256,1024]{1,0:T(8,128)(2,1)}, bf16[256,1024]{1,0:T(8,128)(2,1)}, u32[]{:S(2)}, u32[]{:S(2)}) collective-permute-start(bf16[256,1024]{1,0:T(8,128)(2,1)} %shard_map.158.refs_1_.refs_8_), channel_id=1, source_target_pairs={{0,16},{16,0},{1,17},{17,1},{2,18},{18,2},{3,19},{19,3},{4,20},{20... | collective-permute-start | bytes 1572872 | tf_op jit(solution)/shard_map/ppermute | solution.py:650
  64.7 0.0 collective-permute-start.10
  64.7 0.5 collective-permute-start.11
  65.3 0.1 copy.23.page_table
  65.3 2.6 %collective-permute-start.15 = (bf16[256,1024]{1,0:T(8,128)(2,1)}, bf16[256,1024]{1,0:T(8,128)(2,1)S(1)}, u32[]{:S(2)}, u32[]{:S(2)}) collective-permute-start(bf16[256,1024]{1,0:T(8,128)(2,1)} %shard_map.158.refs_1_.refs_8_), channel_id=1, source_target_pairs={{0,4},{4,12},{12,8},{8,0},{1,5},{5,13},{13,9},{9,1},{2,6},{6,14},{... | collective-permute-start | bytes 1572872 | tf_op jit(solution)/shard_map/ppermute | solution.py:647
  67.9 5.4 %shard_map.151.refs_0_.refs_1_ = bf16[4,12,32,128]{3,2,1,0:T(8,128)(2,1)S(1)} custom-call(s32[48]{0:T(128)S(1)} %get-tuple-element.18.particle, s32[24,4]{1,0:T(8,128)S(1)} %copy.23.page_table, s32[48]{0:T(128)S(1)} %get-tuple-element.19.lengths, bf16[4,12,40,128]{3,2,1,0:T(8,128)(2,1)} %all-to-all-done.blobs, bf16[96,16,512]{2,1,0:T(8,128)(2,1)} %bitcast.20, ...), custom_call_target="tpu_custom_call" | custom-call | flops 1 | bytes 1 | tf_op jit(solution)/shard_map/pallas_call | solution.py:207
  73.4 0.7 copy-done.5
  74.1 0.6 collective-permute-done.13.refs_0_
  74.7 2.3 %collective-permute-done.12.refs_2_.refs_9_ = bf16[256,1024]{1,0:T(8,128)(2,1)} collective-permute-done((bf16[256,1024]{1,0:T(8,128)(2,1)}, bf16[256,1024]{1,0:T(8,128)(2,1)}, u32[]{:S(2)}, u32[]{:S(2)}) %collective-permute-start.12) | collective-permute-done | bytes 524320 | tf_op jit(solution)/shard_map/ppermute | solution.py:650
  77.0 2.6 %collective-permute-start.17 = (bf16[256,1024]{1,0:T(8,128)(2,1)}, bf16[256,1024]{1,0:T(8,128)(2,1)}, u32[]{:S(2)}, u32[]{:S(2)}) collective-permute-start(bf16[256,1024]{1,0:T(8,128)(2,1)} %shard_map.164.refs_10_), channel_id=1, source_target_pairs={{0,4},{4,12},{12,8},{8,0},{1,5},{5,13},{13,9},{9,1},{2,6},{6,14},{... | collective-permute-start | bytes 1572872 | tf_op jit(solution)/shard_map/ppermute | solution.py:647
  79.6 1.5 %collective-permute-start.14 = (bf16[256,1024]{1,0:T(8,128)(2,1)}, bf16[256,1024]{1,0:T(8,128)(2,1)}, u32[]{:S(2)}, u32[]{:S(2)}) collective-permute-start(bf16[256,1024]{1,0:T(8,128)(2,1)} %shard_map.164.refs_10_), channel_id=1, source_target_pairs={{0,16},{16,0},{1,17},{17,1},{2,18},{18,2},{3,19},{19,3},{4,20},{20... | collective-permute-start | bytes 1572872 | tf_op jit(solution)/shard_map/ppermute | solution.py:650
  81.1 4.7 %collective-permute-done.15.refs_0_ = bf16[256,1024]{1,0:T(8,128)(2,1)S(1)} collective-permute-done((bf16[256,1024]{1,0:T(8,128)(2,1)}, bf16[256,1024]{1,0:T(8,128)(2,1)S(1)}, u32[]{:S(2)}, u32[]{:S(2)}) %collective-permute-start.15) | collective-permute-done | bytes 524320 | tf_op jit(solution)/shard_map/ppermute | solution.py:647
  85.8 0.8 copy-done.6
  86.6 0.5 collective-permute-start.16
  87.1 0.0 collective-permute-done.11.refs_7_
  87.1 1.0 copy-done.9
  88.1 8.9 %shard_map.161 = (f32[1024,1024]{1,0:T(8,128)}, f32[8,128]{1,0:T(8,128)S(1)}) custom-call(s32[4]{0:T(128)S(1)} %pad_add_fusion.me, bf16[512,1024]{1,0:T(8,128)(2,1)} %get-tuple-element.21.refs_0_, bf16[512,1024]{1,0:T(8,128)(2,1)} %get-tuple-element.22.refs_1_, bf16[512,1024]{1,0:T(8,128)(2,1)} %shard_map.159.refs_2_, bf16[512,1024]{1,0:T(8,128)(2,1)} %shard_map.160.refs_3_, ...), custom_call_target="tpu_custom_call" | custom-call | flops 1 | bytes 1 | tf_op jit(solution)/shard_map/pallas_call | solution.py:604
  97.0 0.0 copy-start.11
  97.0 0.6 copy-done.11
  97.6 1.6 %collective-permute-start.18 = (bf16[256,1024]{1,0:T(8,128)(2,1)}, bf16[256,1024]{1,0:T(8,128)(2,1)S(1)}, u32[]{:S(2)}, u32[]{:S(2)}) collective-permute-start(bf16[256,1024]{1,0:T(8,128)(2,1)} %shard_map.166.refs_14_), channel_id=1, source_target_pairs={{0,16},{16,0},{1,17},{17,1},{2,18},{18,2},{3,19},{19,3},{4,20},{20... | collective-permute-start | bytes 1572872 | tf_op jit(solution)/shard_map/ppermute | solution.py:650
  99.2 4.9 %all-to-all-start.1 = ((bf16[4,12,32,128]{3,2,1,0:T(8,128)(2,1)}), bf16[4,12,32,128]{3,2,1,0:T(8,128)(2,1)S(1)}, u32[]{:S(2)}, u32[]{:S(2)}) async-start(bf16[4,12,32,128]{3,2,1,0:T(8,128)(2,1)} %shard_map.162), calls=%async_computation.1 | async-start | bytes 786432 | tf_op jit(solution)/shard_map/all_to_all | solution.py:264
  104.2 1.7 %collective-permute-done.16.refs_13_ = bf16[256,1024]{1,0:T(8,128)(2,1)S(1)} collective-permute-done((bf16[256,1024]{1,0:T(8,128)(2,1)}, bf16[256,1024]{1,0:T(8,128)(2,1)S(1)}, u32[]{:S(2)}, u32[]{:S(2)}) %collective-permute-start.16) | collective-permute-done | bytes 524320 | tf_op jit(solution)/shard_map/ppermute | solution.py:650
  105.9 8.0 %shard_map.167 = (f32[1024,1024]{1,0:T(8,128)S(1)}, f32[8,128]{1,0:T(8,128)}, bf16[1024,256]{1,0:T(8,128)(2,1)S(1)}) custom-call(s32[4]{0:T(128)S(1)} %pad_add_fusion.me, bf16[512,1024]{1,0:T(8,128)(2,1)} %get-tuple-element.21.refs_0_, bf16[512,1024]{1,0:T(8,128)(2,1)} %get-tuple-element.22.refs_1_, bf16[512,1024]{1,0:T(8,128)(2,1)} %shard_map.159.refs_2_, ...), custom_call_target="tpu_custom_call" | custom-call | flops 1 | bytes 1 | tf_op jit(solution)/shard_map/pallas_call | solution.py:604
  113.9 0.7 collective-permute-done.18.refs_0_
  114.6 1.7 %shard_map.168 = (f32[1,512]{1,0:T(1,128)S(1)}, f32[1,512]{1,0:T(1,128)S(1)}, f32[1,512]{1,0:T(1,128)S(1)}) custom-call(s32[4]{0:T(128)S(1)} %pad_add_fusion.me, bf16[1024,256]{1,0:T(8,128)(2,1)S(1)} %get-tuple-element.27.x, f32[1024,1024]{1,0:T(8,128)S(1)} %get-tuple-element.28.acc, bf16[256,1024]{1,0:T(8,128)(2,1)S(1)} %collective-permute-done.18.refs_0_, ...), custom_call_target="tpu_custom_call" | custom-call | flops 1 | bytes 1 | tf_op jit(solution)/shard_map/pallas_call | solution.py:575
  116.4 0.1 collective-permute-start.21
  116.4 1.6 %collective-permute-start.20 = (f32[1,512]{1,0:T(1,128)S(1)}, f32[1,512]{1,0:T(1,128)S(1)}, u32[]{:S(2)}, u32[]{:S(2)}) collective-permute-start(f32[1,512]{1,0:T(1,128)S(1)} %get-tuple-element.31), channel_id=1, source_target_pairs={{0,2},{2,0},{1,3},{3,1},{4,6},{6,4},{5,7},{7,5},{8,10},{10,8},{9,1... | collective-permute-start | bytes 6152 | tf_op jit(solution)/shard_map/ppermute | solution.py:726
  118.0 0.3 collective-permute-start.19
  118.3 1.1 collective-permute-done.21
  119.4 0.7 collective-permute-done.20
  120.1 0.6 add_add_fusion
  120.7 1.6 %shard_map.163 = bf16[24,4096]{1,0:T(8,128)(2,1)} custom-call(s32[24]{0:T(128)S(1)} %get-tuple-element.17.pick, bf16[4,12,32,128]{3,2,1,0:T(8,128)(2,1)S(1)} %all-to-all-done.1.parts, f32[8,128]{1,0:T(8,128)S(1)} %copy-done.12), custom_call_target="tpu_custom_call" | custom-call | flops 1 | bytes 1 | tf_op jit(solution)/shard_map/pallas_call | solution.py:237
  (52 shorter events, 0.1 us)
Async XLA Ops:
  0.7 1.6 %copy-start = (bf16[512,2048]{1,0:T(8,128)(2,1)S(1)}, bf16[512,2048]{1,0:T(8,128)(2,1)}, u32[]{:S(2)}) copy-start(bf16[512,2048]{1,0:T(8,128)(2,1)} %refs_8_.1) | copy-start | bytes 6291460
  2.3 1.8 %copy-start.4 = (bf16[512,2048]{1,0:T(8,128)(2,1)S(1)}, bf16[512,2048]{1,0:T(8,128)(2,1)}, u32[]{:S(2)}) copy-start(bf16[512,2048]{1,0:T(8,128)(2,1)} %x.3) | copy-start | bytes 6291460
  2.9 2.1 %collective-permute-start = (bf16[256,1024]{1,0:T(8,128)(2,1)S(1)}, bf16[256,1024]{1,0:T(8,128)(2,1)S(1)}, u32[]{:S(2)}, u32[]{:S(2)}) collective-permute-start(bf16[256,1024]{1,0:T(8,128)(2,1)S(1)} %shard_map.149), channel_id=1, source_target_pairs={{0,1},{1,0},{2,3},{3,2},{4,5},{5,4},{6,7},{7,6},{8,9},{9,8},{10,11... | collective-permute-start | bytes 1572872 | tf_op jit(solution)/shard_map/ppermute | solution.py:654
  4.1 5.5 %copy-start.1 = (bf16[512,2048]{1,0:T(8,128)(2,1)S(1)}, bf16[512,2048]{1,0:T(8,128)(2,1)}, u32[]{:S(2)}) copy-start(bf16[512,2048]{1,0:T(8,128)(2,1)} %refs_8_.1) | copy-start | bytes 6291460
  4.8 6.8 %copy-start.15 = (f32[4096]{0:T(1024)S(1)}, f32[4096]{0:T(1024)}, u32[]{:S(2)}) copy-start(f32[4096]{0:T(1024)} %param.23) | copy-start | bytes 49156
  5.1 27.6 %collective-permute-start.3 = (bf16[512,1024]{1,0:T(8,128)(2,1)S(1)}, bf16[512,1024]{1,0:T(8,128)(2,1)}, u32[]{:S(2)}, u32[]{:S(2)}) collective-permute-start(bf16[512,1024]{1,0:T(8,128)(2,1)S(1)} %shard_map.154.refs_3_), channel_id=1, source_target_pairs={{0,4},{4,12},{12,8},{8,0},{1,5},{5,13},{13,9},{9,1},{2,6},{6,14},{... | collective-permute-start | bytes 3145736 | tf_op jit(solution)/shard_map/ppermute | solution.py:647
  8.0 3.6 %collective-permute-start.1 = (f32[4,128]{1,0:T(4,128)S(1)}, f32[4,128]{1,0:T(4,128)S(1)}, u32[]{:S(2)}, u32[]{:S(2)}) collective-permute-start(f32[4,128]{1,0:T(4,128)S(1)} %shard_map.153.refs_2_.refs_0_), channel_id=1, source_target_pairs={{0,2},{2,0},{1,3},{3,1},{4,6},{6,4},{5,7},{7,5},{8,10},{10,8},{9,1... | collective-permute-start | bytes 6152 | tf_op jit(solution)/shard_map/ppermute | solution.py:659
  14.2 23.6 %copy-start.10 = (bf16[1,24,4096]{2,1,0:T(8,128)(2,1)S(1)}, bf16[1,24,4096]{2,1,0:T(8,128)(2,1)}, u32[]{:S(2)}) copy-start(bf16[1,24,4096]{2,1,0:T(8,128)(2,1)} %param.14) | copy-start | bytes 589828
  14.2 23.6 %copy-start.13 = (bf16[1,24,512]{2,1,0:T(8,128)(2,1)S(1)}, bf16[1,24,512]{2,1,0:T(8,128)(2,1)}, u32[]{:S(2)}) copy-start(bf16[1,24,512]{2,1,0:T(8,128)(2,1)} %param.15) | copy-start | bytes 73732
  14.2 23.6 %copy-start.14 = (bf16[1,24,512]{2,1,0:T(8,128)(2,1)S(1)}, bf16[1,24,512]{2,1,0:T(8,128)(2,1)}, u32[]{:S(2)}) copy-start(bf16[1,24,512]{2,1,0:T(8,128)(2,1)} %param.16) | copy-start | bytes 73732
  14.2 23.6 %copy-start.18 = (s32[96]{0:T(128)S(1)}, s32[96]{0:T(128)}, u32[]{:S(2)}) copy-start(s32[96]{0:T(128)} %ancestry.1) | copy-start | bytes 1156
  14.2 23.6 %copy-start.19 = (s32[96]{0:T(128)S(1)}, s32[96]{0:T(128)}, u32[]{:S(2)}) copy-start(s32[96]{0:T(128)} %lengths.1) | copy-start | bytes 1156
  14.2 20.0 %collective-permute-start.5 = (bf16[512,1024]{1,0:T(8,128)(2,1)}, bf16[512,1024]{1,0:T(8,128)(2,1)S(1)}, u32[]{:S(2)}, u32[]{:S(2)}) collective-permute-start(bf16[512,1024]{1,0:T(8,128)(2,1)} %get-tuple-element.21.refs_0_), channel_id=1, source_target_pairs={{0,1},{1,0},{2,3},{3,2},{4,5},{5,4},{6,7},{7,6},{8,9},{9,8},{10,11... | collective-permute-start | bytes 3145736 | tf_op jit(solution)/shard_map/ppermute | solution.py:667
  14.3 19.9 %collective-permute-start.6 = (bf16[512,1024]{1,0:T(8,128)(2,1)}, bf16[512,1024]{1,0:T(8,128)(2,1)S(1)}, u32[]{:S(2)}, u32[]{:S(2)}) collective-permute-start(bf16[512,1024]{1,0:T(8,128)(2,1)} %get-tuple-element.22.refs_1_), channel_id=1, source_target_pairs={{0,1},{1,0},{2,3},{3,2},{4,5},{5,4},{6,7},{7,6},{8,9},{9,8},{10,11... | collective-permute-start | bytes 3145736 | tf_op jit(solution)/shard_map/ppermute | solution.py:667
  14.8 3.6 %collective-permute-start.4 = (bf16[256,1024]{1,0:T(8,128)(2,1)S(1)}, bf16[256,1024]{1,0:T(8,128)(2,1)S(1)}, u32[]{:S(2)}, u32[]{:S(2)}) collective-permute-start(bf16[256,1024]{1,0:T(8,128)(2,1)S(1)} %shard_map.156), channel_id=1, source_target_pairs={{0,1},{1,0},{2,3},{3,2},{4,5},{5,4},{6,7},{7,6},{8,9},{9,8},{10,11... | collective-permute-start | bytes 1572872 | tf_op jit(solution)/shard_map/ppermute | solution.py:654
  14.8 34.4 %collective-permute-start.2 = (bf16[512,1024]{1,0:T(8,128)(2,1)}, bf16[512,1024]{1,0:T(8,128)(2,1)}, u32[]{:S(2)}, u32[]{:S(2)}) collective-permute-start(bf16[512,1024]{1,0:T(8,128)(2,1)} %get-tuple-element.21.refs_0_), channel_id=1, source_target_pairs={{0,2},{2,0},{1,3},{3,1},{4,6},{6,4},{5,7},{7,5},{8,10},{10,8},{9,1... | collective-permute-start | bytes 3145736 | tf_op jit(solution)/shard_map/ppermute | solution.py:663
  18.4 23.2 %copy-start.8 = (bf16[256,1024]{1,0:T(8,128)(2,1)}, bf16[256,1024]{1,0:T(8,128)(2,1)S(1)}, u32[]{:S(2)}) copy-start(bf16[256,1024]{1,0:T(8,128)(2,1)S(1)} %collective-permute-done.4.refs_0_.refs_10_) | copy-start | bytes 1572868
  18.4 44.7 %collective-permute-start.9 = (bf16[512,1024]{1,0:T(8,128)(2,1)}, bf16[512,1024]{1,0:T(8,128)(2,1)}, u32[]{:S(2)}, u32[]{:S(2)}) collective-permute-start(bf16[512,1024]{1,0:T(8,128)(2,1)} %get-tuple-element.22.refs_1_), channel_id=1, source_target_pairs={{0,2},{2,0},{1,3},{3,1},{4,6},{6,4},{5,7},{7,5},{8,10},{10,8},{9,1... | collective-permute-start | bytes 3145736 | tf_op jit(solution)/shard_map/ppermute | solution.py:663
  32.6 30.5 %collective-permute-start.8 = (bf16[512,1024]{1,0:T(8,128)(2,1)}, bf16[512,1024]{1,0:T(8,128)(2,1)}, u32[]{:S(2)}, u32[]{:S(2)}) collective-permute-start(bf16[512,1024]{1,0:T(8,128)(2,1)} %collective-permute-done.3.source.refs_11_), channel_id=1, source_target_pairs={{0,16},{16,0},{1,17},{17,1},{2,18},{18,2},{3,19},{19,3},{4,20},{20... | collective-permute-start | bytes 3145736 | tf_op jit(solution)/shard_map/ppermute | solution.py:650
  34.2 7.4 %copy-start.2 = (bf16[512,1024]{1,0:T(8,128)(2,1)}, bf16[512,1024]{1,0:T(8,128)(2,1)S(1)}, u32[]{:S(2)}) copy-start(bf16[512,1024]{1,0:T(8,128)(2,1)S(1)} %collective-permute-done.5.refs_1_.refs_4_) | copy-start | bytes 3145732
  34.2 7.4 %copy-start.3 = (bf16[512,1024]{1,0:T(8,128)(2,1)}, bf16[512,1024]{1,0:T(8,128)(2,1)S(1)}, u32[]{:S(2)}) copy-start(bf16[512,1024]{1,0:T(8,128)(2,1)S(1)} %collective-permute-done.6.refs_2_.refs_5_) | copy-start | bytes 3145732
  37.0 26.1 %collective-permute-start.7 = (bf16[256,1024]{1,0:T(8,128)(2,1)S(1)}, bf16[256,1024]{1,0:T(8,128)(2,1)}, u32[]{:S(2)}, u32[]{:S(2)}) collective-permute-start(bf16[256,1024]{1,0:T(8,128)(2,1)S(1)} %get-tuple-element.23), channel_id=1, source_target_pairs={{0,4},{4,12},{12,8},{8,0},{1,5},{5,13},{13,9},{9,1},{2,6},{6,14},{... | collective-permute-start | bytes 1572872 | tf_op jit(solution)/shard_map/ppermute | solution.py:647
  41.6 26.3 %all-to-all-start = ((bf16[4,12,40,128]{3,2,1,0:T(8,128)(2,1)}), bf16[4,12,40,128]{3,2,1,0:T(8,128)(2,1)}, u32[]{:S(2)}, u32[]{:S(2)}) async-start(bf16[4,12,40,128]{3,2,1,0:T(8,128)(2,1)} %get-tuple-element.20.refs_1_), calls=%async_computation | async-start | bytes 983040 | tf_op jit(solution)/shard_map/all_to_all | solution.py:264
  46.4 28.3 %collective-permute-start.13 = (bf16[256,1024]{1,0:T(8,128)(2,1)}, bf16[256,1024]{1,0:T(8,128)(2,1)}, u32[]{:S(2)}, u32[]{:S(2)}) collective-permute-start(bf16[256,1024]{1,0:T(8,128)(2,1)} %get-tuple-element.25), channel_id=1, source_target_pairs={{0,4},{4,12},{12,8},{8,0},{1,5},{5,13},{13,9},{9,1},{2,6},{6,14},{... | collective-permute-start | bytes 1572872 | tf_op jit(solution)/shard_map/ppermute | solution.py:647
  63.1 2.1 %copy-start.21 = (s32[24,4]{0,1:T(4,128)S(1)}, s32[24,4]{0,1:T(4,128)}, u32[]{:S(2)}) copy-start(s32[24,4]{0,1:T(4,128)} %param.19) | copy-start | bytes 1156
  63.1 13.9 %collective-permute-start.12 = (bf16[256,1024]{1,0:T(8,128)(2,1)}, bf16[256,1024]{1,0:T(8,128)(2,1)}, u32[]{:S(2)}, u32[]{:S(2)}) collective-permute-start(bf16[256,1024]{1,0:T(8,128)(2,1)} %shard_map.158.refs_1_.refs_8_), channel_id=1, source_target_pairs={{0,16},{16,0},{1,17},{17,1},{2,18},{18,2},{3,19},{19,3},{4,20},{20... | collective-permute-start | bytes 1572872 | tf_op jit(solution)/shard_map/ppermute | solution.py:650
  64.7 22.3 %collective-permute-start.10 = (bf16[512,1024]{1,0:T(8,128)(2,1)}, bf16[512,1024]{1,0:T(8,128)(2,1)}, u32[]{:S(2)}, u32[]{:S(2)}) collective-permute-start(bf16[512,1024]{1,0:T(8,128)(2,1)} %shard_map.159.refs_2_), channel_id=1, source_target_pairs={{0,1},{1,0},{2,3},{3,2},{4,5},{5,4},{6,7},{7,6},{8,9},{9,8},{10,11... | collective-permute-start | bytes 3145736 | tf_op jit(solution)/shard_map/ppermute | solution.py:704
  64.7 22.3 %collective-permute-start.11 = (bf16[512,1024]{1,0:T(8,128)(2,1)}, bf16[512,1024]{1,0:T(8,128)(2,1)}, u32[]{:S(2)}, u32[]{:S(2)}) collective-permute-start(bf16[512,1024]{1,0:T(8,128)(2,1)} %shard_map.160.refs_3_), channel_id=1, source_target_pairs={{0,1},{1,0},{2,3},{3,2},{4,5},{5,4},{6,7},{7,6},{8,9},{9,8},{10,11... | collective-permute-start | bytes 3145736 | tf_op jit(solution)/shard_map/ppermute | solution.py:704
  65.3 20.5 %collective-permute-start.15 = (bf16[256,1024]{1,0:T(8,128)(2,1)}, bf16[256,1024]{1,0:T(8,128)(2,1)S(1)}, u32[]{:S(2)}, u32[]{:S(2)}) collective-permute-start(bf16[256,1024]{1,0:T(8,128)(2,1)} %shard_map.158.refs_1_.refs_8_), channel_id=1, source_target_pairs={{0,4},{4,12},{12,8},{8,0},{1,5},{5,13},{13,9},{9,1},{2,6},{6,14},{... | collective-permute-start | bytes 1572872 | tf_op jit(solution)/shard_map/ppermute | solution.py:647
  73.4 0.8 copy-start.5
  77.0 20.6 %collective-permute-start.17 = (bf16[256,1024]{1,0:T(8,128)(2,1)}, bf16[256,1024]{1,0:T(8,128)(2,1)}, u32[]{:S(2)}, u32[]{:S(2)}) collective-permute-start(bf16[256,1024]{1,0:T(8,128)(2,1)} %shard_map.164.refs_10_), channel_id=1, source_target_pairs={{0,4},{4,12},{12,8},{8,0},{1,5},{5,13},{13,9},{9,1},{2,6},{6,14},{... | collective-permute-start | bytes 1572872 | tf_op jit(solution)/shard_map/ppermute | solution.py:647
  79.6 24.6 %collective-permute-start.14 = (bf16[256,1024]{1,0:T(8,128)(2,1)}, bf16[256,1024]{1,0:T(8,128)(2,1)}, u32[]{:S(2)}, u32[]{:S(2)}) collective-permute-start(bf16[256,1024]{1,0:T(8,128)(2,1)} %shard_map.164.refs_10_), channel_id=1, source_target_pairs={{0,16},{16,0},{1,17},{17,1},{2,18},{18,2},{3,19},{19,3},{4,20},{20... | collective-permute-start | bytes 1572872 | tf_op jit(solution)/shard_map/ppermute | solution.py:650
  85.8 0.8 copy-start.6
  86.6 19.3 %collective-permute-start.16 = (bf16[256,1024]{1,0:T(8,128)(2,1)}, bf16[256,1024]{1,0:T(8,128)(2,1)S(1)}, u32[]{:S(2)}, u32[]{:S(2)}) collective-permute-start(bf16[256,1024]{1,0:T(8,128)(2,1)} %shard_map.165.refs_12_), channel_id=1, source_target_pairs={{0,16},{16,0},{1,17},{17,1},{2,18},{18,2},{3,19},{19,3},{4,20},{20... | collective-permute-start | bytes 1572872 | tf_op jit(solution)/shard_map/ppermute | solution.py:650
  87.1 1.0 copy-start.9
  97.0 0.6 copy-start.11
  97.6 6.6 %copy-start.20 = (bf16[2048,2]{0,1:T(2,128)(2,1)S(1)}, bf16[2048,2]{0,1:T(2,128)(2,1)}, u32[]{:S(2)}) copy-start(bf16[2048,2]{0,1:T(2,128)(2,1)} %param.26) | copy-start | bytes 24580
  97.6 8.3 %copy-start.7 = (bf16[256,1024]{1,0:T(8,128)(2,1)S(1)}, bf16[256,1024]{1,0:T(8,128)(2,1)}, u32[]{:S(2)}) copy-start(bf16[256,1024]{1,0:T(8,128)(2,1)} %shard_map.165.refs_12_) | copy-start | bytes 1572868
  97.6 17.0 %collective-permute-start.18 = (bf16[256,1024]{1,0:T(8,128)(2,1)}, bf16[256,1024]{1,0:T(8,128)(2,1)S(1)}, u32[]{:S(2)}, u32[]{:S(2)}) collective-permute-start(bf16[256,1024]{1,0:T(8,128)(2,1)} %shard_map.166.refs_14_), channel_id=1, source_target_pairs={{0,16},{16,0},{1,17},{17,1},{2,18},{18,2},{3,19},{19,3},{4,20},{20... | collective-permute-start | bytes 1572872 | tf_op jit(solution)/shard_map/ppermute | solution.py:650
  99.2 21.4 %all-to-all-start.1 = ((bf16[4,12,32,128]{3,2,1,0:T(8,128)(2,1)}), bf16[4,12,32,128]{3,2,1,0:T(8,128)(2,1)S(1)}, u32[]{:S(2)}, u32[]{:S(2)}) async-start(bf16[4,12,32,128]{3,2,1,0:T(8,128)(2,1)} %shard_map.162), calls=%async_computation.1 | async-start | bytes 786432 | tf_op jit(solution)/shard_map/all_to_all | solution.py:264
  105.9 8.7 %copy-start.16 = (f32[2048]{0:T(1024)S(1)}, f32[2048]{0:T(1024)}, u32[]{:S(2)}) copy-start(f32[2048]{0:T(1024)} %param.25) | copy-start | bytes 24580
  105.9 8.7 %copy-start.17 = (f32[2]{0:T(128)S(1)}, f32[2]{0:T(128)}, u32[]{:S(2)}) copy-start(f32[2]{0:T(128)} %refs_3_.1) | copy-start | bytes 28
  114.6 6.1 %copy-start.12 = (f32[8,128]{1,0:T(8,128)S(1)}, f32[8,128]{1,0:T(8,128)}, u32[]{:S(2)}) copy-start(f32[8,128]{1,0:T(8,128)} %copy-done.11) | copy-start | bytes 12292
  116.4 3.1 %collective-permute-start.21 = (f32[1,512]{1,0:T(1,128)S(1)}, f32[1,512]{1,0:T(1,128)S(1)}, u32[]{:S(2)}, u32[]{:S(2)}) collective-permute-start(f32[1,512]{1,0:T(1,128)S(1)} %get-tuple-element.30), channel_id=1, source_target_pairs={{0,3},{1,2},{2,1},{3,0},{4,7},{5,6},{6,5},{7,4},{8,11},{9,10},{10,... | collective-permute-start | bytes 6152 | tf_op jit(solution)/shard_map/ppermute | solution.py:727
  116.4 3.7 %collective-permute-start.20 = (f32[1,512]{1,0:T(1,128)S(1)}, f32[1,512]{1,0:T(1,128)S(1)}, u32[]{:S(2)}, u32[]{:S(2)}) collective-permute-start(f32[1,512]{1,0:T(1,128)S(1)} %get-tuple-element.31), channel_id=1, source_target_pairs={{0,2},{2,0},{1,3},{3,1},{4,6},{6,4},{5,7},{7,5},{8,10},{10,8},{9,1... | collective-permute-start | bytes 6152 | tf_op jit(solution)/shard_map/ppermute | solution.py:726
  118.0 2.1 %collective-permute-start.19 = (f32[1,512]{1,0:T(1,128)S(1)}, f32[1,512]{1,0:T(1,128)S(1)}, u32[]{:S(2)}, u32[]{:S(2)}) collective-permute-start(f32[1,512]{1,0:T(1,128)S(1)} %get-tuple-element.30), channel_id=1, source_target_pairs={{0,1},{1,0},{2,3},{3,2},{4,5},{5,4},{6,7},{7,6},{8,9},{9,8},{10,11... | collective-permute-start | bytes 6152 | tf_op jit(solution)/shard_map/ppermute | solution.py:724
